TPU v7x, 256 devices: a whole 4x4x8 slice. The times are simulated.
256 devices in a mesh: shard: 64 (over x, z, core), code: 4 (over y).
Axes of the slice: x: 4, y: 4, z: 8, core: 2. Of those that a mesh axis runs over, the one named last changes fastest.
Arguments:
- table_rows: float32 [1048576, 128], P(('shard', 'code')), as said below
- adagrad_sums: float32 [1048576, 128], P(('shard', 'code')), as said below
- lost_member: int32 [64], P('shard'), may hold values from 0 to 3, as said below
- code_weight: float32 [4], replicated, may hold values from 0.5 to 2, as said below
- new_owner: int32 [262144, 1], P(('shard', 'code')), may hold values from 0 to 63; in each aligned block of 1024 rows (0 to 1023, 1024 to 2047, ...) at most 32 rows name the same one
- pending_rows: int32 [131072], P(('shard', 'code')), may hold values from 0 to 4095
- pending_grads: float32 [131072, 128], P(('shard', 'code')), may hold values from -6 to 6
Outputs:
- moved_rows: float32 [524288, 128], P(('shard', 'code'))
- moved_sums: float32 [524288, 128], P(('shard', 'code'))
- parity_rows: float32 [131072, 128], P(('shard', 'code'))
- parity_sums: float32 [131072, 128], P(('shard', 'code'))
Inputs may be any that keep to these rules, and one draw needn't show every extreme that they name: `lost_member`: one lost member for each group. `code_weight`: positive. `table_rows`: in every group the parity member's block equals the sum over c < 3 of code_weight[c] times member c's block, except that the group's lost member's block holds unrelated values. `adagrad_sums`: coded as table_rows; positive in every member but the lost one. `new_owner`: at most 32 of one device's rows name the same owner.
All inputs are finite; a program needn't handle non-finite values.
Results may differ from a plain program's by a relative error of at most 0.0003.
Values sent between devices are 32-bit elements; how exact they have to be, the bound alone decides.
No kernel may reach another device: no remote copies, remote signals or barrier semaphores. Data moves between devices by JAX's collectives and lax.ppermute only.
A program may use at most 64 MiB of HBM per device.

v0:
```python
import jax
import jax.numpy as jnp
from jax import lax
from jax.sharding import PartitionSpec as P

step_size = 0.5
epsilon = 1e-08


def decode_weights(code_weight, lost_member):
    which = lost_member[0]
    data_weight = code_weight[:3]
    places = jnp.arange(3)
    lost_weight = jnp.sum(jnp.where(places == which, data_weight, 0.0))
    parity_lost = which == 3
    divisor = jnp.where(parity_lost, 1.0, lost_weight)
    solved = jnp.where(parity_lost, data_weight, -data_weight / divisor)
    solved = jnp.where(places == which, 0.0, solved)
    parity_part = jnp.where(parity_lost, 0.0, 1.0 / divisor)
    return jnp.concatenate([solved, parity_part[None]])


def pending_sum(row_ids, grads, first, count):
    targets = (first + jnp.arange(count)).astype(jnp.float32)
    hits = (row_ids[None, :] == targets[:, None]).astype(jnp.float32)
    return jnp.dot(hits, grads, precision=lax.Precision.HIGHEST, preferred_element_type=jnp.float32)


def slot_rows(owner, rows, capacity, shards):
    earlier = jnp.tril(owner[:, None] == owner[None, :], -1)
    rank = jnp.sum(earlier.astype(jnp.int32), axis=1)
    place = owner * capacity + rank
    empty = jnp.zeros((shards * capacity, rows.shape[1]), rows.dtype)
    return empty.at[place].set(rows)


def per_device(
    table_rows, adagrad_sums, lost_member, code_weight, new_owner, pending_rows, pending_grads
):
    member = lax.axis_index("code")
    members = lax.axis_size("code")
    shards = lax.axis_size("shard")
    block_rows = table_rows.shape[0]
    share_rows = block_rows // members
    capacity = max(2, (2 * share_rows + shards - 1) // shards)
    places = jnp.arange(members)
    own_weight = jnp.sum(jnp.where(places == member, decode_weights(code_weight, lost_member), 0.0))
    term_rows = own_weight * table_rows
    term_sums = own_weight * adagrad_sums
    first = member * share_rows
    group_ids, group_grads = (
        lax.all_gather(pending_rows.astype(jnp.float32), "code", axis=0, tiled=True),
        lax.all_gather(pending_grads, "code", axis=0, tiled=True),
    )
    whole_rows, whole_sums = lax.psum((term_rows, term_sums), "code")
    mine_rows = lax.dynamic_slice_in_dim(whole_rows, first, share_rows, 0)
    mine_sums = lax.dynamic_slice_in_dim(whole_sums, first, share_rows, 0)
    totals = pending_sum(group_ids, group_grads, first, share_rows)
    new_sums = mine_sums + totals * totals
    new_rows = mine_rows - step_size * totals / (jnp.sqrt(new_sums) + epsilon)
    owner = new_owner[:, 0]
    outgoing_rows = slot_rows(owner, new_rows, capacity, shards)
    outgoing_sums = slot_rows(owner, new_sums, capacity, shards)
    moved_rows, moved_sums = (
        lax.all_to_all(outgoing_rows, "shard", split_axis=0, concat_axis=0, tiled=True),
        lax.all_to_all(outgoing_sums, "shard", split_axis=0, concat_axis=0, tiled=True),
    )
    member_weight = jnp.sum(jnp.where(places == member, code_weight, 0.0))
    parity_rows, parity_sums = (
        lax.psum_scatter(member_weight * moved_rows, "code", scatter_dimension=0, tiled=True),
        lax.psum_scatter(member_weight * moved_sums, "code", scatter_dimension=0, tiled=True),
    )
    return (moved_rows, moved_sums, parity_rows, parity_sums)


def solution(mesh):
    in_specs = (
        P(("shard", "code"), None),
        P(("shard", "code"), None),
        P("shard"),
        P(),
        P(("shard", "code"), None),
        P(("shard", "code")),
        P(("shard", "code"), None),
    )
    out_specs = (
        P(("shard", "code"), None),
        P(("shard", "code"), None),
        P(("shard", "code"), None),
        P(("shard", "code"), None),
    )
    return jax.shard_map(
        per_device, mesh=mesh, in_specs=in_specs, out_specs=out_specs, check_vma=False
    )
```

profile of v0, /device:TPU:32, one launch (start us, length us, event | category | flops | bytes accessed | tf_op | source)
XLA Modules:
  0.0 257.1 jit_solution(17790593953733834289)
XLA Ops:
  7.2 0.7 all-gather.3.cloned.1.call-update
  8.6 1.3 fusion.19
  10.6 0.7 compare_select_fusion.1
  11.2 0.7 fusion.17
  11.9 5.1 %broadcast_multiply_fusion = (f32[4096,128]{1,0:T(8,128)}, f32[4096,128]{1,0:T(8,128)}) fusion(f32[4096,128]{1,0:T(8,128)} %param.8, f32[]{:T(128)} %fusion.17, f32[4096,128]{1,0:T(8,128)} %param.7), kind=kLoop, calls=%fused_computation.9 | loop fusion | flops 1048576 | bytes 8388612 | tf_op jit(solution)/shard_map/mul | solution.py:49
  17.0 0.6 copy-done.1
  17.7 11.2 %all-gather = f32[4,1,512]{2,1,0:T(1,128)S(1)} all-gather(f32[1,1,512]{2,1,0:T(1,128)S(1)} %bitcast.20), channel_id=1, replica_groups=mesh['shard'=64,'code'=4] {'code'}, dimensions={0}, use_global_device_ids=true | all-gather | bytes 10240 | tf_op jit(solution)/shard_map/all_gather | solution.py:52
  28.9 1.3 convert_reduce_fusion
  30.2 8.8 %all-gather.3.cloned.1.call-done = f32[2048,128]{1,0:T(8,128)} async-done(((f32[512,128]{1,0:T(8,128)}), f32[2048,128]{1,0:T(8,128)}) %all-gather.3.cloned.1.call-update) | async-done | bytes 1048592 | tf_op jit(solution)/shard_map/all_gather | solution.py:53
  39.0 4.8 %fusion = f32[1024,128]{1,0:T(8,128)S(1)} fusion(f32[2048,128]{1,0:T(8,128)} %all-gather.3.cloned.1.call-done, f32[2048]{0:T(1024)S(1)} %bitcast.19, f32[1024]{0:T(1024)S(1)} %add_convert_fusion), kind=kOutput, calls=%fused_computation.2 | convolution fusion | flops 3223322624 | bytes 1585152 | tf_op jit(solution)/shard_map/dot_general | solution.py:26
  43.9 96.1 %all-reduce.3.cloned.1.call-done = (f32[4096,128]{1,0:T(8,128)}, f32[4096,128]{1,0:T(8,128)}) async-done(((f32[4096,128]{1,0:T(8,128)}, f32[4096,128]{1,0:T(8,128)}), (f32[4096,128]{1,0:T(8,128)}, f32[4096,128]{1,0:T(8,128)})) %all-reduce.3.cloned.1.call-update) | async-done | bytes 4194320 | tf_op jit(solution)/shard_map/psum | solution.py:55
  140.0 4.5 %scatter_custom_fusion.1 = f32[2048,128]{1,0:T(8,128)} fusion(s32[1024]{0:T(1024)S(1)} %bitcast.22, f32[]{:T(128)} %constant.13.clone.1, f32[1024,128]{1,0:T(8,128)S(1)} %fusion, f32[4096,128]{1,0:T(8,128)} %get-tuple-element.5, s32[]{:T(128)S(6)} %select_n.53, s32[]{:T(128)} %constant.6.clone.1), kind=kCustom, calls=%fused_computation.21 | custom fusion | flops 262144 | bytes 2098180 | tf_op jit(solution)/shard_map/scatter | solution.py:34
  144.5 10.5 %all-to-all-start.1 = ((f32[64,32,128]{2,1,0:T(8,128)}), f32[64,32,128]{2,1,0:T(8,128)S(1)}, u32[]{:S(2)}, u32[]{:S(2)}) async-start(f32[64,32,128]{2,1,0:T(8,128)} %bitcast.9), calls=%async_computation.1 | async-start | bytes 2097152 | tf_op jit(solution)/shard_map/all_to_all | solution.py:66
  155.0 0.6 fusion.18
  155.6 4.8 %scatter_custom_fusion = f32[2048,128]{1,0:T(8,128)} fusion(s32[1024]{0:T(1024)S(1)} %bitcast.23, f32[1024,128]{1,0:T(8,128)S(1)} %fusion, f32[4096,128]{1,0:T(8,128)} %get-tuple-element.4, s32[]{:T(128)S(6)} %select_n.53, s32[]{:T(128)} %constant.6.clone.1, f32[]{:T(128)} %constant.13.clone.1, f32[]{:T(128)} %constant.33.clone.1, f32[]{:T(128)} %constant.32.clone.1, ...), kind=kCustom, calls=%fused_computation.13 | custom fusion | flops 786432 | bytes 2623492 | tf_op jit(solution)/shard_map/scatter | solution.py:34
  160.4 22.4 %all-to-all-done.1 = f32[64,32,128]{2,1,0:T(8,128)S(1)} async-done(((f32[64,32,128]{2,1,0:T(8,128)}), f32[64,32,128]{2,1,0:T(8,128)S(1)}, u32[]{:S(2)}, u32[]{:S(2)}) %all-to-all-start.1) | async-done | bytes 1048608 | tf_op jit(solution)/shard_map/all_to_all | solution.py:66
  182.9 6.9 %all-to-all-start = ((f32[64,32,128]{2,1,0:T(8,128)}), f32[64,32,128]{2,1,0:T(8,128)S(1)}, u32[]{:S(2)}, u32[]{:S(2)}) async-start(f32[64,32,128]{2,1,0:T(8,128)} %bitcast.7), calls=%async_computation | async-start | bytes 2097152 | tf_op jit(solution)/shard_map/all_to_all | solution.py:65
  189.8 1.7 broadcast_multiply_fusion.2
  191.5 26.1 %all-to-all-done = f32[64,32,128]{2,1,0:T(8,128)S(1)} async-done(((f32[64,32,128]{2,1,0:T(8,128)}), f32[64,32,128]{2,1,0:T(8,128)S(1)}, u32[]{:S(2)}, u32[]{:S(2)}) %all-to-all-start) | async-done | bytes 1048608 | tf_op jit(solution)/shard_map/all_to_all | solution.py:65
  217.6 1.7 broadcast_multiply_fusion.3
  219.3 0.4 reduce-scatter.5.cloned.1.call-done
  219.8 28.8 %reduce-scatter.3.cloned.1.call-done = f32[512,128]{1,0:T(8,128)} async-done(((f32[2048,128]{1,0:T(8,128)}), f32[512,128]{1,0:T(8,128)}) %reduce-scatter.3.cloned.1.call-update) | async-done | bytes 262160 | tf_op jit(solution)/shard_map/reduce_scatter | solution.py:70
  248.6 1.0 copy.16
  249.6 1.0 copy.17
  (16 shorter events, 0.2 us)
Async XLA Ops:
  7.2 31.9 %all-gather.3.cloned.1.call-start = ((), (), s32[]{:S(2)}) async-start(), calls=%async_computation.4 | async-start | bytes 1310720 | tf_op jit(solution)/shard_map/all_gather | solution.py:53
  7.9 132.1 %all-reduce.3.cloned.1.call-start = ((), (), s32[]{:S(2)}) async-start(), calls=%async_computation.7 | async-start | bytes 8388608 | tf_op jit(solution)/shard_map/psum | solution.py:55
  17.0 0.7 copy-start.1
  17.0 11.9 %copy-start = (s32[1024,1]{0,1:T(1,128)S(1)}, s32[1024,1]{0,1:T(1,128)}, u32[]{:S(2)}) copy-start(s32[1024,1]{0,1:T(1,128)} %param.11) | copy-start | bytes 12292
  140.0 15.0 %copy-start.2 = (f32[4]{0:T(128)S(1)}, f32[4]{0:T(128)}, u32[]{:S(2)}) copy-start(f32[4]{0:T(128)} %param.10) | copy-start | bytes 52
  144.5 38.3 %all-to-all-start.1 = ((f32[64,32,128]{2,1,0:T(8,128)}), f32[64,32,128]{2,1,0:T(8,128)S(1)}, u32[]{:S(2)}, u32[]{:S(2)}) async-start(f32[64,32,128]{2,1,0:T(8,128)} %bitcast.9), calls=%async_computation.1 | async-start | bytes 2097152 | tf_op jit(solution)/shard_map/all_to_all | solution.py:66
  182.9 34.8 %all-to-all-start = ((f32[64,32,128]{2,1,0:T(8,128)}), f32[64,32,128]{2,1,0:T(8,128)S(1)}, u32[]{:S(2)}, u32[]{:S(2)}) async-start(f32[64,32,128]{2,1,0:T(8,128)} %bitcast.7), calls=%async_computation | async-start | bytes 2097152 | tf_op jit(solution)/shard_map/all_to_all | solution.py:65
  189.7 30.0 %reduce-scatter.5.cloned.1.call-start = ((), (), s32[]{:S(2)}) async-start(), calls=%async_computation.6 | async-start | bytes 1310720 | tf_op jit(solution)/shard_map/reduce_scatter | solution.py:71
  191.5 57.1 %reduce-scatter.3.cloned.1.call-start = ((), (), s32[]{:S(2)}) async-start(), calls=%async_computation.5 | async-start | bytes 1310720 | tf_op jit(solution)/shard_map/reduce_scatter | solution.py:70
Sparse Core Ops, SparseCore 0:
  9.8 29.1 all-gather.2
  41.5 98.4 all-reduce.2
  193.9 25.8 reduce-scatter.4
  222.7 25.8 reduce-scatter.2
where the time goes:
time: 258 us; the launch traced here: 257 us
  waiting for transfers between devices  183 us (71%)
  other arithmetic  22.3 us (9%)
  starting transfers between devices  17.5 us (7%)
  between operations  15.2 us (6%)
  blocking collectives  11.2 us (4%)
  matrix products  4.83 us (2%)
  local copies, waits for them, and re-layouts  2.6 us (1%)
    psum x1, waiting for transfers between devices, per_device(): whole_rows, whole_sums = lax.psum((term_rows, term_sums), 'code')  96.1 us
    reduce_scatter x1, waiting for transfers between devices, per_device(): lax.psum_scatter(member_weight * moved_rows, 'code', scatter_dimension=0,...  28.8 us
    all_to_all x1, waiting for transfers between devices, per_device(): lax.all_to_all(outgoing_rows, 'shard', split_axis=0, concat_axis=0, tiled...  26.1 us
    all_to_all x1, waiting for transfers between devices, per_device(): lax.all_to_all(outgoing_sums, 'shard', split_axis=0, concat_axis=0, tiled...  22.4 us
    all_gather x1, blocking collectives, per_device(): lax.all_gather(pending_rows.astype(jnp.float32), 'code', axis=0, tiled=True)  11.2 us
    all_to_all x1, starting transfers between devices, per_device(): lax.all_to_all(outgoing_sums, 'shard', split_axis=0, concat_axis=0, tiled...  10.5 us
    scatter x2, other arithmetic, slot_rows(): return empty.at[place].set(rows)  9.34 us
    all_gather x1, waiting for transfers between devices, per_device(): lax.all_gather(pending_grads, 'code', axis=0, tiled=True)  8.79 us
  transfers between devices with their start and end apart: 6, of which 6 were waited for; matrix products, arithmetic and copies ran while one was open for 9% of the time, Pallas kernels for 0%

commit v1 on v0

v1 whole, which is shorter than its diff:
```python
import jax
import jax.numpy as jnp
from jax import lax
from jax.experimental import pallas as pl
from jax.experimental.pallas import tpu as pltpu
from jax.sharding import PartitionSpec as P

step_size = 0.5
epsilon = 1e-08
MEMBERS = 4
SMEM = pl.BlockSpec(memory_space=pltpu.SMEM)
VMEM = pl.BlockSpec(memory_space=pltpu.VMEM)
PARAMS = pltpu.CompilerParams(vmem_limit_bytes=24 * 1024 * 1024)


def decode_weights(lost_ref, weight_ref):
    which = lost_ref[0]
    rows = [jnp.full((1, 128), weight_ref[c], jnp.float32) for c in range(MEMBERS)]
    parity_lost = which == 3
    divisor = jnp.where(which == 0, rows[0], jnp.where(which == 1, rows[1], rows[2]))
    divisor = jnp.where(parity_lost, jnp.ones_like(divisor), divisor)
    out = []
    for c in range(3):
        solved = jnp.where(parity_lost, rows[c], -rows[c] / divisor)
        out.append(jnp.where(which == c, jnp.zeros_like(solved), solved))
    out.append(jnp.where(parity_lost, jnp.zeros_like(divisor), 1.0 / divisor))
    return out


def split_halves(value):
    high = value.astype(jnp.bfloat16)
    low = (value - high.astype(jnp.float32)).astype(jnp.bfloat16)
    return high, low


def scale_kernel(lost_ref, weight_ref, member_ref, table_ref, out_ref):
    weights = decode_weights(lost_ref, weight_ref)
    member = member_ref[0]
    own = weights[3]
    for c in range(3):
        own = jnp.where(member == c, weights[c], own)
    out_ref[...] = own * table_ref[...]


def scale_table(lost, weight, member, table):
    rows, width = table.shape
    block = 1024
    return pl.pallas_call(
        scale_kernel,
        grid=(rows // block,),
        in_specs=[SMEM, SMEM, SMEM, pl.BlockSpec((block, width), lambda i: (i, 0))],
        out_specs=pl.BlockSpec((block, width), lambda i: (i, 0)),
        out_shape=jax.ShapeDtypeStruct(table.shape, jnp.float32),
        compiler_params=PARAMS,
        name="scale_table",
    )(lost, weight, member, table)


def totals_kernel(count, pieces, member_ref, *refs):
    piece_refs, out_ref = refs[:pieces], refs[pieces]
    first = member_ref[0] * count
    entries = piece_refs[0].shape[0] - 8
    total = jnp.zeros((count, 256), jnp.float32)
    targets = (lax.broadcasted_iota(jnp.int32, (count, 128), 0) + first).astype(jnp.float32)
    for piece in piece_refs:
        high, low = split_halves(piece[:entries, :])
        both = jnp.concatenate([high, low], axis=1)
        hits = jnp.concatenate(
            [
                jnp.where(targets == piece[entries + j : entries + j + 1, :], 1.0, 0.0).astype(jnp.bfloat16)
                for j in range(entries // 128)
            ],
            axis=1,
        )
        total = total + jnp.dot(hits, both, preferred_element_type=jnp.float32)
    out_ref[...] = total[:, :128] + total[:, 128:]


def pending_totals(member, pieces, count):
    return pl.pallas_call(
        lambda *refs: totals_kernel(count, len(pieces), *refs),
        in_specs=[SMEM] + [VMEM] * len(pieces),
        out_specs=VMEM,
        out_shape=jax.ShapeDtypeStruct((count, 128), jnp.float32),
        compiler_params=PARAMS,
        name="pending_totals",
    )(member, *pieces)


def spread(place_ref, values, out_ref, both_ref):
    high, low = split_halves(values)
    both_ref[:, :128] = high
    both_ref[:, 128:] = low
    slots, rows = out_ref.shape[0], values.shape[0]
    step = 256
    place = place_ref[...]
    for start in range(0, slots, step):
        here = lax.broadcasted_iota(jnp.int32, (step, rows), 0) + start
        pick = jnp.where(here == place, 1.0, 0.0).astype(jnp.bfloat16)
        got = jnp.dot(pick, both_ref[...], preferred_element_type=jnp.float32)
        out_ref[start : start + step, :] = got[:, :128] + got[:, 128:]


def sums_kernel(lost_ref, weight_ref, place_ref, got_ref, total_ref, out_ref, new_ref, both_ref):
    weights = decode_weights(lost_ref, weight_ref)
    count = total_ref.shape[0]
    new = weights[0] * got_ref[:count, :]
    for c in range(1, MEMBERS):
        new = new + weights[c] * got_ref[c * count : (c + 1) * count, :]
    total = total_ref[...]
    new = new + total * total
    new_ref[...] = new
    spread(place_ref, new, out_ref, both_ref)


def place_sums(lost, weight, place, got, total, slots):
    count = total.shape[0]
    return pl.pallas_call(
        sums_kernel,
        in_specs=[SMEM, SMEM, VMEM, VMEM, VMEM],
        out_specs=(VMEM, VMEM),
        out_shape=(
            jax.ShapeDtypeStruct((slots, 128), jnp.float32),
            jax.ShapeDtypeStruct((count, 128), jnp.float32),
        ),
        scratch_shapes=[pltpu.VMEM((count, 256), jnp.bfloat16)],
        compiler_params=PARAMS,
        name="place_sums",
    )(lost, weight, place, got, total)


def rows_kernel(place_ref, mine_ref, total_ref, sums_ref, out_ref, both_ref):
    new = mine_ref[...] - step_size * total_ref[...] / (jnp.sqrt(sums_ref[...]) + epsilon)
    spread(place_ref, new, out_ref, both_ref)


def place_rows(place, mine, total, sums, slots):
    count = total.shape[0]
    return pl.pallas_call(
        rows_kernel,
        in_specs=[VMEM, VMEM, VMEM, VMEM],
        out_specs=VMEM,
        out_shape=jax.ShapeDtypeStruct((slots, 128), jnp.float32),
        scratch_shapes=[pltpu.VMEM((count, 256), jnp.bfloat16)],
        compiler_params=PARAMS,
        name="place_rows",
    )(place, mine, total, sums)


def per_device(
    table_rows, adagrad_sums, lost_member, code_weight, new_owner, pending_rows, pending_grads
):
    members = lax.axis_size("code")
    shards = lax.axis_size("shard")
    member = lax.axis_index("code")
    member_ref = member.astype(jnp.int32)[None]
    share_rows = table_rows.shape[0] // members
    capacity = max(2, (2 * share_rows + shards - 1) // shards)
    slots = shards * capacity

    ids = pending_rows.astype(jnp.float32).reshape(-1, 128)
    pad = jnp.zeros((8 - ids.shape[0], 128), jnp.float32)
    packed = jnp.concatenate([pending_grads, ids, pad], axis=0)
    pieces = [packed] + [
        lax.ppermute(packed, "code", [(i, (i + k) % members) for i in range(members)])
        for k in range(1, members)
    ]
    got_sums = lax.all_to_all(adagrad_sums, "code", 0, 0, tiled=True)

    owner = new_owner[:, 0]
    earlier = jnp.tril(owner[:, None] == owner[None, :], -1)
    rank = jnp.sum(earlier.astype(jnp.int32), axis=1)
    place = (owner * capacity + rank)[None, :]

    term_rows = scale_table(lost_member, code_weight, member_ref, table_rows)
    totals = pending_totals(member_ref, pieces, share_rows)
    term_rows, got_sums = lax.optimization_barrier((term_rows, got_sums))
    mine_rows = lax.psum_scatter(term_rows, "code", scatter_dimension=0, tiled=True)

    out_sums, new_sums = place_sums(lost_member, code_weight, place, got_sums, totals, slots)
    moved_sums = lax.all_to_all(out_sums, "shard", 0, 0, tiled=True)
    out_rows = place_rows(place, mine_rows, totals, new_sums, slots)
    moved_rows = lax.all_to_all(out_rows, "shard", 0, 0, tiled=True)

    own_weight = jnp.sum(jnp.where(jnp.arange(members) == member, code_weight, 0.0))
    parity_sums = lax.psum_scatter(own_weight * moved_sums, "code", scatter_dimension=0, tiled=True)
    got = lax.all_to_all(moved_rows, "code", 0, 0, tiled=True).reshape(members, slots // members, -1)
    parity_rows = code_weight[0] * got[0]
    for c in range(1, members):
        parity_rows = parity_rows + code_weight[c] * got[c]
    return (moved_rows, moved_sums, parity_rows, parity_sums)


def solution(mesh):
    in_specs = (
        P(("shard", "code"), None),
        P(("shard", "code"), None),
        P("shard"),
        P(),
        P(("shard", "code"), None),
        P(("shard", "code")),
        P(("shard", "code"), None),
    )
    out_specs = (
        P(("shard", "code"), None),
        P(("shard", "code"), None),
        P(("shard", "code"), None),
        P(("shard", "code"), None),
    )
    return jax.shard_map(
        per_device, mesh=mesh, in_specs=in_specs, out_specs=out_specs, check_vma=False
    )
```

time: 258 us -> 168 us (0.65)
  waiting for transfers between devices: 183 us -> 97.7 us
  other arithmetic: 22.3 us -> 7.05 us
  starting transfers between devices: 17.5 us -> 31.2 us
  blocking collectives: 11.2 us -> 0 us
  Pallas kernels: 0 us -> 8.22 us
  local copies, waits for them, and re-layouts: 2.6 us -> 7.58 us
  matrix products: 4.83 us -> 0 us
    psum x1 -> x0, waiting for transfers between devices: 96.1 us -> none  [per_device(): whole_rows, whole_sums = lax.psum((term_rows, term_sums), 'code')]
    all_to_all x2 -> x4, waiting for transfers between devices: 48.5 us -> 86 us  [the longest x1 25.4 us: per_device(): moved_rows = lax.all_to_all(out_rows, 'shard', 0, 0, tiled=True)]
    reduce_scatter x2, waiting for transfers between devices: 29.3 us -> 0.07 us  [the longest x1 0.07 us: per_device(): lax.psum_scatter(term_rows, 'code', scatter_dimension=0, tiled=True)]
    ppermute x0 -> x3, waiting for transfers between devices: none -> 11.6 us  [per_device(): lax.ppermute(packed, 'code', [(i, (i + k) % members) for i in range(membe...]
    all_gather x1 -> x0, blocking collectives: 11.2 us -> none  [per_device(): lax.all_gather(pending_rows.astype(jnp.float32), 'code', axis=0, tiled=True)]
    all_to_all x2 -> x4, starting transfers between devices: 17.3 us -> 28.4 us  [the longest x1 13.1 us: per_device(): moved_sums = lax.all_to_all(out_sums, 'shard', 0, 0, tiled=True)]
    scatter x2 -> x0, other arithmetic: 9.34 us -> none  [slot_rows(): return empty.at[place].set(rows)]
    all_gather x1 -> x0, waiting for transfers between devices: 8.79 us -> none  [per_device(): lax.all_gather(pending_grads, 'code', axis=0, tiled=True)]
  transfers between devices with their start and end apart: 6 -> 9, of which waited for: 6 -> 8; matrix products, arithmetic and copies ran while one was open for 9% -> 5% of each run, Pallas kernels for 0% -> 5%
where the time goes in v1:
time: 168 us; the launch traced here: 166 us
  waiting for transfers between devices  97.7 us (58%)
  starting transfers between devices  31.2 us (19%)
  between operations  14.8 us (9%)
  Pallas kernels  8.22 us (5%)
  local copies, waits for them, and re-layouts  7.58 us (5%)
  other arithmetic  7.05 us (4%)
    all_to_all x1, waiting for transfers between devices, per_device(): moved_rows = lax.all_to_all(out_rows, 'shard', 0, 0, tiled=True)  25.4 us
    all_to_all x1, waiting for transfers between devices, per_device(): moved_sums = lax.all_to_all(out_sums, 'shard', 0, 0, tiled=True)  24.3 us
    all_to_all x1, waiting for transfers between devices, per_device(): got_sums = lax.all_to_all(adagrad_sums, 'code', 0, 0, tiled=True)  21.6 us
    all_to_all x1, waiting for transfers between devices, per_device(): lax.all_to_all(moved_rows, 'code', 0, 0, tiled=True)  14.6 us
    all_to_all x1, starting transfers between devices, per_device(): moved_sums = lax.all_to_all(out_sums, 'shard', 0, 0, tiled=True)  13.1 us
    ppermute x3, waiting for transfers between devices, per_device(): lax.ppermute(packed, 'code', [(i, (i + k) % members) for i in range(membe...  11.6 us
    all_to_all x1, starting transfers between devices, per_device(): moved_rows = lax.all_to_all(out_rows, 'shard', 0, 0, tiled=True)  7.06 us
    unnamed x16, local copies, waits for them, and re-layouts  6.84 us
  transfers between devices with their start and end apart: 9, of which 8 were waited for; matrix products, arithmetic and copies ran while one was open for 5% of the time, Pallas kernels for 5%

profile of v1, /device:TPU:32, one launch (start us, length us, event | category | flops | bytes accessed | tf_op | source)
XLA Modules:
  0.0 166.5 jit_solution(14994953283399952848)
XLA Ops:
  7.2 4.5 %all-to-all-start = ((f32[4,1024,128]{2,1,0:T(8,128)}), f32[4,1024,128]{2,1,0:T(8,128)S(1)}, u32[]{:S(2)}, u32[]{:S(2)}) async-start(f32[4,1024,128]{2,1,0:T(8,128)} %bitcast.24), calls=%async_computation | async-start | bytes 4194304 | tf_op jit(solution)/shard_map/all_to_all | solution.py:168
  12.3 1.6 copy-done
  13.9 2.4 %scale_table.1 = f32[4096,128]{1,0:T(8,128)} custom-call(s32[1]{0:T(128)S(6)} %copy.13.lost_ref, f32[4]{0:T(128)S(1)} %copy-done.3, s32[1]{0:T(128)} %bitcast.3.member_ref.refs_0_, f32[4096,128]{1,0:T(8,128)S(1)} %copy-done), custom_call_target="tpu_custom_call" | custom-call | tf_op jit(solution)/shard_map/scale_table/pallas_call | solution.py:48
  16.4 21.6 %all-to-all-done = f32[4,1024,128]{2,1,0:T(8,128)S(1)} async-done(((f32[4,1024,128]{2,1,0:T(8,128)}), f32[4,1024,128]{2,1,0:T(8,128)S(1)}, u32[]{:S(2)}, u32[]{:S(2)}) %all-to-all-start) | async-done | bytes 2097184 | tf_op jit(solution)/shard_map/all_to_all | solution.py:168
  38.2 1.2 collective-permute-start.2
  39.5 1.5 collective-permute-start.1
  41.0 1.3 convert_reduce_fusion
  42.2 5.4 %collective-permute-done.2.refs_4_ = f32[520,128]{1,0:T(8,128)S(1)} collective-permute-done((f32[520,128]{1,0:T(8,128)S(1)}, f32[520,128]{1,0:T(8,128)S(1)}, u32[]{:S(2)}, u32[]{:S(2)}) %collective-permute-start.2) | collective-permute-done | bytes 266272 | tf_op jit(solution)/shard_map/ppermute | solution.py:165
  47.6 2.7 %collective-permute-done.1.refs_3_ = f32[520,128]{1,0:T(8,128)S(1)} collective-permute-done((f32[520,128]{1,0:T(8,128)S(1)}, f32[520,128]{1,0:T(8,128)S(1)}, u32[]{:S(2)}, u32[]{:S(2)}) %collective-permute-start.1) | collective-permute-done | bytes 266272 | tf_op jit(solution)/shard_map/ppermute | solution.py:165
  50.3 3.5 %collective-permute-done.refs_2_ = f32[520,128]{1,0:T(8,128)S(1)} collective-permute-done((f32[520,128]{1,0:T(8,128)S(1)}, f32[520,128]{1,0:T(8,128)S(1)}, u32[]{:S(2)}, u32[]{:S(2)}) %collective-permute-start) | collective-permute-done | bytes 266272 | tf_op jit(solution)/shard_map/ppermute | solution.py:165
  53.8 1.3 pending_totals.1.total_ref
  55.1 2.0 %place_sums.1 = (f32[2048,128]{1,0:T(8,128)S(1)}, f32[1024,128]{1,0:T(8,128)S(1)}) custom-call(s32[1]{0:T(128)S(6)} %copy.13.lost_ref, f32[4]{0:T(128)S(1)} %copy-done.3, s32[1,1024]{1,0:T(1,128)S(1)} %bitcast_add_fusion.place_ref, f32[4096,128]{1,0:T(8,128)S(1)} %bitcast.21, f32[1024,128]{1,0:T(8,128)S(1)} %pending_totals.1.total_ref), custom_call_target="tpu_custom_call" | custom-call | tf_op jit(solution)/shard_map/place_sums/pallas_call | solution.py:118
  58.1 13.1 %all-to-all-start.2 = ((f32[64,32,128]{2,1,0:T(8,128)}), f32[64,32,128]{2,1,0:T(8,128)S(1)}, u32[]{:S(2)}, u32[]{:S(2)}) async-start(f32[64,32,128]{2,1,0:T(8,128)} %bitcast.22), calls=%async_computation.3 | async-start | bytes 2097152 | tf_op jit(solution)/shard_map/all_to_all | solution.py:181
  71.3 1.0 copy-done.2
  72.4 2.5 %place_rows.1 = f32[2048,128]{1,0:T(8,128)} custom-call(s32[1,1024]{1,0:T(1,128)S(1)} %bitcast_add_fusion.place_ref, f32[1024,128]{1,0:T(8,128)S(1)} %copy-done.2, f32[1024,128]{1,0:T(8,128)S(1)} %pending_totals.1.total_ref, f32[1024,128]{1,0:T(8,128)S(1)} %get-tuple-element.10.sums_ref), custom_call_target="tpu_custom_call" | custom-call | tf_op jit(solution)/shard_map/place_rows/pallas_call | solution.py:139
  74.9 24.3 %all-to-all-done.2 = f32[64,32,128]{2,1,0:T(8,128)S(1)} async-done(((f32[64,32,128]{2,1,0:T(8,128)}), f32[64,32,128]{2,1,0:T(8,128)S(1)}, u32[]{:S(2)}, u32[]{:S(2)}) %all-to-all-start.2) | async-done | bytes 1048608 | tf_op jit(solution)/shard_map/all_to_all | solution.py:181
  99.1 7.1 %all-to-all-start.1 = ((f32[64,32,128]{2,1,0:T(8,128)}), f32[64,32,128]{2,1,0:T(8,128)}, u32[]{:S(2)}, u32[]{:S(2)}) async-start(f32[64,32,128]{2,1,0:T(8,128)} %bitcast.7), calls=%async_computation.2 | async-start | bytes 2097152 | tf_op jit(solution)/shard_map/all_to_all | solution.py:183
  106.8 1.7 %broadcast_multiply_fusion = f32[2048,128]{1,0:T(8,128)} fusion(f32[]{:T(128)} %fusion.5, f32[64,32,128]{2,1,0:T(8,128)S(1)} %all-to-all-done.2), kind=kLoop, calls=%fused_computation.3 | loop fusion | flops 262144 | bytes 2097156 | tf_op jit(solution)/shard_map/mul | solution.py:186
  108.6 25.4 %all-to-all-done.1 = f32[64,32,128]{2,1,0:T(8,128)} async-done(((f32[64,32,128]{2,1,0:T(8,128)}), f32[64,32,128]{2,1,0:T(8,128)}, u32[]{:S(2)}, u32[]{:S(2)}) %all-to-all-start.1) | async-done | bytes 1048608 | tf_op jit(solution)/shard_map/all_to_all | solution.py:183
  134.0 3.7 %all-to-all-start.3 = ((f32[4,512,128]{2,1,0:T(8,128)}), f32[4,512,128]{2,1,0:T(8,128)S(1)}, u32[]{:S(2)}, u32[]{:S(2)}) async-start(f32[4,512,128]{2,1,0:T(8,128)} %bitcast.12), calls=%async_computation.4 | async-start | bytes 2097152 | tf_op jit(solution)/shard_map/all_to_all | solution.py:187
  138.4 14.6 %all-to-all-done.3 = f32[4,512,128]{2,1,0:T(8,128)S(1)} async-done(((f32[4,512,128]{2,1,0:T(8,128)}), f32[4,512,128]{2,1,0:T(8,128)S(1)}, u32[]{:S(2)}, u32[]{:S(2)}) %all-to-all-start.3) | async-done | bytes 1048608 | tf_op jit(solution)/shard_map/all_to_all | solution.py:187
  153.0 3.4 %fusion.2 = f32[512,128]{1,0:T(8,128)} fusion(f32[4,512,128]{2,1,0:T(8,128)S(1)} %all-to-all-done.3, f32[]{:T(128)} %bitcast.15, f32[]{:T(128)} %bitcast.14, f32[]{:T(128)} %bitcast.13, f32[]{:T(128)} %bitcast.11), kind=kLoop, calls=%fused_computation.7 | loop fusion | flops 458752 | bytes 1310736 | tf_op jit(solution)/shard_map/add | solution.py:190
  156.4 2.3 %copy.14 = f32[2048,128]{1,0:T(8,128)} copy(f32[2048,128]{1,0:T(8,128)} %bitcast.8) | data formatting | bytes 2097152
  158.7 1.0 copy.15
  (27 shorter events, 2.6 us)
Async XLA Ops:
  7.2 5.1 %copy-start.3 = (f32[4]{0:T(128)S(1)}, f32[4]{0:T(128)}, u32[]{:S(2)}) copy-start(f32[4]{0:T(128)} %weight_ref.3) | copy-start | bytes 52
  7.2 30.8 %all-to-all-start = ((f32[4,1024,128]{2,1,0:T(8,128)}), f32[4,1024,128]{2,1,0:T(8,128)S(1)}, u32[]{:S(2)}, u32[]{:S(2)}) async-start(f32[4,1024,128]{2,1,0:T(8,128)} %bitcast.24), calls=%async_computation | async-start | bytes 4194304 | tf_op jit(solution)/shard_map/all_to_all | solution.py:168
  11.7 59.7 %reduce-scatter.3.cloned.1.call-start = ((), (), s32[]{:S(2)}) async-start(), calls=%async_computation.6 | async-start | bytes 2621440 | tf_op jit(solution)/shard_map/reduce_scatter | solution.py:178
  12.3 1.6 copy-start
  16.3 21.7 %copy-start.6 = (s32[512]{0:T(512)S(1)}, s32[512]{0:T(512)}, u32[]{:S(2)}) copy-start(s32[512]{0:T(512)} %param.12) | copy-start | bytes 6148
  16.4 21.7 %copy-start.4 = (f32[512,128]{1,0:T(8,128)S(1)}, f32[512,128]{1,0:T(8,128)}, u32[]{:S(2)}) copy-start(f32[512,128]{1,0:T(8,128)} %param.13) | copy-start | bytes 786436
  16.4 24.6 %copy-start.5 = (s32[1024,1]{0,1:T(1,128)S(1)}, s32[1024,1]{0,1:T(1,128)}, u32[]{:S(2)}) copy-start(s32[1024,1]{0,1:T(1,128)} %param.11) | copy-start | bytes 12292
  38.2 9.4 %collective-permute-start.2 = (f32[520,128]{1,0:T(8,128)S(1)}, f32[520,128]{1,0:T(8,128)S(1)}, u32[]{:S(2)}, u32[]{:S(2)}) collective-permute-start(f32[520,128]{1,0:T(8,128)S(1)} %maximum_maximum_fusion.refs_1_), channel_id=1, source_target_pairs={{0,3},{1,0},{2,1},{3,2},{4,7},{5,4},{6,5},{7,6},{8,11},{9,8},{10,9... | collective-permute-start | bytes 798728 | tf_op jit(solution)/shard_map/ppermute | solution.py:165
  39.5 10.9 %collective-permute-start.1 = (f32[520,128]{1,0:T(8,128)S(1)}, f32[520,128]{1,0:T(8,128)S(1)}, u32[]{:S(2)}, u32[]{:S(2)}) collective-permute-start(f32[520,128]{1,0:T(8,128)S(1)} %maximum_maximum_fusion.refs_1_), channel_id=1, source_target_pairs={{0,2},{1,3},{2,0},{3,1},{4,6},{5,7},{6,4},{7,5},{8,10},{9,11},{10,... | collective-permute-start | bytes 798728 | tf_op jit(solution)/shard_map/ppermute | solution.py:165
  40.9 12.9 %collective-permute-start = (f32[520,128]{1,0:T(8,128)S(1)}, f32[520,128]{1,0:T(8,128)S(1)}, u32[]{:S(2)}, u32[]{:S(2)}) collective-permute-start(f32[520,128]{1,0:T(8,128)S(1)} %maximum_maximum_fusion.refs_1_), channel_id=1, source_target_pairs={{0,1},{1,2},{2,3},{3,0},{4,5},{5,6},{6,7},{7,4},{8,9},{9,10},{10,1... | collective-permute-start | bytes 798728 | tf_op jit(solution)/shard_map/ppermute | solution.py:165
  57.1 1.0 copy-start.1
  58.1 41.0 %all-to-all-start.2 = ((f32[64,32,128]{2,1,0:T(8,128)}), f32[64,32,128]{2,1,0:T(8,128)S(1)}, u32[]{:S(2)}, u32[]{:S(2)}) async-start(f32[64,32,128]{2,1,0:T(8,128)} %bitcast.22), calls=%async_computation.3 | async-start | bytes 2097152 | tf_op jit(solution)/shard_map/all_to_all | solution.py:181
  71.3 1.0 copy-start.2
  99.1 34.9 %all-to-all-start.1 = ((f32[64,32,128]{2,1,0:T(8,128)}), f32[64,32,128]{2,1,0:T(8,128)}, u32[]{:S(2)}, u32[]{:S(2)}) async-start(f32[64,32,128]{2,1,0:T(8,128)} %bitcast.7), calls=%async_computation.2 | async-start | bytes 2097152 | tf_op jit(solution)/shard_map/all_to_all | solution.py:183
  106.2 50.2 %reduce-scatter.5.cloned.1.call-start = ((), (), s32[]{:S(2)}) async-start(), calls=%async_computation.7 | async-start | bytes 1310720 | tf_op jit(solution)/shard_map/reduce_scatter | solution.py:186
  134.0 19.0 %all-to-all-start.3 = ((f32[4,512,128]{2,1,0:T(8,128)}), f32[4,512,128]{2,1,0:T(8,128)S(1)}, u32[]{:S(2)}, u32[]{:S(2)}) async-start(f32[4,512,128]{2,1,0:T(8,128)} %bitcast.12), calls=%async_computation.4 | async-start | bytes 2097152 | tf_op jit(solution)/shard_map/all_to_all | solution.py:187
Sparse Core Ops, SparseCore 0:
  38.1 33.1 reduce-scatter.2
  110.3 26.7 reduce-scatter.4

commit v2 on v1

--- a/solution.py
+++ b/solution.py
@@ -33,27 +33,79 @@
     return high, low
 
 
-def scale_kernel(lost_ref, weight_ref, member_ref, table_ref, out_ref):
-    weights = decode_weights(lost_ref, weight_ref)
-    member = member_ref[0]
+def own_row(weights, member):
     own = weights[3]
     for c in range(3):
         own = jnp.where(member == c, weights[c], own)
-    out_ref[...] = own * table_ref[...]
+    return own
+
+
+def kernel_call(body, name, out_shape, in_specs, out_specs, cost=0, **kwargs):
+    return pl.pallas_call(
+        body,
+        in_specs=in_specs,
+        out_specs=out_specs,
+        out_shape=out_shape,
+        compiler_params=PARAMS,
+        cost_estimate=pl.CostEstimate(flops=cost, bytes_accessed=cost, transcendentals=0),
+        name=name,
+        **kwargs,
+    )
+
+
+def flat(rows):
+    return jax.ShapeDtypeStruct((rows, 128), jnp.float32)
+
+
+def scale_kernel(lost_ref, weight_ref, member_ref, table_ref, out_ref):
+    out_ref[...] = own_row(decode_weights(lost_ref, weight_ref), member_ref[0]) * table_ref[...]
 
 
 def scale_table(lost, weight, member, table):
     rows, width = table.shape
     block = 1024
-    return pl.pallas_call(
+    return kernel_call(
         scale_kernel,
+        "scale_table",
+        flat(rows),
+        [SMEM, SMEM, SMEM, pl.BlockSpec((block, width), lambda i: (i, 0))],
+        pl.BlockSpec((block, width), lambda i: (i, 0)),
+        cost=2 * rows * width * 4,
         grid=(rows // block,),
-        in_specs=[SMEM, SMEM, SMEM, pl.BlockSpec((block, width), lambda i: (i, 0))],
-        out_specs=pl.BlockSpec((block, width), lambda i: (i, 0)),
-        out_shape=jax.ShapeDtypeStruct(table.shape, jnp.float32),
-        compiler_params=PARAMS,
-        name="scale_table",
     )(lost, weight, member, table)
+
+
+def piece_of(quarter, half, count):
+    return pl.ds(pl.multiple_of(quarter * count + half * (count // 2), 8), count // 2)
+
+
+def near(member):
+    return member + 1 - 2 * lax.rem(member, 2), 3 - member
+
+
+def first_kernel(count, lost_ref, weight_ref, member_ref, table_ref, a_ref, b_ref):
+    member = member_ref[0]
+    own = own_row(decode_weights(lost_ref, weight_ref), member)
+    half = count // 2
+    one, two = near(member)
+    a_ref[:half, :] = own * table_ref[piece_of(one, 0, count), :]
+    a_ref[half:, :] = own * table_ref[piece_of(3 - one, 0, count), :]
+    b_ref[:half, :] = own * table_ref[piece_of(two, 1, count), :]
+    b_ref[half:, :] = own * table_ref[piece_of(near(two)[0], 1, count), :]
+
+
+def second_kernel(count, lost_ref, weight_ref, member_ref, table_ref, a_ref, b_ref, c_ref, d_ref):
+    member = member_ref[0]
+    own = own_row(decode_weights(lost_ref, weight_ref), member)
+    half = count // 2
+    one, two = near(member)
+    c_ref[...] = own * table_ref[piece_of(two, 0, count), :] + a_ref[half:, :]
+    d_ref[...] = own * table_ref[piece_of(one, 1, count), :] + b_ref[half:, :]
+
+
+def swap(array, which, members):
+    pairs = [(i, i ^ 1) for i in range(members)] if which == 0 else [(i, 3 - i) for i in range(members)]
+    return lax.ppermute(array, "code", pairs)
 
 
 def totals_kernel(count, pieces, member_ref, *refs):
@@ -101,32 +153,19 @@
         out_ref[start : start + step, :] = got[:, :128] + got[:, 128:]
 
 
-def sums_kernel(lost_ref, weight_ref, place_ref, got_ref, total_ref, out_ref, new_ref, both_ref):
-    weights = decode_weights(lost_ref, weight_ref)
+def sums_kernel(
+    lost_ref, weight_ref, member_ref, place_ref, table_ref, a_ref, b_ref, c_ref, d_ref, total_ref, out_ref, new_ref, both_ref
+):
+    member = member_ref[0]
     count = total_ref.shape[0]
-    new = weights[0] * got_ref[:count, :]
-    for c in range(1, MEMBERS):
-        new = new + weights[c] * got_ref[c * count : (c + 1) * count, :]
+    half = count // 2
+    own = own_row(decode_weights(lost_ref, weight_ref), member)
     total = total_ref[...]
-    new = new + total * total
+    first = (own * table_ref[piece_of(member, 0, count), :] + a_ref[:half, :]) + c_ref[...]
+    last = (own * table_ref[piece_of(member, 1, count), :] + b_ref[:half, :]) + d_ref[...]
+    new = jnp.concatenate([first, last], axis=0) + total * total
     new_ref[...] = new
     spread(place_ref, new, out_ref, both_ref)
-
-
-def place_sums(lost, weight, place, got, total, slots):
-    count = total.shape[0]
-    return pl.pallas_call(
-        sums_kernel,
-        in_specs=[SMEM, SMEM, VMEM, VMEM, VMEM],
-        out_specs=(VMEM, VMEM),
-        out_shape=(
-            jax.ShapeDtypeStruct((slots, 128), jnp.float32),
-            jax.ShapeDtypeStruct((count, 128), jnp.float32),
-        ),
-        scratch_shapes=[pltpu.VMEM((count, 256), jnp.bfloat16)],
-        compiler_params=PARAMS,
-        name="place_sums",
-    )(lost, weight, place, got, total)
 
 
 def rows_kernel(place_ref, mine_ref, total_ref, sums_ref, out_ref, both_ref):
@@ -134,17 +173,44 @@
     spread(place_ref, new, out_ref, both_ref)
 
 
-def place_rows(place, mine, total, sums, slots):
-    count = total.shape[0]
-    return pl.pallas_call(
-        rows_kernel,
-        in_specs=[VMEM, VMEM, VMEM, VMEM],
-        out_specs=VMEM,
-        out_shape=jax.ShapeDtypeStruct((slots, 128), jnp.float32),
-        scratch_shapes=[pltpu.VMEM((count, 256), jnp.bfloat16)],
-        compiler_params=PARAMS,
-        name="place_rows",
-    )(place, mine, total, sums)
+def own_code_weight(weight_ref, member):
+    own = weight_ref[3]
+    for c in range(3):
+        own = jnp.where(member == c, weight_ref[c], own)
+    return own
+
+
+def emit_kernel(weight_ref, member_ref, moved_ref, out_ref, term_ref):
+    moved = moved_ref[...]
+    out_ref[...] = moved
+    term_ref[...] = own_code_weight(weight_ref, member_ref[0]) * moved
+
+
+def copy_kernel(moved_ref, out_ref):
+    out_ref[...] = moved_ref[...]
+
+
+def quarter_of(which, count):
+    return pl.ds(pl.multiple_of(lax.rem(which, MEMBERS) * count, 8), count)
+
+
+def parity_send_kernel(weight_ref, member_ref, moved_ref, *out_refs):
+    member = member_ref[0]
+    own = own_code_weight(weight_ref, member)
+    count = out_refs[0].shape[0]
+    for k, out_ref in enumerate(out_refs):
+        out_ref[...] = own * moved_ref[quarter_of(member + k + 1, count), :]
+
+
+def parity_sum_kernel(weight_ref, member_ref, moved_ref, a_ref, b_ref, c_ref, out_ref):
+    member = member_ref[0]
+    own = own_code_weight(weight_ref, member)
+    mine = own * moved_ref[quarter_of(member, out_ref.shape[0]), :]
+    out_ref[...] = (mine + a_ref[...]) + (b_ref[...] + c_ref[...])
+
+
+def turn(array, k, members):
+    return lax.ppermute(array, "code", [(i, (i + k) % members) for i in range(members)])
 
 
 def per_device(
@@ -152,43 +218,82 @@
 ):
     members = lax.axis_size("code")
     shards = lax.axis_size("shard")
-    member = lax.axis_index("code")
-    member_ref = member.astype(jnp.int32)[None]
+    member = lax.axis_index("code").astype(jnp.int32)[None]
     share_rows = table_rows.shape[0] // members
     capacity = max(2, (2 * share_rows + shards - 1) // shards)
     slots = shards * capacity
+    half, quarter = share_rows // 2, slots // members
+    scalars = [SMEM, SMEM, SMEM]
+    key = (lost_member, code_weight, member)
 
     ids = pending_rows.astype(jnp.float32).reshape(-1, 128)
     pad = jnp.zeros((8 - ids.shape[0], 128), jnp.float32)
     packed = jnp.concatenate([pending_grads, ids, pad], axis=0)
-    pieces = [packed] + [
-        lax.ppermute(packed, "code", [(i, (i + k) % members) for i in range(members)])
-        for k in range(1, members)
-    ]
-    got_sums = lax.all_to_all(adagrad_sums, "code", 0, 0, tiled=True)
+    pieces = [packed] + [turn(packed, k, members) for k in (1, 3, 2)]
+
+    send_a, send_b = kernel_call(
+        lambda *refs: first_kernel(share_rows, *refs),
+        "first_send",
+        (flat(share_rows), flat(share_rows)),
+        scalars + [VMEM],
+        (VMEM, VMEM),
+        cost=3 << 20,
+    )(*key, adagrad_sums)
+    got_a, got_b = swap(send_a, 0, members), swap(send_b, 1, members)
+    send_c, send_d = kernel_call(
+        lambda *refs: second_kernel(share_rows, *refs),
+        "second_send",
+        (flat(half), flat(half)),
+        scalars + [VMEM] * 3,
+        (VMEM, VMEM),
+        cost=3 << 20,
+    )(*key, adagrad_sums, got_a, got_b)
+    got_c, got_d = swap(send_c, 1, members), swap(send_d, 0, members)
 
     owner = new_owner[:, 0]
     earlier = jnp.tril(owner[:, None] == owner[None, :], -1)
     rank = jnp.sum(earlier.astype(jnp.int32), axis=1)
     place = (owner * capacity + rank)[None, :]
 
-    term_rows = scale_table(lost_member, code_weight, member_ref, table_rows)
-    totals = pending_totals(member_ref, pieces, share_rows)
-    term_rows, got_sums = lax.optimization_barrier((term_rows, got_sums))
+    term_rows = scale_table(*key, table_rows)
+    totals = pending_totals(member, pieces, share_rows)
+    term_rows, send_c, send_d = lax.optimization_barrier((term_rows, send_c, send_d))
     mine_rows = lax.psum_scatter(term_rows, "code", scatter_dimension=0, tiled=True)
 
-    out_sums, new_sums = place_sums(lost_member, code_weight, place, got_sums, totals, slots)
+    scratch = [pltpu.VMEM((share_rows, 256), jnp.bfloat16)]
+    out_sums, new_sums = kernel_call(
+        sums_kernel,
+        "place_sums",
+        (flat(slots), flat(share_rows)),
+        scalars + [VMEM] * 7,
+        (VMEM, VMEM),
+        cost=6 << 20,
+        scratch_shapes=scratch,
+    )(*key, place, adagrad_sums, got_a, got_b, got_c, got_d, totals)
     moved_sums = lax.all_to_all(out_sums, "shard", 0, 0, tiled=True)
-    out_rows = place_rows(place, mine_rows, totals, new_sums, slots)
+    out_rows = kernel_call(
+        rows_kernel, "place_rows", flat(slots), [VMEM] * 4, VMEM, cost=6 << 20, scratch_shapes=scratch
+    )(place, mine_rows, totals, new_sums)
     moved_rows = lax.all_to_all(out_rows, "shard", 0, 0, tiled=True)
 
-    own_weight = jnp.sum(jnp.where(jnp.arange(members) == member, code_weight, 0.0))
-    parity_sums = lax.psum_scatter(own_weight * moved_sums, "code", scatter_dimension=0, tiled=True)
-    got = lax.all_to_all(moved_rows, "code", 0, 0, tiled=True).reshape(members, slots // members, -1)
-    parity_rows = code_weight[0] * got[0]
-    for c in range(1, members):
-        parity_rows = parity_rows + code_weight[c] * got[c]
-    return (moved_rows, moved_sums, parity_rows, parity_sums)
+    final_sums, term_sums = kernel_call(
+        emit_kernel, "emit_sums", (flat(slots), flat(slots)), [SMEM, SMEM, VMEM], (VMEM, VMEM), cost=3 << 20
+    )(code_weight, member, moved_sums)
+    parity_sums = lax.psum_scatter(term_sums, "code", scatter_dimension=0, tiled=True)
+    sends = kernel_call(
+        parity_send_kernel,
+        "parity_send",
+        tuple(flat(quarter) for _ in range(members - 1)),
+        [SMEM, SMEM, VMEM],
+        (VMEM,) * (members - 1),
+        cost=2 << 20,
+    )(code_weight, member, moved_rows)
+    gots = [turn(send, k + 1, members) for k, send in enumerate(sends)]
+    final_rows = kernel_call(copy_kernel, "emit_rows", flat(slots), [VMEM], VMEM, cost=2 << 20)(moved_rows)
+    parity_rows = kernel_call(
+        parity_sum_kernel, "parity_sum", flat(quarter), [SMEM, SMEM] + [VMEM] * 4, VMEM, cost=2 << 20
+    )(code_weight, member, moved_rows, *gots)
+    return (final_rows, final_sums, parity_rows, parity_sums)
 
 
 def solution(mesh):

time: 168 us -> 164 us (0.976)
  waiting for transfers between devices: 97.7 us -> 88.3 us
  Pallas kernels: 8.22 us -> 13.6 us
  other arithmetic: 7.05 us -> 2.4 us
  starting transfers between devices: 31.2 us -> 35.7 us
    all_to_all x2 -> x0, waiting for transfers between devices: 36.3 us -> none  [the longest x1 21.6 us: per_device(): got_sums = lax.all_to_all(adagrad_sums, 'code', 0, 0, tiled=True)]
    ppermute x3 -> x10, waiting for transfers between devices: 11.6 us -> 38.1 us  [the longest x6 20.2 us: turn(): lax.ppermute(array, 'code', [(i, (i + k) % members) for i in range(member...]
    ppermute x3 -> x10, starting transfers between devices: 2.71 us -> 16.5 us  [the longest x6 9.7 us: turn(): lax.ppermute(array, 'code', [(i, (i + k) % members) for i in range(member...]
    all_to_all x2 -> x0, starting transfers between devices: 8.22 us -> none  [the longest x1 4.48 us: per_device(): got_sums = lax.all_to_all(adagrad_sums, 'code', 0, 0, tiled=True)]
    pallas_call x3 -> x9, Pallas kernels: 6.96 us -> 12.4 us  [the longest x1 2.49 us: per_device(): kernel_call(rows_kernel, 'place_rows', flat(slots), [VMEM] * 4, VMEM, cos...]
    add x1 -> x0, other arithmetic: 3.35 us -> none  [per_device(): parity_rows = parity_rows + code_weight[c] * got[c]]
    mul x1 -> x0, other arithmetic: 1.68 us -> none  [per_device(): own_weight * moved_sums]
    unnamed x16 -> x30, local copies, waits for them, and re-layouts: 6.84 us -> 7.1 us
  transfers between devices with their start and end apart: 9 -> 14, of which waited for: 8 -> 10; matrix products, arithmetic and copies ran while one was open for 5% -> 2% of each run, Pallas kernels for 5% -> 7%
where the time goes in v2:
time: 164 us; the launch traced here: 162 us
  waiting for transfers between devices  88.3 us (54%)
  starting transfers between devices  35.7 us (22%)
  between operations  14.9 us (9%)
  Pallas kernels  13.6 us (8%)
  local copies, waits for them, and re-layouts  7.18 us (4%)
  other arithmetic  2.4 us (1%)
    all_to_all x1, waiting for transfers between devices, per_device(): moved_rows = lax.all_to_all(out_rows, 'shard', 0, 0, tiled=True)  25.8 us
    all_to_all x1, waiting for transfers between devices, per_device(): moved_sums = lax.all_to_all(out_sums, 'shard', 0, 0, tiled=True)  24.3 us
    ppermute x6, waiting for transfers between devices, turn(): lax.ppermute(array, 'code', [(i, (i + k) % members) for i in range(member...  20.2 us
    ppermute x4, waiting for transfers between devices, swap(): return lax.ppermute(array, 'code', pairs)  17.9 us
    all_to_all x1, starting transfers between devices, per_device(): moved_sums = lax.all_to_all(out_sums, 'shard', 0, 0, tiled=True)  12.3 us
    ppermute x6, starting transfers between devices, turn(): lax.ppermute(array, 'code', [(i, (i + k) % members) for i in range(member...  9.7 us
    unnamed x30, local copies, waits for them, and re-layouts  7.1 us
    all_to_all x1, starting transfers between devices, per_device(): moved_rows = lax.all_to_all(out_rows, 'shard', 0, 0, tiled=True)  6.87 us
  transfers between devices with their start and end apart: 14, of which 10 were waited for; matrix products, arithmetic and copies ran while one was open for 2% of the time, Pallas kernels for 7%

profile of v2, /device:TPU:32, one launch (start us, length us, event | category | flops | bytes accessed | tf_op | source)
XLA Modules:
  0.0 162.1 jit_solution(13434514984457060915)
XLA Ops:
  7.9 1.6 copy-done
  10.1 1.6 first_send.1
  11.7 1.6 collective-permute-start
  13.3 2.2 %collective-permute-start.1 = (f32[1024,128]{1,0:T(8,128)}, f32[1024,128]{1,0:T(8,128)S(1)}, u32[]{:S(2)}, u32[]{:S(2)}) collective-permute-start(f32[1024,128]{1,0:T(8,128)} %get-tuple-element.17), channel_id=1, source_target_pairs={{0,3},{1,2},{2,1},{3,0},{4,7},{5,6},{6,5},{7,4},{8,11},{9,10},{10,... | collective-permute-start | bytes 1572872 | tf_op jit(solution)/shard_map/ppermute | solution.py:108
  16.3 1.3 copy-done.2
  17.6 7.9 %collective-permute-done.refs_4_.a_ref = f32[1024,128]{1,0:T(8,128)S(1)} collective-permute-done((f32[1024,128]{1,0:T(8,128)}, f32[1024,128]{1,0:T(8,128)S(1)}, u32[]{:S(2)}, u32[]{:S(2)}) %collective-permute-start) | collective-permute-done | bytes 524320 | tf_op jit(solution)/shard_map/ppermute | solution.py:108
  25.6 2.5 %collective-permute-done.1.refs_5_.b_ref = f32[1024,128]{1,0:T(8,128)S(1)} collective-permute-done((f32[1024,128]{1,0:T(8,128)}, f32[1024,128]{1,0:T(8,128)S(1)}, u32[]{:S(2)}, u32[]{:S(2)}) %collective-permute-start.1) | collective-permute-done | bytes 524320 | tf_op jit(solution)/shard_map/ppermute | solution.py:108
  30.8 3.2 %collective-permute-start.3 = (f32[520,128]{1,0:T(8,128)S(1)}, f32[520,128]{1,0:T(8,128)S(1)}, u32[]{:S(2)}, u32[]{:S(2)}) collective-permute-start(f32[520,128]{1,0:T(8,128)S(1)} %maximum_maximum_fusion.refs_1_), channel_id=1, source_target_pairs={{0,3},{1,0},{2,1},{3,2},{4,7},{5,4},{6,5},{7,6},{8,11},{9,8},{10,9... | collective-permute-start | bytes 798728 | tf_op jit(solution)/shard_map/ppermute | solution.py:213
  35.6 1.9 %collective-permute-start.6 = (f32[512,128]{1,0:T(8,128)S(1)}, f32[512,128]{1,0:T(8,128)S(1)}, u32[]{:S(2)}, u32[]{:S(2)}) collective-permute-start(f32[512,128]{1,0:T(8,128)S(1)} %get-tuple-element.19), channel_id=1, source_target_pairs={{0,1},{1,0},{2,3},{3,2},{4,5},{5,4},{6,7},{7,6},{8,9},{9,8},{10,11... | collective-permute-start | bytes 786440 | tf_op jit(solution)/shard_map/ppermute | solution.py:108
  38.8 8.1 %collective-permute-done.2.refs_2_ = f32[520,128]{1,0:T(8,128)S(1)} collective-permute-done((f32[520,128]{1,0:T(8,128)S(1)}, f32[520,128]{1,0:T(8,128)S(1)}, u32[]{:S(2)}, u32[]{:S(2)}) %collective-permute-start.2) | collective-permute-done | bytes 266272 | tf_op jit(solution)/shard_map/ppermute | solution.py:213
  46.9 1.8 %collective-permute-done.3.refs_3_ = f32[520,128]{1,0:T(8,128)S(1)} collective-permute-done((f32[520,128]{1,0:T(8,128)S(1)}, f32[520,128]{1,0:T(8,128)S(1)}, u32[]{:S(2)}, u32[]{:S(2)}) %collective-permute-start.3) | collective-permute-done | bytes 266272 | tf_op jit(solution)/shard_map/ppermute | solution.py:213
  49.0 1.3 pending_totals.1.total_ref
  50.2 7.5 %collective-permute-done.5.c_ref = f32[512,128]{1,0:T(8,128)S(1)} collective-permute-done((f32[512,128]{1,0:T(8,128)}, f32[512,128]{1,0:T(8,128)S(1)}, u32[]{:S(2)}, u32[]{:S(2)}) %collective-permute-start.5) | collective-permute-done | bytes 262176 | tf_op jit(solution)/shard_map/ppermute | solution.py:108
  57.7 1.9 %place_sums.1 = (f32[2048,128]{1,0:T(8,128)S(1)}, f32[1024,128]{1,0:T(8,128)S(1)}) custom-call(s32[1]{0:T(128)S(6)} %copy.11.lost_ref.refs_0_, f32[4]{0:T(128)S(1)} %copy-done.11, s32[1]{0:T(128)} %bitcast.3.member_ref.refs_2_.refs_0_, s32[1,1024]{1,0:T(1,128)S(1)} %bitcast_add_fusion.place_ref, f32[4096,128]{1,0:T(8,128)S(1)} %copy-done.1, ...), custom_call_target="tpu_custom_call" | custom-call | flops 6291456 | bytes 6291456 | tf_op jit(solution)/shard_map/place_sums/pallas_call | solution.py:264
  61.4 12.3 %all-to-all-start.1 = ((f32[64,32,128]{2,1,0:T(8,128)}), f32[64,32,128]{2,1,0:T(8,128)S(1)}, u32[]{:S(2)}, u32[]{:S(2)}) async-start(f32[64,32,128]{2,1,0:T(8,128)} %bitcast.15), calls=%async_computation.2 | async-start | bytes 2097152 | tf_op jit(solution)/shard_map/all_to_all | solution.py:273
  74.8 2.5 %place_rows.1 = f32[2048,128]{1,0:T(8,128)} custom-call(s32[1,1024]{1,0:T(1,128)S(1)} %bitcast_add_fusion.place_ref, f32[1024,128]{1,0:T(8,128)S(1)} %copy-done.7, f32[1024,128]{1,0:T(8,128)S(1)} %pending_totals.1.total_ref, f32[1024,128]{1,0:T(8,128)S(1)} %copy-done.9), custom_call_target="tpu_custom_call" | custom-call | flops 6291456 | bytes 6291456 | tf_op jit(solution)/shard_map/place_rows/pallas_call | solution.py:274
  77.3 24.3 %all-to-all-done.1 = f32[64,32,128]{2,1,0:T(8,128)S(1)} async-done(((f32[64,32,128]{2,1,0:T(8,128)}), f32[64,32,128]{2,1,0:T(8,128)S(1)}, u32[]{:S(2)}, u32[]{:S(2)}) %all-to-all-start.1) | async-done | bytes 1048608 | tf_op jit(solution)/shard_map/all_to_all | solution.py:273
  101.6 6.9 %all-to-all-start = ((f32[64,32,128]{2,1,0:T(8,128)}), f32[64,32,128]{2,1,0:T(8,128)S(1)}, u32[]{:S(2)}, u32[]{:S(2)}) async-start(f32[64,32,128]{2,1,0:T(8,128)} %bitcast.5), calls=%async_computation.1 | async-start | bytes 2097152 | tf_op jit(solution)/shard_map/all_to_all | solution.py:277
  108.5 2.0 %emit_sums.1 = (f32[2048,128]{1,0:T(8,128)}, f32[2048,128]{1,0:T(8,128)}) custom-call(f32[4]{0:T(128)S(1)} %copy-done.11, s32[1]{0:T(128)} %bitcast.3.member_ref.refs_2_.refs_0_, f32[2048,128]{1,0:T(8,128)S(1)} %bitcast.14), custom_call_target="tpu_custom_call" | custom-call | flops 3145728 | bytes 3145728 | tf_op jit(solution)/shard_map/emit_sums/pallas_call | solution.py:279
  110.6 25.8 %all-to-all-done = f32[64,32,128]{2,1,0:T(8,128)S(1)} async-done(((f32[64,32,128]{2,1,0:T(8,128)}), f32[64,32,128]{2,1,0:T(8,128)S(1)}, u32[]{:S(2)}, u32[]{:S(2)}) %all-to-all-start) | async-done | bytes 1048608 | tf_op jit(solution)/shard_map/all_to_all | solution.py:277
  137.1 5.0 %collective-permute-start.8 = (f32[512,128]{1,0:T(8,128)S(1)}, f32[512,128]{1,0:T(8,128)S(1)}, u32[]{:S(2)}, u32[]{:S(2)}) collective-permute-start(f32[512,128]{1,0:T(8,128)S(1)} %get-tuple-element.25), channel_id=1, source_target_pairs={{0,2},{1,3},{2,0},{3,1},{4,6},{5,7},{6,4},{7,5},{8,10},{9,11},{10,... | collective-permute-start | bytes 786440 | tf_op jit(solution)/shard_map/ppermute | solution.py:213
  143.9 3.2 %collective-permute-done.7.a_ref = f32[512,128]{1,0:T(8,128)S(1)} collective-permute-done((f32[512,128]{1,0:T(8,128)S(1)}, f32[512,128]{1,0:T(8,128)S(1)}, u32[]{:S(2)}, u32[]{:S(2)}) %collective-permute-start.7) | collective-permute-done | bytes 262176 | tf_op jit(solution)/shard_map/ppermute | solution.py:213
  147.1 6.8 %collective-permute-done.8.b_ref = f32[512,128]{1,0:T(8,128)S(1)} collective-permute-done((f32[512,128]{1,0:T(8,128)S(1)}, f32[512,128]{1,0:T(8,128)S(1)}, u32[]{:S(2)}, u32[]{:S(2)}) %collective-permute-start.8) | collective-permute-done | bytes 262176 | tf_op jit(solution)/shard_map/ppermute | solution.py:213
  153.9 1.3 parity_sum.1
  (53 shorter events, 12.6 us)
Async XLA Ops:
  7.2 66.6 %reduce-scatter.3.cloned.1.call-start = ((), (), s32[]{:S(2)}) async-start(), calls=%async_computation.4 | async-start | bytes 2621440 | tf_op jit(solution)/shard_map/reduce_scatter | solution.py:261
  7.9 1.6 copy-start
  10.1 5.3 %copy-start.3 = (f32[4096,128]{1,0:T(8,128)S(1)}, f32[4096,128]{1,0:T(8,128)}, u32[]{:S(2)}) copy-start(f32[4096,128]{1,0:T(8,128)} %table_ref.2) | copy-start | bytes 6291460
  11.7 13.9 %collective-permute-start = (f32[1024,128]{1,0:T(8,128)}, f32[1024,128]{1,0:T(8,128)S(1)}, u32[]{:S(2)}, u32[]{:S(2)}) collective-permute-start(f32[1024,128]{1,0:T(8,128)} %get-tuple-element.16), channel_id=1, source_target_pairs={{0,1},{1,0},{2,3},{3,2},{4,5},{5,4},{6,7},{7,6},{8,9},{9,8},{10,11... | collective-permute-start | bytes 1572872 | tf_op jit(solution)/shard_map/ppermute | solution.py:108
  13.3 14.8 %copy-start.1 = (f32[4096,128]{1,0:T(8,128)S(1)}, f32[4096,128]{1,0:T(8,128)}, u32[]{:S(2)}) copy-start(f32[4096,128]{1,0:T(8,128)} %table_ref.3) | copy-start | bytes 6291460
  13.3 14.8 %copy-start.11 = (f32[4]{0:T(128)S(1)}, f32[4]{0:T(128)}, u32[]{:S(2)}) copy-start(f32[4]{0:T(128)} %weight_ref.9) | copy-start | bytes 52
  13.3 14.8 %collective-permute-start.1 = (f32[1024,128]{1,0:T(8,128)}, f32[1024,128]{1,0:T(8,128)S(1)}, u32[]{:S(2)}, u32[]{:S(2)}) collective-permute-start(f32[1024,128]{1,0:T(8,128)} %get-tuple-element.17), channel_id=1, source_target_pairs={{0,3},{1,2},{2,1},{3,0},{4,7},{5,6},{6,5},{7,4},{8,11},{9,10},{10,... | collective-permute-start | bytes 1572872 | tf_op jit(solution)/shard_map/ppermute | solution.py:108
  16.3 1.3 copy-start.2
  17.6 11.9 %copy-start.14 = (s32[512]{0:T(512)S(1)}, s32[512]{0:T(512)}, u32[]{:S(2)}) copy-start(s32[512]{0:T(512)} %param.12) | copy-start | bytes 6148
  28.1 1.3 copy-start.4
  29.4 8.1 %copy-start.13 = (s32[1024,1]{0,1:T(1,128)S(1)}, s32[1024,1]{0,1:T(1,128)}, u32[]{:S(2)}) copy-start(s32[1024,1]{0,1:T(1,128)} %param.11) | copy-start | bytes 12292
  29.5 28.3 %copy-start.5 = (f32[1024,128]{1,0:T(8,128)S(1)}, f32[1024,128]{1,0:T(8,128)}, u32[]{:S(2)}) copy-start(f32[1024,128]{1,0:T(8,128)} %copy-done.4) | copy-start | bytes 1572868
  30.7 16.2 %collective-permute-start.2 = (f32[520,128]{1,0:T(8,128)S(1)}, f32[520,128]{1,0:T(8,128)S(1)}, u32[]{:S(2)}, u32[]{:S(2)}) collective-permute-start(f32[520,128]{1,0:T(8,128)S(1)} %maximum_maximum_fusion.refs_1_), channel_id=1, source_target_pairs={{0,1},{1,2},{2,3},{3,0},{4,5},{5,6},{6,7},{7,4},{8,9},{9,10},{10,1... | collective-permute-start | bytes 798728 | tf_op jit(solution)/shard_map/ppermute | solution.py:213
  30.8 17.9 %collective-permute-start.3 = (f32[520,128]{1,0:T(8,128)S(1)}, f32[520,128]{1,0:T(8,128)S(1)}, u32[]{:S(2)}, u32[]{:S(2)}) collective-permute-start(f32[520,128]{1,0:T(8,128)S(1)} %maximum_maximum_fusion.refs_1_), channel_id=1, source_target_pairs={{0,3},{1,0},{2,1},{3,2},{4,7},{5,4},{6,5},{7,6},{8,11},{9,8},{10,9... | collective-permute-start | bytes 798728 | tf_op jit(solution)/shard_map/ppermute | solution.py:213
  34.0 15.0 %collective-permute-start.4 = (f32[520,128]{1,0:T(8,128)S(1)}, f32[520,128]{1,0:T(8,128)S(1)}, u32[]{:S(2)}, u32[]{:S(2)}) collective-permute-start(f32[520,128]{1,0:T(8,128)S(1)} %maximum_maximum_fusion.refs_1_), channel_id=1, source_target_pairs={{0,2},{1,3},{2,0},{3,1},{4,6},{5,7},{6,4},{7,5},{8,10},{9,11},{10,... | collective-permute-start | bytes 798728 | tf_op jit(solution)/shard_map/ppermute | solution.py:213
  34.5 23.2 %collective-permute-start.5 = (f32[512,128]{1,0:T(8,128)}, f32[512,128]{1,0:T(8,128)S(1)}, u32[]{:S(2)}, u32[]{:S(2)}) collective-permute-start(f32[512,128]{1,0:T(8,128)} %copy-done.12), channel_id=1, source_target_pairs={{0,3},{1,2},{2,1},{3,0},{4,7},{5,6},{6,5},{7,4},{8,11},{9,10},{10,... | collective-permute-start | bytes 786440 | tf_op jit(solution)/shard_map/ppermute | solution.py:108
  35.6 22.2 %collective-permute-start.6 = (f32[512,128]{1,0:T(8,128)S(1)}, f32[512,128]{1,0:T(8,128)S(1)}, u32[]{:S(2)}, u32[]{:S(2)}) collective-permute-start(f32[512,128]{1,0:T(8,128)S(1)} %get-tuple-element.19), channel_id=1, source_target_pairs={{0,1},{1,0},{2,3},{3,2},{4,5},{5,4},{6,7},{7,6},{8,9},{9,8},{10,11... | collective-permute-start | bytes 786440 | tf_op jit(solution)/shard_map/ppermute | solution.py:108
  61.4 12.3 %copy-start.9 = (f32[1024,128]{1,0:T(8,128)S(1)}, f32[1024,128]{1,0:T(8,128)}, u32[]{:S(2)}) copy-start(f32[1024,128]{1,0:T(8,128)} %copy-done.8) | copy-start | bytes 1572868
  61.4 40.2 %all-to-all-start.1 = ((f32[64,32,128]{2,1,0:T(8,128)}), f32[64,32,128]{2,1,0:T(8,128)S(1)}, u32[]{:S(2)}, u32[]{:S(2)}) async-start(f32[64,32,128]{2,1,0:T(8,128)} %bitcast.15), calls=%async_computation.2 | async-start | bytes 2097152 | tf_op jit(solution)/shard_map/all_to_all | solution.py:273
  101.6 34.8 %all-to-all-start = ((f32[64,32,128]{2,1,0:T(8,128)}), f32[64,32,128]{2,1,0:T(8,128)S(1)}, u32[]{:S(2)}, u32[]{:S(2)}) async-start(f32[64,32,128]{2,1,0:T(8,128)} %bitcast.5), calls=%async_computation.1 | async-start | bytes 2097152 | tf_op jit(solution)/shard_map/all_to_all | solution.py:277
  108.5 46.7 %reduce-scatter.5.cloned.1.call-start = ((), (), s32[]{:S(2)}) async-start(), calls=%async_computation.5 | async-start | bytes 1310720 | tf_op jit(solution)/shard_map/reduce_scatter | solution.py:282
  137.0 10.2 %collective-permute-start.7 = (f32[512,128]{1,0:T(8,128)S(1)}, f32[512,128]{1,0:T(8,128)S(1)}, u32[]{:S(2)}, u32[]{:S(2)}) collective-permute-start(f32[512,128]{1,0:T(8,128)S(1)} %get-tuple-element.24), channel_id=1, source_target_pairs={{0,1},{1,2},{2,3},{3,0},{4,5},{5,6},{6,7},{7,4},{8,9},{9,10},{10,1... | collective-permute-start | bytes 786440 | tf_op jit(solution)/shard_map/ppermute | solution.py:213
  137.1 16.9 %collective-permute-start.8 = (f32[512,128]{1,0:T(8,128)S(1)}, f32[512,128]{1,0:T(8,128)S(1)}, u32[]{:S(2)}, u32[]{:S(2)}) collective-permute-start(f32[512,128]{1,0:T(8,128)S(1)} %get-tuple-element.25), channel_id=1, source_target_pairs={{0,2},{1,3},{2,0},{3,1},{4,6},{5,7},{6,4},{7,5},{8,10},{9,11},{10,... | collective-permute-start | bytes 786440 | tf_op jit(solution)/shard_map/ppermute | solution.py:213
  142.1 11.8 %collective-permute-start.9 = (f32[512,128]{1,0:T(8,128)S(1)}, f32[512,128]{1,0:T(8,128)S(1)}, u32[]{:S(2)}, u32[]{:S(2)}) collective-permute-start(f32[512,128]{1,0:T(8,128)S(1)} %get-tuple-element.26), channel_id=1, source_target_pairs={{0,3},{1,0},{2,1},{3,2},{4,7},{5,4},{6,5},{7,6},{8,11},{9,8},{10,9... | collective-permute-start | bytes 786440 | tf_op jit(solution)/shard_map/ppermute | solution.py:213
  (5 other events, 4.2 us)
Sparse Core Ops, SparseCore 0:
  29.6 38.5 reduce-scatter.2
  112.6 27.8 reduce-scatter.4

commit v3 on v2

v3 whole, which is shorter than its diff:
```python
import jax
import jax.numpy as jnp
from jax import lax
from jax.experimental import pallas as pl
from jax.experimental.pallas import tpu as pltpu
from jax.sharding import PartitionSpec as P

step_size = 0.5
epsilon = 1e-08
MEMBERS = 4
SMEM = pl.BlockSpec(memory_space=pltpu.SMEM)
VMEM = pl.BlockSpec(memory_space=pltpu.VMEM)
HBM = pl.BlockSpec(memory_space=pltpu.HBM)
PARAMS = pltpu.CompilerParams(vmem_limit_bytes=24 * 1024 * 1024)


def decode_weights(lost_ref, weight_ref):
    which = lost_ref[0]
    rows = [jnp.full((1, 128), weight_ref[c], jnp.float32) for c in range(MEMBERS)]
    parity_lost = which == 3
    divisor = jnp.where(which == 0, rows[0], jnp.where(which == 1, rows[1], rows[2]))
    divisor = jnp.where(parity_lost, jnp.ones_like(divisor), divisor)
    out = []
    for c in range(3):
        solved = jnp.where(parity_lost, rows[c], -rows[c] / divisor)
        out.append(jnp.where(which == c, jnp.zeros_like(solved), solved))
    out.append(jnp.where(parity_lost, jnp.zeros_like(divisor), 1.0 / divisor))
    return out


def split_halves(value):
    high = value.astype(jnp.bfloat16)
    low = (value - high.astype(jnp.float32)).astype(jnp.bfloat16)
    return high, low


def own_row(weights, member):
    own = weights[3]
    for c in range(3):
        own = jnp.where(member == c, weights[c], own)
    return own


def kernel_call(body, name, out_shape, in_specs, out_specs, cost=0, **kwargs):
    return pl.pallas_call(
        body,
        in_specs=in_specs,
        out_specs=out_specs,
        out_shape=out_shape,
        compiler_params=PARAMS,
        cost_estimate=pl.CostEstimate(flops=cost, bytes_accessed=cost, transcendentals=0),
        name=name,
        **kwargs,
    )


def flat(rows):
    return jax.ShapeDtypeStruct((rows, 128), jnp.float32)


def near(member):
    return member + 1 - 2 * lax.rem(member, 2), 3 - member


def scaled_pieces(table_ref, own, where, outs, buf_ref, sem_ref):
    half = buf_ref.shape[1]
    copies = []
    for i, (quarter, part) in enumerate(where):
        rows = pl.ds(pl.multiple_of(quarter * (2 * half) + part * half, 8), half)
        copies.append(pltpu.make_async_copy(table_ref.at[rows, :], buf_ref.at[i], sem_ref.at[i]))
        copies[-1].start()
    for i, (out_ref, start) in enumerate(outs):
        copies[i].wait()
        out_ref[start : start + half, :] = own * buf_ref[i]


def sent_pieces(member):
    one, two = near(member)
    return [(one, 0), (3 - one, 0), (two, 1), (near(two)[0], 1)]


def kept_pieces(member):
    one, two = near(member)
    return [(two, 0), (one, 1), (member, 0), (member, 1)]


def front_kernel(
    lost_ref, weight_ref, member_ref, table_ref, grads_ref, ids_ref, a_ref, b_ref, packed_ref, buf_ref, sem_ref, pack_sem
):
    member = member_ref[0]
    entries = grads_ref.shape[0]
    grads = pltpu.make_async_copy(grads_ref, packed_ref.at[pl.ds(0, entries), :], pack_sem)
    grads.start()
    own = own_row(decode_weights(lost_ref, weight_ref), member)
    lines = ids_ref.shape[0]
    packed_ref[entries : entries + lines, :] = ids_ref[...].astype(jnp.float32)
    packed_ref[entries + lines :, :] = jnp.zeros((8 - lines, 128), jnp.float32)
    half = buf_ref.shape[1]
    outs = [(a_ref, 0), (a_ref, half), (b_ref, 0), (b_ref, half)]
    scaled_pieces(table_ref, own, sent_pieces(member), outs, buf_ref, sem_ref)
    grads.wait()


def keep_kernel(lost_ref, weight_ref, member_ref, table_ref, c_ref, d_ref, mine_ref, buf_ref, sem_ref):
    member = member_ref[0]
    own = own_row(decode_weights(lost_ref, weight_ref), member)
    half = buf_ref.shape[1]
    outs = [(c_ref, 0), (d_ref, 0), (mine_ref, 0), (mine_ref, half)]
    scaled_pieces(table_ref, own, kept_pieces(member), outs, buf_ref, sem_ref)


def both_kernel(
    lost_ref, weight_ref, member_ref, table_ref, a_ref, b_ref, c_ref, d_ref, mine_ref, buf_ref, sem_ref
):
    member = member_ref[0]
    own = own_row(decode_weights(lost_ref, weight_ref), member)
    half = buf_ref.shape[1]
    outs = [(a_ref, 0), (a_ref, half), (b_ref, 0), (b_ref, half), (c_ref, 0), (d_ref, 0), (mine_ref, 0), (mine_ref, half)]
    scaled_pieces(table_ref, own, sent_pieces(member) + kept_pieces(member), outs, buf_ref, sem_ref)


def second_kernel(c_ref, d_ref, a_ref, b_ref, out_c_ref, out_d_ref):
    half = c_ref.shape[0]
    out_c_ref[...] = c_ref[...] + a_ref[half:, :]
    out_d_ref[...] = d_ref[...] + b_ref[half:, :]


def swap(array, which, members):
    pairs = [(i, i ^ 1) for i in range(members)] if which == 0 else [(i, 3 - i) for i in range(members)]
    return lax.ppermute(array, "code", pairs)


def finish(mine_ref, a_ref, b_ref, c_ref, d_ref):
    half = c_ref.shape[0]
    first = (mine_ref[:half, :] + a_ref[:half, :]) + c_ref[...]
    last = (mine_ref[half:, :] + b_ref[:half, :]) + d_ref[...]
    return jnp.concatenate([first, last], axis=0)


def totals_kernel(count, pieces, member_ref, *refs):
    piece_refs, out_ref = refs[:pieces], refs[pieces]
    first = member_ref[0] * count
    entries = piece_refs[0].shape[0] - 8
    total = jnp.zeros((count, 256), jnp.float32)
    targets = (lax.broadcasted_iota(jnp.int32, (count, 128), 0) + first).astype(jnp.float32)
    for piece in piece_refs:
        high, low = split_halves(piece[:entries, :])
        both = jnp.concatenate([high, low], axis=1)
        hits = jnp.concatenate(
            [
                jnp.where(targets == piece[entries + j : entries + j + 1, :], 1.0, 0.0).astype(jnp.bfloat16)
                for j in range(entries // 128)
            ],
            axis=1,
        )
        total = total + jnp.dot(hits, both, preferred_element_type=jnp.float32)
    out_ref[...] = total[:, :128] + total[:, 128:]


def pending_totals(member, pieces, count):
    return pl.pallas_call(
        lambda *refs: totals_kernel(count, len(pieces), *refs),
        in_specs=[SMEM] + [VMEM] * len(pieces),
        out_specs=VMEM,
        out_shape=jax.ShapeDtypeStruct((count, 128), jnp.float32),
        compiler_params=PARAMS,
        name="pending_totals",
    )(member, *pieces)


def spread(place_ref, values, out_ref, both_ref):
    high, low = split_halves(values)
    both_ref[:, :128] = high
    both_ref[:, 128:] = low
    slots, rows = out_ref.shape[0], values.shape[0]
    step = 256
    place = place_ref[...]
    for start in range(0, slots, step):
        here = lax.broadcasted_iota(jnp.int32, (step, rows), 0) + start
        pick = jnp.where(here == place, 1.0, 0.0).astype(jnp.bfloat16)
        got = jnp.dot(pick, both_ref[...], preferred_element_type=jnp.float32)
        out_ref[start : start + step, :] = got[:, :128] + got[:, 128:]


def sums_kernel(
    place_ref, mine_ref, a_ref, b_ref, c_ref, d_ref, total_ref, out_ref, new_ref, both_ref
):
    total = total_ref[...]
    new = finish(mine_ref, a_ref, b_ref, c_ref, d_ref) + total * total
    new_ref[...] = new
    spread(place_ref, new, out_ref, both_ref)


def rows_kernel(
    place_ref, mine_ref, a_ref, b_ref, c_ref, d_ref, total_ref, sums_ref, out_ref, both_ref
):
    mine = finish(mine_ref, a_ref, b_ref, c_ref, d_ref)
    new = mine - step_size * total_ref[...] / (jnp.sqrt(sums_ref[...]) + epsilon)
    spread(place_ref, new, out_ref, both_ref)


def own_code_weight(weight_ref, member):
    own = weight_ref[3]
    for c in range(3):
        own = jnp.where(member == c, weight_ref[c], own)
    return own


def copy_kernel(moved_ref, out_ref):
    out_ref[...] = moved_ref[...]


def quarter_of(which, count):
    return pl.ds(pl.multiple_of(lax.rem(which, MEMBERS) * count, 8), count)


def parity_send_kernel(weight_ref, member_ref, moved_ref, *out_refs):
    member = member_ref[0]
    own = own_code_weight(weight_ref, member)
    count = out_refs[0].shape[0]
    for k, out_ref in enumerate(out_refs):
        out_ref[...] = own * moved_ref[quarter_of(member + k + 1, count), :]


def parity_sum_kernel(weight_ref, member_ref, moved_ref, a_ref, b_ref, c_ref, out_ref):
    member = member_ref[0]
    own = own_code_weight(weight_ref, member)
    mine = own * moved_ref[quarter_of(member, out_ref.shape[0]), :]
    out_ref[...] = (mine + a_ref[...]) + (b_ref[...] + c_ref[...])


def turn(array, k, members):
    return lax.ppermute(array, "code", [(i, (i + k) % members) for i in range(members)])


def parity_of(name, key, moved, members):
    slots = moved.shape[0]
    quarter = slots // members
    sends = kernel_call(
        parity_send_kernel,
        "parity_send_" + name,
        tuple(flat(quarter) for _ in range(members - 1)),
        [SMEM, SMEM, VMEM],
        (VMEM,) * (members - 1),
        cost=2 << 20,
    )(*key, moved)
    gots = [turn(send, k + 1, members) for k, send in enumerate(sends)]
    out = kernel_call(copy_kernel, "emit_" + name, flat(slots), [VMEM], VMEM, cost=2 << 20)(moved)
    parity = kernel_call(
        parity_sum_kernel, "parity_sum_" + name, flat(quarter), [SMEM, SMEM] + [VMEM] * 4, VMEM, cost=2 << 20
    )(*key, moved, *gots)
    return out, parity


def per_device(
    table_rows, adagrad_sums, lost_member, code_weight, new_owner, pending_rows, pending_grads
):
    members = lax.axis_size("code")
    shards = lax.axis_size("shard")
    member = lax.axis_index("code").astype(jnp.int32)[None]
    share = table_rows.shape[0] // members
    capacity = max(2, (2 * share + shards - 1) // shards)
    slots = shards * capacity
    half = share // 2
    entries = pending_grads.shape[0]
    scalars = [SMEM, SMEM, SMEM]
    key = (lost_member, code_weight, member)
    owner = new_owner[:, 0]

    def buffers(count):
        return [pltpu.VMEM((count, half, 128), jnp.float32), pltpu.SemaphoreType.DMA((count,))]

    send_a, send_b, packed = kernel_call(
        front_kernel,
        "front_send",
        (flat(share), flat(share), flat(entries + 8)),
        scalars + [HBM, HBM, VMEM],
        (VMEM, VMEM, VMEM),
        cost=3 << 20,
        scratch_shapes=buffers(4) + [pltpu.SemaphoreType.DMA],
    )(*key, adagrad_sums, pending_grads, pending_rows.reshape(-1, 128))
    got_a, got_b = swap(send_a, 0, members), swap(send_b, 1, members)
    pieces = [packed] + [turn(packed, k, members) for k in (1, 3, 2)]

    keep_c, keep_d, mine_sums = kernel_call(
        keep_kernel,
        "keep_sums",
        (flat(half), flat(half), flat(share)),
        scalars + [HBM],
        (VMEM, VMEM, VMEM),
        cost=3 << 20,
        scratch_shapes=buffers(4),
    )(*key, adagrad_sums)
    row_a, row_b, row_c, row_d, mine_rows = kernel_call(
        both_kernel,
        "weigh_rows",
        (flat(share), flat(share), flat(half), flat(half), flat(share)),
        scalars + [HBM],
        (VMEM,) * 5,
        cost=4 << 20,
        scratch_shapes=buffers(8),
    )(*key, table_rows)
    earlier = jnp.tril(owner[:, None] == owner[None, :], -1)
    rank = jnp.sum(earlier.astype(jnp.int32), axis=1)
    place = (owner * capacity + rank)[None, :]
    totals = pending_totals(member, pieces, share)

    def second(name, *args):
        return kernel_call(
            second_kernel, "second_" + name, (flat(half), flat(half)), [VMEM] * 4, (VMEM, VMEM), cost=1 << 20
        )(*args)

    totals, got_a, got_b = lax.optimization_barrier((totals, got_a, got_b))
    send_c, send_d = second("sums", keep_c, keep_d, got_a, got_b)
    got_c, got_d = swap(send_c, 1, members), swap(send_d, 0, members)
    row_a, row_b, got_c, got_d = lax.optimization_barrier((row_a, row_b, got_c, got_d))
    back_a, back_b = swap(row_a, 0, members), swap(row_b, 1, members)

    scratch = [pltpu.VMEM((share, 256), jnp.bfloat16)]
    out_sums, new_sums = kernel_call(
        sums_kernel,
        "place_sums",
        (flat(slots), flat(share)),
        [VMEM] * 7,
        (VMEM, VMEM),
        cost=6 << 20,
        scratch_shapes=scratch,
    )(place, mine_sums, got_a, got_b, got_c, got_d, totals)
    moved_sums = lax.all_to_all(out_sums, "shard", 0, 0, tiled=True)

    send_c, send_d = second("rows", row_c, row_d, back_a, back_b)
    back_c, back_d = swap(send_c, 1, members), swap(send_d, 0, members)
    out_rows = kernel_call(
        rows_kernel, "place_rows", flat(slots), [VMEM] * 8, VMEM, cost=6 << 20, scratch_shapes=scratch
    )(place, mine_rows, back_a, back_b, back_c, back_d, totals, new_sums)
    moved_rows = lax.all_to_all(out_rows, "shard", 0, 0, tiled=True)

    final_sums, parity_sums = parity_of("sums", (code_weight, member), moved_sums, members)
    final_rows, parity_rows = parity_of("rows", (code_weight, member), moved_rows, members)
    return (final_rows, final_sums, parity_rows, parity_sums)


def solution(mesh):
    in_specs = (
        P(("shard", "code"), None),
        P(("shard", "code"), None),
        P("shard"),
        P(),
        P(("shard", "code"), None),
        P(("shard", "code")),
        P(("shard", "code"), None),
    )
    out_specs = (
        P(("shard", "code"), None),
        P(("shard", "code"), None),
        P(("shard", "code"), None),
        P(("shard", "code"), None),
    )
    return jax.shard_map(
        per_device, mesh=mesh, in_specs=in_specs, out_specs=out_specs, check_vma=False
    )
```

time: 164 us -> 142 us (0.87)
  between operations: 14.9 us -> 1.46 us
  waiting for transfers between devices: 88.3 us -> 76.4 us
  starting transfers between devices: 35.7 us -> 41.6 us
  local copies, waits for them, and re-layouts: 7.18 us -> 4.68 us
    all_to_all x1, waiting for transfers between devices: 24.3 us -> 0.85 us  [per_device(): moved_sums = lax.all_to_all(out_sums, 'shard', 0, 0, tiled=True)]
    ppermute x6 -> x9, waiting for transfers between devices: 20.2 us -> 28.1 us  [turn(): lax.ppermute(array, 'code', [(i, (i + k) % members) for i in range(member...]
    ppermute x4 -> x8, waiting for transfers between devices: 17.9 us -> 24.7 us  [swap(): return lax.ppermute(array, 'code', pairs)]
    all_to_all x1, waiting for transfers between devices: 25.8 us -> 22.7 us  [per_device(): moved_rows = lax.all_to_all(out_rows, 'shard', 0, 0, tiled=True)]
    ppermute x4 -> x8, starting transfers between devices: 6.77 us -> 9.38 us  [swap(): return lax.ppermute(array, 'code', pairs)]
    all_to_all x1, starting transfers between devices: 6.87 us -> 9.48 us  [per_device(): moved_rows = lax.all_to_all(out_rows, 'shard', 0, 0, tiled=True)]
    unnamed x30 -> x18, local copies, waits for them, and re-layouts: 7.1 us -> 4.68 us
    pallas_call x9 -> x13, Pallas kernels: 12.4 us -> 14 us  [the longest x2 2.58 us: parity_of(): kernel_call(parity_sum_kernel, 'parity_sum_' + name, flat(quarter), [SMEM...]
  transfers between devices with their start and end apart: 14 -> 19, of which waited for: 10 -> 13; matrix products, arithmetic and copies ran while one was open for 2% -> 1% of each run, Pallas kernels for 7% -> 8%
where the time goes in v3:
time: 142 us; the launch traced here: 141 us
  waiting for transfers between devices  76.4 us (54%)
  starting transfers between devices  41.6 us (29%)
  Pallas kernels  15.2 us (11%)
  local copies, waits for them, and re-layouts  4.68 us (3%)
  between operations  1.46 us (1%)
    ppermute x9, waiting for transfers between devices, turn(): lax.ppermute(array, 'code', [(i, (i + k) % members) for i in range(member...  28.1 us
    ppermute x8, waiting for transfers between devices, swap(): return lax.ppermute(array, 'code', pairs)  24.7 us
    all_to_all x1, waiting for transfers between devices, per_device(): moved_rows = lax.all_to_all(out_rows, 'shard', 0, 0, tiled=True)  22.7 us
    all_to_all x1, starting transfers between devices, per_device(): moved_sums = lax.all_to_all(out_sums, 'shard', 0, 0, tiled=True)  11.6 us
    ppermute x9, starting transfers between devices, turn(): lax.ppermute(array, 'code', [(i, (i + k) % members) for i in range(member...  11.2 us
    all_to_all x1, starting transfers between devices, per_device(): moved_rows = lax.all_to_all(out_rows, 'shard', 0, 0, tiled=True)  9.48 us
    ppermute x8, starting transfers between devices, swap(): return lax.ppermute(array, 'code', pairs)  9.38 us
    unnamed x18, local copies, waits for them, and re-layouts  4.68 us
  transfers between devices with their start and end apart: 19, of which 13 were waited for; matrix products, arithmetic and copies ran while one was open for 1% of the time, Pallas kernels for 8%

profile of v3, /device:TPU:32, one launch (start us, length us, event | category | flops | bytes accessed | tf_op | source)
XLA Modules:
  0.0 140.6 jit_solution(10357639527513997909)
XLA Ops:
  1.3 1.6 %copy-done = f32[4096,128]{1,0:T(8,128)S(1)} copy-done((f32[4096,128]{1,0:T(8,128)S(1)}, f32[4096,128]{1,0:T(8,128)}, u32[]{:S(2)}) %copy-start) | copy-done | bytes 2097176
  5.9 1.7 %collective-permute-start.3 = (f32[1024,128]{1,0:T(8,128)S(1)}, f32[1024,128]{1,0:T(8,128)S(1)}, u32[]{:S(2)}, u32[]{:S(2)}) collective-permute-start(f32[1024,128]{1,0:T(8,128)S(1)} %get-tuple-element.40), channel_id=1, source_target_pairs={{0,1},{1,0},{2,3},{3,2},{4,5},{5,4},{6,7},{7,6},{8,9},{9,8},{10,11... | collective-permute-start | bytes 1572872 | tf_op jit(solution)/shard_map/ppermute | solution.py:130
  7.6 2.2 %collective-permute-start.4 = (f32[1024,128]{1,0:T(8,128)S(1)}, f32[1024,128]{1,0:T(8,128)S(1)}, u32[]{:S(2)}, u32[]{:S(2)}) collective-permute-start(f32[1024,128]{1,0:T(8,128)S(1)} %get-tuple-element.41), channel_id=1, source_target_pairs={{0,3},{1,2},{2,1},{3,0},{4,7},{5,6},{6,5},{7,4},{8,11},{9,10},{10,... | collective-permute-start | bytes 1572872 | tf_op jit(solution)/shard_map/ppermute | solution.py:130
  10.5 2.6 %collective-permute-start.1 = (f32[520,128]{1,0:T(8,128)S(1)}, f32[520,128]{1,0:T(8,128)S(1)}, u32[]{:S(2)}, u32[]{:S(2)}) collective-permute-start(f32[520,128]{1,0:T(8,128)S(1)} %get-tuple-element.39.refs_1_), channel_id=1, source_target_pairs={{0,3},{1,0},{2,1},{3,2},{4,7},{5,4},{6,5},{7,6},{8,11},{9,8},{10,9... | collective-permute-start | bytes 798728 | tf_op jit(solution)/shard_map/ppermute | solution.py:233
  13.9 15.1 %collective-permute-done.2.refs_4_ = f32[520,128]{1,0:T(8,128)S(1)} collective-permute-done((f32[520,128]{1,0:T(8,128)S(1)}, f32[520,128]{1,0:T(8,128)S(1)}, u32[]{:S(2)}, u32[]{:S(2)}) %collective-permute-start.2) | collective-permute-done | bytes 266272 | tf_op jit(solution)/shard_map/ppermute | solution.py:233
  29.0 3.1 %collective-permute-done.1.refs_3_ = f32[520,128]{1,0:T(8,128)S(1)} collective-permute-done((f32[520,128]{1,0:T(8,128)S(1)}, f32[520,128]{1,0:T(8,128)S(1)}, u32[]{:S(2)}, u32[]{:S(2)}) %collective-permute-start.1) | collective-permute-done | bytes 266272 | tf_op jit(solution)/shard_map/ppermute | solution.py:233
  32.1 1.5 %collective-permute-done.refs_2_ = f32[520,128]{1,0:T(8,128)S(1)} collective-permute-done((f32[520,128]{1,0:T(8,128)S(1)}, f32[520,128]{1,0:T(8,128)S(1)}, u32[]{:S(2)}, u32[]{:S(2)}) %collective-permute-start) | collective-permute-done | bytes 266272 | tf_op jit(solution)/shard_map/ppermute | solution.py:233
  35.0 2.3 %collective-permute-start.5 = (f32[512,128]{1,0:T(8,128)S(1)}, f32[512,128]{1,0:T(8,128)S(1)}, u32[]{:S(2)}, u32[]{:S(2)}) collective-permute-start(f32[512,128]{1,0:T(8,128)S(1)} %get-tuple-element.44), channel_id=1, source_target_pairs={{0,3},{1,2},{2,1},{3,0},{4,7},{5,6},{6,5},{7,4},{8,11},{9,10},{10,... | collective-permute-start | bytes 786440 | tf_op jit(solution)/shard_map/ppermute | solution.py:130
  40.3 2.8 %collective-permute-done.5.c_ref = f32[512,128]{1,0:T(8,128)S(1)} collective-permute-done((f32[512,128]{1,0:T(8,128)S(1)}, f32[512,128]{1,0:T(8,128)S(1)}, u32[]{:S(2)}, u32[]{:S(2)}) %collective-permute-start.5) | collective-permute-done | bytes 262176 | tf_op jit(solution)/shard_map/ppermute | solution.py:130
  43.8 2.3 %place_sums.1 = (f32[2048,128]{1,0:T(8,128)}, f32[1024,128]{1,0:T(8,128)S(1)}) custom-call(s32[1,1024]{1,0:T(1,128)S(1)} %bitcast_add_fusion.place_ref, f32[1024,128]{1,0:T(8,128)S(1)} %get-tuple-element.53.mine_ref, f32[1024,128]{1,0:T(8,128)S(1)} %collective-permute-done.3.a_ref, f32[1024,128]{1,0:T(8,128)S(1)} %collective-permute-done.4.b_ref, ...), custom_call_target="tpu_custom_call" | custom-call | flops 6291456 | bytes 6291456 | tf_op jit(solution)/shard_map/place_sums/pallas_call | solution.py:320
  46.1 11.6 %all-to-all-start.1 = ((f32[64,32,128]{2,1,0:T(8,128)}), f32[64,32,128]{2,1,0:T(8,128)S(1)}, u32[]{:S(2)}, u32[]{:S(2)}) async-start(f32[64,32,128]{2,1,0:T(8,128)} %bitcast.7), calls=%async_computation.1 | async-start | bytes 2097152 | tf_op jit(solution)/shard_map/all_to_all | solution.py:329
  58.1 1.3 collective-permute-start.8
  59.4 12.6 %collective-permute-done.7.a_ref = f32[1024,128]{1,0:T(8,128)S(1)} collective-permute-done((f32[1024,128]{1,0:T(8,128)}, f32[1024,128]{1,0:T(8,128)S(1)}, u32[]{:S(2)}, u32[]{:S(2)}) %collective-permute-start.7) | collective-permute-done | bytes 524320 | tf_op jit(solution)/shard_map/ppermute | solution.py:130
  72.0 1.3 collective-permute-done.8.b_ref
  73.4 1.6 %collective-permute-start.9 = (f32[512,128]{1,0:T(8,128)S(1)}, f32[512,128]{1,0:T(8,128)S(1)}, u32[]{:S(2)}, u32[]{:S(2)}) collective-permute-start(f32[512,128]{1,0:T(8,128)S(1)} %get-tuple-element.50), channel_id=1, source_target_pairs={{0,3},{1,2},{2,1},{3,0},{4,7},{5,6},{6,5},{7,4},{8,11},{9,10},{10,... | collective-permute-start | bytes 786440 | tf_op jit(solution)/shard_map/ppermute | solution.py:130
  75.0 7.0 %collective-permute-done.9.c_ref = f32[512,128]{1,0:T(8,128)S(1)} collective-permute-done((f32[512,128]{1,0:T(8,128)S(1)}, f32[512,128]{1,0:T(8,128)S(1)}, u32[]{:S(2)}, u32[]{:S(2)}) %collective-permute-start.9) | collective-permute-done | bytes 262176 | tf_op jit(solution)/shard_map/ppermute | solution.py:130
  82.2 2.6 %place_rows.1 = f32[2048,128]{1,0:T(8,128)} custom-call(s32[1,1024]{1,0:T(1,128)S(1)} %bitcast_add_fusion.place_ref, f32[1024,128]{1,0:T(8,128)S(1)} %get-tuple-element.34.mine_ref, f32[1024,128]{1,0:T(8,128)S(1)} %collective-permute-done.7.a_ref, f32[1024,128]{1,0:T(8,128)S(1)} %collective-permute-done.8.b_ref, ...), custom_call_target="tpu_custom_call" | custom-call | flops 6291456 | bytes 6291456 | tf_op jit(solution)/shard_map/place_rows/pallas_call | solution.py:333
  85.6 9.5 %all-to-all-start = ((f32[64,32,128]{2,1,0:T(8,128)}), f32[64,32,128]{2,1,0:T(8,128)S(1)}, u32[]{:S(2)}, u32[]{:S(2)}) async-start(f32[64,32,128]{2,1,0:T(8,128)} %bitcast.5), calls=%async_computation | async-start | bytes 2097152 | tf_op jit(solution)/shard_map/all_to_all | solution.py:336
  95.1 1.3 parity_send_sums.1
  96.7 2.7 %collective-permute-start.15 = (f32[512,128]{1,0:T(8,128)S(1)}, f32[512,128]{1,0:T(8,128)S(1)}, u32[]{:S(2)}, u32[]{:S(2)}) collective-permute-start(f32[512,128]{1,0:T(8,128)S(1)} %get-tuple-element.62), channel_id=1, source_target_pairs={{0,2},{1,3},{2,0},{3,1},{4,6},{5,7},{6,4},{7,5},{8,10},{9,11},{10,... | collective-permute-start | bytes 786440 | tf_op jit(solution)/shard_map/ppermute | solution.py:233
  100.3 22.7 %all-to-all-done = f32[64,32,128]{2,1,0:T(8,128)S(1)} async-done(((f32[64,32,128]{2,1,0:T(8,128)}), f32[64,32,128]{2,1,0:T(8,128)S(1)}, u32[]{:S(2)}, u32[]{:S(2)}) %all-to-all-start) | async-done | bytes 1048608 | tf_op jit(solution)/shard_map/all_to_all | solution.py:336
  123.9 2.7 %collective-permute-start.12 = (f32[512,128]{1,0:T(8,128)S(1)}, f32[512,128]{1,0:T(8,128)S(1)}, u32[]{:S(2)}, u32[]{:S(2)}) collective-permute-start(f32[512,128]{1,0:T(8,128)S(1)} %get-tuple-element.59), channel_id=1, source_target_pairs={{0,2},{1,3},{2,0},{3,1},{4,6},{5,7},{6,4},{7,5},{8,10},{9,11},{10,... | collective-permute-start | bytes 786440 | tf_op jit(solution)/shard_map/ppermute | solution.py:233
  128.6 1.3 parity_sum_sums.1
  130.9 7.8 %collective-permute-done.11.a_ref = f32[512,128]{1,0:T(8,128)S(1)} collective-permute-done((f32[512,128]{1,0:T(8,128)S(1)}, f32[512,128]{1,0:T(8,128)S(1)}, u32[]{:S(2)}, u32[]{:S(2)}) %collective-permute-start.11) | collective-permute-done | bytes 262176 | tf_op jit(solution)/shard_map/ppermute | solution.py:233
  (49 shorter events, 18.1 us)
Async XLA Ops:
  1.3 1.6 %copy-start = (f32[4096,128]{1,0:T(8,128)S(1)}, f32[4096,128]{1,0:T(8,128)}, u32[]{:S(2)}) copy-start(f32[4096,128]{1,0:T(8,128)} %table_ref.5) | copy-start | bytes 6291460
  5.9 28.9 %collective-permute-start.3 = (f32[1024,128]{1,0:T(8,128)S(1)}, f32[1024,128]{1,0:T(8,128)S(1)}, u32[]{:S(2)}, u32[]{:S(2)}) collective-permute-start(f32[1024,128]{1,0:T(8,128)S(1)} %get-tuple-element.40), channel_id=1, source_target_pairs={{0,1},{1,0},{2,3},{3,2},{4,5},{5,4},{6,7},{7,6},{8,9},{9,8},{10,11... | collective-permute-start | bytes 1572872 | tf_op jit(solution)/shard_map/ppermute | solution.py:130
  7.6 27.3 %collective-permute-start.4 = (f32[1024,128]{1,0:T(8,128)S(1)}, f32[1024,128]{1,0:T(8,128)S(1)}, u32[]{:S(2)}, u32[]{:S(2)}) collective-permute-start(f32[1024,128]{1,0:T(8,128)S(1)} %get-tuple-element.41), channel_id=1, source_target_pairs={{0,3},{1,2},{2,1},{3,0},{4,7},{5,6},{6,5},{7,4},{8,11},{9,10},{10,... | collective-permute-start | bytes 1572872 | tf_op jit(solution)/shard_map/ppermute | solution.py:130
  9.8 19.3 %collective-permute-start.2 = (f32[520,128]{1,0:T(8,128)S(1)}, f32[520,128]{1,0:T(8,128)S(1)}, u32[]{:S(2)}, u32[]{:S(2)}) collective-permute-start(f32[520,128]{1,0:T(8,128)S(1)} %get-tuple-element.39.refs_1_), channel_id=1, source_target_pairs={{0,2},{1,3},{2,0},{3,1},{4,6},{5,7},{6,4},{7,5},{8,10},{9,11},{10,... | collective-permute-start | bytes 798728 | tf_op jit(solution)/shard_map/ppermute | solution.py:233
  10.5 21.6 %collective-permute-start.1 = (f32[520,128]{1,0:T(8,128)S(1)}, f32[520,128]{1,0:T(8,128)S(1)}, u32[]{:S(2)}, u32[]{:S(2)}) collective-permute-start(f32[520,128]{1,0:T(8,128)S(1)} %get-tuple-element.39.refs_1_), channel_id=1, source_target_pairs={{0,3},{1,0},{2,1},{3,2},{4,7},{5,4},{6,5},{7,6},{8,11},{9,8},{10,9... | collective-permute-start | bytes 798728 | tf_op jit(solution)/shard_map/ppermute | solution.py:233
  13.1 20.5 %collective-permute-start = (f32[520,128]{1,0:T(8,128)S(1)}, f32[520,128]{1,0:T(8,128)S(1)}, u32[]{:S(2)}, u32[]{:S(2)}) collective-permute-start(f32[520,128]{1,0:T(8,128)S(1)} %get-tuple-element.39.refs_1_), channel_id=1, source_target_pairs={{0,1},{1,2},{2,3},{3,0},{4,5},{5,6},{6,7},{7,4},{8,9},{9,10},{10,1... | collective-permute-start | bytes 798728 | tf_op jit(solution)/shard_map/ppermute | solution.py:233
  13.9 23.3 %copy-start.8 = (s32[1024,1]{0,1:T(1,128)S(1)}, s32[1024,1]{0,1:T(1,128)}, u32[]{:S(2)}) copy-start(s32[1024,1]{0,1:T(1,128)} %param.11) | copy-start | bytes 12292
  13.9 24.6 %copy-start.1 = (f32[4096,128]{1,0:T(8,128)S(1)}, f32[4096,128]{1,0:T(8,128)}, u32[]{:S(2)}) copy-start(f32[4096,128]{1,0:T(8,128)} %table_ref.3) | copy-start | bytes 6291460
  13.9 24.6 %copy-start.4 = (f32[4]{0:T(128)S(1)}, f32[4]{0:T(128)}, u32[]{:S(2)}) copy-start(f32[4]{0:T(128)} %weight_ref.13) | copy-start | bytes 52
  35.0 8.2 %collective-permute-start.5 = (f32[512,128]{1,0:T(8,128)S(1)}, f32[512,128]{1,0:T(8,128)S(1)}, u32[]{:S(2)}, u32[]{:S(2)}) collective-permute-start(f32[512,128]{1,0:T(8,128)S(1)} %get-tuple-element.44), channel_id=1, source_target_pairs={{0,3},{1,2},{2,1},{3,0},{4,7},{5,6},{6,5},{7,4},{8,11},{9,10},{10,... | collective-permute-start | bytes 786440 | tf_op jit(solution)/shard_map/ppermute | solution.py:130
  37.2 6.6 %collective-permute-start.6 = (f32[512,128]{1,0:T(8,128)S(1)}, f32[512,128]{1,0:T(8,128)S(1)}, u32[]{:S(2)}, u32[]{:S(2)}) collective-permute-start(f32[512,128]{1,0:T(8,128)S(1)} %get-tuple-element.45), channel_id=1, source_target_pairs={{0,1},{1,0},{2,3},{3,2},{4,5},{5,4},{6,7},{7,6},{8,9},{9,8},{10,11... | collective-permute-start | bytes 786440 | tf_op jit(solution)/shard_map/ppermute | solution.py:130
  40.3 5.9 %copy-start.6 = (f32[1024,128]{1,0:T(8,128)}, f32[1024,128]{1,0:T(8,128)S(1)}, u32[]{:S(2)}) copy-start(f32[1024,128]{1,0:T(8,128)S(1)} %get-tuple-element.47) | copy-start | bytes 1572868
  46.1 39.5 %all-to-all-start.1 = ((f32[64,32,128]{2,1,0:T(8,128)}), f32[64,32,128]{2,1,0:T(8,128)S(1)}, u32[]{:S(2)}, u32[]{:S(2)}) async-start(f32[64,32,128]{2,1,0:T(8,128)} %bitcast.7), calls=%async_computation.1 | async-start | bytes 2097152 | tf_op jit(solution)/shard_map/all_to_all | solution.py:329
  57.7 14.3 %collective-permute-start.7 = (f32[1024,128]{1,0:T(8,128)}, f32[1024,128]{1,0:T(8,128)S(1)}, u32[]{:S(2)}, u32[]{:S(2)}) collective-permute-start(f32[1024,128]{1,0:T(8,128)} %copy-done.7), channel_id=1, source_target_pairs={{0,1},{1,0},{2,3},{3,2},{4,5},{5,4},{6,7},{7,6},{8,9},{9,8},{10,11... | collective-permute-start | bytes 1572872 | tf_op jit(solution)/shard_map/ppermute | solution.py:130
  58.1 15.2 %collective-permute-start.8 = (f32[1024,128]{1,0:T(8,128)}, f32[1024,128]{1,0:T(8,128)S(1)}, u32[]{:S(2)}, u32[]{:S(2)}) collective-permute-start(f32[1024,128]{1,0:T(8,128)} %copy-done.6), channel_id=1, source_target_pairs={{0,3},{1,2},{2,1},{3,0},{4,7},{5,6},{6,5},{7,4},{8,11},{9,10},{10,... | collective-permute-start | bytes 1572872 | tf_op jit(solution)/shard_map/ppermute | solution.py:130
  73.4 8.6 %collective-permute-start.9 = (f32[512,128]{1,0:T(8,128)S(1)}, f32[512,128]{1,0:T(8,128)S(1)}, u32[]{:S(2)}, u32[]{:S(2)}) collective-permute-start(f32[512,128]{1,0:T(8,128)S(1)} %get-tuple-element.50), channel_id=1, source_target_pairs={{0,3},{1,2},{2,1},{3,0},{4,7},{5,6},{6,5},{7,4},{8,11},{9,10},{10,... | collective-permute-start | bytes 786440 | tf_op jit(solution)/shard_map/ppermute | solution.py:130
  75.0 7.3 %collective-permute-start.10 = (f32[512,128]{1,0:T(8,128)S(1)}, f32[512,128]{1,0:T(8,128)S(1)}, u32[]{:S(2)}, u32[]{:S(2)}) collective-permute-start(f32[512,128]{1,0:T(8,128)S(1)} %get-tuple-element.51), channel_id=1, source_target_pairs={{0,1},{1,0},{2,3},{3,2},{4,5},{5,4},{6,7},{7,6},{8,9},{9,8},{10,11... | collective-permute-start | bytes 786440 | tf_op jit(solution)/shard_map/ppermute | solution.py:130
  85.6 37.4 %all-to-all-start = ((f32[64,32,128]{2,1,0:T(8,128)}), f32[64,32,128]{2,1,0:T(8,128)S(1)}, u32[]{:S(2)}, u32[]{:S(2)}) async-start(f32[64,32,128]{2,1,0:T(8,128)} %bitcast.5), calls=%async_computation | async-start | bytes 2097152 | tf_op jit(solution)/shard_map/all_to_all | solution.py:336
  96.4 30.3 %collective-permute-start.14 = (f32[512,128]{1,0:T(8,128)}, f32[512,128]{1,0:T(8,128)S(1)}, u32[]{:S(2)}, u32[]{:S(2)}) collective-permute-start(f32[512,128]{1,0:T(8,128)} %get-tuple-element.61), channel_id=1, source_target_pairs={{0,1},{1,2},{2,3},{3,0},{4,5},{5,6},{6,7},{7,4},{8,9},{9,10},{10,1... | collective-permute-start | bytes 786440 | tf_op jit(solution)/shard_map/ppermute | solution.py:233
  96.7 31.9 %collective-permute-start.15 = (f32[512,128]{1,0:T(8,128)S(1)}, f32[512,128]{1,0:T(8,128)S(1)}, u32[]{:S(2)}, u32[]{:S(2)}) collective-permute-start(f32[512,128]{1,0:T(8,128)S(1)} %get-tuple-element.62), channel_id=1, source_target_pairs={{0,2},{1,3},{2,0},{3,1},{4,6},{5,7},{6,4},{7,5},{8,10},{9,11},{10,... | collective-permute-start | bytes 786440 | tf_op jit(solution)/shard_map/ppermute | solution.py:233
  99.4 29.2 %collective-permute-start.16 = (f32[512,128]{1,0:T(8,128)S(1)}, f32[512,128]{1,0:T(8,128)S(1)}, u32[]{:S(2)}, u32[]{:S(2)}) collective-permute-start(f32[512,128]{1,0:T(8,128)S(1)} %get-tuple-element.63), channel_id=1, source_target_pairs={{0,3},{1,0},{2,1},{3,2},{4,7},{5,4},{6,5},{7,6},{8,11},{9,8},{10,9... | collective-permute-start | bytes 786440 | tf_op jit(solution)/shard_map/ppermute | solution.py:233
  123.6 15.1 %collective-permute-start.11 = (f32[512,128]{1,0:T(8,128)S(1)}, f32[512,128]{1,0:T(8,128)S(1)}, u32[]{:S(2)}, u32[]{:S(2)}) collective-permute-start(f32[512,128]{1,0:T(8,128)S(1)} %get-tuple-element.58), channel_id=1, source_target_pairs={{0,1},{1,2},{2,3},{3,0},{4,5},{5,6},{6,7},{7,4},{8,9},{9,10},{10,1... | collective-permute-start | bytes 786440 | tf_op jit(solution)/shard_map/ppermute | solution.py:233
  123.9 14.8 %collective-permute-start.12 = (f32[512,128]{1,0:T(8,128)S(1)}, f32[512,128]{1,0:T(8,128)S(1)}, u32[]{:S(2)}, u32[]{:S(2)}) collective-permute-start(f32[512,128]{1,0:T(8,128)S(1)} %get-tuple-element.59), channel_id=1, source_target_pairs={{0,2},{1,3},{2,0},{3,1},{4,6},{5,7},{6,4},{7,5},{8,10},{9,11},{10,... | collective-permute-start | bytes 786440 | tf_op jit(solution)/shard_map/ppermute | solution.py:233
  126.7 12.7 %collective-permute-start.13 = (f32[512,128]{1,0:T(8,128)S(1)}, f32[512,128]{1,0:T(8,128)S(1)}, u32[]{:S(2)}, u32[]{:S(2)}) collective-permute-start(f32[512,128]{1,0:T(8,128)S(1)} %get-tuple-element.60), channel_id=1, source_target_pairs={{0,3},{1,0},{2,1},{3,2},{4,7},{5,4},{6,5},{7,6},{8,11},{9,8},{10,9... | collective-permute-start | bytes 786440 | tf_op jit(solution)/shard_map/ppermute | solution.py:233
  (4 other events, 3.1 us)

commit v4 on v3

v4 whole, which is shorter than its diff:
```python
import jax
import jax.numpy as jnp
from jax import lax
from jax.experimental import pallas as pl
from jax.experimental.pallas import tpu as pltpu
from jax.sharding import PartitionSpec as P

step_size = 0.5
epsilon = 1e-08
MEMBERS = 4
SMEM = pl.BlockSpec(memory_space=pltpu.SMEM)
VMEM = pl.BlockSpec(memory_space=pltpu.VMEM)
HBM = pl.BlockSpec(memory_space=pltpu.HBM)
PARAMS = pltpu.CompilerParams(vmem_limit_bytes=16 * 1024 * 1024)


def decode_weights(lost_ref, weight_ref):
    which = lost_ref[0]
    rows = [jnp.full((1, 128), weight_ref[c], jnp.float32) for c in range(MEMBERS)]
    parity_lost = which == 3
    divisor = jnp.where(which == 0, rows[0], jnp.where(which == 1, rows[1], rows[2]))
    divisor = jnp.where(parity_lost, jnp.ones_like(divisor), divisor)
    out = []
    for c in range(3):
        solved = jnp.where(parity_lost, rows[c], -rows[c] / divisor)
        out.append(jnp.where(which == c, jnp.zeros_like(solved), solved))
    out.append(jnp.where(parity_lost, jnp.zeros_like(divisor), 1.0 / divisor))
    return out


def split_halves(value):
    high = value.astype(jnp.bfloat16)
    low = (value - high.astype(jnp.float32)).astype(jnp.bfloat16)
    return high, low


def own_row(weights, member):
    own = weights[3]
    for c in range(3):
        own = jnp.where(member == c, weights[c], own)
    return own


def kernel_call(body, name, out_shape, in_specs, out_specs, cost=0, **kwargs):
    return pl.pallas_call(
        body,
        in_specs=in_specs,
        out_specs=out_specs,
        out_shape=out_shape,
        compiler_params=PARAMS,
        cost_estimate=pl.CostEstimate(flops=cost, bytes_accessed=cost, transcendentals=0),
        name=name,
        **kwargs,
    )


def flat(rows):
    return jax.ShapeDtypeStruct((rows, 128), jnp.float32)


def near(member):
    return member + 1 - 2 * lax.rem(member, 2), 3 - member


def scaled_pieces(table_ref, own, where, outs, buf_ref, sem_ref, others=()):
    half = buf_ref.shape[1]
    copies = []
    for i, (quarter, part) in enumerate(where):
        rows = pl.ds(pl.multiple_of(quarter * (2 * half) + part * half, 8), half)
        copies.append(pltpu.make_async_copy(table_ref.at[rows, :], buf_ref.at[i], sem_ref.at[i]))
        copies[-1].start()
    for copy in others:
        copy.start()
    for i, (out_ref, start) in enumerate(outs):
        copies[i].wait()
        out_ref[start : start + half, :] = own * buf_ref[i]
    for copy in others:
        copy.wait()


def passed_pieces(member):
    one, two = near(member)
    return [(3 - one, 0), (near(two)[0], 1)]


def given_pieces(member):
    one, two = near(member)
    return [(one, 0), (two, 1)]


def kept_pieces(member):
    one, two = near(member)
    return [(two, 0), (one, 1), (member, 0), (member, 1)]


def front_kernel(
    lost_ref, weight_ref, member_ref, table_ref, grads_ref, ids_hbm, a_ref, b_ref, buf_ref, sem_ref, grad_sem, ids_ref, ids_sem
):
    member = member_ref[0]
    part, lines = grads_ref.shape[0] // 2, ids_ref.shape[0] // 2
    half = buf_ref.shape[1]
    copies = [pltpu.make_async_copy(ids_hbm, ids_ref, ids_sem)]
    for i, out_ref in enumerate((a_ref, b_ref)):
        for h in range(2):
            start = half + h * (part + 8)
            source = grads_ref.at[pl.ds(h * part, part), :]
            copies.append(pltpu.make_async_copy(source, out_ref.at[pl.ds(start, part), :], grad_sem.at[2 * i + h]))
    own = own_row(decode_weights(lost_ref, weight_ref), member)
    scaled_pieces(table_ref, own, passed_pieces(member), [(a_ref, 0), (b_ref, 0)], buf_ref, sem_ref, copies)
    ids = ids_ref[...].astype(jnp.float32)
    for out_ref in (a_ref, b_ref):
        for h in range(2):
            start = half + h * (part + 8) + part
            out_ref[start : start + lines, :] = ids[h * lines : (h + 1) * lines, :]
            out_ref[start + lines : start + 8, :] = jnp.zeros((8 - lines, 128), jnp.float32)


def keep_kernel(
    lost_ref, weight_ref, member_ref, table_ref, a_ref, b_ref, c_ref, d_ref, mine_ref, buf_ref, sem_ref
):
    member = member_ref[0]
    own = own_row(decode_weights(lost_ref, weight_ref), member)
    half = buf_ref.shape[1]
    outs = [(a_ref, 0), (b_ref, 0), (c_ref, 0), (d_ref, 0), (mine_ref, 0), (mine_ref, half)]
    scaled_pieces(table_ref, own, given_pieces(member) + kept_pieces(member), outs, buf_ref, sem_ref)


def both_kernel(
    lost_ref, weight_ref, member_ref, table_ref, a_ref, b_ref, c_ref, d_ref, mine_ref, buf_ref, sem_ref
):
    member = member_ref[0]
    own = own_row(decode_weights(lost_ref, weight_ref), member)
    half = buf_ref.shape[1]
    outs = [(a_ref, 0), (a_ref, half), (b_ref, 0), (b_ref, half), (c_ref, 0), (d_ref, 0), (mine_ref, 0), (mine_ref, half)]
    passed, given = passed_pieces(member), given_pieces(member)
    where = [passed[0], given[0], passed[1], given[1]] + kept_pieces(member)
    scaled_pieces(table_ref, own, where, outs, buf_ref, sem_ref)


def second_kernel(c_ref, d_ref, a_ref, b_ref, out_c_ref, out_d_ref):
    half = c_ref.shape[0]
    out_c_ref[:half, :] = c_ref[...] + a_ref[:half, :]
    out_d_ref[:half, :] = d_ref[...] + b_ref[:half, :]
    extra = out_c_ref.shape[0] - half
    if extra:
        out_c_ref[half:, :] = a_ref[half : half + extra, :]
        out_d_ref[half:, :] = b_ref[half + extra :, :]


def swap(array, which, members):
    pairs = [(i, i ^ 1) for i in range(members)] if which == 0 else [(i, 3 - i) for i in range(members)]
    return lax.ppermute(array, "code", pairs)


def finish(mine_ref, a_ref, b_ref, c_ref, d_ref):
    half = mine_ref.shape[0] // 2
    first = (mine_ref[:half, :] + a_ref[a_ref.shape[0] - half :, :]) + c_ref[:half, :]
    last = (mine_ref[half:, :] + b_ref[b_ref.shape[0] - half :, :]) + d_ref[:half, :]
    return jnp.concatenate([first, last], axis=0)


def add_hits(total, first, part_ref, start, entries):
    high, low = split_halves(part_ref[start : start + entries, :])
    both = jnp.concatenate([high, low], axis=1)
    targets = (lax.broadcasted_iota(jnp.int32, (total.shape[0], 128), 0) + first).astype(jnp.float32)
    lines = [part_ref[start + entries + j : start + entries + j + 1, :] for j in range(entries // 128)]
    hits = [jnp.where(targets == line, 1.0, 0.0).astype(jnp.bfloat16) for line in lines]
    return total + jnp.dot(jnp.concatenate(hits, axis=1), both, preferred_element_type=jnp.float32)


def totals_kernel(member_ref, own_ref, a_ref, b_ref, out_ref):
    count = out_ref.shape[0]
    half = count // 2
    size = (own_ref.shape[0] - half) // 2
    total = jnp.zeros((count, 256), jnp.float32)
    for ref in (own_ref, a_ref, b_ref):
        for h in range(2):
            total = add_hits(total, member_ref[0] * count, ref, half + h * size, size - 8)
    out_ref[...] = total[:, :128] + total[:, 128:]


def spread(place_ref, values, out_ref, both_ref):
    high, low = split_halves(values)
    both_ref[:, :128] = high
    both_ref[:, 128:] = low
    slots, rows = out_ref.shape[0], values.shape[0]
    step = 256
    place = place_ref[...]
    for start in range(0, slots, step):
        here = lax.broadcasted_iota(jnp.int32, (step, rows), 0) + start
        pick = jnp.where(here == place, 1.0, 0.0).astype(jnp.bfloat16)
        got = jnp.dot(pick, both_ref[...], preferred_element_type=jnp.float32)
        out_ref[start : start + step, :] = got[:, :128] + got[:, 128:]


def sums_kernel(
    member_ref, place_ref, mine_ref, a_ref, b_ref, c_ref, d_ref, part_ref, out_ref, new_ref, total_ref, both_ref
):
    count = mine_ref.shape[0]
    half = count // 2
    more = jnp.zeros((count, 256), jnp.float32)
    for ref in (c_ref, d_ref):
        more = add_hits(more, member_ref[0] * count, ref, half, ref.shape[0] - half - 8)
    total = part_ref[...] + (more[:, :128] + more[:, 128:])
    total_ref[...] = total
    new = finish(mine_ref, a_ref, b_ref, c_ref, d_ref) + total * total
    new_ref[...] = new
    spread(place_ref, new, out_ref, both_ref)


def rows_kernel(
    place_ref, mine_ref, a_ref, b_ref, c_ref, d_ref, total_ref, sums_ref, out_ref, both_ref
):
    mine = finish(mine_ref, a_ref, b_ref, c_ref, d_ref)
    new = mine - step_size * total_ref[...] / (jnp.sqrt(sums_ref[...]) + epsilon)
    spread(place_ref, new, out_ref, both_ref)


def own_code_weight(weight_ref, member):
    own = weight_ref[3]
    for c in range(3):
        own = jnp.where(member == c, weight_ref[c], own)
    return own


def copy_kernel(moved_ref, out_ref):
    out_ref[...] = moved_ref[...]


def quarter_of(which, count):
    return pl.ds(pl.multiple_of(lax.rem(which, MEMBERS) * count, 8), count)


def parity_send_kernel(weight_ref, member_ref, moved_ref, mine_ref, *out_refs):
    member = member_ref[0]
    own = own_code_weight(weight_ref, member)
    count = mine_ref.shape[0]
    for k, out_ref in enumerate(out_refs):
        out_ref[...] = own * moved_ref[quarter_of(member + k + 1, count), :]
    mine_ref[...] = own * moved_ref[quarter_of(member, count), :]


def parity_sum_kernel(mine_ref, a_ref, b_ref, c_ref, out_ref):
    out_ref[...] = (mine_ref[...] + a_ref[...]) + (b_ref[...] + c_ref[...])


def turn(array, k, members):
    return lax.ppermute(array, "code", [(i, (i + k) % members) for i in range(members)])


def parity_of(name, key, moved, members):
    slots = moved.shape[0]
    quarter = slots // members
    mine, *sends = kernel_call(
        parity_send_kernel,
        "parity_send_" + name,
        (flat(quarter),) * members,
        [SMEM, SMEM, VMEM],
        (VMEM,) * members,
        cost=2 << 20,
    )(*key, moved)
    gots = {k: turn(sends[k - 1], k, members) for k in (2, 1, 3)}
    out = kernel_call(copy_kernel, "emit_" + name, flat(slots), [VMEM], VMEM, cost=2 << 20)(moved)
    parity = kernel_call(
        parity_sum_kernel, "parity_sum_" + name, flat(quarter), [VMEM] * members, VMEM, cost=1 << 20
    )(mine, gots[1], gots[2], gots[3])
    return out, parity


def per_device(
    table_rows, adagrad_sums, lost_member, code_weight, new_owner, pending_rows, pending_grads
):
    members = lax.axis_size("code")
    shards = lax.axis_size("shard")
    member = lax.axis_index("code").astype(jnp.int32)[None]
    share = table_rows.shape[0] // members
    capacity = max(2, (2 * share + shards - 1) // shards)
    slots = shards * capacity
    half = share // 2
    entries = pending_grads.shape[0]
    scalars = [SMEM, SMEM, SMEM]
    key = (lost_member, pltpu.with_memory_space_constraint(code_weight, pltpu.HBM), member)
    owner = new_owner[:, 0]

    def buffers(count):
        return [pltpu.VMEM((count, half, 128), jnp.float32), pltpu.SemaphoreType.DMA((count,))]

    def keep_out(array):
        return pltpu.with_memory_space_constraint(array, pltpu.HBM)

    part = entries // 2 + 8
    send_a, send_b = kernel_call(
        front_kernel,
        "front_send",
        (flat(half + 2 * part), flat(half + 2 * part)),
        scalars + [HBM, HBM, HBM],
        (VMEM, VMEM),
        cost=3 << 20,
        scratch_shapes=buffers(2)
        + [pltpu.SemaphoreType.DMA((4,)), pltpu.VMEM((entries // 128, 128), jnp.int32), pltpu.SemaphoreType.DMA],
    )(*key, keep_out(adagrad_sums), keep_out(pending_grads), keep_out(pending_rows.reshape(-1, 128)))
    got_a, got_b = swap(send_a, 0, members), swap(send_b, 1, members)

    give_a, give_b, keep_c, keep_d, mine_sums = kernel_call(
        keep_kernel,
        "keep_sums",
        (flat(half), flat(half), flat(half), flat(half), flat(share)),
        scalars + [HBM],
        (VMEM,) * 5,
        cost=3 << 20,
        scratch_shapes=buffers(6),
    )(*key, keep_out(adagrad_sums))
    row_a, row_b, row_c, row_d, mine_rows = kernel_call(
        both_kernel,
        "weigh_rows",
        (flat(share), flat(share), flat(half), flat(half), flat(share)),
        scalars + [HBM],
        (VMEM,) * 5,
        cost=4 << 20,
        scratch_shapes=buffers(8),
    )(*key, keep_out(table_rows))
    give_a, give_b, row_a, row_b = lax.optimization_barrier((give_a, give_b, row_a, row_b))
    kept_a, kept_b = swap(give_a, 0, members), swap(give_b, 1, members)
    earlier = jnp.tril(owner[:, None] == owner[None, :], -1)
    rank = jnp.sum(earlier.astype(jnp.int32), axis=1)
    place = (owner * capacity + rank)[None, :]

    def second(name, extra, hint, *args):
        return kernel_call(
            second_kernel,
            "second_" + name,
            (flat(half + extra), flat(half + extra)),
            [VMEM] * 4,
            (VMEM, VMEM),
            cost=hint,
        )(*args)

    send_c, send_d = second("sums", part, 1 << 38, keep_c, keep_d, got_a, got_b)
    got_c, got_d = swap(send_c, 1, members), swap(send_d, 0, members)
    kept_a, kept_b, got_a, got_b = lax.optimization_barrier((kept_a, kept_b, got_a, got_b))
    part_totals = kernel_call(
        totals_kernel, "pending_totals", flat(share), [SMEM] + [VMEM] * 3, VMEM, cost=4 << 20
    )(member, send_a, got_a, got_b)
    row_a, row_b, got_c, got_d, part_totals, place = lax.optimization_barrier(
        (row_a, row_b, got_c, got_d, part_totals, place)
    )
    back_a, back_b = swap(row_a, 0, members), swap(row_b, 1, members)

    scratch = [pltpu.VMEM((share, 256), jnp.bfloat16)]
    out_sums, new_sums, totals = kernel_call(
        sums_kernel,
        "place_sums",
        (pltpu.VMEM((slots, 128), jnp.float32), flat(share), flat(share)),
        [SMEM] + [VMEM] * 7,
        (VMEM, VMEM, VMEM),
        cost=6 << 20,
        scratch_shapes=scratch,
    )(member, place, mine_sums, kept_a, kept_b, got_c, got_d, part_totals)
    moved_sums = lax.all_to_all(out_sums, "shard", 0, 0, tiled=True)

    send_c, send_d = second("rows", 0, 1 << 38, row_c, row_d, back_a, back_b)
    back_c, back_d = swap(send_c, 1, members), swap(send_d, 0, members)
    out_rows = kernel_call(
        rows_kernel, "place_rows", pltpu.VMEM((slots, 128), jnp.float32), [VMEM] * 8, VMEM, cost=6 << 20, scratch_shapes=scratch
    )(place, mine_rows, back_a, back_b, back_c, back_d, totals, new_sums)
    moved_rows = lax.all_to_all(out_rows, "shard", 0, 0, tiled=True)

    final_sums, parity_sums = parity_of("sums", (code_weight, member), moved_sums, members)
    final_rows, parity_rows = parity_of("rows", (code_weight, member), moved_rows, members)
    return (final_rows, final_sums, parity_rows, parity_sums)


def solution(mesh):
    in_specs = (
        P(("shard", "code"), None),
        P(("shard", "code"), None),
        P("shard"),
        P(),
        P(("shard", "code"), None),
        P(("shard", "code")),
        P(("shard", "code"), None),
    )
    out_specs = (
        P(("shard", "code"), None),
        P(("shard", "code"), None),
        P(("shard", "code"), None),
        P(("shard", "code"), None),
    )
    return jax.shard_map(
        per_device, mesh=mesh, in_specs=in_specs, out_specs=out_specs, check_vma=False
    )
```

time: 142 us -> 133 us (0.937)
  waiting for transfers between devices: 76.4 us -> 63.8 us
  Pallas kernels: 15.2 us -> 22.4 us
  local copies, waits for them, and re-layouts: 4.68 us -> 1.67 us
  starting transfers between devices: 41.6 us -> 40 us
    ppermute x9 -> x6, waiting for transfers between devices: 28.1 us -> 6.39 us  [turn(): lax.ppermute(array, 'code', [(i, (i + k) % members) for i in range(member...]
    all_to_all x1, waiting for transfers between devices: 0.85 us -> 14 us  [per_device(): moved_sums = lax.all_to_all(out_sums, 'shard', 0, 0, tiled=True)]
    pallas_call x11, Pallas kernels: 12.2 us -> 16 us  [the longest x1 4.09 us: per_device(): kernel_call(sums_kernel, 'place_sums', (pltpu.VMEM((slots, 128), jnp.floa...]
    unnamed x18, local copies, waits for them, and re-layouts: 4.68 us -> 1.67 us
    all_to_all x1, starting transfers between devices: 9.48 us -> 6.87 us  [per_device(): moved_rows = lax.all_to_all(out_rows, 'shard', 0, 0, tiled=True)]
    ppermute x8 -> x10, waiting for transfers between devices: 24.7 us -> 22.1 us  [swap(): return lax.ppermute(array, 'code', pairs)]
    pallas_call x1, Pallas kernels: 0.94 us -> 3.04 us  [per_device(): kernel_call(both_kernel, 'weigh_rows', (flat(share), flat(share), flat(ha...]
    all_to_all x1, waiting for transfers between devices: 22.7 us -> 21.2 us  [per_device(): moved_rows = lax.all_to_all(out_rows, 'shard', 0, 0, tiled=True)]
  transfers between devices with their start and end apart: 19 -> 18, of which waited for: 13 -> 12; matrix products, arithmetic and copies ran while one was open for 1% -> 1% of each run, Pallas kernels for 8% -> 15%
where the time goes in v4:
time: 133 us; the launch traced here: 131 us
  waiting for transfers between devices  63.8 us (48%)
  starting transfers between devices  40 us (30%)
  Pallas kernels  22.4 us (17%)
  other arithmetic  1.87 us (1%)
  local copies, waits for them, and re-layouts  1.67 us (1%)
  between operations  1.45 us (1%)
    ppermute x10, waiting for transfers between devices, swap(): return lax.ppermute(array, 'code', pairs)  22.1 us
    all_to_all x1, waiting for transfers between devices, per_device(): moved_rows = lax.all_to_all(out_rows, 'shard', 0, 0, tiled=True)  21.2 us
    all_to_all x1, waiting for transfers between devices, per_device(): moved_sums = lax.all_to_all(out_sums, 'shard', 0, 0, tiled=True)  14 us
    all_to_all x1, starting transfers between devices, per_device(): moved_sums = lax.all_to_all(out_sums, 'shard', 0, 0, tiled=True)  11.8 us
    ppermute x10, starting transfers between devices, swap(): return lax.ppermute(array, 'code', pairs)  10.8 us
    ppermute x6, starting transfers between devices, turn(): lax.ppermute(array, 'code', [(i, (i + k) % members) for i in range(member...  10.6 us
    all_to_all x1, starting transfers between devices, per_device(): moved_rows = lax.all_to_all(out_rows, 'shard', 0, 0, tiled=True)  6.87 us
    ppermute x6, waiting for transfers between devices, turn(): lax.ppermute(array, 'code', [(i, (i + k) % members) for i in range(member...  6.39 us
  transfers between devices with their start and end apart: 18, of which 12 were waited for; matrix products, arithmetic and copies ran while one was open for 1% of the time, Pallas kernels for 15%

profile of v4, /device:TPU:32, one launch (start us, length us, event | category | flops | bytes accessed | tf_op | source)
XLA Modules:
  0.0 131.1 jit_solution(10401101931274972713)
XLA Ops:
  1.3 2.0 %front_send.1 = (f32[1040,128]{1,0:T(8,128)S(1)}, f32[1040,128]{1,0:T(8,128)S(1)}) custom-call(s32[1]{0:T(128)S(6)} %copy.11.lost_ref, f32[4]{0:T(128)} %weight_ref.9, s32[1]{0:T(128)} %bitcast.member_ref, f32[4096,128]{1,0:T(8,128)} %table_ref.5, f32[512,128]{1,0:T(8,128)} %grads_ref.1, s32[4,128]{1,0:T(4,128)} %bitcast.14), custom_call_target="tpu_custom_call" | custom-call | flops 3145728 | bytes 3145728 | tf_op jit(solution)/shard_map/front_send/pallas_call | solution.py:292
  3.3 3.1 %collective-permute-start.1 = (f32[1040,128]{1,0:T(8,128)S(1)}, f32[1040,128]{1,0:T(8,128)S(1)}, u32[]{:S(2)}, u32[]{:S(2)}) collective-permute-start(f32[1040,128]{1,0:T(8,128)S(1)} %get-tuple-element.54), channel_id=1, source_target_pairs={{0,3},{1,2},{2,1},{3,0},{4,7},{5,6},{6,5},{7,4},{8,11},{9,10},{10,... | collective-permute-start | bytes 1597448 | tf_op jit(solution)/shard_map/ppermute | solution.py:152
  6.5 2.8 %keep_sums.1 = (f32[512,128]{1,0:T(8,128)}, f32[512,128]{1,0:T(8,128)}, f32[512,128]{1,0:T(8,128)S(1)}, f32[512,128]{1,0:T(8,128)S(1)}, f32[1024,128]{1,0:T(8,128)S(1)}) custom-call(s32[1]{0:T(128)S(6)} %copy.11.lost_ref, f32[4]{0:T(128)} %weight_ref.9, s32[1]{0:T(128)} %bitcast.member_ref, f32[4096,128]{1,0:T(8,128)} %table_ref.5), custom_call_target="tpu_custom_call" | custom-call | flops 3145728 | bytes 3145728 | tf_op jit(solution)/shard_map/keep_sums/pallas_call | solution.py:304
  9.4 3.0 %weigh_rows.1 = (f32[1024,128]{1,0:T(8,128)}, f32[1024,128]{1,0:T(8,128)S(1)}, f32[512,128]{1,0:T(8,128)S(1)}, f32[512,128]{1,0:T(8,128)S(1)}, f32[1024,128]{1,0:T(8,128)S(1)}) custom-call(s32[1]{0:T(128)S(6)} %copy.11.lost_ref, f32[4]{0:T(128)} %weight_ref.9, s32[1]{0:T(128)} %bitcast.member_ref, f32[4096,128]{1,0:T(8,128)} %table_ref.4), custom_call_target="tpu_custom_call" | custom-call | flops 4194304 | bytes 4194304 | tf_op jit(solution)/shard_map/weigh_rows/pallas_call | solution.py:313
  13.1 1.9 %collective-permute-start.4 = (f32[512,128]{1,0:T(8,128)}, f32[512,128]{1,0:T(8,128)}, u32[]{:S(2)}, u32[]{:S(2)}) collective-permute-start(f32[512,128]{1,0:T(8,128)} %get-tuple-element.57), channel_id=1, source_target_pairs={{0,1},{1,0},{2,3},{3,2},{4,5},{5,4},{6,7},{7,6},{8,9},{9,8},{10,11... | collective-permute-start | bytes 786440 | tf_op jit(solution)/shard_map/ppermute | solution.py:152
  15.9 3.0 %collective-permute-done.1.b_ref = f32[1040,128]{1,0:T(8,128)S(1)} collective-permute-done((f32[1040,128]{1,0:T(8,128)S(1)}, f32[1040,128]{1,0:T(8,128)S(1)}, u32[]{:S(2)}, u32[]{:S(2)}) %collective-permute-start.1) | collective-permute-done | bytes 532512 | tf_op jit(solution)/shard_map/ppermute | solution.py:152
  18.9 2.5 %collective-permute-done.a_ref = f32[1040,128]{1,0:T(8,128)S(1)} collective-permute-done((f32[1040,128]{1,0:T(8,128)S(1)}, f32[1040,128]{1,0:T(8,128)S(1)}, u32[]{:S(2)}, u32[]{:S(2)}) %collective-permute-start) | collective-permute-done | bytes 532512 | tf_op jit(solution)/shard_map/ppermute | solution.py:152
  24.1 3.1 %collective-permute-done.4.a_ref = f32[512,128]{1,0:T(8,128)} collective-permute-done((f32[512,128]{1,0:T(8,128)}, f32[512,128]{1,0:T(8,128)}, u32[]{:S(2)}, u32[]{:S(2)}) %collective-permute-start.4) | collective-permute-done | bytes 262176 | tf_op jit(solution)/shard_map/ppermute | solution.py:152
  28.1 4.5 %collective-permute-done.2.c_ref = f32[776,128]{1,0:T(8,128)S(1)} collective-permute-done((f32[776,128]{1,0:T(8,128)S(1)}, f32[776,128]{1,0:T(8,128)S(1)}, u32[]{:S(2)}, u32[]{:S(2)}) %collective-permute-start.2) | collective-permute-done | bytes 397344 | tf_op jit(solution)/shard_map/ppermute | solution.py:152
  35.6 4.1 %place_sums.1 = (f32[2048,128]{1,0:T(8,128)}, f32[1024,128]{1,0:T(8,128)S(1)}, f32[1024,128]{1,0:T(8,128)S(1)}) custom-call(s32[1]{0:T(128)} %bitcast.member_ref, s32[1,1024]{1,0:T(1,128)S(1)} %bitcast_add_fusion.place_ref, f32[1024,128]{1,0:T(8,128)S(1)} %get-tuple-element.69.mine_ref, f32[512,128]{1,0:T(8,128)} %collective-permute-done.4.a_ref, ...), custom_call_target="tpu_custom_call" | custom-call | flops 6291456 | bytes 6291456 | tf_op jit(solution)/shard_map/place_sums/pallas_call | solution.py:350
  39.7 11.8 %all-to-all-start.1 = ((f32[64,32,128]{2,1,0:T(8,128)}), f32[64,32,128]{2,1,0:T(8,128)}, u32[]{:S(2)}, u32[]{:S(2)}) async-start(f32[64,32,128]{2,1,0:T(8,128)} %bitcast.7), calls=%async_computation.1 | async-start | bytes 2097152 | tf_op jit(solution)/shard_map/all_to_all | solution.py:359
  52.5 2.1 %collective-permute-start.8 = (f32[512,128]{1,0:T(8,128)S(1)}, f32[512,128]{1,0:T(8,128)S(1)}, u32[]{:S(2)}, u32[]{:S(2)}) collective-permute-start(f32[512,128]{1,0:T(8,128)S(1)} %get-tuple-element.67), channel_id=1, source_target_pairs={{0,3},{1,2},{2,1},{3,0},{4,7},{5,6},{6,5},{7,4},{8,11},{9,10},{10,... | collective-permute-start | bytes 786440 | tf_op jit(solution)/shard_map/ppermute | solution.py:152
  55.1 7.0 %collective-permute-done.8.c_ref = f32[512,128]{1,0:T(8,128)S(1)} collective-permute-done((f32[512,128]{1,0:T(8,128)S(1)}, f32[512,128]{1,0:T(8,128)S(1)}, u32[]{:S(2)}, u32[]{:S(2)}) %collective-permute-start.8) | collective-permute-done | bytes 262176 | tf_op jit(solution)/shard_map/ppermute | solution.py:152
  62.7 2.5 %place_rows.1 = f32[2048,128]{1,0:T(8,128)} custom-call(s32[1,1024]{1,0:T(1,128)S(1)} %copy-done.3, f32[1024,128]{1,0:T(8,128)S(1)} %get-tuple-element.62.mine_ref, f32[1024,128]{1,0:T(8,128)S(1)} %collective-permute-done.6.a_ref, f32[1024,128]{1,0:T(8,128)S(1)} %collective-permute-done.7.b_ref, f32[512,128]{1,0:T(8,128)S(1)} %collective-permute-done.8.c_ref, ...), custom_call_target="tpu_custom_call" | custom-call | flops 6291456 | bytes 6291456 | tf_op jit(solution)/shard_map/place_rows/pallas_call | solution.py:363
  65.2 14.0 %all-to-all-done.1 = f32[64,32,128]{2,1,0:T(8,128)} async-done(((f32[64,32,128]{2,1,0:T(8,128)}), f32[64,32,128]{2,1,0:T(8,128)}, u32[]{:S(2)}, u32[]{:S(2)}) %all-to-all-start.1) | async-done | bytes 1048608 | tf_op jit(solution)/shard_map/all_to_all | solution.py:359
  79.2 6.9 %all-to-all-start = ((f32[64,32,128]{2,1,0:T(8,128)}), f32[64,32,128]{2,1,0:T(8,128)S(1)}, u32[]{:S(2)}, u32[]{:S(2)}) async-start(f32[64,32,128]{2,1,0:T(8,128)} %bitcast.5), calls=%async_computation | async-start | bytes 2097152 | tf_op jit(solution)/shard_map/all_to_all | solution.py:366
  87.5 1.5 %collective-permute-start.13 = (f32[512,128]{1,0:T(8,128)S(1)}, f32[512,128]{1,0:T(8,128)S(1)}, u32[]{:S(2)}, u32[]{:S(2)}) collective-permute-start(f32[512,128]{1,0:T(8,128)S(1)} %get-tuple-element.83), channel_id=1, source_target_pairs={{0,1},{1,2},{2,3},{3,0},{4,5},{5,6},{6,7},{7,4},{8,9},{9,10},{10,1... | collective-permute-start | bytes 786440 | tf_op jit(solution)/shard_map/ppermute | solution.py:248
  89.0 2.1 %collective-permute-start.14 = (f32[512,128]{1,0:T(8,128)S(1)}, f32[512,128]{1,0:T(8,128)S(1)}, u32[]{:S(2)}, u32[]{:S(2)}) collective-permute-start(f32[512,128]{1,0:T(8,128)S(1)} %get-tuple-element.84), channel_id=1, source_target_pairs={{0,2},{1,3},{2,0},{3,1},{4,6},{5,7},{6,4},{7,5},{8,10},{9,11},{10,... | collective-permute-start | bytes 786440 | tf_op jit(solution)/shard_map/ppermute | solution.py:248
  91.0 1.7 %collective-permute-start.15 = (f32[512,128]{1,0:T(8,128)S(1)}, f32[512,128]{1,0:T(8,128)S(1)}, u32[]{:S(2)}, u32[]{:S(2)}) collective-permute-start(f32[512,128]{1,0:T(8,128)S(1)} %get-tuple-element.85), channel_id=1, source_target_pairs={{0,3},{1,0},{2,1},{3,2},{4,7},{5,4},{6,5},{7,6},{8,11},{9,8},{10,9... | collective-permute-start | bytes 786440 | tf_op jit(solution)/shard_map/ppermute | solution.py:248
  92.8 21.2 %all-to-all-done = f32[64,32,128]{2,1,0:T(8,128)S(1)} async-done(((f32[64,32,128]{2,1,0:T(8,128)}), f32[64,32,128]{2,1,0:T(8,128)S(1)}, u32[]{:S(2)}, u32[]{:S(2)}) %all-to-all-start) | async-done | bytes 1048608 | tf_op jit(solution)/shard_map/all_to_all | solution.py:366
  116.1 2.1 %collective-permute-start.11 = (f32[512,128]{1,0:T(8,128)S(1)}, f32[512,128]{1,0:T(8,128)S(1)}, u32[]{:S(2)}, u32[]{:S(2)}) collective-permute-start(f32[512,128]{1,0:T(8,128)S(1)} %get-tuple-element.80), channel_id=1, source_target_pairs={{0,2},{1,3},{2,0},{3,1},{4,6},{5,7},{6,4},{7,5},{8,10},{9,11},{10,... | collective-permute-start | bytes 786440 | tf_op jit(solution)/shard_map/ppermute | solution.py:248
  118.2 1.7 %collective-permute-start.12 = (f32[512,128]{1,0:T(8,128)S(1)}, f32[512,128]{1,0:T(8,128)S(1)}, u32[]{:S(2)}, u32[]{:S(2)}) collective-permute-start(f32[512,128]{1,0:T(8,128)S(1)} %get-tuple-element.81), channel_id=1, source_target_pairs={{0,3},{1,0},{2,1},{3,2},{4,7},{5,4},{6,5},{7,6},{8,11},{9,8},{10,9... | collective-permute-start | bytes 786440 | tf_op jit(solution)/shard_map/ppermute | solution.py:248
  119.9 2.3 %emit_sums.1 = f32[2048,128]{1,0:T(8,128)} custom-call(f32[2048,128]{1,0:T(8,128)} %bitcast.8.moved_ref), custom_call_target="tpu_custom_call" | custom-call | flops 2097152 | bytes 2097152 | tf_op jit(solution)/shard_map/emit_sums/pallas_call | solution.py:263
  124.8 5.2 %collective-permute-done.11.b_ref = f32[512,128]{1,0:T(8,128)S(1)} collective-permute-done((f32[512,128]{1,0:T(8,128)S(1)}, f32[512,128]{1,0:T(8,128)S(1)}, u32[]{:S(2)}, u32[]{:S(2)}) %collective-permute-start.11) | collective-permute-done | bytes 262176 | tf_op jit(solution)/shard_map/ppermute | solution.py:248
  (47 shorter events, 17.5 us)
Async XLA Ops:
  3.3 9.2 %copy-start = (f32[1040,128]{1,0:T(8,128)}, f32[1040,128]{1,0:T(8,128)S(1)}, u32[]{:S(2)}) copy-start(f32[1040,128]{1,0:T(8,128)S(1)} %get-tuple-element.53.own_ref) | copy-start | bytes 1597444
  3.3 15.6 %collective-permute-start.1 = (f32[1040,128]{1,0:T(8,128)S(1)}, f32[1040,128]{1,0:T(8,128)S(1)}, u32[]{:S(2)}, u32[]{:S(2)}) collective-permute-start(f32[1040,128]{1,0:T(8,128)S(1)} %get-tuple-element.54), channel_id=1, source_target_pairs={{0,3},{1,2},{2,1},{3,0},{4,7},{5,6},{6,5},{7,4},{8,11},{9,10},{10,... | collective-permute-start | bytes 1597448 | tf_op jit(solution)/shard_map/ppermute | solution.py:152
  6.4 15.0 %collective-permute-start = (f32[1040,128]{1,0:T(8,128)S(1)}, f32[1040,128]{1,0:T(8,128)S(1)}, u32[]{:S(2)}, u32[]{:S(2)}) collective-permute-start(f32[1040,128]{1,0:T(8,128)S(1)} %get-tuple-element.53.own_ref), channel_id=1, source_target_pairs={{0,1},{1,0},{2,3},{3,2},{4,5},{5,4},{6,7},{7,6},{8,9},{9,8},{10,11... | collective-permute-start | bytes 1597448 | tf_op jit(solution)/shard_map/ppermute | solution.py:152
  13.1 14.0 %collective-permute-start.4 = (f32[512,128]{1,0:T(8,128)}, f32[512,128]{1,0:T(8,128)}, u32[]{:S(2)}, u32[]{:S(2)}) collective-permute-start(f32[512,128]{1,0:T(8,128)} %get-tuple-element.57), channel_id=1, source_target_pairs={{0,1},{1,0},{2,3},{3,2},{4,5},{5,4},{6,7},{7,6},{8,9},{9,8},{10,11... | collective-permute-start | bytes 786440 | tf_op jit(solution)/shard_map/ppermute | solution.py:152
  15.0 12.1 %collective-permute-start.5 = (f32[512,128]{1,0:T(8,128)}, f32[512,128]{1,0:T(8,128)}, u32[]{:S(2)}, u32[]{:S(2)}) collective-permute-start(f32[512,128]{1,0:T(8,128)} %get-tuple-element.58), channel_id=1, source_target_pairs={{0,3},{1,2},{2,1},{3,0},{4,7},{5,6},{6,5},{7,4},{8,11},{9,10},{10,... | collective-permute-start | bytes 786440 | tf_op jit(solution)/shard_map/ppermute | solution.py:152
  21.4 1.4 %copy-start.8 = (s32[1024]{0:T(1024)S(1)}, s32[1024]{0:T(1024)}, u32[]{:S(2)}) copy-start(s32[1024]{0:T(1024)} %iota_add_fusion) | copy-start | bytes 12292
  21.4 5.7 %copy-start.1 = (f32[1040,128]{1,0:T(8,128)S(1)}, f32[1040,128]{1,0:T(8,128)}, u32[]{:S(2)}) copy-start(f32[1040,128]{1,0:T(8,128)} %copy-done) | copy-start | bytes 1597444
  21.5 11.1 %collective-permute-start.2 = (f32[776,128]{1,0:T(8,128)S(1)}, f32[776,128]{1,0:T(8,128)S(1)}, u32[]{:S(2)}, u32[]{:S(2)}) collective-permute-start(f32[776,128]{1,0:T(8,128)S(1)} %get-tuple-element.55), channel_id=1, source_target_pairs={{0,3},{1,2},{2,1},{3,0},{4,7},{5,6},{6,5},{7,4},{8,11},{9,10},{10,... | collective-permute-start | bytes 1191944 | tf_op jit(solution)/shard_map/ppermute | solution.py:152
  22.8 11.3 %collective-permute-start.3 = (f32[776,128]{1,0:T(8,128)S(1)}, f32[776,128]{1,0:T(8,128)S(1)}, u32[]{:S(2)}, u32[]{:S(2)}) collective-permute-start(f32[776,128]{1,0:T(8,128)S(1)} %get-tuple-element.56), channel_id=1, source_target_pairs={{0,1},{1,0},{2,3},{3,2},{4,5},{5,4},{6,7},{7,6},{8,9},{9,8},{10,11... | collective-permute-start | bytes 1191944 | tf_op jit(solution)/shard_map/ppermute | solution.py:152
  24.1 15.6 %copy-start.2 = (s32[1,1024]{1,0:T(1,128)}, s32[1,1024]{1,0:T(1,128)S(1)}, u32[]{:S(2)}) copy-start(s32[1,1024]{1,0:T(1,128)S(1)} %bitcast_add_fusion.place_ref) | copy-start | bytes 12292
  34.1 17.4 %collective-permute-start.6 = (f32[1024,128]{1,0:T(8,128)}, f32[1024,128]{1,0:T(8,128)S(1)}, u32[]{:S(2)}, u32[]{:S(2)}) collective-permute-start(f32[1024,128]{1,0:T(8,128)} %get-tuple-element.63), channel_id=1, source_target_pairs={{0,1},{1,0},{2,3},{3,2},{4,5},{5,4},{6,7},{7,6},{8,9},{9,8},{10,11... | collective-permute-start | bytes 1572872 | tf_op jit(solution)/shard_map/ppermute | solution.py:152
  34.4 17.1 %collective-permute-start.7 = (f32[1024,128]{1,0:T(8,128)S(1)}, f32[1024,128]{1,0:T(8,128)S(1)}, u32[]{:S(2)}, u32[]{:S(2)}) collective-permute-start(f32[1024,128]{1,0:T(8,128)S(1)} %get-tuple-element.64), channel_id=1, source_target_pairs={{0,3},{1,2},{2,1},{3,0},{4,7},{5,6},{6,5},{7,4},{8,11},{9,10},{10,... | collective-permute-start | bytes 1572872 | tf_op jit(solution)/shard_map/ppermute | solution.py:152
  39.7 39.6 %all-to-all-start.1 = ((f32[64,32,128]{2,1,0:T(8,128)}), f32[64,32,128]{2,1,0:T(8,128)}, u32[]{:S(2)}, u32[]{:S(2)}) async-start(f32[64,32,128]{2,1,0:T(8,128)} %bitcast.7), calls=%async_computation.1 | async-start | bytes 2097152 | tf_op jit(solution)/shard_map/all_to_all | solution.py:359
  52.4 10.3 %copy-start.3 = (s32[1,1024]{1,0:T(1,128)S(1)}, s32[1,1024]{1,0:T(1,128)}, u32[]{:S(2)}) copy-start(s32[1,1024]{1,0:T(1,128)} %copy-done.2) | copy-start | bytes 12292
  52.5 9.7 %collective-permute-start.8 = (f32[512,128]{1,0:T(8,128)S(1)}, f32[512,128]{1,0:T(8,128)S(1)}, u32[]{:S(2)}, u32[]{:S(2)}) collective-permute-start(f32[512,128]{1,0:T(8,128)S(1)} %get-tuple-element.67), channel_id=1, source_target_pairs={{0,3},{1,2},{2,1},{3,0},{4,7},{5,6},{6,5},{7,4},{8,11},{9,10},{10,... | collective-permute-start | bytes 786440 | tf_op jit(solution)/shard_map/ppermute | solution.py:152
  54.6 8.1 %collective-permute-start.9 = (f32[512,128]{1,0:T(8,128)S(1)}, f32[512,128]{1,0:T(8,128)S(1)}, u32[]{:S(2)}, u32[]{:S(2)}) collective-permute-start(f32[512,128]{1,0:T(8,128)S(1)} %get-tuple-element.68), channel_id=1, source_target_pairs={{0,1},{1,0},{2,3},{3,2},{4,5},{5,4},{6,7},{7,6},{8,9},{9,8},{10,11... | collective-permute-start | bytes 786440 | tf_op jit(solution)/shard_map/ppermute | solution.py:152
  65.2 20.9 %copy-start.4 = (f32[4]{0:T(128)S(1)}, f32[4]{0:T(128)}, u32[]{:S(2)}) copy-start(f32[4]{0:T(128)} %weight_ref.9) | copy-start | bytes 52
  79.2 34.8 %all-to-all-start = ((f32[64,32,128]{2,1,0:T(8,128)}), f32[64,32,128]{2,1,0:T(8,128)S(1)}, u32[]{:S(2)}, u32[]{:S(2)}) async-start(f32[64,32,128]{2,1,0:T(8,128)} %bitcast.5), calls=%async_computation | async-start | bytes 2097152 | tf_op jit(solution)/shard_map/all_to_all | solution.py:366
  87.5 30.7 %collective-permute-start.13 = (f32[512,128]{1,0:T(8,128)S(1)}, f32[512,128]{1,0:T(8,128)S(1)}, u32[]{:S(2)}, u32[]{:S(2)}) collective-permute-start(f32[512,128]{1,0:T(8,128)S(1)} %get-tuple-element.83), channel_id=1, source_target_pairs={{0,1},{1,2},{2,3},{3,0},{4,5},{5,6},{6,7},{7,4},{8,9},{9,10},{10,1... | collective-permute-start | bytes 786440 | tf_op jit(solution)/shard_map/ppermute | solution.py:248
  89.0 33.3 %collective-permute-start.14 = (f32[512,128]{1,0:T(8,128)S(1)}, f32[512,128]{1,0:T(8,128)S(1)}, u32[]{:S(2)}, u32[]{:S(2)}) collective-permute-start(f32[512,128]{1,0:T(8,128)S(1)} %get-tuple-element.84), channel_id=1, source_target_pairs={{0,2},{1,3},{2,0},{3,1},{4,6},{5,7},{6,4},{7,5},{8,10},{9,11},{10,... | collective-permute-start | bytes 786440 | tf_op jit(solution)/shard_map/ppermute | solution.py:248
  91.0 31.2 %collective-permute-start.15 = (f32[512,128]{1,0:T(8,128)S(1)}, f32[512,128]{1,0:T(8,128)S(1)}, u32[]{:S(2)}, u32[]{:S(2)}) collective-permute-start(f32[512,128]{1,0:T(8,128)S(1)} %get-tuple-element.85), channel_id=1, source_target_pairs={{0,3},{1,0},{2,1},{3,2},{4,7},{5,4},{6,5},{7,6},{8,11},{9,8},{10,9... | collective-permute-start | bytes 786440 | tf_op jit(solution)/shard_map/ppermute | solution.py:248
  114.6 10.2 %collective-permute-start.10 = (f32[512,128]{1,0:T(8,128)S(1)}, f32[512,128]{1,0:T(8,128)S(1)}, u32[]{:S(2)}, u32[]{:S(2)}) collective-permute-start(f32[512,128]{1,0:T(8,128)S(1)} %get-tuple-element.79), channel_id=1, source_target_pairs={{0,1},{1,2},{2,3},{3,0},{4,5},{5,6},{6,7},{7,4},{8,9},{9,10},{10,1... | collective-permute-start | bytes 786440 | tf_op jit(solution)/shard_map/ppermute | solution.py:248
  116.1 13.9 %collective-permute-start.11 = (f32[512,128]{1,0:T(8,128)S(1)}, f32[512,128]{1,0:T(8,128)S(1)}, u32[]{:S(2)}, u32[]{:S(2)}) collective-permute-start(f32[512,128]{1,0:T(8,128)S(1)} %get-tuple-element.80), channel_id=1, source_target_pairs={{0,2},{1,3},{2,0},{3,1},{4,6},{5,7},{6,4},{7,5},{8,10},{9,11},{10,... | collective-permute-start | bytes 786440 | tf_op jit(solution)/shard_map/ppermute | solution.py:248
  118.2 12.2 %collective-permute-start.12 = (f32[512,128]{1,0:T(8,128)S(1)}, f32[512,128]{1,0:T(8,128)S(1)}, u32[]{:S(2)}, u32[]{:S(2)}) collective-permute-start(f32[512,128]{1,0:T(8,128)S(1)} %get-tuple-element.81), channel_id=1, source_target_pairs={{0,3},{1,0},{2,1},{3,2},{4,7},{5,4},{6,5},{7,6},{8,11},{9,8},{10,9... | collective-permute-start | bytes 786440 | tf_op jit(solution)/shard_map/ppermute | solution.py:248
  (3 other events, 3.0 us)

commit v5 on v4

--- a/solution.py
+++ b/solution.py
@@ -71,6 +71,7 @@
         copies[-1].start()
     for copy in others:
         copy.start()
+    own = own()
     for i, (out_ref, start) in enumerate(outs):
         copies[i].wait()
         out_ref[start : start + half, :] = own * buf_ref[i]
@@ -94,18 +95,25 @@
 
 
 def front_kernel(
-    lost_ref, weight_ref, member_ref, table_ref, grads_ref, ids_hbm, a_ref, b_ref, buf_ref, sem_ref, grad_sem, ids_ref, ids_sem
+    lost_ref, weight_hbm, member_ref, table_ref, grads_ref, ids_hbm, a_ref, b_ref,
+    buf_ref, sem_ref, grad_sem, ids_ref, weight_ref, small_sem
 ):
     member = member_ref[0]
     part, lines = grads_ref.shape[0] // 2, ids_ref.shape[0] // 2
     half = buf_ref.shape[1]
-    copies = [pltpu.make_async_copy(ids_hbm, ids_ref, ids_sem)]
+    copies = [pltpu.make_async_copy(ids_hbm, ids_ref, small_sem.at[0])]
     for i, out_ref in enumerate((a_ref, b_ref)):
         for h in range(2):
             start = half + h * (part + 8)
             source = grads_ref.at[pl.ds(h * part, part), :]
             copies.append(pltpu.make_async_copy(source, out_ref.at[pl.ds(start, part), :], grad_sem.at[2 * i + h]))
-    own = own_row(decode_weights(lost_ref, weight_ref), member)
+    weights = pltpu.make_async_copy(weight_hbm, weight_ref, small_sem.at[1])
+    weights.start()
+
+    def own():
+        weights.wait()
+        return own_row(decode_weights(lost_ref, weight_ref), member)
+
     scaled_pieces(table_ref, own, passed_pieces(member), [(a_ref, 0), (b_ref, 0)], buf_ref, sem_ref, copies)
     ids = ids_ref[...].astype(jnp.float32)
     for out_ref in (a_ref, b_ref):
@@ -119,21 +127,20 @@
     lost_ref, weight_ref, member_ref, table_ref, a_ref, b_ref, c_ref, d_ref, mine_ref, buf_ref, sem_ref
 ):
     member = member_ref[0]
-    own = own_row(decode_weights(lost_ref, weight_ref), member)
+    own = lambda: own_row(decode_weights(lost_ref, weight_ref), member)
     half = buf_ref.shape[1]
     outs = [(a_ref, 0), (b_ref, 0), (c_ref, 0), (d_ref, 0), (mine_ref, 0), (mine_ref, half)]
     scaled_pieces(table_ref, own, given_pieces(member) + kept_pieces(member), outs, buf_ref, sem_ref)
 
 
 def both_kernel(
-    lost_ref, weight_ref, member_ref, table_ref, a_ref, b_ref, c_ref, d_ref, mine_ref, buf_ref, sem_ref
+    lost_ref, weight_ref, member_ref, table_ref, a_ref, b_ref, give_a_ref, give_b_ref, c_ref, d_ref, mine_ref, buf_ref, sem_ref
 ):
     member = member_ref[0]
-    own = own_row(decode_weights(lost_ref, weight_ref), member)
+    own = lambda: own_row(decode_weights(lost_ref, weight_ref), member)
     half = buf_ref.shape[1]
-    outs = [(a_ref, 0), (a_ref, half), (b_ref, 0), (b_ref, half), (c_ref, 0), (d_ref, 0), (mine_ref, 0), (mine_ref, half)]
-    passed, given = passed_pieces(member), given_pieces(member)
-    where = [passed[0], given[0], passed[1], given[1]] + kept_pieces(member)
+    outs = [(ref, 0) for ref in (a_ref, b_ref, give_a_ref, give_b_ref, c_ref, d_ref, mine_ref)] + [(mine_ref, half)]
+    where = passed_pieces(member) + given_pieces(member) + kept_pieces(member)
     scaled_pieces(table_ref, own, where, outs, buf_ref, sem_ref)
 
 
@@ -168,7 +175,7 @@
     return total + jnp.dot(jnp.concatenate(hits, axis=1), both, preferred_element_type=jnp.float32)
 
 
-def totals_kernel(member_ref, own_ref, a_ref, b_ref, out_ref):
+def totals_kernel(member_ref, own_ref, a_ref, b_ref, mine_ref, kept_a_ref, kept_b_ref, out_ref, base_ref):
     count = out_ref.shape[0]
     half = count // 2
     size = (own_ref.shape[0] - half) // 2
@@ -177,43 +184,51 @@
         for h in range(2):
             total = add_hits(total, member_ref[0] * count, ref, half + h * size, size - 8)
     out_ref[...] = total[:, :128] + total[:, 128:]
-
-
-def spread(place_ref, values, out_ref, both_ref):
+    base_ref[:half, :] = mine_ref[:half, :] + kept_a_ref[...]
+    base_ref[half:, :] = mine_ref[half:, :] + kept_b_ref[...]
+
+
+def spread(place_ref, values, out_ref, both_ref, stage_ref, sem_ref):
     high, low = split_halves(values)
     both_ref[:, :128] = high
     both_ref[:, 128:] = low
     slots, rows = out_ref.shape[0], values.shape[0]
-    step = 256
+    step = slots // sem_ref.shape[0]
     place = place_ref[...]
-    for start in range(0, slots, step):
-        here = lax.broadcasted_iota(jnp.int32, (step, rows), 0) + start
+    copies = []
+    for i in range(sem_ref.shape[0]):
+        here = lax.broadcasted_iota(jnp.int32, (step, rows), 0) + i * step
         pick = jnp.where(here == place, 1.0, 0.0).astype(jnp.bfloat16)
         got = jnp.dot(pick, both_ref[...], preferred_element_type=jnp.float32)
-        out_ref[start : start + step, :] = got[:, :128] + got[:, 128:]
+        block = pl.ds(i * step, step)
+        stage_ref[block, :] = got[:, :128] + got[:, 128:]
+        copies.append(pltpu.make_async_copy(stage_ref.at[block, :], out_ref.at[block, :], sem_ref.at[i]))
+        copies[-1].start()
+    for copy in copies:
+        copy.wait()
 
 
 def sums_kernel(
-    member_ref, place_ref, mine_ref, a_ref, b_ref, c_ref, d_ref, part_ref, out_ref, new_ref, total_ref, both_ref
-):
-    count = mine_ref.shape[0]
+    member_ref, place_ref, base_ref, c_ref, d_ref, part_ref, out_ref, new_ref, total_ref, both_ref, stage_ref, sem_ref
+):
+    count = base_ref.shape[0]
     half = count // 2
     more = jnp.zeros((count, 256), jnp.float32)
     for ref in (c_ref, d_ref):
         more = add_hits(more, member_ref[0] * count, ref, half, ref.shape[0] - half - 8)
     total = part_ref[...] + (more[:, :128] + more[:, 128:])
     total_ref[...] = total
-    new = finish(mine_ref, a_ref, b_ref, c_ref, d_ref) + total * total
+    new = base_ref[...] + jnp.concatenate([c_ref[:half, :], d_ref[:half, :]], axis=0) + total * total
     new_ref[...] = new
-    spread(place_ref, new, out_ref, both_ref)
+    spread(place_ref, new, out_ref, both_ref, stage_ref, sem_ref)
 
 
 def rows_kernel(
-    place_ref, mine_ref, a_ref, b_ref, c_ref, d_ref, total_ref, sums_ref, out_ref, both_ref
+    place_ref, mine_ref, a_ref, b_ref, c_ref, d_ref, total_ref, sums_ref, out_ref, both_ref, stage_ref, sem_ref
 ):
     mine = finish(mine_ref, a_ref, b_ref, c_ref, d_ref)
     new = mine - step_size * total_ref[...] / (jnp.sqrt(sums_ref[...]) + epsilon)
-    spread(place_ref, new, out_ref, both_ref)
+    spread(place_ref, new, out_ref, both_ref, stage_ref, sem_ref)
 
 
 def own_code_weight(weight_ref, member):
@@ -244,8 +259,58 @@
     out_ref[...] = (mine_ref[...] + a_ref[...]) + (b_ref[...] + c_ref[...])
 
 
+def parity_first_kernel(weight_ref, member_ref, moved_ref, *refs):
+    member = member_ref[0]
+    own = own_code_weight(weight_ref, member)
+    half = refs[0].shape[0]
+    outs = [(ref, 0) for ref in refs] + [(refs[-1], half)]
+    where = passed_pieces(member) + given_pieces(member) + kept_pieces(member)
+    for (out_ref, start), (quarter, part) in zip(outs, where):
+        rows = pl.ds(pl.multiple_of(quarter * (2 * half) + part * half, 8), half)
+        out_ref[start : start + half, :] = own * moved_ref[rows, :]
+
+
+def parity_last_kernel(mine_ref, a_ref, b_ref, c_ref, d_ref, out_ref):
+    out_ref[...] = finish(mine_ref, a_ref, b_ref, c_ref, d_ref)
+
+
 def turn(array, k, members):
     return lax.ppermute(array, "code", [(i, (i + k) % members) for i in range(members)])
+
+
+def second(name, extra, hint, *args):
+    half = args[0].shape[0]
+    return kernel_call(
+        second_kernel,
+        "second_" + name,
+        (flat(half + extra), flat(half + extra)),
+        [VMEM] * 4,
+        (VMEM, VMEM),
+        cost=hint,
+    )(*args)
+
+
+def parity_relayed(name, key, moved, members):
+    slots = moved.shape[0]
+    quarter = slots // members
+    half = quarter // 2
+    a, b, give_a, give_b, keep_c, keep_d, mine = kernel_call(
+        parity_first_kernel,
+        "parity_first_" + name,
+        (flat(half),) * 6 + (flat(quarter),),
+        [SMEM, SMEM, VMEM],
+        (VMEM,) * 7,
+        cost=2 << 20,
+    )(*key, moved)
+    back_a, back_b = swap(a, 0, members), swap(b, 1, members)
+    stay_a, stay_b = swap(give_a, 0, members), swap(give_b, 1, members)
+    send_c, send_d = second("parity_" + name, 0, 1 << 33, keep_c, keep_d, back_a, back_b)
+    back_c, back_d = swap(send_c, 1, members), swap(send_d, 0, members)
+    out = kernel_call(copy_kernel, "emit_" + name, flat(slots), [VMEM], VMEM, cost=2 << 20)(moved)
+    parity = kernel_call(
+        parity_last_kernel, "parity_last_" + name, flat(quarter), [VMEM] * 5, VMEM, cost=1 << 20
+    )(mine, stay_a, stay_b, back_c, back_d)
+    return out, parity
 
 
 def parity_of(name, key, moved, members):
@@ -293,11 +358,12 @@
         front_kernel,
         "front_send",
         (flat(half + 2 * part), flat(half + 2 * part)),
-        scalars + [HBM, HBM, HBM],
+        [SMEM, HBM, SMEM, HBM, HBM, HBM],
         (VMEM, VMEM),
         cost=3 << 20,
         scratch_shapes=buffers(2)
-        + [pltpu.SemaphoreType.DMA((4,)), pltpu.VMEM((entries // 128, 128), jnp.int32), pltpu.SemaphoreType.DMA],
+        + [pltpu.SemaphoreType.DMA((4,)), pltpu.VMEM((entries // 128, 128), jnp.int32)]
+        + [pltpu.SMEM((members,), jnp.float32), pltpu.SemaphoreType.DMA((2,))],
     )(*key, keep_out(adagrad_sums), keep_out(pending_grads), keep_out(pending_rows.reshape(-1, 128)))
     got_a, got_b = swap(send_a, 0, members), swap(send_b, 1, members)
 
@@ -310,12 +376,12 @@
         cost=3 << 20,
         scratch_shapes=buffers(6),
     )(*key, keep_out(adagrad_sums))
-    row_a, row_b, row_c, row_d, mine_rows = kernel_call(
+    row_a, row_b, row_give_a, row_give_b, row_c, row_d, mine_rows = kernel_call(
         both_kernel,
         "weigh_rows",
-        (flat(share), flat(share), flat(half), flat(half), flat(share)),
+        (flat(half),) * 6 + (flat(share),),
         scalars + [HBM],
-        (VMEM,) * 5,
+        (VMEM,) * 7,
         cost=4 << 20,
         scratch_shapes=buffers(8),
     )(*key, keep_out(table_rows))
@@ -325,48 +391,44 @@
     rank = jnp.sum(earlier.astype(jnp.int32), axis=1)
     place = (owner * capacity + rank)[None, :]
 
-    def second(name, extra, hint, *args):
-        return kernel_call(
-            second_kernel,
-            "second_" + name,
-            (flat(half + extra), flat(half + extra)),
-            [VMEM] * 4,
-            (VMEM, VMEM),
-            cost=hint,
-        )(*args)
-
     send_c, send_d = second("sums", part, 1 << 38, keep_c, keep_d, got_a, got_b)
     got_c, got_d = swap(send_c, 1, members), swap(send_d, 0, members)
     kept_a, kept_b, got_a, got_b = lax.optimization_barrier((kept_a, kept_b, got_a, got_b))
-    part_totals = kernel_call(
-        totals_kernel, "pending_totals", flat(share), [SMEM] + [VMEM] * 3, VMEM, cost=4 << 20
-    )(member, send_a, got_a, got_b)
-    row_a, row_b, got_c, got_d, part_totals, place = lax.optimization_barrier(
-        (row_a, row_b, got_c, got_d, part_totals, place)
+    part_totals, base_sums = kernel_call(
+        totals_kernel, "pending_totals", (flat(share), flat(share)), [SMEM] + [VMEM] * 6, (VMEM, VMEM), cost=4 << 20
+    )(member, send_a, got_a, got_b, mine_sums, kept_a, kept_b)
+    row_a, row_b, row_give_a, row_give_b, got_c, got_d, part_totals, place = lax.optimization_barrier(
+        (row_a, row_b, row_give_a, row_give_b, got_c, got_d, part_totals, place)
     )
     back_a, back_b = swap(row_a, 0, members), swap(row_b, 1, members)
-
-    scratch = [pltpu.VMEM((share, 256), jnp.bfloat16)]
+    stay_a, stay_b = swap(row_give_a, 0, members), swap(row_give_b, 1, members)
+
+    scratch = [
+        pltpu.VMEM((share, 256), jnp.bfloat16),
+        pltpu.VMEM((slots, 128), jnp.float32),
+        pltpu.SemaphoreType.DMA((8,)),
+    ]
     out_sums, new_sums, totals = kernel_call(
         sums_kernel,
         "place_sums",
-        (pltpu.VMEM((slots, 128), jnp.float32), flat(share), flat(share)),
-        [SMEM] + [VMEM] * 7,
-        (VMEM, VMEM, VMEM),
+        (flat(slots), flat(share), flat(share)),
+        [SMEM] + [VMEM] * 5,
+        (HBM, VMEM, VMEM),
         cost=6 << 20,
         scratch_shapes=scratch,
-    )(member, place, mine_sums, kept_a, kept_b, got_c, got_d, part_totals)
+    )(member, place, base_sums, got_c, got_d, part_totals)
     moved_sums = lax.all_to_all(out_sums, "shard", 0, 0, tiled=True)
 
-    send_c, send_d = second("rows", 0, 1 << 38, row_c, row_d, back_a, back_b)
+    send_c, send_d = second("rows", 0, 1 << 33, row_c, row_d, back_a, back_b)
     back_c, back_d = swap(send_c, 1, members), swap(send_d, 0, members)
     out_rows = kernel_call(
-        rows_kernel, "place_rows", pltpu.VMEM((slots, 128), jnp.float32), [VMEM] * 8, VMEM, cost=6 << 20, scratch_shapes=scratch
-    )(place, mine_rows, back_a, back_b, back_c, back_d, totals, new_sums)
+        rows_kernel, "place_rows", flat(slots), [VMEM] * 8, HBM, cost=6 << 20, scratch_shapes=scratch
+    )(place, mine_rows, stay_a, stay_b, back_c, back_d, totals, new_sums)
     moved_rows = lax.all_to_all(out_rows, "shard", 0, 0, tiled=True)
 
     final_sums, parity_sums = parity_of("sums", (code_weight, member), moved_sums, members)
-    final_rows, parity_rows = parity_of("rows", (code_weight, member), moved_rows, members)
+    moved_rows, final_sums, parity_sums = lax.optimization_barrier((moved_rows, final_sums, parity_sums))
+    final_rows, parity_rows = parity_relayed("rows", (code_weight, member), moved_rows, members)
     return (final_rows, final_sums, parity_rows, parity_sums)
 
 

time: 133 us -> 127 us (0.955); the launches traced: 131 us -> 127 us
  waiting for transfers between devices: 63.8 us -> 56.9 us
  starting transfers between devices: 40 us -> 45.4 us
  Pallas kernels: 22.4 us -> 18.7 us
    ppermute x10 -> x18, starting transfers between devices: 10.8 us -> 22.6 us  [swap(): return lax.ppermute(array, 'code', pairs)]
    all_to_all x1, waiting for transfers between devices: 21.2 us -> 10.6 us  [per_device(): moved_rows = lax.all_to_all(out_rows, 'shard', 0, 0, tiled=True)]
    all_to_all x1, waiting for transfers between devices: 14 us -> 4.3 us  [per_device(): moved_sums = lax.all_to_all(out_sums, 'shard', 0, 0, tiled=True)]
    ppermute x10 -> x18, waiting for transfers between devices: 22.1 us -> 31.5 us  [swap(): return lax.ppermute(array, 'code', pairs)]
    ppermute x6 -> x3, starting transfers between devices: 10.6 us -> 4.39 us  [turn(): lax.ppermute(array, 'code', [(i, (i + k) % members) for i in range(member...]
    ppermute x6 -> x3, waiting for transfers between devices: 6.39 us -> 10.4 us  [turn(): lax.ppermute(array, 'code', [(i, (i + k) % members) for i in range(member...]
    pallas_call x2 -> x1, Pallas kernels: 3.3 us -> 1.04 us  [parity_of(): kernel_call(copy_kernel, 'emit_' + name, flat(slots), [VMEM], VMEM, cost=...]
    pallas_call x4 -> x7, Pallas kernels: 10.7 us -> 11.9 us  [the longest x1 2.82 us: per_device(): kernel_call(sums_kernel, 'place_sums', (flat(slots), flat(share), flat(sh...]
  transfers between devices with their start and end apart: 18 -> 23, of which waited for: 12 -> 18; matrix products, arithmetic and copies ran while one was open for 1% -> 1% of each run, Pallas kernels for 15% -> 10%
where the time goes in v5:
time: 127 us
  waiting for transfers between devices  56.9 us (45%)
  starting transfers between devices  45.4 us (36%)
  Pallas kernels  18.7 us (15%)
  local copies, waits for them, and re-layouts  2.37 us (2%)
  other arithmetic  1.87 us (1%)
  between operations  1.49 us (1%)
    ppermute x18, waiting for transfers between devices, swap(): return lax.ppermute(array, 'code', pairs)  31.5 us
    ppermute x18, starting transfers between devices, swap(): return lax.ppermute(array, 'code', pairs)  22.6 us
    all_to_all x1, starting transfers between devices, per_device(): moved_sums = lax.all_to_all(out_sums, 'shard', 0, 0, tiled=True)  11.6 us
    all_to_all x1, waiting for transfers between devices, per_device(): moved_rows = lax.all_to_all(out_rows, 'shard', 0, 0, tiled=True)  10.6 us
    ppermute x3, waiting for transfers between devices, turn(): lax.ppermute(array, 'code', [(i, (i + k) % members) for i in range(member...  10.4 us
    all_to_all x1, starting transfers between devices, per_device(): moved_rows = lax.all_to_all(out_rows, 'shard', 0, 0, tiled=True)  6.87 us
    ppermute x3, starting transfers between devices, turn(): lax.ppermute(array, 'code', [(i, (i + k) % members) for i in range(member...  4.39 us
    all_to_all x1, waiting for transfers between devices, per_device(): moved_sums = lax.all_to_all(out_sums, 'shard', 0, 0, tiled=True)  4.3 us
  transfers between devices with their start and end apart: 23, of which 18 were waited for; matrix products, arithmetic and copies ran while one was open for 1% of the time, Pallas kernels for 10%

profile of v5, /device:TPU:32, one launch (start us, length us, event | category | flops | bytes accessed | tf_op | source)
XLA Modules:
  0.0 126.7 jit_solution(7316001177323162243)
XLA Ops:
  4.3 2.2 %collective-permute-start.1 = (f32[1040,128]{1,0:T(8,128)S(1)}, f32[1040,128]{1,0:T(8,128)S(1)}, u32[]{:S(2)}, u32[]{:S(2)}) collective-permute-start(f32[1040,128]{1,0:T(8,128)S(1)} %get-tuple-element.70), channel_id=1, source_target_pairs={{0,3},{1,2},{2,1},{3,0},{4,7},{5,6},{6,5},{7,4},{8,11},{9,10},{10,... | collective-permute-start | bytes 1597448 | tf_op jit(solution)/shard_map/ppermute | solution.py:159
  6.5 2.8 %keep_sums.1 = (f32[512,128]{1,0:T(8,128)}, f32[512,128]{1,0:T(8,128)}, f32[512,128]{1,0:T(8,128)S(1)}, f32[512,128]{1,0:T(8,128)S(1)}, f32[1024,128]{1,0:T(8,128)S(1)}) custom-call(s32[1]{0:T(128)S(6)} %copy.11.lost_ref, f32[4]{0:T(128)} %weight_ref.7, s32[1]{0:T(128)} %bitcast.member_ref, f32[4096,128]{1,0:T(8,128)} %table_ref.5), custom_call_target="tpu_custom_call" | custom-call | flops 3145728 | bytes 3145728 | tf_op jit(solution)/shard_map/keep_sums/pallas_call | solution.py:370
  9.3 2.3 %weigh_rows.1 = (f32[512,128]{1,0:T(8,128)S(1)}, f32[512,128]{1,0:T(8,128)S(1)}, f32[512,128]{1,0:T(8,128)S(1)}, f32[512,128]{1,0:T(8,128)S(1)}, f32[512,128]{1,...) custom-call(s32[1]{0:T(128)S(6)} %copy.11.lost_ref, f32[4]{0:T(128)} %weight_ref.7, s32[1]{0:T(128)} %bitcast.member_ref, ...), custom_call_target="tpu_custom_call" | custom-call | flops 4194304 | bytes 4194304 | tf_op jit(solution)/shard_map/weigh_rows/pallas_call | solution.py:379
  14.9 2.8 %collective-permute-done.a_ref = f32[1040,128]{1,0:T(8,128)S(1)} collective-permute-done((f32[1040,128]{1,0:T(8,128)S(1)}, f32[1040,128]{1,0:T(8,128)S(1)}, u32[]{:S(2)}, u32[]{:S(2)}) %collective-permute-start) | collective-permute-done | bytes 532512 | tf_op jit(solution)/shard_map/ppermute | solution.py:159
  17.7 2.8 %collective-permute-done.1.b_ref = f32[1040,128]{1,0:T(8,128)S(1)} collective-permute-done((f32[1040,128]{1,0:T(8,128)S(1)}, f32[1040,128]{1,0:T(8,128)S(1)}, u32[]{:S(2)}, u32[]{:S(2)}) %collective-permute-start.1) | collective-permute-done | bytes 532512 | tf_op jit(solution)/shard_map/ppermute | solution.py:159
  20.6 2.3 %collective-permute-start.2 = (f32[776,128]{1,0:T(8,128)S(1)}, f32[776,128]{1,0:T(8,128)S(1)}, u32[]{:S(2)}, u32[]{:S(2)}) collective-permute-start(f32[776,128]{1,0:T(8,128)S(1)} %get-tuple-element.71), channel_id=1, source_target_pairs={{0,3},{1,2},{2,1},{3,0},{4,7},{5,6},{6,5},{7,4},{8,11},{9,10},{10,... | collective-permute-start | bytes 1191944 | tf_op jit(solution)/shard_map/ppermute | solution.py:159
  26.3 2.1 %pending_totals.1 = (f32[1024,128]{1,0:T(8,128)S(1)}, f32[1024,128]{1,0:T(8,128)S(1)}) custom-call(s32[1]{0:T(128)} %bitcast.member_ref, f32[1040,128]{1,0:T(8,128)S(1)} %copy-done.1, f32[1040,128]{1,0:T(8,128)S(1)} %collective-permute-done.a_ref, f32[1040,128]{1,0:T(8,128)S(1)} %collective-permute-done.1.b_ref, f32[1024,128]{1,0:T(8,128)S(1)} %get-tuple-element.77.mine_ref, ...), custom_call_target="tpu_custom_call" | custom-call | flops 4194304 | bytes 4194304 | tf_op jit(solution)/shard_map/pending_totals/pallas_call | solution.py:397
  28.3 4.9 %collective-permute-done.2.c_ref = f32[776,128]{1,0:T(8,128)S(1)} collective-permute-done((f32[776,128]{1,0:T(8,128)S(1)}, f32[776,128]{1,0:T(8,128)S(1)}, u32[]{:S(2)}, u32[]{:S(2)}) %collective-permute-start.2) | collective-permute-done | bytes 397344 | tf_op jit(solution)/shard_map/ppermute | solution.py:159
  33.2 2.8 %place_sums.1 = (f32[2048,128]{1,0:T(8,128)}, f32[1024,128]{1,0:T(8,128)S(1)}, f32[1024,128]{1,0:T(8,128)S(1)}) custom-call(s32[1]{0:T(128)} %bitcast.member_ref, s32[1,1024]{1,0:T(1,128)S(1)} %bitcast_add_fusion.place_ref, f32[1024,128]{1,0:T(8,128)S(1)} %get-tuple-element.91.base_ref, f32[776,128]{1,0:T(8,128)S(1)} %collective-permute-done.2.c_ref, ...), custom_call_target="tpu_custom_call" | custom-call | flops 6291456 | bytes 6291456 | tf_op jit(solution)/shard_map/place_sums/pallas_call | solution.py:411
  36.0 11.6 %all-to-all-start.1 = ((f32[64,32,128]{2,1,0:T(8,128)}), f32[64,32,128]{2,1,0:T(8,128)S(1)}, u32[]{:S(2)}, u32[]{:S(2)}) async-start(f32[64,32,128]{2,1,0:T(8,128)} %bitcast.7), calls=%async_computation.1 | async-start | bytes 2097152 | tf_op jit(solution)/shard_map/all_to_all | solution.py:420
  47.7 2.3 %collective-permute-start.9 = (f32[512,128]{1,0:T(8,128)}, f32[512,128]{1,0:T(8,128)S(1)}, u32[]{:S(2)}, u32[]{:S(2)}) collective-permute-start(f32[512,128]{1,0:T(8,128)} %copy-done.5), channel_id=1, source_target_pairs={{0,3},{1,2},{2,1},{3,0},{4,7},{5,6},{6,5},{7,4},{8,11},{9,10},{10,... | collective-permute-start | bytes 786440 | tf_op jit(solution)/shard_map/ppermute | solution.py:159
  52.4 4.7 %collective-permute-done.8.a_ref = f32[512,128]{1,0:T(8,128)S(1)} collective-permute-done((f32[512,128]{1,0:T(8,128)}, f32[512,128]{1,0:T(8,128)S(1)}, u32[]{:S(2)}, u32[]{:S(2)}) %collective-permute-start.8) | collective-permute-done | bytes 262176 | tf_op jit(solution)/shard_map/ppermute | solution.py:159
  59.4 2.3 %collective-permute-start.10 = (f32[512,128]{1,0:T(8,128)S(1)}, f32[512,128]{1,0:T(8,128)S(1)}, u32[]{:S(2)}, u32[]{:S(2)}) collective-permute-start(f32[512,128]{1,0:T(8,128)S(1)} %get-tuple-element.89), channel_id=1, source_target_pairs={{0,3},{1,2},{2,1},{3,0},{4,7},{5,6},{6,5},{7,4},{8,11},{9,10},{10,... | collective-permute-start | bytes 786440 | tf_op jit(solution)/shard_map/ppermute | solution.py:159
  61.9 2.1 %collective-permute-done.7.b_ref = f32[512,128]{1,0:T(8,128)S(1)} collective-permute-done((f32[512,128]{1,0:T(8,128)S(1)}, f32[512,128]{1,0:T(8,128)S(1)}, u32[]{:S(2)}, u32[]{:S(2)}) %collective-permute-start.7) | collective-permute-done | bytes 262176 | tf_op jit(solution)/shard_map/ppermute | solution.py:159
  64.0 4.8 %collective-permute-done.10.c_ref = f32[512,128]{1,0:T(8,128)S(1)} collective-permute-done((f32[512,128]{1,0:T(8,128)S(1)}, f32[512,128]{1,0:T(8,128)S(1)}, u32[]{:S(2)}, u32[]{:S(2)}) %collective-permute-start.10) | collective-permute-done | bytes 262176 | tf_op jit(solution)/shard_map/ppermute | solution.py:159
  68.8 2.4 %place_rows.1 = f32[2048,128]{1,0:T(8,128)} custom-call(s32[1,1024]{1,0:T(1,128)S(1)} %bitcast_add_fusion.place_ref, f32[1024,128]{1,0:T(8,128)S(1)} %get-tuple-element.82.mine_ref, f32[512,128]{1,0:T(8,128)S(1)} %collective-permute-done.6.a_ref, f32[512,128]{1,0:T(8,128)S(1)} %collective-permute-done.7.b_ref, f32[512,128]{1,0:T(8,128)S(1)} %collective-permute-done.10.c_ref, ...), custom_call_target="tpu_custom_call" | custom-call | flops 6291456 | bytes 6291456 | tf_op jit(solution)/shard_map/place_rows/pallas_call | solution.py:424
  71.2 4.3 %all-to-all-done.1 = f32[64,32,128]{2,1,0:T(8,128)S(1)} async-done(((f32[64,32,128]{2,1,0:T(8,128)}), f32[64,32,128]{2,1,0:T(8,128)S(1)}, u32[]{:S(2)}, u32[]{:S(2)}) %all-to-all-start.1) | async-done | bytes 1048608 | tf_op jit(solution)/shard_map/all_to_all | solution.py:420
  75.5 6.9 %all-to-all-start = ((f32[64,32,128]{2,1,0:T(8,128)}), f32[64,32,128]{2,1,0:T(8,128)S(1)}, u32[]{:S(2)}, u32[]{:S(2)}) async-start(f32[64,32,128]{2,1,0:T(8,128)} %bitcast.5), calls=%async_computation | async-start | bytes 2097152 | tf_op jit(solution)/shard_map/all_to_all | solution.py:427
  83.1 3.6 %collective-permute-start.13 = (f32[512,128]{1,0:T(8,128)S(1)}, f32[512,128]{1,0:T(8,128)S(1)}, u32[]{:S(2)}, u32[]{:S(2)}) collective-permute-start(f32[512,128]{1,0:T(8,128)S(1)} %get-tuple-element.100), channel_id=1, source_target_pairs={{0,2},{1,3},{2,0},{3,1},{4,6},{5,7},{6,4},{7,5},{8,10},{9,11},{10,... | collective-permute-start | bytes 786440 | tf_op jit(solution)/shard_map/ppermute | solution.py:278
  88.5 4.6 %collective-permute-done.12.a_ref = f32[512,128]{1,0:T(8,128)S(1)} collective-permute-done((f32[512,128]{1,0:T(8,128)S(1)}, f32[512,128]{1,0:T(8,128)S(1)}, u32[]{:S(2)}, u32[]{:S(2)}) %collective-permute-start.12) | collective-permute-done | bytes 262176 | tf_op jit(solution)/shard_map/ppermute | solution.py:278
  93.1 5.6 %collective-permute-done.13.b_ref = f32[512,128]{1,0:T(8,128)S(1)} collective-permute-done((f32[512,128]{1,0:T(8,128)S(1)}, f32[512,128]{1,0:T(8,128)S(1)}, u32[]{:S(2)}, u32[]{:S(2)}) %collective-permute-start.13) | collective-permute-done | bytes 262176 | tf_op jit(solution)/shard_map/ppermute | solution.py:278
  99.7 10.6 %all-to-all-done = f32[64,32,128]{2,1,0:T(8,128)S(1)} async-done(((f32[64,32,128]{2,1,0:T(8,128)}), f32[64,32,128]{2,1,0:T(8,128)S(1)}, u32[]{:S(2)}, u32[]{:S(2)}) %all-to-all-start) | async-done | bytes 1048608 | tf_op jit(solution)/shard_map/all_to_all | solution.py:427
  111.0 2.3 %collective-permute-start.18 = (f32[256,128]{1,0:T(8,128)S(1)}, f32[256,128]{1,0:T(8,128)S(1)}, u32[]{:S(2)}, u32[]{:S(2)}) collective-permute-start(f32[256,128]{1,0:T(8,128)S(1)} %get-tuple-element.110), channel_id=1, source_target_pairs={{0,3},{1,2},{2,1},{3,0},{4,7},{5,6},{6,5},{7,4},{8,11},{9,10},{10,... | collective-permute-start | bytes 393224 | tf_op jit(solution)/shard_map/ppermute | solution.py:159
  117.8 3.1 %collective-permute-start.19 = (f32[256,128]{1,0:T(8,128)S(1)}, f32[256,128]{1,0:T(8,128)S(1)}, u32[]{:S(2)}, u32[]{:S(2)}) collective-permute-start(f32[256,128]{1,0:T(8,128)S(1)} %get-tuple-element.111), channel_id=1, source_target_pairs={{0,3},{1,2},{2,1},{3,0},{4,7},{5,6},{6,5},{7,4},{8,11},{9,10},{10,... | collective-permute-start | bytes 393224 | tf_op jit(solution)/shard_map/ppermute | solution.py:159
  (58 shorter events, 29.1 us)
Async XLA Ops:
  2.6 15.1 %collective-permute-start = (f32[1040,128]{1,0:T(8,128)S(1)}, f32[1040,128]{1,0:T(8,128)S(1)}, u32[]{:S(2)}, u32[]{:S(2)}) collective-permute-start(f32[1040,128]{1,0:T(8,128)S(1)} %get-tuple-element.69.own_ref), channel_id=1, source_target_pairs={{0,1},{1,0},{2,3},{3,2},{4,5},{5,4},{6,7},{7,6},{8,9},{9,8},{10,11... | collective-permute-start | bytes 1597448 | tf_op jit(solution)/shard_map/ppermute | solution.py:159
  4.3 16.2 %collective-permute-start.1 = (f32[1040,128]{1,0:T(8,128)S(1)}, f32[1040,128]{1,0:T(8,128)S(1)}, u32[]{:S(2)}, u32[]{:S(2)}) collective-permute-start(f32[1040,128]{1,0:T(8,128)S(1)} %get-tuple-element.70), channel_id=1, source_target_pairs={{0,3},{1,2},{2,1},{3,0},{4,7},{5,6},{6,5},{7,4},{8,11},{9,10},{10,... | collective-permute-start | bytes 1597448 | tf_op jit(solution)/shard_map/ppermute | solution.py:159
  13.0 11.2 %collective-permute-start.4 = (f32[512,128]{1,0:T(8,128)}, f32[512,128]{1,0:T(8,128)}, u32[]{:S(2)}, u32[]{:S(2)}) collective-permute-start(f32[512,128]{1,0:T(8,128)} %get-tuple-element.73), channel_id=1, source_target_pairs={{0,1},{1,0},{2,3},{3,2},{4,5},{5,4},{6,7},{7,6},{8,9},{9,8},{10,11... | collective-permute-start | bytes 786440 | tf_op jit(solution)/shard_map/ppermute | solution.py:159
  13.7 12.6 %collective-permute-start.5 = (f32[512,128]{1,0:T(8,128)}, f32[512,128]{1,0:T(8,128)}, u32[]{:S(2)}, u32[]{:S(2)}) collective-permute-start(f32[512,128]{1,0:T(8,128)} %get-tuple-element.74), channel_id=1, source_target_pairs={{0,3},{1,2},{2,1},{3,0},{4,7},{5,6},{6,5},{7,4},{8,11},{9,10},{10,... | collective-permute-start | bytes 786440 | tf_op jit(solution)/shard_map/ppermute | solution.py:159
  20.6 12.6 %collective-permute-start.2 = (f32[776,128]{1,0:T(8,128)S(1)}, f32[776,128]{1,0:T(8,128)S(1)}, u32[]{:S(2)}, u32[]{:S(2)}) collective-permute-start(f32[776,128]{1,0:T(8,128)S(1)} %get-tuple-element.71), channel_id=1, source_target_pairs={{0,3},{1,2},{2,1},{3,0},{4,7},{5,6},{6,5},{7,4},{8,11},{9,10},{10,... | collective-permute-start | bytes 1191944 | tf_op jit(solution)/shard_map/ppermute | solution.py:159
  22.9 10.3 %collective-permute-start.3 = (f32[776,128]{1,0:T(8,128)S(1)}, f32[776,128]{1,0:T(8,128)S(1)}, u32[]{:S(2)}, u32[]{:S(2)}) collective-permute-start(f32[776,128]{1,0:T(8,128)S(1)} %get-tuple-element.72), channel_id=1, source_target_pairs={{0,1},{1,0},{2,3},{3,2},{4,5},{5,4},{6,7},{7,6},{8,9},{9,8},{10,11... | collective-permute-start | bytes 1191944 | tf_op jit(solution)/shard_map/ppermute | solution.py:159
  36.0 39.5 %all-to-all-start.1 = ((f32[64,32,128]{2,1,0:T(8,128)}), f32[64,32,128]{2,1,0:T(8,128)S(1)}, u32[]{:S(2)}, u32[]{:S(2)}) async-start(f32[64,32,128]{2,1,0:T(8,128)} %bitcast.7), calls=%async_computation.1 | async-start | bytes 2097152 | tf_op jit(solution)/shard_map/all_to_all | solution.py:420
  47.6 9.4 %collective-permute-start.8 = (f32[512,128]{1,0:T(8,128)}, f32[512,128]{1,0:T(8,128)S(1)}, u32[]{:S(2)}, u32[]{:S(2)}) collective-permute-start(f32[512,128]{1,0:T(8,128)} %copy-done.6), channel_id=1, source_target_pairs={{0,1},{1,0},{2,3},{3,2},{4,5},{5,4},{6,7},{7,6},{8,9},{9,8},{10,11... | collective-permute-start | bytes 786440 | tf_op jit(solution)/shard_map/ppermute | solution.py:159
  47.7 10.7 %collective-permute-start.9 = (f32[512,128]{1,0:T(8,128)}, f32[512,128]{1,0:T(8,128)S(1)}, u32[]{:S(2)}, u32[]{:S(2)}) collective-permute-start(f32[512,128]{1,0:T(8,128)} %copy-done.5), channel_id=1, source_target_pairs={{0,3},{1,2},{2,1},{3,0},{4,7},{5,6},{6,5},{7,4},{8,11},{9,10},{10,... | collective-permute-start | bytes 786440 | tf_op jit(solution)/shard_map/ppermute | solution.py:159
  50.0 11.9 %collective-permute-start.6 = (f32[512,128]{1,0:T(8,128)S(1)}, f32[512,128]{1,0:T(8,128)S(1)}, u32[]{:S(2)}, u32[]{:S(2)}) collective-permute-start(f32[512,128]{1,0:T(8,128)S(1)} %get-tuple-element.83), channel_id=1, source_target_pairs={{0,1},{1,0},{2,3},{3,2},{4,5},{5,4},{6,7},{7,6},{8,9},{9,8},{10,11... | collective-permute-start | bytes 786440 | tf_op jit(solution)/shard_map/ppermute | solution.py:159
  51.3 12.7 %collective-permute-start.7 = (f32[512,128]{1,0:T(8,128)S(1)}, f32[512,128]{1,0:T(8,128)S(1)}, u32[]{:S(2)}, u32[]{:S(2)}) collective-permute-start(f32[512,128]{1,0:T(8,128)S(1)} %get-tuple-element.84), channel_id=1, source_target_pairs={{0,3},{1,2},{2,1},{3,0},{4,7},{5,6},{6,5},{7,4},{8,11},{9,10},{10,... | collective-permute-start | bytes 786440 | tf_op jit(solution)/shard_map/ppermute | solution.py:159
  59.4 9.4 %collective-permute-start.10 = (f32[512,128]{1,0:T(8,128)S(1)}, f32[512,128]{1,0:T(8,128)S(1)}, u32[]{:S(2)}, u32[]{:S(2)}) collective-permute-start(f32[512,128]{1,0:T(8,128)S(1)} %get-tuple-element.89), channel_id=1, source_target_pairs={{0,3},{1,2},{2,1},{3,0},{4,7},{5,6},{6,5},{7,4},{8,11},{9,10},{10,... | collective-permute-start | bytes 786440 | tf_op jit(solution)/shard_map/ppermute | solution.py:159
  61.7 7.2 %collective-permute-start.11 = (f32[512,128]{1,0:T(8,128)S(1)}, f32[512,128]{1,0:T(8,128)S(1)}, u32[]{:S(2)}, u32[]{:S(2)}) collective-permute-start(f32[512,128]{1,0:T(8,128)S(1)} %get-tuple-element.90), channel_id=1, source_target_pairs={{0,1},{1,0},{2,3},{3,2},{4,5},{5,4},{6,7},{7,6},{8,9},{9,8},{10,11... | collective-permute-start | bytes 786440 | tf_op jit(solution)/shard_map/ppermute | solution.py:159
  68.8 13.6 %copy-start.2 = (f32[4]{0:T(128)S(1)}, f32[4]{0:T(128)}, u32[]{:S(2)}) copy-start(f32[4]{0:T(128)} %weight_ref.7) | copy-start | bytes 52
  75.5 34.8 %all-to-all-start = ((f32[64,32,128]{2,1,0:T(8,128)}), f32[64,32,128]{2,1,0:T(8,128)S(1)}, u32[]{:S(2)}, u32[]{:S(2)}) async-start(f32[64,32,128]{2,1,0:T(8,128)} %bitcast.5), calls=%async_computation | async-start | bytes 2097152 | tf_op jit(solution)/shard_map/all_to_all | solution.py:427
  83.0 10.0 %collective-permute-start.12 = (f32[512,128]{1,0:T(8,128)S(1)}, f32[512,128]{1,0:T(8,128)S(1)}, u32[]{:S(2)}, u32[]{:S(2)}) collective-permute-start(f32[512,128]{1,0:T(8,128)S(1)} %get-tuple-element.99), channel_id=1, source_target_pairs={{0,1},{1,2},{2,3},{3,0},{4,5},{5,6},{6,7},{7,4},{8,9},{9,10},{10,1... | collective-permute-start | bytes 786440 | tf_op jit(solution)/shard_map/ppermute | solution.py:278
  83.1 15.6 %collective-permute-start.13 = (f32[512,128]{1,0:T(8,128)S(1)}, f32[512,128]{1,0:T(8,128)S(1)}, u32[]{:S(2)}, u32[]{:S(2)}) collective-permute-start(f32[512,128]{1,0:T(8,128)S(1)} %get-tuple-element.100), channel_id=1, source_target_pairs={{0,2},{1,3},{2,0},{3,1},{4,6},{5,7},{6,4},{7,5},{8,10},{9,11},{10,... | collective-permute-start | bytes 786440 | tf_op jit(solution)/shard_map/ppermute | solution.py:278
  86.7 12.2 %collective-permute-start.14 = (f32[512,128]{1,0:T(8,128)S(1)}, f32[512,128]{1,0:T(8,128)S(1)}, u32[]{:S(2)}, u32[]{:S(2)}) collective-permute-start(f32[512,128]{1,0:T(8,128)S(1)} %get-tuple-element.101), channel_id=1, source_target_pairs={{0,3},{1,0},{2,1},{3,2},{4,7},{5,4},{6,5},{7,6},{8,11},{9,8},{10,9... | collective-permute-start | bytes 786440 | tf_op jit(solution)/shard_map/ppermute | solution.py:278
  110.9 6.3 %collective-permute-start.17 = (f32[256,128]{1,0:T(8,128)S(1)}, f32[256,128]{1,0:T(8,128)S(1)}, u32[]{:S(2)}, u32[]{:S(2)}) collective-permute-start(f32[256,128]{1,0:T(8,128)S(1)} %get-tuple-element.109), channel_id=1, source_target_pairs={{0,1},{1,0},{2,3},{3,2},{4,5},{5,4},{6,7},{7,6},{8,9},{9,8},{10,11... | collective-permute-start | bytes 393224 | tf_op jit(solution)/shard_map/ppermute | solution.py:159
  111.0 6.8 %collective-permute-start.18 = (f32[256,128]{1,0:T(8,128)S(1)}, f32[256,128]{1,0:T(8,128)S(1)}, u32[]{:S(2)}, u32[]{:S(2)}) collective-permute-start(f32[256,128]{1,0:T(8,128)S(1)} %get-tuple-element.110), channel_id=1, source_target_pairs={{0,3},{1,2},{2,1},{3,0},{4,7},{5,6},{6,5},{7,4},{8,11},{9,10},{10,... | collective-permute-start | bytes 393224 | tf_op jit(solution)/shard_map/ppermute | solution.py:159
  113.3 8.9 %collective-permute-start.15 = (f32[256,128]{1,0:T(8,128)S(1)}, f32[256,128]{1,0:T(8,128)S(1)}, u32[]{:S(2)}, u32[]{:S(2)}) collective-permute-start(f32[256,128]{1,0:T(8,128)S(1)} %get-tuple-element.105), channel_id=1, source_target_pairs={{0,1},{1,0},{2,3},{3,2},{4,5},{5,4},{6,7},{7,6},{8,9},{9,8},{10,11... | collective-permute-start | bytes 393224 | tf_op jit(solution)/shard_map/ppermute | solution.py:159
  114.6 7.6 %collective-permute-start.16 = (f32[256,128]{1,0:T(8,128)S(1)}, f32[256,128]{1,0:T(8,128)S(1)}, u32[]{:S(2)}, u32[]{:S(2)}) collective-permute-start(f32[256,128]{1,0:T(8,128)S(1)} %get-tuple-element.106), channel_id=1, source_target_pairs={{0,3},{1,2},{2,1},{3,0},{4,7},{5,6},{6,5},{7,4},{8,11},{9,10},{10,... | collective-permute-start | bytes 393224 | tf_op jit(solution)/shard_map/ppermute | solution.py:159
  117.8 6.3 %collective-permute-start.19 = (f32[256,128]{1,0:T(8,128)S(1)}, f32[256,128]{1,0:T(8,128)S(1)}, u32[]{:S(2)}, u32[]{:S(2)}) collective-permute-start(f32[256,128]{1,0:T(8,128)S(1)} %get-tuple-element.111), channel_id=1, source_target_pairs={{0,3},{1,2},{2,1},{3,0},{4,7},{5,6},{6,5},{7,4},{8,11},{9,10},{10,... | collective-permute-start | bytes 393224 | tf_op jit(solution)/shard_map/ppermute | solution.py:159
  120.9 5.0 %collective-permute-start.20 = (f32[256,128]{1,0:T(8,128)S(1)}, f32[256,128]{1,0:T(8,128)S(1)}, u32[]{:S(2)}, u32[]{:S(2)}) collective-permute-start(f32[256,128]{1,0:T(8,128)S(1)} %get-tuple-element.112), channel_id=1, source_target_pairs={{0,1},{1,0},{2,3},{3,2},{4,5},{5,4},{6,7},{7,6},{8,9},{9,8},{10,11... | collective-permute-start | bytes 393224 | tf_op jit(solution)/shard_map/ppermute | solution.py:159
  (8 other events, 29.4 us)

commit v6 on v5

--- a/solution.py
+++ b/solution.py
@@ -8,6 +8,7 @@
 step_size = 0.5
 epsilon = 1e-08
 MEMBERS = 4
+SLOT = 32
 SMEM = pl.BlockSpec(memory_space=pltpu.SMEM)
 VMEM = pl.BlockSpec(memory_space=pltpu.VMEM)
 HBM = pl.BlockSpec(memory_space=pltpu.HBM)
@@ -253,6 +254,23 @@
     for k, out_ref in enumerate(out_refs):
         out_ref[...] = own * moved_ref[quarter_of(member + k + 1, count), :]
     mine_ref[...] = own * moved_ref[quarter_of(member, count), :]
+
+
+def other_core_kernel(shard_ref, got_ref, out_ref):
+    core = lax.rem(shard_ref[0], 2)
+    for i in range(out_ref.shape[0] // SLOT):
+        start = pl.multiple_of((2 * i + 1 - core) * SLOT, 8)
+        out_ref[i * SLOT : (i + 1) * SLOT, :] = got_ref[pl.ds(start, SLOT), :]
+
+
+def emit_kernel(weight_ref, member_ref, shard_ref, got_ref, side_ref, out_ref, mine_ref, *send_refs):
+    core = lax.rem(shard_ref[0], 2)
+    for i in range(side_ref.shape[0] // SLOT):
+        start = pl.multiple_of((2 * i + core) * SLOT, 8)
+        out_ref[pl.ds(start, SLOT), :] = got_ref[pl.ds(start, SLOT), :]
+        start = pl.multiple_of((2 * i + 1 - core) * SLOT, 8)
+        out_ref[pl.ds(start, SLOT), :] = side_ref[i * SLOT : (i + 1) * SLOT, :]
+    parity_send_kernel(weight_ref, member_ref, out_ref, mine_ref, *send_refs)
 
 
 def parity_sum_kernel(mine_ref, a_ref, b_ref, c_ref, out_ref):
@@ -313,19 +331,22 @@
     return out, parity
 
 
-def parity_of(name, key, moved, members):
-    slots = moved.shape[0]
+def parity_direct(name, key, shard, got, shards, members):
+    slots = got.shape[0]
     quarter = slots // members
-    mine, *sends = kernel_call(
-        parity_send_kernel,
-        "parity_send_" + name,
-        (flat(quarter),) * members,
-        [SMEM, SMEM, VMEM],
-        (VMEM,) * members,
-        cost=2 << 20,
-    )(*key, moved)
+    side = kernel_call(
+        other_core_kernel, "other_core_" + name, flat(slots // 2), [SMEM, VMEM], VMEM, cost=1 << 20
+    )(shard, got)
+    side = lax.ppermute(side, "shard", [(i, i ^ 1) for i in range(shards)])
+    out, mine, *sends = kernel_call(
+        emit_kernel,
+        "emit_" + name,
+        (flat(slots),) + (flat(quarter),) * members,
+        [SMEM, SMEM, SMEM, VMEM, VMEM],
+        (VMEM,) * (members + 1),
+        cost=3 << 20,
+    )(*key, shard, got, side)
     gots = {k: turn(sends[k - 1], k, members) for k in (2, 1, 3)}
-    out = kernel_call(copy_kernel, "emit_" + name, flat(slots), [VMEM], VMEM, cost=2 << 20)(moved)
     parity = kernel_call(
         parity_sum_kernel, "parity_sum_" + name, flat(quarter), [VMEM] * members, VMEM, cost=1 << 20
     )(mine, gots[1], gots[2], gots[3])
@@ -417,7 +438,8 @@
         cost=6 << 20,
         scratch_shapes=scratch,
     )(member, place, base_sums, got_c, got_d, part_totals)
-    moved_sums = lax.all_to_all(out_sums, "shard", 0, 0, tiled=True)
+    same_core = [list(range(core, shards, 2)) for core in range(2)]
+    got_sums = lax.all_to_all(out_sums, "shard", 0, 0, tiled=True, axis_index_groups=same_core)
 
     send_c, send_d = second("rows", 0, 1 << 33, row_c, row_d, back_a, back_b)
     back_c, back_d = swap(send_c, 1, members), swap(send_d, 0, members)
@@ -426,7 +448,8 @@
     )(place, mine_rows, stay_a, stay_b, back_c, back_d, totals, new_sums)
     moved_rows = lax.all_to_all(out_rows, "shard", 0, 0, tiled=True)
 
-    final_sums, parity_sums = parity_of("sums", (code_weight, member), moved_sums, members)
+    shard = lax.axis_index("shard").astype(jnp.int32)[None]
+    final_sums, parity_sums = parity_direct("sums", (code_weight, member), shard, got_sums, shards, members)
     moved_rows, final_sums, parity_sums = lax.optimization_barrier((moved_rows, final_sums, parity_sums))
     final_rows, parity_rows = parity_relayed("rows", (code_weight, member), moved_rows, members)
     return (final_rows, final_sums, parity_rows, parity_sums)

time: 127 us -> 125 us (0.984)
  starting transfers between devices: 45.4 us -> 43.5 us
    all_to_all x1, waiting for transfers between devices: 10.6 us -> 7.61 us  [per_device(): moved_rows = lax.all_to_all(out_rows, 'shard', 0, 0, tiled=True)]
    ppermute x0 -> x1, waiting for transfers between devices: none -> 1.76 us  [parity_direct(): side = lax.ppermute(side, 'shard', [(i, i ^ 1) for i in range(shards)])]
  transfers between devices with their start and end apart: 23 -> 24, of which waited for: 18 -> 19; matrix products, arithmetic and copies ran while one was open for 1% -> 1% of each run, Pallas kernels for 10% -> 11%
where the time goes in v6:
time: 125 us; the launch traced here: 124 us
  waiting for transfers between devices  55.9 us (45%)
  starting transfers between devices  43.5 us (35%)
  Pallas kernels  18.7 us (15%)
  local copies, waits for them, and re-layouts  3.07 us (2%)
  other arithmetic  1.85 us (1%)
  between operations  1.47 us (1%)
    ppermute x18, waiting for transfers between devices, swap(): return lax.ppermute(array, 'code', pairs)  30.3 us
    ppermute x18, starting transfers between devices, swap(): return lax.ppermute(array, 'code', pairs)  22.2 us
    ppermute x3, waiting for transfers between devices, turn(): lax.ppermute(array, 'code', [(i, (i + k) % members) for i in range(member...  11.7 us
    all_to_all x1, starting transfers between devices, per_device(): lax.all_to_all(out_sums, 'shard', 0, 0, tiled=True, axis_index_groups=sam...  11.2 us
    all_to_all x1, waiting for transfers between devices, per_device(): moved_rows = lax.all_to_all(out_rows, 'shard', 0, 0, tiled=True)  7.61 us
    all_to_all x1, starting transfers between devices, per_device(): moved_rows = lax.all_to_all(out_rows, 'shard', 0, 0, tiled=True)  5.69 us
    all_to_all x1, waiting for transfers between devices, per_device(): lax.all_to_all(out_sums, 'shard', 0, 0, tiled=True, axis_index_groups=sam...  4.51 us
    ppermute x3, starting transfers between devices, turn(): lax.ppermute(array, 'code', [(i, (i + k) % members) for i in range(member...  4.15 us
  transfers between devices with their start and end apart: 24, of which 19 were waited for; matrix products, arithmetic and copies ran while one was open for 1% of the time, Pallas kernels for 11%

profile of v6, /device:TPU:32, one launch (start us, length us, event | category | flops | bytes accessed | tf_op | source)
XLA Modules:
  0.0 124.4 jit_solution(11260942287258443960)
XLA Ops:
  4.3 2.2 %collective-permute-start.1 = (f32[1040,128]{1,0:T(8,128)S(1)}, f32[1040,128]{1,0:T(8,128)S(1)}, u32[]{:S(2)}, u32[]{:S(2)}) collective-permute-start(f32[1040,128]{1,0:T(8,128)S(1)} %get-tuple-element.71), channel_id=1, source_target_pairs={{0,3},{1,2},{2,1},{3,0},{4,7},{5,6},{6,5},{7,4},{8,11},{9,10},{10,... | collective-permute-start | bytes 1597448 | tf_op jit(solution)/shard_map/ppermute | solution.py:160
  6.5 2.8 %keep_sums.1 = (f32[512,128]{1,0:T(8,128)}, f32[512,128]{1,0:T(8,128)}, f32[512,128]{1,0:T(8,128)S(1)}, f32[512,128]{1,0:T(8,128)S(1)}, f32[1024,128]{1,0:T(8,128)S(1)}) custom-call(s32[1]{0:T(128)S(6)} %copy.11.lost_ref, f32[4]{0:T(128)} %weight_ref.7, s32[1]{0:T(128)} %bitcast.member_ref, f32[4096,128]{1,0:T(8,128)} %table_ref.5), custom_call_target="tpu_custom_call" | custom-call | flops 3145728 | bytes 3145728 | tf_op jit(solution)/shard_map/keep_sums/pallas_call | solution.py:391
  9.3 2.3 %weigh_rows.1 = (f32[512,128]{1,0:T(8,128)S(1)}, f32[512,128]{1,0:T(8,128)S(1)}, f32[512,128]{1,0:T(8,128)S(1)}, f32[512,128]{1,0:T(8,128)S(1)}, f32[512,128]{1,...) custom-call(s32[1]{0:T(128)S(6)} %copy.11.lost_ref, f32[4]{0:T(128)} %weight_ref.7, s32[1]{0:T(128)} %bitcast.member_ref, ...), custom_call_target="tpu_custom_call" | custom-call | flops 4194304 | bytes 4194304 | tf_op jit(solution)/shard_map/weigh_rows/pallas_call | solution.py:400
  17.2 3.3 %collective-permute-done.1.b_ref = f32[1040,128]{1,0:T(8,128)S(1)} collective-permute-done((f32[1040,128]{1,0:T(8,128)S(1)}, f32[1040,128]{1,0:T(8,128)S(1)}, u32[]{:S(2)}, u32[]{:S(2)}) %collective-permute-start.1) | collective-permute-done | bytes 532512 | tf_op jit(solution)/shard_map/ppermute | solution.py:160
  20.6 2.3 %collective-permute-start.2 = (f32[776,128]{1,0:T(8,128)S(1)}, f32[776,128]{1,0:T(8,128)S(1)}, u32[]{:S(2)}, u32[]{:S(2)}) collective-permute-start(f32[776,128]{1,0:T(8,128)S(1)} %get-tuple-element.72), channel_id=1, source_target_pairs={{0,3},{1,2},{2,1},{3,0},{4,7},{5,6},{6,5},{7,4},{8,11},{9,10},{10,... | collective-permute-start | bytes 1191944 | tf_op jit(solution)/shard_map/ppermute | solution.py:160
  24.2 2.1 %collective-permute-done.5.kept_b_ref = f32[512,128]{1,0:T(8,128)} collective-permute-done((f32[512,128]{1,0:T(8,128)}, f32[512,128]{1,0:T(8,128)}, u32[]{:S(2)}, u32[]{:S(2)}) %collective-permute-start.5) | collective-permute-done | bytes 262176 | tf_op jit(solution)/shard_map/ppermute | solution.py:160
  26.3 2.1 %pending_totals.1 = (f32[1024,128]{1,0:T(8,128)S(1)}, f32[1024,128]{1,0:T(8,128)S(1)}) custom-call(s32[1]{0:T(128)} %bitcast.member_ref, f32[1040,128]{1,0:T(8,128)S(1)} %copy-done.1, f32[1040,128]{1,0:T(8,128)S(1)} %collective-permute-done.a_ref, f32[1040,128]{1,0:T(8,128)S(1)} %collective-permute-done.1.b_ref, f32[1024,128]{1,0:T(8,128)S(1)} %get-tuple-element.78.mine_ref, ...), custom_call_target="tpu_custom_call" | custom-call | flops 4194304 | bytes 4194304 | tf_op jit(solution)/shard_map/pending_totals/pallas_call | solution.py:418
  28.3 4.9 %collective-permute-done.2.c_ref = f32[776,128]{1,0:T(8,128)S(1)} collective-permute-done((f32[776,128]{1,0:T(8,128)S(1)}, f32[776,128]{1,0:T(8,128)S(1)}, u32[]{:S(2)}, u32[]{:S(2)}) %collective-permute-start.2) | collective-permute-done | bytes 397344 | tf_op jit(solution)/shard_map/ppermute | solution.py:160
  33.2 2.8 %place_sums.1 = (f32[2048,128]{1,0:T(8,128)}, f32[1024,128]{1,0:T(8,128)S(1)}, f32[1024,128]{1,0:T(8,128)S(1)}) custom-call(s32[1]{0:T(128)} %bitcast.member_ref, s32[1,1024]{1,0:T(1,128)S(1)} %bitcast_add_fusion.place_ref, f32[1024,128]{1,0:T(8,128)S(1)} %get-tuple-element.92.base_ref, f32[776,128]{1,0:T(8,128)S(1)} %collective-permute-done.2.c_ref, ...), custom_call_target="tpu_custom_call" | custom-call | flops 6291456 | bytes 6291456 | tf_op jit(solution)/shard_map/place_sums/pallas_call | solution.py:432
  36.0 11.2 %all-to-all-start.1 = ((f32[32,64,128]{2,1,0:T(8,128)}), f32[32,64,128]{2,1,0:T(8,128)S(1)}, u32[]{:S(2)}, u32[]{:S(2)}) async-start(f32[32,64,128]{2,1,0:T(8,128)} %bitcast.8), calls=%async_computation.1 | async-start | bytes 2097152 | tf_op jit(solution)/shard_map/all_to_all | solution.py:442
  47.3 2.3 %collective-permute-start.9 = (f32[512,128]{1,0:T(8,128)}, f32[512,128]{1,0:T(8,128)S(1)}, u32[]{:S(2)}, u32[]{:S(2)}) collective-permute-start(f32[512,128]{1,0:T(8,128)} %copy-done.5), channel_id=1, source_target_pairs={{0,3},{1,2},{2,1},{3,0},{4,7},{5,6},{6,5},{7,4},{8,11},{9,10},{10,... | collective-permute-start | bytes 786440 | tf_op jit(solution)/shard_map/ppermute | solution.py:160
  52.0 4.7 %collective-permute-done.8.a_ref = f32[512,128]{1,0:T(8,128)S(1)} collective-permute-done((f32[512,128]{1,0:T(8,128)}, f32[512,128]{1,0:T(8,128)S(1)}, u32[]{:S(2)}, u32[]{:S(2)}) %collective-permute-start.8) | collective-permute-done | bytes 262176 | tf_op jit(solution)/shard_map/ppermute | solution.py:160
  59.1 2.3 %collective-permute-start.10 = (f32[512,128]{1,0:T(8,128)S(1)}, f32[512,128]{1,0:T(8,128)S(1)}, u32[]{:S(2)}, u32[]{:S(2)}) collective-permute-start(f32[512,128]{1,0:T(8,128)S(1)} %get-tuple-element.90), channel_id=1, source_target_pairs={{0,3},{1,2},{2,1},{3,0},{4,7},{5,6},{6,5},{7,4},{8,11},{9,10},{10,... | collective-permute-start | bytes 786440 | tf_op jit(solution)/shard_map/ppermute | solution.py:160
  61.5 2.1 %collective-permute-done.7.b_ref = f32[512,128]{1,0:T(8,128)S(1)} collective-permute-done((f32[512,128]{1,0:T(8,128)S(1)}, f32[512,128]{1,0:T(8,128)S(1)}, u32[]{:S(2)}, u32[]{:S(2)}) %collective-permute-start.7) | collective-permute-done | bytes 262176 | tf_op jit(solution)/shard_map/ppermute | solution.py:160
  63.6 3.2 %collective-permute-done.10.c_ref = f32[512,128]{1,0:T(8,128)S(1)} collective-permute-done((f32[512,128]{1,0:T(8,128)S(1)}, f32[512,128]{1,0:T(8,128)S(1)}, u32[]{:S(2)}, u32[]{:S(2)}) %collective-permute-start.10) | collective-permute-done | bytes 262176 | tf_op jit(solution)/shard_map/ppermute | solution.py:160
  67.7 2.4 %place_rows.1 = f32[2048,128]{1,0:T(8,128)} custom-call(s32[1,1024]{1,0:T(1,128)S(1)} %bitcast_add_fusion.place_ref, f32[1024,128]{1,0:T(8,128)S(1)} %get-tuple-element.83.mine_ref, f32[512,128]{1,0:T(8,128)S(1)} %collective-permute-done.6.a_ref, f32[512,128]{1,0:T(8,128)S(1)} %collective-permute-done.7.b_ref, f32[512,128]{1,0:T(8,128)S(1)} %collective-permute-done.10.c_ref, ...), custom_call_target="tpu_custom_call" | custom-call | flops 6291456 | bytes 6291456 | tf_op jit(solution)/shard_map/place_rows/pallas_call | solution.py:446
  70.1 4.5 %all-to-all-done.1 = f32[32,64,128]{2,1,0:T(8,128)S(1)} async-done(((f32[32,64,128]{2,1,0:T(8,128)}), f32[32,64,128]{2,1,0:T(8,128)S(1)}, u32[]{:S(2)}, u32[]{:S(2)}) %all-to-all-start.1) | async-done | bytes 1048608 | tf_op jit(solution)/shard_map/all_to_all | solution.py:442
  74.6 5.7 %all-to-all-start = ((f32[64,32,128]{2,1,0:T(8,128)}), f32[64,32,128]{2,1,0:T(8,128)S(1)}, u32[]{:S(2)}, u32[]{:S(2)}) async-start(f32[64,32,128]{2,1,0:T(8,128)} %bitcast.5), calls=%async_computation | async-start | bytes 2097152 | tf_op jit(solution)/shard_map/all_to_all | solution.py:449
  84.2 3.4 %collective-permute-start.14 = (f32[512,128]{1,0:T(8,128)S(1)}, f32[512,128]{1,0:T(8,128)S(1)}, u32[]{:S(2)}, u32[]{:S(2)}) collective-permute-start(f32[512,128]{1,0:T(8,128)S(1)} %get-tuple-element.102), channel_id=1, source_target_pairs={{0,2},{1,3},{2,0},{3,1},{4,6},{5,7},{6,4},{7,5},{8,10},{9,11},{10,... | collective-permute-start | bytes 786440 | tf_op jit(solution)/shard_map/ppermute | solution.py:296
  88.2 6.0 %collective-permute-done.13.a_ref = f32[512,128]{1,0:T(8,128)S(1)} collective-permute-done((f32[512,128]{1,0:T(8,128)S(1)}, f32[512,128]{1,0:T(8,128)S(1)}, u32[]{:S(2)}, u32[]{:S(2)}) %collective-permute-start.13) | collective-permute-done | bytes 262176 | tf_op jit(solution)/shard_map/ppermute | solution.py:296
  94.2 5.3 %collective-permute-done.14.b_ref = f32[512,128]{1,0:T(8,128)S(1)} collective-permute-done((f32[512,128]{1,0:T(8,128)S(1)}, f32[512,128]{1,0:T(8,128)S(1)}, u32[]{:S(2)}, u32[]{:S(2)}) %collective-permute-start.14) | collective-permute-done | bytes 262176 | tf_op jit(solution)/shard_map/ppermute | solution.py:296
  100.6 7.6 %all-to-all-done = f32[64,32,128]{2,1,0:T(8,128)S(1)} async-done(((f32[64,32,128]{2,1,0:T(8,128)}), f32[64,32,128]{2,1,0:T(8,128)S(1)}, u32[]{:S(2)}, u32[]{:S(2)}) %all-to-all-start) | async-done | bytes 1048608 | tf_op jit(solution)/shard_map/all_to_all | solution.py:449
  115.9 2.8 %collective-permute-start.20 = (f32[256,128]{1,0:T(8,128)S(1)}, f32[256,128]{1,0:T(8,128)S(1)}, u32[]{:S(2)}, u32[]{:S(2)}) collective-permute-start(f32[256,128]{1,0:T(8,128)S(1)} %get-tuple-element.113), channel_id=1, source_target_pairs={{0,3},{1,2},{2,1},{3,0},{4,7},{5,6},{6,5},{7,4},{8,11},{9,10},{10,... | collective-permute-start | bytes 393224 | tf_op jit(solution)/shard_map/ppermute | solution.py:160
  119.9 2.3 %collective-permute-done.20.c_ref = f32[256,128]{1,0:T(8,128)S(1)} collective-permute-done((f32[256,128]{1,0:T(8,128)S(1)}, f32[256,128]{1,0:T(8,128)S(1)}, u32[]{:S(2)}, u32[]{:S(2)}) %collective-permute-start.20) | collective-permute-done | bytes 131104 | tf_op jit(solution)/shard_map/ppermute | solution.py:160
  (60 shorter events, 32.8 us)
Async XLA Ops:
  2.6 14.6 %collective-permute-start = (f32[1040,128]{1,0:T(8,128)S(1)}, f32[1040,128]{1,0:T(8,128)S(1)}, u32[]{:S(2)}, u32[]{:S(2)}) collective-permute-start(f32[1040,128]{1,0:T(8,128)S(1)} %get-tuple-element.70.own_ref), channel_id=1, source_target_pairs={{0,1},{1,0},{2,3},{3,2},{4,5},{5,4},{6,7},{7,6},{8,9},{9,8},{10,11... | collective-permute-start | bytes 1597448 | tf_op jit(solution)/shard_map/ppermute | solution.py:160
  4.3 16.2 %collective-permute-start.1 = (f32[1040,128]{1,0:T(8,128)S(1)}, f32[1040,128]{1,0:T(8,128)S(1)}, u32[]{:S(2)}, u32[]{:S(2)}) collective-permute-start(f32[1040,128]{1,0:T(8,128)S(1)} %get-tuple-element.71), channel_id=1, source_target_pairs={{0,3},{1,2},{2,1},{3,0},{4,7},{5,6},{6,5},{7,4},{8,11},{9,10},{10,... | collective-permute-start | bytes 1597448 | tf_op jit(solution)/shard_map/ppermute | solution.py:160
  13.7 10.5 %collective-permute-start.4 = (f32[512,128]{1,0:T(8,128)}, f32[512,128]{1,0:T(8,128)}, u32[]{:S(2)}, u32[]{:S(2)}) collective-permute-start(f32[512,128]{1,0:T(8,128)} %get-tuple-element.74), channel_id=1, source_target_pairs={{0,1},{1,0},{2,3},{3,2},{4,5},{5,4},{6,7},{7,6},{8,9},{9,8},{10,11... | collective-permute-start | bytes 786440 | tf_op jit(solution)/shard_map/ppermute | solution.py:160
  14.4 11.9 %collective-permute-start.5 = (f32[512,128]{1,0:T(8,128)}, f32[512,128]{1,0:T(8,128)}, u32[]{:S(2)}, u32[]{:S(2)}) collective-permute-start(f32[512,128]{1,0:T(8,128)} %get-tuple-element.75), channel_id=1, source_target_pairs={{0,3},{1,2},{2,1},{3,0},{4,7},{5,6},{6,5},{7,4},{8,11},{9,10},{10,... | collective-permute-start | bytes 786440 | tf_op jit(solution)/shard_map/ppermute | solution.py:160
  20.6 12.6 %collective-permute-start.2 = (f32[776,128]{1,0:T(8,128)S(1)}, f32[776,128]{1,0:T(8,128)S(1)}, u32[]{:S(2)}, u32[]{:S(2)}) collective-permute-start(f32[776,128]{1,0:T(8,128)S(1)} %get-tuple-element.72), channel_id=1, source_target_pairs={{0,3},{1,2},{2,1},{3,0},{4,7},{5,6},{6,5},{7,4},{8,11},{9,10},{10,... | collective-permute-start | bytes 1191944 | tf_op jit(solution)/shard_map/ppermute | solution.py:160
  22.9 10.3 %collective-permute-start.3 = (f32[776,128]{1,0:T(8,128)S(1)}, f32[776,128]{1,0:T(8,128)S(1)}, u32[]{:S(2)}, u32[]{:S(2)}) collective-permute-start(f32[776,128]{1,0:T(8,128)S(1)} %get-tuple-element.73), channel_id=1, source_target_pairs={{0,1},{1,0},{2,3},{3,2},{4,5},{5,4},{6,7},{7,6},{8,9},{9,8},{10,11... | collective-permute-start | bytes 1191944 | tf_op jit(solution)/shard_map/ppermute | solution.py:160
  36.0 38.6 %all-to-all-start.1 = ((f32[32,64,128]{2,1,0:T(8,128)}), f32[32,64,128]{2,1,0:T(8,128)S(1)}, u32[]{:S(2)}, u32[]{:S(2)}) async-start(f32[32,64,128]{2,1,0:T(8,128)} %bitcast.8), calls=%async_computation.1 | async-start | bytes 2097152 | tf_op jit(solution)/shard_map/all_to_all | solution.py:442
  47.2 9.4 %collective-permute-start.8 = (f32[512,128]{1,0:T(8,128)}, f32[512,128]{1,0:T(8,128)S(1)}, u32[]{:S(2)}, u32[]{:S(2)}) collective-permute-start(f32[512,128]{1,0:T(8,128)} %copy-done.6), channel_id=1, source_target_pairs={{0,1},{1,0},{2,3},{3,2},{4,5},{5,4},{6,7},{7,6},{8,9},{9,8},{10,11... | collective-permute-start | bytes 786440 | tf_op jit(solution)/shard_map/ppermute | solution.py:160
  47.3 10.8 %collective-permute-start.9 = (f32[512,128]{1,0:T(8,128)}, f32[512,128]{1,0:T(8,128)S(1)}, u32[]{:S(2)}, u32[]{:S(2)}) collective-permute-start(f32[512,128]{1,0:T(8,128)} %copy-done.5), channel_id=1, source_target_pairs={{0,3},{1,2},{2,1},{3,0},{4,7},{5,6},{6,5},{7,4},{8,11},{9,10},{10,... | collective-permute-start | bytes 786440 | tf_op jit(solution)/shard_map/ppermute | solution.py:160
  49.6 11.9 %collective-permute-start.6 = (f32[512,128]{1,0:T(8,128)S(1)}, f32[512,128]{1,0:T(8,128)S(1)}, u32[]{:S(2)}, u32[]{:S(2)}) collective-permute-start(f32[512,128]{1,0:T(8,128)S(1)} %get-tuple-element.84), channel_id=1, source_target_pairs={{0,1},{1,0},{2,3},{3,2},{4,5},{5,4},{6,7},{7,6},{8,9},{9,8},{10,11... | collective-permute-start | bytes 786440 | tf_op jit(solution)/shard_map/ppermute | solution.py:160
  50.9 12.6 %collective-permute-start.7 = (f32[512,128]{1,0:T(8,128)S(1)}, f32[512,128]{1,0:T(8,128)S(1)}, u32[]{:S(2)}, u32[]{:S(2)}) collective-permute-start(f32[512,128]{1,0:T(8,128)S(1)} %get-tuple-element.85), channel_id=1, source_target_pairs={{0,3},{1,2},{2,1},{3,0},{4,7},{5,6},{6,5},{7,4},{8,11},{9,10},{10,... | collective-permute-start | bytes 786440 | tf_op jit(solution)/shard_map/ppermute | solution.py:160
  59.1 7.7 %collective-permute-start.10 = (f32[512,128]{1,0:T(8,128)S(1)}, f32[512,128]{1,0:T(8,128)S(1)}, u32[]{:S(2)}, u32[]{:S(2)}) collective-permute-start(f32[512,128]{1,0:T(8,128)S(1)} %get-tuple-element.90), channel_id=1, source_target_pairs={{0,3},{1,2},{2,1},{3,0},{4,7},{5,6},{6,5},{7,4},{8,11},{9,10},{10,... | collective-permute-start | bytes 786440 | tf_op jit(solution)/shard_map/ppermute | solution.py:160
  61.4 6.4 %collective-permute-start.11 = (f32[512,128]{1,0:T(8,128)S(1)}, f32[512,128]{1,0:T(8,128)S(1)}, u32[]{:S(2)}, u32[]{:S(2)}) collective-permute-start(f32[512,128]{1,0:T(8,128)S(1)} %get-tuple-element.91), channel_id=1, source_target_pairs={{0,1},{1,0},{2,3},{3,2},{4,5},{5,4},{6,7},{7,6},{8,9},{9,8},{10,11... | collective-permute-start | bytes 786440 | tf_op jit(solution)/shard_map/ppermute | solution.py:160
  74.6 33.6 %all-to-all-start = ((f32[64,32,128]{2,1,0:T(8,128)}), f32[64,32,128]{2,1,0:T(8,128)S(1)}, u32[]{:S(2)}, u32[]{:S(2)}) async-start(f32[64,32,128]{2,1,0:T(8,128)} %bitcast.5), calls=%async_computation | async-start | bytes 2097152 | tf_op jit(solution)/shard_map/all_to_all | solution.py:449
  80.4 2.0 %collective-permute-start.12 = (f32[1024,128]{1,0:T(8,128)S(1)}, f32[1024,128]{1,0:T(8,128)S(1)}, u32[]{:S(2)}, u32[]{:S(2)}) collective-permute-start(f32[1024,128]{1,0:T(8,128)S(1)} %other_core_sums.1), channel_id=1, source_target_pairs={{0,4},{4,0},{8,12},{12,8},{16,20},{20,16},{24,28},{28,24},{32,36},... | collective-permute-start | bytes 1572872 | tf_op jit(solution)/shard_map/ppermute | solution.py:340
  84.0 10.1 %collective-permute-start.13 = (f32[512,128]{1,0:T(8,128)S(1)}, f32[512,128]{1,0:T(8,128)S(1)}, u32[]{:S(2)}, u32[]{:S(2)}) collective-permute-start(f32[512,128]{1,0:T(8,128)S(1)} %get-tuple-element.101), channel_id=1, source_target_pairs={{0,1},{1,2},{2,3},{3,0},{4,5},{5,6},{6,7},{7,4},{8,9},{9,10},{10,1... | collective-permute-start | bytes 786440 | tf_op jit(solution)/shard_map/ppermute | solution.py:296
  84.2 15.3 %collective-permute-start.14 = (f32[512,128]{1,0:T(8,128)S(1)}, f32[512,128]{1,0:T(8,128)S(1)}, u32[]{:S(2)}, u32[]{:S(2)}) collective-permute-start(f32[512,128]{1,0:T(8,128)S(1)} %get-tuple-element.102), channel_id=1, source_target_pairs={{0,2},{1,3},{2,0},{3,1},{4,6},{5,7},{6,4},{7,5},{8,10},{9,11},{10,... | collective-permute-start | bytes 786440 | tf_op jit(solution)/shard_map/ppermute | solution.py:296
  87.5 12.3 %collective-permute-start.15 = (f32[512,128]{1,0:T(8,128)S(1)}, f32[512,128]{1,0:T(8,128)S(1)}, u32[]{:S(2)}, u32[]{:S(2)}) collective-permute-start(f32[512,128]{1,0:T(8,128)S(1)} %get-tuple-element.103), channel_id=1, source_target_pairs={{0,3},{1,0},{2,1},{3,2},{4,7},{5,4},{6,5},{7,6},{8,11},{9,8},{10,9... | collective-permute-start | bytes 786440 | tf_op jit(solution)/shard_map/ppermute | solution.py:296
  108.8 6.4 %collective-permute-start.18 = (f32[256,128]{1,0:T(8,128)S(1)}, f32[256,128]{1,0:T(8,128)S(1)}, u32[]{:S(2)}, u32[]{:S(2)}) collective-permute-start(f32[256,128]{1,0:T(8,128)S(1)} %get-tuple-element.111), channel_id=1, source_target_pairs={{0,1},{1,0},{2,3},{3,2},{4,5},{5,4},{6,7},{7,6},{8,9},{9,8},{10,11... | collective-permute-start | bytes 393224 | tf_op jit(solution)/shard_map/ppermute | solution.py:160
  109.0 6.9 %collective-permute-start.19 = (f32[256,128]{1,0:T(8,128)S(1)}, f32[256,128]{1,0:T(8,128)S(1)}, u32[]{:S(2)}, u32[]{:S(2)}) collective-permute-start(f32[256,128]{1,0:T(8,128)S(1)} %get-tuple-element.112), channel_id=1, source_target_pairs={{0,3},{1,2},{2,1},{3,0},{4,7},{5,6},{6,5},{7,4},{8,11},{9,10},{10,... | collective-permute-start | bytes 393224 | tf_op jit(solution)/shard_map/ppermute | solution.py:160
  111.0 8.9 %collective-permute-start.16 = (f32[256,128]{1,0:T(8,128)S(1)}, f32[256,128]{1,0:T(8,128)S(1)}, u32[]{:S(2)}, u32[]{:S(2)}) collective-permute-start(f32[256,128]{1,0:T(8,128)S(1)} %get-tuple-element.107), channel_id=1, source_target_pairs={{0,1},{1,0},{2,3},{3,2},{4,5},{5,4},{6,7},{7,6},{8,9},{9,8},{10,11... | collective-permute-start | bytes 393224 | tf_op jit(solution)/shard_map/ppermute | solution.py:160
  112.4 7.6 %collective-permute-start.17 = (f32[256,128]{1,0:T(8,128)S(1)}, f32[256,128]{1,0:T(8,128)S(1)}, u32[]{:S(2)}, u32[]{:S(2)}) collective-permute-start(f32[256,128]{1,0:T(8,128)S(1)} %get-tuple-element.108), channel_id=1, source_target_pairs={{0,3},{1,2},{2,1},{3,0},{4,7},{5,6},{6,5},{7,4},{8,11},{9,10},{10,... | collective-permute-start | bytes 393224 | tf_op jit(solution)/shard_map/ppermute | solution.py:160
  115.9 6.3 %collective-permute-start.20 = (f32[256,128]{1,0:T(8,128)S(1)}, f32[256,128]{1,0:T(8,128)S(1)}, u32[]{:S(2)}, u32[]{:S(2)}) collective-permute-start(f32[256,128]{1,0:T(8,128)S(1)} %get-tuple-element.113), channel_id=1, source_target_pairs={{0,3},{1,2},{2,1},{3,0},{4,7},{5,6},{6,5},{7,4},{8,11},{9,10},{10,... | collective-permute-start | bytes 393224 | tf_op jit(solution)/shard_map/ppermute | solution.py:160
  118.7 5.0 %collective-permute-start.21 = (f32[256,128]{1,0:T(8,128)S(1)}, f32[256,128]{1,0:T(8,128)S(1)}, u32[]{:S(2)}, u32[]{:S(2)}) collective-permute-start(f32[256,128]{1,0:T(8,128)S(1)} %get-tuple-element.114), channel_id=1, source_target_pairs={{0,1},{1,0},{2,3},{3,2},{4,5},{5,4},{6,7},{7,6},{8,9},{9,8},{10,11... | collective-permute-start | bytes 393224 | tf_op jit(solution)/shard_map/ppermute | solution.py:160
  (9 other events, 34.8 us)

commit v7 on v6

--- a/solution.py
+++ b/solution.py
@@ -134,15 +134,19 @@
     scaled_pieces(table_ref, own, given_pieces(member) + kept_pieces(member), outs, buf_ref, sem_ref)
 
 
-def both_kernel(
-    lost_ref, weight_ref, member_ref, table_ref, a_ref, b_ref, give_a_ref, give_b_ref, c_ref, d_ref, mine_ref, buf_ref, sem_ref
-):
+def send_kernel(lost_ref, weight_ref, member_ref, table_ref, a_ref, b_ref, give_a_ref, give_b_ref, buf_ref, sem_ref):
+    member = member_ref[0]
+    own = lambda: own_row(decode_weights(lost_ref, weight_ref), member)
+    outs = [(ref, 0) for ref in (a_ref, b_ref, give_a_ref, give_b_ref)]
+    scaled_pieces(table_ref, own, passed_pieces(member) + given_pieces(member), outs, buf_ref, sem_ref)
+
+
+def stay_kernel(lost_ref, weight_ref, member_ref, table_ref, c_ref, d_ref, mine_ref, buf_ref, sem_ref):
     member = member_ref[0]
     own = lambda: own_row(decode_weights(lost_ref, weight_ref), member)
     half = buf_ref.shape[1]
-    outs = [(ref, 0) for ref in (a_ref, b_ref, give_a_ref, give_b_ref, c_ref, d_ref, mine_ref)] + [(mine_ref, half)]
-    where = passed_pieces(member) + given_pieces(member) + kept_pieces(member)
-    scaled_pieces(table_ref, own, where, outs, buf_ref, sem_ref)
+    outs = [(c_ref, 0), (d_ref, 0), (mine_ref, 0), (mine_ref, half)]
+    scaled_pieces(table_ref, own, kept_pieces(member), outs, buf_ref, sem_ref)
 
 
 def second_kernel(c_ref, d_ref, a_ref, b_ref, out_c_ref, out_d_ref):
@@ -397,14 +401,14 @@
         cost=3 << 20,
         scratch_shapes=buffers(6),
     )(*key, keep_out(adagrad_sums))
-    row_a, row_b, row_give_a, row_give_b, row_c, row_d, mine_rows = kernel_call(
-        both_kernel,
-        "weigh_rows",
-        (flat(half),) * 6 + (flat(share),),
+    row_a, row_b, row_give_a, row_give_b = kernel_call(
+        send_kernel,
+        "send_rows",
+        (flat(half),) * 4,
         scalars + [HBM],
-        (VMEM,) * 7,
-        cost=4 << 20,
-        scratch_shapes=buffers(8),
+        (VMEM,) * 4,
+        cost=2 << 20,
+        scratch_shapes=buffers(4),
     )(*key, keep_out(table_rows))
     give_a, give_b, row_a, row_b = lax.optimization_barrier((give_a, give_b, row_a, row_b))
     kept_a, kept_b = swap(give_a, 0, members), swap(give_b, 1, members)
@@ -418,8 +422,8 @@
     part_totals, base_sums = kernel_call(
         totals_kernel, "pending_totals", (flat(share), flat(share)), [SMEM] + [VMEM] * 6, (VMEM, VMEM), cost=4 << 20
     )(member, send_a, got_a, got_b, mine_sums, kept_a, kept_b)
-    row_a, row_b, row_give_a, row_give_b, got_c, got_d, part_totals, place = lax.optimization_barrier(
-        (row_a, row_b, row_give_a, row_give_b, got_c, got_d, part_totals, place)
+    row_a, row_b, row_give_a, row_give_b, got_c, got_d, part_totals, place, late_rows = lax.optimization_barrier(
+        (row_a, row_b, row_give_a, row_give_b, got_c, got_d, part_totals, place, table_rows)
     )
     back_a, back_b = swap(row_a, 0, members), swap(row_b, 1, members)
     stay_a, stay_b = swap(row_give_a, 0, members), swap(row_give_b, 1, members)
@@ -441,6 +445,15 @@
     same_core = [list(range(core, shards, 2)) for core in range(2)]
     got_sums = lax.all_to_all(out_sums, "shard", 0, 0, tiled=True, axis_index_groups=same_core)
 
+    row_c, row_d, mine_rows = kernel_call(
+        stay_kernel,
+        "stay_rows",
+        (flat(half), flat(half), flat(share)),
+        scalars + [HBM],
+        (VMEM,) * 3,
+        cost=2 << 20,
+        scratch_shapes=buffers(4),
+    )(*key, keep_out(late_rows))
     send_c, send_d = second("rows", 0, 1 << 33, row_c, row_d, back_a, back_b)
     back_c, back_d = swap(send_c, 1, members), swap(send_d, 0, members)
     out_rows = kernel_call(

time: 125 us -> 125 us (level)
  waiting for transfers between devices: 55.9 us -> 60.2 us
  starting transfers between devices: 43.5 us -> 40.4 us
  local copies, waits for them, and re-layouts: 3.07 us -> 0.02 us
  Pallas kernels: 18.7 us -> 20.3 us
    unnamed x18 -> x10, local copies, waits for them, and re-layouts: 3.07 us -> 0.02 us
    ppermute x18, starting transfers between devices: 22.2 us -> 20.1 us  [swap(): return lax.ppermute(array, 'code', pairs)]
    ppermute x18, waiting for transfers between devices: 30.3 us -> 32.5 us  [swap(): return lax.ppermute(array, 'code', pairs)]
    pallas_call x1 -> x2, Pallas kernels: 2.26 us -> 3.81 us  [the longest x1 1.91 us: per_device(): kernel_call(send_kernel, 'send_rows', (flat(half),) * 4, scalars + [HBM],...]
    all_to_all x1, waiting for transfers between devices: 4.51 us -> 6.02 us  [per_device(): lax.all_to_all(out_sums, 'shard', 0, 0, tiled=True, axis_index_groups=sam...]
  transfers between devices with their start and end apart: 24 -> 24, of which waited for: 19 -> 20; matrix products, arithmetic and copies ran while one was open for 1% -> 2% of each run, Pallas kernels for 11% -> 12%
where the time goes in v7:
time: 125 us; the launch traced here: 124 us
  waiting for transfers between devices  60.2 us (48%)
  starting transfers between devices  40.4 us (32%)
  Pallas kernels  20.3 us (16%)
  other arithmetic  1.87 us (1%)
  between operations  1.45 us (1%)
    ppermute x18, waiting for transfers between devices, swap(): return lax.ppermute(array, 'code', pairs)  32.5 us
    ppermute x18, starting transfers between devices, swap(): return lax.ppermute(array, 'code', pairs)  20.1 us
    ppermute x3, waiting for transfers between devices, turn(): lax.ppermute(array, 'code', [(i, (i + k) % members) for i in range(member...  12.4 us
    all_to_all x1, starting transfers between devices, per_device(): lax.all_to_all(out_sums, 'shard', 0, 0, tiled=True, axis_index_groups=sam...  11.2 us
    all_to_all x1, waiting for transfers between devices, per_device(): moved_rows = lax.all_to_all(out_rows, 'shard', 0, 0, tiled=True)  7.61 us
    all_to_all x1, waiting for transfers between devices, per_device(): lax.all_to_all(out_sums, 'shard', 0, 0, tiled=True, axis_index_groups=sam...  6.02 us
    all_to_all x1, starting transfers between devices, per_device(): moved_rows = lax.all_to_all(out_rows, 'shard', 0, 0, tiled=True)  5.53 us
    ppermute x3, starting transfers between devices, turn(): lax.ppermute(array, 'code', [(i, (i + k) % members) for i in range(member...  3.41 us
  transfers between devices with their start and end apart: 24, of which 20 were waited for; matrix products, arithmetic and copies ran while one was open for 2% of the time, Pallas kernels for 12%

profile of v7, /device:TPU:32, one launch (start us, length us, event | category | flops | bytes accessed | tf_op | source)
XLA Modules:
  0.0 124.3 jit_solution(5101725346111968435)
XLA Ops:
  2.6 3.1 %collective-permute-start.1 = (f32[1040,128]{1,0:T(8,128)S(1)}, f32[1040,128]{1,0:T(8,128)S(1)}, u32[]{:S(2)}, u32[]{:S(2)}) collective-permute-start(f32[1040,128]{1,0:T(8,128)S(1)} %get-tuple-element.72), channel_id=1, source_target_pairs={{0,3},{1,2},{2,1},{3,0},{4,7},{5,6},{6,5},{7,4},{8,11},{9,10},{10,... | collective-permute-start | bytes 1597448 | tf_op jit(solution)/shard_map/ppermute | solution.py:164
  5.9 1.9 %send_rows.1 = (f32[512,128]{1,0:T(8,128)S(1)}, f32[512,128]{1,0:T(8,128)S(1)}, f32[512,128]{1,0:T(8,128)S(1)}, f32[512,128]{1,0:T(8,128)S(1)}) custom-call(s32[1]{0:T(128)S(6)} %copy.11.lost_ref, f32[4]{0:T(128)} %weight_ref.9, s32[1]{0:T(128)} %bitcast.member_ref, f32[4096,128]{1,0:T(8,128)} %table_ref.6), custom_call_target="tpu_custom_call" | custom-call | flops 2097152 | bytes 2097152 | tf_op jit(solution)/shard_map/send_rows/pallas_call | solution.py:404
  7.8 2.9 %keep_sums.1 = (f32[512,128]{1,0:T(8,128)}, f32[512,128]{1,0:T(8,128)}, f32[512,128]{1,0:T(8,128)S(1)}, f32[512,128]{1,0:T(8,128)S(1)}, f32[1024,128]{1,0:T(8,128)S(1)}) custom-call(s32[1]{0:T(128)S(6)} %copy.11.lost_ref, f32[4]{0:T(128)} %weight_ref.9, s32[1]{0:T(128)} %bitcast.member_ref, f32[4096,128]{1,0:T(8,128)} %table_ref.5), custom_call_target="tpu_custom_call" | custom-call | flops 3145728 | bytes 3145728 | tf_op jit(solution)/shard_map/keep_sums/pallas_call | solution.py:395
  10.7 2.0 %collective-permute-start.4 = (f32[512,128]{1,0:T(8,128)}, f32[512,128]{1,0:T(8,128)}, u32[]{:S(2)}, u32[]{:S(2)}) collective-permute-start(f32[512,128]{1,0:T(8,128)} %get-tuple-element.75), channel_id=1, source_target_pairs={{0,1},{1,0},{2,3},{3,2},{4,5},{5,4},{6,7},{7,6},{8,9},{9,8},{10,11... | collective-permute-start | bytes 786440 | tf_op jit(solution)/shard_map/ppermute | solution.py:164
  13.4 5.5 %collective-permute-done.1.b_ref = f32[1040,128]{1,0:T(8,128)S(1)} collective-permute-done((f32[1040,128]{1,0:T(8,128)S(1)}, f32[1040,128]{1,0:T(8,128)S(1)}, u32[]{:S(2)}, u32[]{:S(2)}) %collective-permute-start.1) | collective-permute-done | bytes 532512 | tf_op jit(solution)/shard_map/ppermute | solution.py:164
  18.9 1.8 %collective-permute-done.a_ref = f32[1040,128]{1,0:T(8,128)S(1)} collective-permute-done((f32[1040,128]{1,0:T(8,128)S(1)}, f32[1040,128]{1,0:T(8,128)S(1)}, u32[]{:S(2)}, u32[]{:S(2)}) %collective-permute-start) | collective-permute-done | bytes 532512 | tf_op jit(solution)/shard_map/ppermute | solution.py:164
  23.4 3.1 %collective-permute-done.4.kept_a_ref = f32[512,128]{1,0:T(8,128)} collective-permute-done((f32[512,128]{1,0:T(8,128)}, f32[512,128]{1,0:T(8,128)}, u32[]{:S(2)}, u32[]{:S(2)}) %collective-permute-start.4) | collective-permute-done | bytes 262176 | tf_op jit(solution)/shard_map/ppermute | solution.py:164
  26.5 2.1 %pending_totals.1 = (f32[1024,128]{1,0:T(8,128)S(1)}, f32[1024,128]{1,0:T(8,128)S(1)}) custom-call(s32[1]{0:T(128)} %bitcast.member_ref, f32[1040,128]{1,0:T(8,128)S(1)} %copy-done.1, f32[1040,128]{1,0:T(8,128)S(1)} %collective-permute-done.a_ref, f32[1040,128]{1,0:T(8,128)S(1)} %collective-permute-done.1.b_ref, f32[1024,128]{1,0:T(8,128)S(1)} %get-tuple-element.79.mine_ref, ...), custom_call_target="tpu_custom_call" | custom-call | flops 4194304 | bytes 4194304 | tf_op jit(solution)/shard_map/pending_totals/pallas_call | solution.py:422
  28.6 3.4 %collective-permute-done.2.c_ref = f32[776,128]{1,0:T(8,128)S(1)} collective-permute-done((f32[776,128]{1,0:T(8,128)S(1)}, f32[776,128]{1,0:T(8,128)S(1)}, u32[]{:S(2)}, u32[]{:S(2)}) %collective-permute-start.2) | collective-permute-done | bytes 397344 | tf_op jit(solution)/shard_map/ppermute | solution.py:164
  33.4 2.8 %place_sums.1 = (f32[2048,128]{1,0:T(8,128)}, f32[1024,128]{1,0:T(8,128)S(1)}, f32[1024,128]{1,0:T(8,128)S(1)}) custom-call(s32[1]{0:T(128)} %bitcast.member_ref, s32[1,1024]{1,0:T(1,128)S(1)} %bitcast_add_fusion.place_ref, f32[1024,128]{1,0:T(8,128)S(1)} %get-tuple-element.94.base_ref, f32[776,128]{1,0:T(8,128)S(1)} %collective-permute-done.2.c_ref, ...), custom_call_target="tpu_custom_call" | custom-call | flops 6291456 | bytes 6291456 | tf_op jit(solution)/shard_map/place_sums/pallas_call | solution.py:436
  36.2 11.2 %all-to-all-start.1 = ((f32[32,64,128]{2,1,0:T(8,128)}), f32[32,64,128]{2,1,0:T(8,128)S(1)}, u32[]{:S(2)}, u32[]{:S(2)}) async-start(f32[32,64,128]{2,1,0:T(8,128)} %bitcast.8), calls=%async_computation.1 | async-start | bytes 2097152 | tf_op jit(solution)/shard_map/all_to_all | solution.py:446
  52.2 1.9 %stay_rows.1 = (f32[512,128]{1,0:T(8,128)S(1)}, f32[512,128]{1,0:T(8,128)S(1)}, f32[1024,128]{1,0:T(8,128)S(1)}) custom-call(s32[1]{0:T(128)S(6)} %copy.11.lost_ref, f32[4]{0:T(128)} %weight_ref.9, s32[1]{0:T(128)} %bitcast.member_ref, f32[4096,128]{1,0:T(8,128)} %table_ref.6), custom_call_target="tpu_custom_call" | custom-call | flops 2097152 | bytes 2097152 | tf_op jit(solution)/shard_map/stay_rows/pallas_call | solution.py:448
  54.1 2.5 %collective-permute-done.8.a_ref = f32[512,128]{1,0:T(8,128)S(1)} collective-permute-done((f32[512,128]{1,0:T(8,128)S(1)}, f32[512,128]{1,0:T(8,128)S(1)}, u32[]{:S(2)}, u32[]{:S(2)}) %collective-permute-start.8) | collective-permute-done | bytes 262176 | tf_op jit(solution)/shard_map/ppermute | solution.py:164
  59.8 2.1 %collective-permute-done.6.a_ref = f32[512,128]{1,0:T(8,128)S(1)} collective-permute-done((f32[512,128]{1,0:T(8,128)S(1)}, f32[512,128]{1,0:T(8,128)S(1)}, u32[]{:S(2)}, u32[]{:S(2)}) %collective-permute-start.6) | collective-permute-done | bytes 262176 | tf_op jit(solution)/shard_map/ppermute | solution.py:164
  63.6 2.8 %collective-permute-done.10.c_ref = f32[512,128]{1,0:T(8,128)S(1)} collective-permute-done((f32[512,128]{1,0:T(8,128)S(1)}, f32[512,128]{1,0:T(8,128)S(1)}, u32[]{:S(2)}, u32[]{:S(2)}) %collective-permute-start.10) | collective-permute-done | bytes 262176 | tf_op jit(solution)/shard_map/ppermute | solution.py:164
  66.4 2.4 %place_rows.1 = f32[2048,128]{1,0:T(8,128)} custom-call(s32[1,1024]{1,0:T(1,128)S(1)} %bitcast_add_fusion.place_ref, f32[1024,128]{1,0:T(8,128)S(1)} %get-tuple-element.85.mine_ref, f32[512,128]{1,0:T(8,128)S(1)} %collective-permute-done.6.a_ref, f32[512,128]{1,0:T(8,128)S(1)} %collective-permute-done.7.b_ref, f32[512,128]{1,0:T(8,128)S(1)} %collective-permute-done.10.c_ref, ...), custom_call_target="tpu_custom_call" | custom-call | flops 6291456 | bytes 6291456 | tf_op jit(solution)/shard_map/place_rows/pallas_call | solution.py:459
  68.8 6.0 %all-to-all-done.1 = f32[32,64,128]{2,1,0:T(8,128)S(1)} async-done(((f32[32,64,128]{2,1,0:T(8,128)}), f32[32,64,128]{2,1,0:T(8,128)S(1)}, u32[]{:S(2)}, u32[]{:S(2)}) %all-to-all-start.1) | async-done | bytes 1048608 | tf_op jit(solution)/shard_map/all_to_all | solution.py:446
  74.9 5.5 %all-to-all-start = ((f32[64,32,128]{2,1,0:T(8,128)}), f32[64,32,128]{2,1,0:T(8,128)S(1)}, u32[]{:S(2)}, u32[]{:S(2)}) async-start(f32[64,32,128]{2,1,0:T(8,128)} %bitcast.5), calls=%async_computation | async-start | bytes 2097152 | tf_op jit(solution)/shard_map/all_to_all | solution.py:462
  84.5 2.8 %collective-permute-start.14 = (f32[512,128]{1,0:T(8,128)S(1)}, f32[512,128]{1,0:T(8,128)S(1)}, u32[]{:S(2)}, u32[]{:S(2)}) collective-permute-start(f32[512,128]{1,0:T(8,128)S(1)} %get-tuple-element.104), channel_id=1, source_target_pairs={{0,2},{1,3},{2,0},{3,1},{4,6},{5,7},{6,4},{7,5},{8,10},{9,11},{10,... | collective-permute-start | bytes 786440 | tf_op jit(solution)/shard_map/ppermute | solution.py:300
  87.5 6.9 %collective-permute-done.13.a_ref = f32[512,128]{1,0:T(8,128)S(1)} collective-permute-done((f32[512,128]{1,0:T(8,128)S(1)}, f32[512,128]{1,0:T(8,128)S(1)}, u32[]{:S(2)}, u32[]{:S(2)}) %collective-permute-start.13) | collective-permute-done | bytes 262176 | tf_op jit(solution)/shard_map/ppermute | solution.py:300
  94.4 4.9 %collective-permute-done.14.b_ref = f32[512,128]{1,0:T(8,128)S(1)} collective-permute-done((f32[512,128]{1,0:T(8,128)S(1)}, f32[512,128]{1,0:T(8,128)S(1)}, u32[]{:S(2)}, u32[]{:S(2)}) %collective-permute-start.14) | collective-permute-done | bytes 262176 | tf_op jit(solution)/shard_map/ppermute | solution.py:300
  100.7 7.6 %all-to-all-done = f32[64,32,128]{2,1,0:T(8,128)S(1)} async-done(((f32[64,32,128]{2,1,0:T(8,128)}), f32[64,32,128]{2,1,0:T(8,128)S(1)}, u32[]{:S(2)}, u32[]{:S(2)}) %all-to-all-start) | async-done | bytes 1048608 | tf_op jit(solution)/shard_map/all_to_all | solution.py:462
  116.4 2.2 %collective-permute-start.20 = (f32[256,128]{1,0:T(8,128)S(1)}, f32[256,128]{1,0:T(8,128)S(1)}, u32[]{:S(2)}, u32[]{:S(2)}) collective-permute-start(f32[256,128]{1,0:T(8,128)S(1)} %get-tuple-element.115), channel_id=1, source_target_pairs={{0,3},{1,2},{2,1},{3,0},{4,7},{5,6},{6,5},{7,4},{8,11},{9,10},{10,... | collective-permute-start | bytes 393224 | tf_op jit(solution)/shard_map/ppermute | solution.py:164
  119.8 2.9 %collective-permute-done.20.c_ref = f32[256,128]{1,0:T(8,128)S(1)} collective-permute-done((f32[256,128]{1,0:T(8,128)S(1)}, f32[256,128]{1,0:T(8,128)S(1)}, u32[]{:S(2)}, u32[]{:S(2)}) %collective-permute-start.20) | collective-permute-done | bytes 131104 | tf_op jit(solution)/shard_map/ppermute | solution.py:164
  (53 shorter events, 32.6 us)
Async XLA Ops:
  2.6 16.3 %collective-permute-start.1 = (f32[1040,128]{1,0:T(8,128)S(1)}, f32[1040,128]{1,0:T(8,128)S(1)}, u32[]{:S(2)}, u32[]{:S(2)}) collective-permute-start(f32[1040,128]{1,0:T(8,128)S(1)} %get-tuple-element.72), channel_id=1, source_target_pairs={{0,3},{1,2},{2,1},{3,0},{4,7},{5,6},{6,5},{7,4},{8,11},{9,10},{10,... | collective-permute-start | bytes 1597448 | tf_op jit(solution)/shard_map/ppermute | solution.py:164
  5.7 15.0 %collective-permute-start = (f32[1040,128]{1,0:T(8,128)S(1)}, f32[1040,128]{1,0:T(8,128)S(1)}, u32[]{:S(2)}, u32[]{:S(2)}) collective-permute-start(f32[1040,128]{1,0:T(8,128)S(1)} %get-tuple-element.71.own_ref), channel_id=1, source_target_pairs={{0,1},{1,0},{2,3},{3,2},{4,5},{5,4},{6,7},{7,6},{8,9},{9,8},{10,11... | collective-permute-start | bytes 1597448 | tf_op jit(solution)/shard_map/ppermute | solution.py:164
  10.7 15.8 %collective-permute-start.4 = (f32[512,128]{1,0:T(8,128)}, f32[512,128]{1,0:T(8,128)}, u32[]{:S(2)}, u32[]{:S(2)}) collective-permute-start(f32[512,128]{1,0:T(8,128)} %get-tuple-element.75), channel_id=1, source_target_pairs={{0,1},{1,0},{2,3},{3,2},{4,5},{5,4},{6,7},{7,6},{8,9},{9,8},{10,11... | collective-permute-start | bytes 786440 | tf_op jit(solution)/shard_map/ppermute | solution.py:164
  12.6 13.8 %collective-permute-start.5 = (f32[512,128]{1,0:T(8,128)}, f32[512,128]{1,0:T(8,128)}, u32[]{:S(2)}, u32[]{:S(2)}) collective-permute-start(f32[512,128]{1,0:T(8,128)} %get-tuple-element.76), channel_id=1, source_target_pairs={{0,3},{1,2},{2,1},{3,0},{4,7},{5,6},{6,5},{7,4},{8,11},{9,10},{10,... | collective-permute-start | bytes 786440 | tf_op jit(solution)/shard_map/ppermute | solution.py:164
  20.8 11.1 %collective-permute-start.2 = (f32[776,128]{1,0:T(8,128)S(1)}, f32[776,128]{1,0:T(8,128)S(1)}, u32[]{:S(2)}, u32[]{:S(2)}) collective-permute-start(f32[776,128]{1,0:T(8,128)S(1)} %get-tuple-element.73), channel_id=1, source_target_pairs={{0,3},{1,2},{2,1},{3,0},{4,7},{5,6},{6,5},{7,4},{8,11},{9,10},{10,... | collective-permute-start | bytes 1191944 | tf_op jit(solution)/shard_map/ppermute | solution.py:164
  22.1 11.3 %collective-permute-start.3 = (f32[776,128]{1,0:T(8,128)S(1)}, f32[776,128]{1,0:T(8,128)S(1)}, u32[]{:S(2)}, u32[]{:S(2)}) collective-permute-start(f32[776,128]{1,0:T(8,128)S(1)} %get-tuple-element.74), channel_id=1, source_target_pairs={{0,1},{1,0},{2,3},{3,2},{4,5},{5,4},{6,7},{7,6},{8,9},{9,8},{10,11... | collective-permute-start | bytes 1191944 | tf_op jit(solution)/shard_map/ppermute | solution.py:164
  36.2 38.6 %all-to-all-start.1 = ((f32[32,64,128]{2,1,0:T(8,128)}), f32[32,64,128]{2,1,0:T(8,128)S(1)}, u32[]{:S(2)}, u32[]{:S(2)}) async-start(f32[32,64,128]{2,1,0:T(8,128)} %bitcast.8), calls=%async_computation.1 | async-start | bytes 2097152 | tf_op jit(solution)/shard_map/all_to_all | solution.py:446
  47.5 9.2 %collective-permute-start.8 = (f32[512,128]{1,0:T(8,128)S(1)}, f32[512,128]{1,0:T(8,128)S(1)}, u32[]{:S(2)}, u32[]{:S(2)}) collective-permute-start(f32[512,128]{1,0:T(8,128)S(1)} %get-tuple-element.90), channel_id=1, source_target_pairs={{0,1},{1,0},{2,3},{3,2},{4,5},{5,4},{6,7},{7,6},{8,9},{9,8},{10,11... | collective-permute-start | bytes 786440 | tf_op jit(solution)/shard_map/ppermute | solution.py:164
  47.8 10.5 %collective-permute-start.9 = (f32[512,128]{1,0:T(8,128)S(1)}, f32[512,128]{1,0:T(8,128)S(1)}, u32[]{:S(2)}, u32[]{:S(2)}) collective-permute-start(f32[512,128]{1,0:T(8,128)S(1)} %get-tuple-element.91), channel_id=1, source_target_pairs={{0,3},{1,2},{2,1},{3,0},{4,7},{5,6},{6,5},{7,4},{8,11},{9,10},{10,... | collective-permute-start | bytes 786440 | tf_op jit(solution)/shard_map/ppermute | solution.py:164
  49.1 12.8 %collective-permute-start.6 = (f32[512,128]{1,0:T(8,128)S(1)}, f32[512,128]{1,0:T(8,128)S(1)}, u32[]{:S(2)}, u32[]{:S(2)}) collective-permute-start(f32[512,128]{1,0:T(8,128)S(1)} %get-tuple-element.86), channel_id=1, source_target_pairs={{0,1},{1,0},{2,3},{3,2},{4,5},{5,4},{6,7},{7,6},{8,9},{9,8},{10,11... | collective-permute-start | bytes 786440 | tf_op jit(solution)/shard_map/ppermute | solution.py:164
  50.5 13.2 %collective-permute-start.7 = (f32[512,128]{1,0:T(8,128)S(1)}, f32[512,128]{1,0:T(8,128)S(1)}, u32[]{:S(2)}, u32[]{:S(2)}) collective-permute-start(f32[512,128]{1,0:T(8,128)S(1)} %get-tuple-element.87), channel_id=1, source_target_pairs={{0,3},{1,2},{2,1},{3,0},{4,7},{5,6},{6,5},{7,4},{8,11},{9,10},{10,... | collective-permute-start | bytes 786440 | tf_op jit(solution)/shard_map/ppermute | solution.py:164
  58.3 8.1 %collective-permute-start.10 = (f32[512,128]{1,0:T(8,128)S(1)}, f32[512,128]{1,0:T(8,128)S(1)}, u32[]{:S(2)}, u32[]{:S(2)}) collective-permute-start(f32[512,128]{1,0:T(8,128)S(1)} %get-tuple-element.92), channel_id=1, source_target_pairs={{0,3},{1,2},{2,1},{3,0},{4,7},{5,6},{6,5},{7,4},{8,11},{9,10},{10,... | collective-permute-start | bytes 786440 | tf_op jit(solution)/shard_map/ppermute | solution.py:164
  59.7 6.7 %collective-permute-start.11 = (f32[512,128]{1,0:T(8,128)S(1)}, f32[512,128]{1,0:T(8,128)S(1)}, u32[]{:S(2)}, u32[]{:S(2)}) collective-permute-start(f32[512,128]{1,0:T(8,128)S(1)} %get-tuple-element.93), channel_id=1, source_target_pairs={{0,1},{1,0},{2,3},{3,2},{4,5},{5,4},{6,7},{7,6},{8,9},{9,8},{10,11... | collective-permute-start | bytes 786440 | tf_op jit(solution)/shard_map/ppermute | solution.py:164
  74.9 33.4 %all-to-all-start = ((f32[64,32,128]{2,1,0:T(8,128)}), f32[64,32,128]{2,1,0:T(8,128)S(1)}, u32[]{:S(2)}, u32[]{:S(2)}) async-start(f32[64,32,128]{2,1,0:T(8,128)} %bitcast.5), calls=%async_computation | async-start | bytes 2097152 | tf_op jit(solution)/shard_map/all_to_all | solution.py:462
  80.4 2.0 %collective-permute-start.12 = (f32[1024,128]{1,0:T(8,128)S(1)}, f32[1024,128]{1,0:T(8,128)S(1)}, u32[]{:S(2)}, u32[]{:S(2)}) collective-permute-start(f32[1024,128]{1,0:T(8,128)S(1)} %other_core_sums.1), channel_id=1, source_target_pairs={{0,4},{4,0},{8,12},{12,8},{16,20},{20,16},{24,28},{28,24},{32,36},... | collective-permute-start | bytes 1572872 | tf_op jit(solution)/shard_map/ppermute | solution.py:344
  84.1 10.3 %collective-permute-start.13 = (f32[512,128]{1,0:T(8,128)S(1)}, f32[512,128]{1,0:T(8,128)S(1)}, u32[]{:S(2)}, u32[]{:S(2)}) collective-permute-start(f32[512,128]{1,0:T(8,128)S(1)} %get-tuple-element.103), channel_id=1, source_target_pairs={{0,1},{1,2},{2,3},{3,0},{4,5},{5,6},{6,7},{7,4},{8,9},{9,10},{10,1... | collective-permute-start | bytes 786440 | tf_op jit(solution)/shard_map/ppermute | solution.py:300
  84.5 14.8 %collective-permute-start.14 = (f32[512,128]{1,0:T(8,128)S(1)}, f32[512,128]{1,0:T(8,128)S(1)}, u32[]{:S(2)}, u32[]{:S(2)}) collective-permute-start(f32[512,128]{1,0:T(8,128)S(1)} %get-tuple-element.104), channel_id=1, source_target_pairs={{0,2},{1,3},{2,0},{3,1},{4,6},{5,7},{6,4},{7,5},{8,10},{9,11},{10,... | collective-permute-start | bytes 786440 | tf_op jit(solution)/shard_map/ppermute | solution.py:300
  87.4 12.5 %collective-permute-start.15 = (f32[512,128]{1,0:T(8,128)S(1)}, f32[512,128]{1,0:T(8,128)S(1)}, u32[]{:S(2)}, u32[]{:S(2)}) collective-permute-start(f32[512,128]{1,0:T(8,128)S(1)} %get-tuple-element.105), channel_id=1, source_target_pairs={{0,3},{1,0},{2,1},{3,2},{4,7},{5,4},{6,5},{7,6},{8,11},{9,8},{10,9... | collective-permute-start | bytes 786440 | tf_op jit(solution)/shard_map/ppermute | solution.py:300
  108.9 6.4 %collective-permute-start.18 = (f32[256,128]{1,0:T(8,128)S(1)}, f32[256,128]{1,0:T(8,128)S(1)}, u32[]{:S(2)}, u32[]{:S(2)}) collective-permute-start(f32[256,128]{1,0:T(8,128)S(1)} %get-tuple-element.113), channel_id=1, source_target_pairs={{0,1},{1,0},{2,3},{3,2},{4,5},{5,4},{6,7},{7,6},{8,9},{9,8},{10,11... | collective-permute-start | bytes 393224 | tf_op jit(solution)/shard_map/ppermute | solution.py:164
  109.4 6.9 %collective-permute-start.19 = (f32[256,128]{1,0:T(8,128)S(1)}, f32[256,128]{1,0:T(8,128)S(1)}, u32[]{:S(2)}, u32[]{:S(2)}) collective-permute-start(f32[256,128]{1,0:T(8,128)S(1)} %get-tuple-element.114), channel_id=1, source_target_pairs={{0,3},{1,2},{2,1},{3,0},{4,7},{5,6},{6,5},{7,4},{8,11},{9,10},{10,... | collective-permute-start | bytes 393224 | tf_op jit(solution)/shard_map/ppermute | solution.py:164
  110.9 8.9 %collective-permute-start.16 = (f32[256,128]{1,0:T(8,128)S(1)}, f32[256,128]{1,0:T(8,128)S(1)}, u32[]{:S(2)}, u32[]{:S(2)}) collective-permute-start(f32[256,128]{1,0:T(8,128)S(1)} %get-tuple-element.109), channel_id=1, source_target_pairs={{0,1},{1,0},{2,3},{3,2},{4,5},{5,4},{6,7},{7,6},{8,9},{9,8},{10,11... | collective-permute-start | bytes 393224 | tf_op jit(solution)/shard_map/ppermute | solution.py:164
  112.2 7.6 %collective-permute-start.17 = (f32[256,128]{1,0:T(8,128)S(1)}, f32[256,128]{1,0:T(8,128)S(1)}, u32[]{:S(2)}, u32[]{:S(2)}) collective-permute-start(f32[256,128]{1,0:T(8,128)S(1)} %get-tuple-element.110), channel_id=1, source_target_pairs={{0,3},{1,2},{2,1},{3,0},{4,7},{5,6},{6,5},{7,4},{8,11},{9,10},{10,... | collective-permute-start | bytes 393224 | tf_op jit(solution)/shard_map/ppermute | solution.py:164
  116.4 6.3 %collective-permute-start.20 = (f32[256,128]{1,0:T(8,128)S(1)}, f32[256,128]{1,0:T(8,128)S(1)}, u32[]{:S(2)}, u32[]{:S(2)}) collective-permute-start(f32[256,128]{1,0:T(8,128)S(1)} %get-tuple-element.115), channel_id=1, source_target_pairs={{0,3},{1,2},{2,1},{3,0},{4,7},{5,6},{6,5},{7,4},{8,11},{9,10},{10,... | collective-permute-start | bytes 393224 | tf_op jit(solution)/shard_map/ppermute | solution.py:164
  118.6 5.0 %collective-permute-start.21 = (f32[256,128]{1,0:T(8,128)S(1)}, f32[256,128]{1,0:T(8,128)S(1)}, u32[]{:S(2)}, u32[]{:S(2)}) collective-permute-start(f32[256,128]{1,0:T(8,128)S(1)} %get-tuple-element.116), channel_id=1, source_target_pairs={{0,1},{1,0},{2,3},{3,2},{4,5},{5,4},{6,7},{7,6},{8,9},{9,8},{10,11... | collective-permute-start | bytes 393224 | tf_op jit(solution)/shard_map/ppermute | solution.py:164
  (5 other events, 30.1 us)

commit v8 on v7

--- a/solution.py
+++ b/solution.py
@@ -8,6 +8,7 @@
 step_size = 0.5
 epsilon = 1e-08
 MEMBERS = 4
+TOP = float(jnp.finfo(jnp.bfloat16).max)
 SLOT = 32
 SMEM = pl.BlockSpec(memory_space=pltpu.SMEM)
 VMEM = pl.BlockSpec(memory_space=pltpu.VMEM)
@@ -30,7 +31,7 @@
 
 
 def split_halves(value):
-    high = value.astype(jnp.bfloat16)
+    high = jnp.clip(value, -TOP, TOP).astype(jnp.bfloat16)
     low = (value - high.astype(jnp.float32)).astype(jnp.bfloat16)
     return high, low
 
@@ -431,7 +432,7 @@
     scratch = [
         pltpu.VMEM((share, 256), jnp.bfloat16),
         pltpu.VMEM((slots, 128), jnp.float32),
-        pltpu.SemaphoreType.DMA((8,)),
+        pltpu.SemaphoreType.DMA((4,)),
     ]
     out_sums, new_sums, totals = kernel_call(
         sums_kernel,

time: 125 us -> 125 us (level)
  no operation moved by 1% of the time
where the time goes in v8:
time: 125 us; the launch traced here: 124 us
  waiting for transfers between devices  60.3 us (48%)
  starting transfers between devices  40.6 us (32%)
  Pallas kernels  19.8 us (16%)
  other arithmetic  1.87 us (1%)
  between operations  1.45 us (1%)
    ppermute x18, waiting for transfers between devices, swap(): return lax.ppermute(array, 'code', pairs)  32.5 us
    ppermute x18, starting transfers between devices, swap(): return lax.ppermute(array, 'code', pairs)  20 us
    ppermute x3, waiting for transfers between devices, turn(): lax.ppermute(array, 'code', [(i, (i + k) % members) for i in range(member...  12.4 us
    all_to_all x1, starting transfers between devices, per_device(): lax.all_to_all(out_sums, 'shard', 0, 0, tiled=True, axis_index_groups=sam...  11.2 us
    all_to_all x1, waiting for transfers between devices, per_device(): moved_rows = lax.all_to_all(out_rows, 'shard', 0, 0, tiled=True)  7.61 us
    all_to_all x1, waiting for transfers between devices, per_device(): lax.all_to_all(out_sums, 'shard', 0, 0, tiled=True, axis_index_groups=sam...  6.1 us
    all_to_all x1, starting transfers between devices, per_device(): moved_rows = lax.all_to_all(out_rows, 'shard', 0, 0, tiled=True)  5.71 us
    ppermute x3, starting transfers between devices, turn(): lax.ppermute(array, 'code', [(i, (i + k) % members) for i in range(member...  3.41 us
  transfers between devices with their start and end apart: 24, of which 20 were waited for; matrix products, arithmetic and copies ran while one was open for 2% of the time, Pallas kernels for 12%

profile of v8, /device:TPU:32, one launch (start us, length us, event | category | flops | bytes accessed | tf_op | source)
XLA Modules:
  0.0 124.1 jit_solution(18411529057792012520)
XLA Ops:
  2.6 3.1 %collective-permute-start.1 = (f32[1040,128]{1,0:T(8,128)S(1)}, f32[1040,128]{1,0:T(8,128)S(1)}, u32[]{:S(2)}, u32[]{:S(2)}) collective-permute-start(f32[1040,128]{1,0:T(8,128)S(1)} %get-tuple-element.72), channel_id=1, source_target_pairs={{0,3},{1,2},{2,1},{3,0},{4,7},{5,6},{6,5},{7,4},{8,11},{9,10},{10,... | collective-permute-start | bytes 1597448 | tf_op jit(solution)/shard_map/ppermute | solution.py:165
  5.9 1.9 %send_rows.1 = (f32[512,128]{1,0:T(8,128)S(1)}, f32[512,128]{1,0:T(8,128)S(1)}, f32[512,128]{1,0:T(8,128)S(1)}, f32[512,128]{1,0:T(8,128)S(1)}) custom-call(s32[1]{0:T(128)S(6)} %copy.11.lost_ref, f32[4]{0:T(128)} %weight_ref.9, s32[1]{0:T(128)} %bitcast.member_ref, f32[4096,128]{1,0:T(8,128)} %table_ref.6), custom_call_target="tpu_custom_call" | custom-call | flops 2097152 | bytes 2097152 | tf_op jit(solution)/shard_map/send_rows/pallas_call | solution.py:405
  7.8 2.9 %keep_sums.1 = (f32[512,128]{1,0:T(8,128)}, f32[512,128]{1,0:T(8,128)}, f32[512,128]{1,0:T(8,128)S(1)}, f32[512,128]{1,0:T(8,128)S(1)}, f32[1024,128]{1,0:T(8,128)S(1)}) custom-call(s32[1]{0:T(128)S(6)} %copy.11.lost_ref, f32[4]{0:T(128)} %weight_ref.9, s32[1]{0:T(128)} %bitcast.member_ref, f32[4096,128]{1,0:T(8,128)} %table_ref.5), custom_call_target="tpu_custom_call" | custom-call | flops 3145728 | bytes 3145728 | tf_op jit(solution)/shard_map/keep_sums/pallas_call | solution.py:396
  10.7 2.0 %collective-permute-start.4 = (f32[512,128]{1,0:T(8,128)}, f32[512,128]{1,0:T(8,128)}, u32[]{:S(2)}, u32[]{:S(2)}) collective-permute-start(f32[512,128]{1,0:T(8,128)} %get-tuple-element.75), channel_id=1, source_target_pairs={{0,1},{1,0},{2,3},{3,2},{4,5},{5,4},{6,7},{7,6},{8,9},{9,8},{10,11... | collective-permute-start | bytes 786440 | tf_op jit(solution)/shard_map/ppermute | solution.py:165
  13.4 5.5 %collective-permute-done.1.b_ref = f32[1040,128]{1,0:T(8,128)S(1)} collective-permute-done((f32[1040,128]{1,0:T(8,128)S(1)}, f32[1040,128]{1,0:T(8,128)S(1)}, u32[]{:S(2)}, u32[]{:S(2)}) %collective-permute-start.1) | collective-permute-done | bytes 532512 | tf_op jit(solution)/shard_map/ppermute | solution.py:165
  18.9 1.8 %collective-permute-done.a_ref = f32[1040,128]{1,0:T(8,128)S(1)} collective-permute-done((f32[1040,128]{1,0:T(8,128)S(1)}, f32[1040,128]{1,0:T(8,128)S(1)}, u32[]{:S(2)}, u32[]{:S(2)}) %collective-permute-start) | collective-permute-done | bytes 532512 | tf_op jit(solution)/shard_map/ppermute | solution.py:165
  23.4 3.1 %collective-permute-done.4.kept_a_ref = f32[512,128]{1,0:T(8,128)} collective-permute-done((f32[512,128]{1,0:T(8,128)}, f32[512,128]{1,0:T(8,128)}, u32[]{:S(2)}, u32[]{:S(2)}) %collective-permute-start.4) | collective-permute-done | bytes 262176 | tf_op jit(solution)/shard_map/ppermute | solution.py:165
  26.5 2.1 %pending_totals.1 = (f32[1024,128]{1,0:T(8,128)S(1)}, f32[1024,128]{1,0:T(8,128)S(1)}) custom-call(s32[1]{0:T(128)} %bitcast.member_ref, f32[1040,128]{1,0:T(8,128)S(1)} %copy-done.1, f32[1040,128]{1,0:T(8,128)S(1)} %collective-permute-done.a_ref, f32[1040,128]{1,0:T(8,128)S(1)} %collective-permute-done.1.b_ref, f32[1024,128]{1,0:T(8,128)S(1)} %get-tuple-element.79.mine_ref, ...), custom_call_target="tpu_custom_call" | custom-call | flops 4194304 | bytes 4194304 | tf_op jit(solution)/shard_map/pending_totals/pallas_call | solution.py:423
  28.6 3.4 %collective-permute-done.2.c_ref = f32[776,128]{1,0:T(8,128)S(1)} collective-permute-done((f32[776,128]{1,0:T(8,128)S(1)}, f32[776,128]{1,0:T(8,128)S(1)}, u32[]{:S(2)}, u32[]{:S(2)}) %collective-permute-start.2) | collective-permute-done | bytes 397344 | tf_op jit(solution)/shard_map/ppermute | solution.py:165
  33.4 2.5 %place_sums.1 = (f32[2048,128]{1,0:T(8,128)}, f32[1024,128]{1,0:T(8,128)S(1)}, f32[1024,128]{1,0:T(8,128)S(1)}) custom-call(s32[1]{0:T(128)} %bitcast.member_ref, s32[1,1024]{1,0:T(1,128)S(1)} %bitcast_add_fusion.place_ref, f32[1024,128]{1,0:T(8,128)S(1)} %get-tuple-element.94.base_ref, f32[776,128]{1,0:T(8,128)S(1)} %collective-permute-done.2.c_ref, ...), custom_call_target="tpu_custom_call" | custom-call | flops 6291456 | bytes 6291456 | tf_op jit(solution)/shard_map/place_sums/pallas_call | solution.py:437
  35.9 11.2 %all-to-all-start.1 = ((f32[32,64,128]{2,1,0:T(8,128)}), f32[32,64,128]{2,1,0:T(8,128)S(1)}, u32[]{:S(2)}, u32[]{:S(2)}) async-start(f32[32,64,128]{2,1,0:T(8,128)} %bitcast.8), calls=%async_computation.1 | async-start | bytes 2097152 | tf_op jit(solution)/shard_map/all_to_all | solution.py:447
  51.8 1.9 %stay_rows.1 = (f32[512,128]{1,0:T(8,128)S(1)}, f32[512,128]{1,0:T(8,128)S(1)}, f32[1024,128]{1,0:T(8,128)S(1)}) custom-call(s32[1]{0:T(128)S(6)} %copy.11.lost_ref, f32[4]{0:T(128)} %weight_ref.9, s32[1]{0:T(128)} %bitcast.member_ref, f32[4096,128]{1,0:T(8,128)} %table_ref.6), custom_call_target="tpu_custom_call" | custom-call | flops 2097152 | bytes 2097152 | tf_op jit(solution)/shard_map/stay_rows/pallas_call | solution.py:449
  53.8 2.5 %collective-permute-done.8.a_ref = f32[512,128]{1,0:T(8,128)S(1)} collective-permute-done((f32[512,128]{1,0:T(8,128)S(1)}, f32[512,128]{1,0:T(8,128)S(1)}, u32[]{:S(2)}, u32[]{:S(2)}) %collective-permute-start.8) | collective-permute-done | bytes 262176 | tf_op jit(solution)/shard_map/ppermute | solution.py:165
  59.5 2.1 %collective-permute-done.6.a_ref = f32[512,128]{1,0:T(8,128)S(1)} collective-permute-done((f32[512,128]{1,0:T(8,128)S(1)}, f32[512,128]{1,0:T(8,128)S(1)}, u32[]{:S(2)}, u32[]{:S(2)}) %collective-permute-start.6) | collective-permute-done | bytes 262176 | tf_op jit(solution)/shard_map/ppermute | solution.py:165
  63.3 2.8 %collective-permute-done.10.c_ref = f32[512,128]{1,0:T(8,128)S(1)} collective-permute-done((f32[512,128]{1,0:T(8,128)S(1)}, f32[512,128]{1,0:T(8,128)S(1)}, u32[]{:S(2)}, u32[]{:S(2)}) %collective-permute-start.10) | collective-permute-done | bytes 262176 | tf_op jit(solution)/shard_map/ppermute | solution.py:165
  66.1 2.3 %place_rows.1 = f32[2048,128]{1,0:T(8,128)} custom-call(s32[1,1024]{1,0:T(1,128)S(1)} %bitcast_add_fusion.place_ref, f32[1024,128]{1,0:T(8,128)S(1)} %get-tuple-element.85.mine_ref, f32[512,128]{1,0:T(8,128)S(1)} %collective-permute-done.6.a_ref, f32[512,128]{1,0:T(8,128)S(1)} %collective-permute-done.7.b_ref, f32[512,128]{1,0:T(8,128)S(1)} %collective-permute-done.10.c_ref, ...), custom_call_target="tpu_custom_call" | custom-call | flops 6291456 | bytes 6291456 | tf_op jit(solution)/shard_map/place_rows/pallas_call | solution.py:460
  68.4 6.1 %all-to-all-done.1 = f32[32,64,128]{2,1,0:T(8,128)S(1)} async-done(((f32[32,64,128]{2,1,0:T(8,128)}), f32[32,64,128]{2,1,0:T(8,128)S(1)}, u32[]{:S(2)}, u32[]{:S(2)}) %all-to-all-start.1) | async-done | bytes 1048608 | tf_op jit(solution)/shard_map/all_to_all | solution.py:447
  74.5 5.7 %all-to-all-start = ((f32[64,32,128]{2,1,0:T(8,128)}), f32[64,32,128]{2,1,0:T(8,128)S(1)}, u32[]{:S(2)}, u32[]{:S(2)}) async-start(f32[64,32,128]{2,1,0:T(8,128)} %bitcast.5), calls=%async_computation | async-start | bytes 2097152 | tf_op jit(solution)/shard_map/all_to_all | solution.py:463
  84.4 2.8 %collective-permute-start.14 = (f32[512,128]{1,0:T(8,128)S(1)}, f32[512,128]{1,0:T(8,128)S(1)}, u32[]{:S(2)}, u32[]{:S(2)}) collective-permute-start(f32[512,128]{1,0:T(8,128)S(1)} %get-tuple-element.104), channel_id=1, source_target_pairs={{0,2},{1,3},{2,0},{3,1},{4,6},{5,7},{6,4},{7,5},{8,10},{9,11},{10,... | collective-permute-start | bytes 786440 | tf_op jit(solution)/shard_map/ppermute | solution.py:301
  87.3 6.9 %collective-permute-done.13.a_ref = f32[512,128]{1,0:T(8,128)S(1)} collective-permute-done((f32[512,128]{1,0:T(8,128)S(1)}, f32[512,128]{1,0:T(8,128)S(1)}, u32[]{:S(2)}, u32[]{:S(2)}) %collective-permute-start.13) | collective-permute-done | bytes 262176 | tf_op jit(solution)/shard_map/ppermute | solution.py:301
  94.2 4.9 %collective-permute-done.14.b_ref = f32[512,128]{1,0:T(8,128)S(1)} collective-permute-done((f32[512,128]{1,0:T(8,128)S(1)}, f32[512,128]{1,0:T(8,128)S(1)}, u32[]{:S(2)}, u32[]{:S(2)}) %collective-permute-start.14) | collective-permute-done | bytes 262176 | tf_op jit(solution)/shard_map/ppermute | solution.py:301
  100.5 7.6 %all-to-all-done = f32[64,32,128]{2,1,0:T(8,128)S(1)} async-done(((f32[64,32,128]{2,1,0:T(8,128)}), f32[64,32,128]{2,1,0:T(8,128)S(1)}, u32[]{:S(2)}, u32[]{:S(2)}) %all-to-all-start) | async-done | bytes 1048608 | tf_op jit(solution)/shard_map/all_to_all | solution.py:463
  116.2 2.2 %collective-permute-start.20 = (f32[256,128]{1,0:T(8,128)S(1)}, f32[256,128]{1,0:T(8,128)S(1)}, u32[]{:S(2)}, u32[]{:S(2)}) collective-permute-start(f32[256,128]{1,0:T(8,128)S(1)} %get-tuple-element.115), channel_id=1, source_target_pairs={{0,3},{1,2},{2,1},{3,0},{4,7},{5,6},{6,5},{7,4},{8,11},{9,10},{10,... | collective-permute-start | bytes 393224 | tf_op jit(solution)/shard_map/ppermute | solution.py:165
  119.6 2.9 %collective-permute-done.20.c_ref = f32[256,128]{1,0:T(8,128)S(1)} collective-permute-done((f32[256,128]{1,0:T(8,128)S(1)}, f32[256,128]{1,0:T(8,128)S(1)}, u32[]{:S(2)}, u32[]{:S(2)}) %collective-permute-start.20) | collective-permute-done | bytes 131104 | tf_op jit(solution)/shard_map/ppermute | solution.py:165
  (53 shorter events, 32.6 us)
Async XLA Ops:
  2.6 16.3 %collective-permute-start.1 = (f32[1040,128]{1,0:T(8,128)S(1)}, f32[1040,128]{1,0:T(8,128)S(1)}, u32[]{:S(2)}, u32[]{:S(2)}) collective-permute-start(f32[1040,128]{1,0:T(8,128)S(1)} %get-tuple-element.72), channel_id=1, source_target_pairs={{0,3},{1,2},{2,1},{3,0},{4,7},{5,6},{6,5},{7,4},{8,11},{9,10},{10,... | collective-permute-start | bytes 1597448 | tf_op jit(solution)/shard_map/ppermute | solution.py:165
  5.7 15.0 %collective-permute-start = (f32[1040,128]{1,0:T(8,128)S(1)}, f32[1040,128]{1,0:T(8,128)S(1)}, u32[]{:S(2)}, u32[]{:S(2)}) collective-permute-start(f32[1040,128]{1,0:T(8,128)S(1)} %get-tuple-element.71.own_ref), channel_id=1, source_target_pairs={{0,1},{1,0},{2,3},{3,2},{4,5},{5,4},{6,7},{7,6},{8,9},{9,8},{10,11... | collective-permute-start | bytes 1597448 | tf_op jit(solution)/shard_map/ppermute | solution.py:165
  10.7 15.8 %collective-permute-start.4 = (f32[512,128]{1,0:T(8,128)}, f32[512,128]{1,0:T(8,128)}, u32[]{:S(2)}, u32[]{:S(2)}) collective-permute-start(f32[512,128]{1,0:T(8,128)} %get-tuple-element.75), channel_id=1, source_target_pairs={{0,1},{1,0},{2,3},{3,2},{4,5},{5,4},{6,7},{7,6},{8,9},{9,8},{10,11... | collective-permute-start | bytes 786440 | tf_op jit(solution)/shard_map/ppermute | solution.py:165
  12.6 13.8 %collective-permute-start.5 = (f32[512,128]{1,0:T(8,128)}, f32[512,128]{1,0:T(8,128)}, u32[]{:S(2)}, u32[]{:S(2)}) collective-permute-start(f32[512,128]{1,0:T(8,128)} %get-tuple-element.76), channel_id=1, source_target_pairs={{0,3},{1,2},{2,1},{3,0},{4,7},{5,6},{6,5},{7,4},{8,11},{9,10},{10,... | collective-permute-start | bytes 786440 | tf_op jit(solution)/shard_map/ppermute | solution.py:165
  20.8 11.1 %collective-permute-start.2 = (f32[776,128]{1,0:T(8,128)S(1)}, f32[776,128]{1,0:T(8,128)S(1)}, u32[]{:S(2)}, u32[]{:S(2)}) collective-permute-start(f32[776,128]{1,0:T(8,128)S(1)} %get-tuple-element.73), channel_id=1, source_target_pairs={{0,3},{1,2},{2,1},{3,0},{4,7},{5,6},{6,5},{7,4},{8,11},{9,10},{10,... | collective-permute-start | bytes 1191944 | tf_op jit(solution)/shard_map/ppermute | solution.py:165
  22.1 11.3 %collective-permute-start.3 = (f32[776,128]{1,0:T(8,128)S(1)}, f32[776,128]{1,0:T(8,128)S(1)}, u32[]{:S(2)}, u32[]{:S(2)}) collective-permute-start(f32[776,128]{1,0:T(8,128)S(1)} %get-tuple-element.74), channel_id=1, source_target_pairs={{0,1},{1,0},{2,3},{3,2},{4,5},{5,4},{6,7},{7,6},{8,9},{9,8},{10,11... | collective-permute-start | bytes 1191944 | tf_op jit(solution)/shard_map/ppermute | solution.py:165
  35.9 38.6 %all-to-all-start.1 = ((f32[32,64,128]{2,1,0:T(8,128)}), f32[32,64,128]{2,1,0:T(8,128)S(1)}, u32[]{:S(2)}, u32[]{:S(2)}) async-start(f32[32,64,128]{2,1,0:T(8,128)} %bitcast.8), calls=%async_computation.1 | async-start | bytes 2097152 | tf_op jit(solution)/shard_map/all_to_all | solution.py:447
  47.1 9.2 %collective-permute-start.8 = (f32[512,128]{1,0:T(8,128)S(1)}, f32[512,128]{1,0:T(8,128)S(1)}, u32[]{:S(2)}, u32[]{:S(2)}) collective-permute-start(f32[512,128]{1,0:T(8,128)S(1)} %get-tuple-element.90), channel_id=1, source_target_pairs={{0,1},{1,0},{2,3},{3,2},{4,5},{5,4},{6,7},{7,6},{8,9},{9,8},{10,11... | collective-permute-start | bytes 786440 | tf_op jit(solution)/shard_map/ppermute | solution.py:165
  47.5 10.5 %collective-permute-start.9 = (f32[512,128]{1,0:T(8,128)S(1)}, f32[512,128]{1,0:T(8,128)S(1)}, u32[]{:S(2)}, u32[]{:S(2)}) collective-permute-start(f32[512,128]{1,0:T(8,128)S(1)} %get-tuple-element.91), channel_id=1, source_target_pairs={{0,3},{1,2},{2,1},{3,0},{4,7},{5,6},{6,5},{7,4},{8,11},{9,10},{10,... | collective-permute-start | bytes 786440 | tf_op jit(solution)/shard_map/ppermute | solution.py:165
  48.8 12.8 %collective-permute-start.6 = (f32[512,128]{1,0:T(8,128)S(1)}, f32[512,128]{1,0:T(8,128)S(1)}, u32[]{:S(2)}, u32[]{:S(2)}) collective-permute-start(f32[512,128]{1,0:T(8,128)S(1)} %get-tuple-element.86), channel_id=1, source_target_pairs={{0,1},{1,0},{2,3},{3,2},{4,5},{5,4},{6,7},{7,6},{8,9},{9,8},{10,11... | collective-permute-start | bytes 786440 | tf_op jit(solution)/shard_map/ppermute | solution.py:165
  50.1 13.2 %collective-permute-start.7 = (f32[512,128]{1,0:T(8,128)S(1)}, f32[512,128]{1,0:T(8,128)S(1)}, u32[]{:S(2)}, u32[]{:S(2)}) collective-permute-start(f32[512,128]{1,0:T(8,128)S(1)} %get-tuple-element.87), channel_id=1, source_target_pairs={{0,3},{1,2},{2,1},{3,0},{4,7},{5,6},{6,5},{7,4},{8,11},{9,10},{10,... | collective-permute-start | bytes 786440 | tf_op jit(solution)/shard_map/ppermute | solution.py:165
  58.0 8.1 %collective-permute-start.10 = (f32[512,128]{1,0:T(8,128)S(1)}, f32[512,128]{1,0:T(8,128)S(1)}, u32[]{:S(2)}, u32[]{:S(2)}) collective-permute-start(f32[512,128]{1,0:T(8,128)S(1)} %get-tuple-element.92), channel_id=1, source_target_pairs={{0,3},{1,2},{2,1},{3,0},{4,7},{5,6},{6,5},{7,4},{8,11},{9,10},{10,... | collective-permute-start | bytes 786440 | tf_op jit(solution)/shard_map/ppermute | solution.py:165
  59.4 6.7 %collective-permute-start.11 = (f32[512,128]{1,0:T(8,128)S(1)}, f32[512,128]{1,0:T(8,128)S(1)}, u32[]{:S(2)}, u32[]{:S(2)}) collective-permute-start(f32[512,128]{1,0:T(8,128)S(1)} %get-tuple-element.93), channel_id=1, source_target_pairs={{0,1},{1,0},{2,3},{3,2},{4,5},{5,4},{6,7},{7,6},{8,9},{9,8},{10,11... | collective-permute-start | bytes 786440 | tf_op jit(solution)/shard_map/ppermute | solution.py:165
  74.5 33.6 %all-to-all-start = ((f32[64,32,128]{2,1,0:T(8,128)}), f32[64,32,128]{2,1,0:T(8,128)S(1)}, u32[]{:S(2)}, u32[]{:S(2)}) async-start(f32[64,32,128]{2,1,0:T(8,128)} %bitcast.5), calls=%async_computation | async-start | bytes 2097152 | tf_op jit(solution)/shard_map/all_to_all | solution.py:463
  80.3 2.0 %collective-permute-start.12 = (f32[1024,128]{1,0:T(8,128)S(1)}, f32[1024,128]{1,0:T(8,128)S(1)}, u32[]{:S(2)}, u32[]{:S(2)}) collective-permute-start(f32[1024,128]{1,0:T(8,128)S(1)} %other_core_sums.1), channel_id=1, source_target_pairs={{0,4},{4,0},{8,12},{12,8},{16,20},{20,16},{24,28},{28,24},{32,36},... | collective-permute-start | bytes 1572872 | tf_op jit(solution)/shard_map/ppermute | solution.py:345
  83.9 10.3 %collective-permute-start.13 = (f32[512,128]{1,0:T(8,128)S(1)}, f32[512,128]{1,0:T(8,128)S(1)}, u32[]{:S(2)}, u32[]{:S(2)}) collective-permute-start(f32[512,128]{1,0:T(8,128)S(1)} %get-tuple-element.103), channel_id=1, source_target_pairs={{0,1},{1,2},{2,3},{3,0},{4,5},{5,6},{6,7},{7,4},{8,9},{9,10},{10,1... | collective-permute-start | bytes 786440 | tf_op jit(solution)/shard_map/ppermute | solution.py:301
  84.4 14.8 %collective-permute-start.14 = (f32[512,128]{1,0:T(8,128)S(1)}, f32[512,128]{1,0:T(8,128)S(1)}, u32[]{:S(2)}, u32[]{:S(2)}) collective-permute-start(f32[512,128]{1,0:T(8,128)S(1)} %get-tuple-element.104), channel_id=1, source_target_pairs={{0,2},{1,3},{2,0},{3,1},{4,6},{5,7},{6,4},{7,5},{8,10},{9,11},{10,... | collective-permute-start | bytes 786440 | tf_op jit(solution)/shard_map/ppermute | solution.py:301
  87.2 12.5 %collective-permute-start.15 = (f32[512,128]{1,0:T(8,128)S(1)}, f32[512,128]{1,0:T(8,128)S(1)}, u32[]{:S(2)}, u32[]{:S(2)}) collective-permute-start(f32[512,128]{1,0:T(8,128)S(1)} %get-tuple-element.105), channel_id=1, source_target_pairs={{0,3},{1,0},{2,1},{3,2},{4,7},{5,4},{6,5},{7,6},{8,11},{9,8},{10,9... | collective-permute-start | bytes 786440 | tf_op jit(solution)/shard_map/ppermute | solution.py:301
  108.7 6.4 %collective-permute-start.18 = (f32[256,128]{1,0:T(8,128)S(1)}, f32[256,128]{1,0:T(8,128)S(1)}, u32[]{:S(2)}, u32[]{:S(2)}) collective-permute-start(f32[256,128]{1,0:T(8,128)S(1)} %get-tuple-element.113), channel_id=1, source_target_pairs={{0,1},{1,0},{2,3},{3,2},{4,5},{5,4},{6,7},{7,6},{8,9},{9,8},{10,11... | collective-permute-start | bytes 393224 | tf_op jit(solution)/shard_map/ppermute | solution.py:165
  109.2 6.9 %collective-permute-start.19 = (f32[256,128]{1,0:T(8,128)S(1)}, f32[256,128]{1,0:T(8,128)S(1)}, u32[]{:S(2)}, u32[]{:S(2)}) collective-permute-start(f32[256,128]{1,0:T(8,128)S(1)} %get-tuple-element.114), channel_id=1, source_target_pairs={{0,3},{1,2},{2,1},{3,0},{4,7},{5,6},{6,5},{7,4},{8,11},{9,10},{10,... | collective-permute-start | bytes 393224 | tf_op jit(solution)/shard_map/ppermute | solution.py:165
  110.7 8.9 %collective-permute-start.16 = (f32[256,128]{1,0:T(8,128)S(1)}, f32[256,128]{1,0:T(8,128)S(1)}, u32[]{:S(2)}, u32[]{:S(2)}) collective-permute-start(f32[256,128]{1,0:T(8,128)S(1)} %get-tuple-element.109), channel_id=1, source_target_pairs={{0,1},{1,0},{2,3},{3,2},{4,5},{5,4},{6,7},{7,6},{8,9},{9,8},{10,11... | collective-permute-start | bytes 393224 | tf_op jit(solution)/shard_map/ppermute | solution.py:165
  112.0 7.6 %collective-permute-start.17 = (f32[256,128]{1,0:T(8,128)S(1)}, f32[256,128]{1,0:T(8,128)S(1)}, u32[]{:S(2)}, u32[]{:S(2)}) collective-permute-start(f32[256,128]{1,0:T(8,128)S(1)} %get-tuple-element.110), channel_id=1, source_target_pairs={{0,3},{1,2},{2,1},{3,0},{4,7},{5,6},{6,5},{7,4},{8,11},{9,10},{10,... | collective-permute-start | bytes 393224 | tf_op jit(solution)/shard_map/ppermute | solution.py:165
  116.2 6.3 %collective-permute-start.20 = (f32[256,128]{1,0:T(8,128)S(1)}, f32[256,128]{1,0:T(8,128)S(1)}, u32[]{:S(2)}, u32[]{:S(2)}) collective-permute-start(f32[256,128]{1,0:T(8,128)S(1)} %get-tuple-element.115), channel_id=1, source_target_pairs={{0,3},{1,2},{2,1},{3,0},{4,7},{5,6},{6,5},{7,4},{8,11},{9,10},{10,... | collective-permute-start | bytes 393224 | tf_op jit(solution)/shard_map/ppermute | solution.py:165
  118.4 5.0 %collective-permute-start.21 = (f32[256,128]{1,0:T(8,128)S(1)}, f32[256,128]{1,0:T(8,128)S(1)}, u32[]{:S(2)}, u32[]{:S(2)}) collective-permute-start(f32[256,128]{1,0:T(8,128)S(1)} %get-tuple-element.116), channel_id=1, source_target_pairs={{0,1},{1,0},{2,3},{3,2},{4,5},{5,4},{6,7},{7,6},{8,9},{9,8},{10,11... | collective-permute-start | bytes 393224 | tf_op jit(solution)/shard_map/ppermute | solution.py:165
  (5 other events, 30.4 us)

commit v9 on v8

--- a/solution.py
+++ b/solution.py
@@ -142,8 +142,9 @@
     scaled_pieces(table_ref, own, passed_pieces(member) + given_pieces(member), outs, buf_ref, sem_ref)
 
 
-def stay_kernel(lost_ref, weight_ref, member_ref, table_ref, c_ref, d_ref, mine_ref, buf_ref, sem_ref):
+def stay_kernel(lost_ref, weight_ref, member_ref, table_ref, c_ref, d_ref, mine_ref, code_ref, buf_ref, sem_ref):
     member = member_ref[0]
+    code_ref[...] = jnp.full(code_ref.shape, own_code_weight(weight_ref, member), jnp.float32)
     own = lambda: own_row(decode_weights(lost_ref, weight_ref), member)
     half = buf_ref.shape[1]
     outs = [(c_ref, 0), (d_ref, 0), (mine_ref, 0), (mine_ref, half)]
@@ -215,13 +216,13 @@
 
 
 def sums_kernel(
-    member_ref, place_ref, base_ref, c_ref, d_ref, part_ref, out_ref, new_ref, total_ref, both_ref, stage_ref, sem_ref
+    place_ref, base_ref, c_ref, d_ref, part_ref, out_ref, new_ref, total_ref, both_ref, stage_ref, sem_ref
 ):
     count = base_ref.shape[0]
     half = count // 2
     more = jnp.zeros((count, 256), jnp.float32)
     for ref in (c_ref, d_ref):
-        more = add_hits(more, member_ref[0] * count, ref, half, ref.shape[0] - half - 8)
+        more = add_hits(more, lax.axis_index("code") * count, ref, half, ref.shape[0] - half - 8)
     total = part_ref[...] + (more[:, :128] + more[:, 128:])
     total_ref[...] = total
     new = base_ref[...] + jnp.concatenate([c_ref[:half, :], d_ref[:half, :]], axis=0) + total * total
@@ -282,9 +283,9 @@
     out_ref[...] = (mine_ref[...] + a_ref[...]) + (b_ref[...] + c_ref[...])
 
 
-def parity_first_kernel(weight_ref, member_ref, moved_ref, *refs):
-    member = member_ref[0]
-    own = own_code_weight(weight_ref, member)
+def parity_first_kernel(code_ref, moved_ref, *refs):
+    member = lax.axis_index("code")
+    own = code_ref[0:1, :]
     half = refs[0].shape[0]
     outs = [(ref, 0) for ref in refs] + [(refs[-1], half)]
     where = passed_pieces(member) + given_pieces(member) + kept_pieces(member)
@@ -313,7 +314,7 @@
     )(*args)
 
 
-def parity_relayed(name, key, moved, members):
+def parity_relayed(name, code_row, moved, members):
     slots = moved.shape[0]
     quarter = slots // members
     half = quarter // 2
@@ -321,10 +322,10 @@
         parity_first_kernel,
         "parity_first_" + name,
         (flat(half),) * 6 + (flat(quarter),),
-        [SMEM, SMEM, VMEM],
+        [VMEM, VMEM],
         (VMEM,) * 7,
         cost=2 << 20,
-    )(*key, moved)
+    )(code_row, moved)
     back_a, back_b = swap(a, 0, members), swap(b, 1, members)
     stay_a, stay_b = swap(give_a, 0, members), swap(give_b, 1, members)
     send_c, send_d = second("parity_" + name, 0, 1 << 33, keep_c, keep_d, back_a, back_b)
@@ -438,20 +439,20 @@
         sums_kernel,
         "place_sums",
         (flat(slots), flat(share), flat(share)),
-        [SMEM] + [VMEM] * 5,
+        [VMEM] * 5,
         (HBM, VMEM, VMEM),
         cost=6 << 20,
         scratch_shapes=scratch,
-    )(member, place, base_sums, got_c, got_d, part_totals)
+    )(place, base_sums, got_c, got_d, part_totals)
     same_core = [list(range(core, shards, 2)) for core in range(2)]
     got_sums = lax.all_to_all(out_sums, "shard", 0, 0, tiled=True, axis_index_groups=same_core)
 
-    row_c, row_d, mine_rows = kernel_call(
+    row_c, row_d, mine_rows, code_row = kernel_call(
         stay_kernel,
         "stay_rows",
-        (flat(half), flat(half), flat(share)),
+        (flat(half), flat(half), flat(share), flat(8)),
         scalars + [HBM],
-        (VMEM,) * 3,
+        (VMEM,) * 4,
         cost=2 << 20,
         scratch_shapes=buffers(4),
     )(*key, keep_out(late_rows))
@@ -465,7 +466,7 @@
     shard = lax.axis_index("shard").astype(jnp.int32)[None]
     final_sums, parity_sums = parity_direct("sums", (code_weight, member), shard, got_sums, shards, members)
     moved_rows, final_sums, parity_sums = lax.optimization_barrier((moved_rows, final_sums, parity_sums))
-    final_rows, parity_rows = parity_relayed("rows", (code_weight, member), moved_rows, members)
+    final_rows, parity_rows = parity_relayed("rows", code_row, moved_rows, members)
     return (final_rows, final_sums, parity_rows, parity_sums)
 
 

time: 125 us -> 124 us (level)
  no operation moved by 1% of the time
where the time goes in v9:
time: 124 us
  waiting for transfers between devices  60.3 us (49%)
  starting transfers between devices  40.6 us (33%)
  Pallas kernels  19.3 us (16%)
  other arithmetic  1.87 us (2%)
  between operations  1.45 us (1%)
    ppermute x18, waiting for transfers between devices, swap(): return lax.ppermute(array, 'code', pairs)  32.5 us
    ppermute x18, starting transfers between devices, swap(): return lax.ppermute(array, 'code', pairs)  20 us
    ppermute x3, waiting for transfers between devices, turn(): lax.ppermute(array, 'code', [(i, (i + k) % members) for i in range(member...  12.4 us
    all_to_all x1, starting transfers between devices, per_device(): lax.all_to_all(out_sums, 'shard', 0, 0, tiled=True, axis_index_groups=sam...  11.2 us
    all_to_all x1, waiting for transfers between devices, per_device(): moved_rows = lax.all_to_all(out_rows, 'shard', 0, 0, tiled=True)  7.61 us
    all_to_all x1, waiting for transfers between devices, per_device(): lax.all_to_all(out_sums, 'shard', 0, 0, tiled=True, axis_index_groups=sam...  6.09 us
    all_to_all x1, starting transfers between devices, per_device(): moved_rows = lax.all_to_all(out_rows, 'shard', 0, 0, tiled=True)  5.71 us
    ppermute x3, starting transfers between devices, turn(): lax.ppermute(array, 'code', [(i, (i + k) % members) for i in range(member...  3.41 us
  transfers between devices with their start and end apart: 24, of which 20 were waited for; matrix products, arithmetic and copies ran while one was open for 2% of the time, Pallas kernels for 12%

profile of v9, /device:TPU:32, one launch (start us, length us, event | category | flops | bytes accessed | tf_op | source)
XLA Modules:
  0.0 123.6 jit_solution(4433773866198547820)
XLA Ops:
  2.6 3.1 %collective-permute-start.1 = (f32[1040,128]{1,0:T(8,128)S(1)}, f32[1040,128]{1,0:T(8,128)S(1)}, u32[]{:S(2)}, u32[]{:S(2)}) collective-permute-start(f32[1040,128]{1,0:T(8,128)S(1)} %get-tuple-element.73), channel_id=1, source_target_pairs={{0,3},{1,2},{2,1},{3,0},{4,7},{5,6},{6,5},{7,4},{8,11},{9,10},{10,... | collective-permute-start | bytes 1597448 | tf_op jit(solution)/shard_map/ppermute | solution.py:166
  5.9 1.9 %send_rows.1 = (f32[512,128]{1,0:T(8,128)S(1)}, f32[512,128]{1,0:T(8,128)S(1)}, f32[512,128]{1,0:T(8,128)S(1)}, f32[512,128]{1,0:T(8,128)S(1)}) custom-call(s32[1]{0:T(128)S(6)} %copy.11.lost_ref, f32[4]{0:T(128)} %weight_ref.7, s32[1]{0:T(128)} %bitcast.member_ref, f32[4096,128]{1,0:T(8,128)} %table_ref.6), custom_call_target="tpu_custom_call" | custom-call | flops 2097152 | bytes 2097152 | tf_op jit(solution)/shard_map/send_rows/pallas_call | solution.py:406
  7.8 2.9 %keep_sums.1 = (f32[512,128]{1,0:T(8,128)}, f32[512,128]{1,0:T(8,128)}, f32[512,128]{1,0:T(8,128)S(1)}, f32[512,128]{1,0:T(8,128)S(1)}, f32[1024,128]{1,0:T(8,128)S(1)}) custom-call(s32[1]{0:T(128)S(6)} %copy.11.lost_ref, f32[4]{0:T(128)} %weight_ref.7, s32[1]{0:T(128)} %bitcast.member_ref, f32[4096,128]{1,0:T(8,128)} %table_ref.5), custom_call_target="tpu_custom_call" | custom-call | flops 3145728 | bytes 3145728 | tf_op jit(solution)/shard_map/keep_sums/pallas_call | solution.py:397
  10.7 2.0 %collective-permute-start.4 = (f32[512,128]{1,0:T(8,128)}, f32[512,128]{1,0:T(8,128)}, u32[]{:S(2)}, u32[]{:S(2)}) collective-permute-start(f32[512,128]{1,0:T(8,128)} %get-tuple-element.76), channel_id=1, source_target_pairs={{0,1},{1,0},{2,3},{3,2},{4,5},{5,4},{6,7},{7,6},{8,9},{9,8},{10,11... | collective-permute-start | bytes 786440 | tf_op jit(solution)/shard_map/ppermute | solution.py:166
  13.4 5.5 %collective-permute-done.1.b_ref = f32[1040,128]{1,0:T(8,128)S(1)} collective-permute-done((f32[1040,128]{1,0:T(8,128)S(1)}, f32[1040,128]{1,0:T(8,128)S(1)}, u32[]{:S(2)}, u32[]{:S(2)}) %collective-permute-start.1) | collective-permute-done | bytes 532512 | tf_op jit(solution)/shard_map/ppermute | solution.py:166
  18.9 1.8 %collective-permute-done.a_ref = f32[1040,128]{1,0:T(8,128)S(1)} collective-permute-done((f32[1040,128]{1,0:T(8,128)S(1)}, f32[1040,128]{1,0:T(8,128)S(1)}, u32[]{:S(2)}, u32[]{:S(2)}) %collective-permute-start) | collective-permute-done | bytes 532512 | tf_op jit(solution)/shard_map/ppermute | solution.py:166
  23.4 3.1 %collective-permute-done.4.kept_a_ref = f32[512,128]{1,0:T(8,128)} collective-permute-done((f32[512,128]{1,0:T(8,128)}, f32[512,128]{1,0:T(8,128)}, u32[]{:S(2)}, u32[]{:S(2)}) %collective-permute-start.4) | collective-permute-done | bytes 262176 | tf_op jit(solution)/shard_map/ppermute | solution.py:166
  26.5 2.1 %pending_totals.1 = (f32[1024,128]{1,0:T(8,128)S(1)}, f32[1024,128]{1,0:T(8,128)S(1)}) custom-call(s32[1]{0:T(128)} %bitcast.member_ref, f32[1040,128]{1,0:T(8,128)S(1)} %copy-done.1, f32[1040,128]{1,0:T(8,128)S(1)} %collective-permute-done.a_ref, f32[1040,128]{1,0:T(8,128)S(1)} %collective-permute-done.1.b_ref, f32[1024,128]{1,0:T(8,128)S(1)} %get-tuple-element.80.mine_ref, ...), custom_call_target="tpu_custom_call" | custom-call | flops 4194304 | bytes 4194304 | tf_op jit(solution)/shard_map/pending_totals/pallas_call | solution.py:424
  28.6 3.4 %collective-permute-done.2.c_ref = f32[776,128]{1,0:T(8,128)S(1)} collective-permute-done((f32[776,128]{1,0:T(8,128)S(1)}, f32[776,128]{1,0:T(8,128)S(1)}, u32[]{:S(2)}, u32[]{:S(2)}) %collective-permute-start.2) | collective-permute-done | bytes 397344 | tf_op jit(solution)/shard_map/ppermute | solution.py:166
  33.4 2.5 %place_sums.1 = (f32[2048,128]{1,0:T(8,128)}, f32[1024,128]{1,0:T(8,128)S(1)}, f32[1024,128]{1,0:T(8,128)S(1)}) custom-call(s32[1,1024]{1,0:T(1,128)S(1)} %bitcast_add_fusion.place_ref, f32[1024,128]{1,0:T(8,128)S(1)} %get-tuple-element.95.base_ref, f32[776,128]{1,0:T(8,128)S(1)} %collective-permute-done.2.c_ref, ...), custom_call_target="tpu_custom_call" | custom-call | flops 6291456 | bytes 6291456 | tf_op jit(solution)/shard_map/place_sums/pallas_call | solution.py:438
  35.9 11.2 %all-to-all-start.1 = ((f32[32,64,128]{2,1,0:T(8,128)}), f32[32,64,128]{2,1,0:T(8,128)S(1)}, u32[]{:S(2)}, u32[]{:S(2)}) async-start(f32[32,64,128]{2,1,0:T(8,128)} %bitcast.8), calls=%async_computation.1 | async-start | bytes 2097152 | tf_op jit(solution)/shard_map/all_to_all | solution.py:448
  51.9 1.9 %stay_rows.1 = (f32[512,128]{1,0:T(8,128)S(1)}, f32[512,128]{1,0:T(8,128)S(1)}, f32[1024,128]{1,0:T(8,128)S(1)}, f32[8,128]{1,0:T(8,128)S(1)}) custom-call(s32[1]{0:T(128)S(6)} %copy.11.lost_ref, f32[4]{0:T(128)} %weight_ref.7, s32[1]{0:T(128)} %bitcast.member_ref, f32[4096,128]{1,0:T(8,128)} %table_ref.6), custom_call_target="tpu_custom_call" | custom-call | flops 2097152 | bytes 2097152 | tf_op jit(solution)/shard_map/stay_rows/pallas_call | solution.py:450
  53.8 2.5 %collective-permute-done.8.a_ref = f32[512,128]{1,0:T(8,128)S(1)} collective-permute-done((f32[512,128]{1,0:T(8,128)S(1)}, f32[512,128]{1,0:T(8,128)S(1)}, u32[]{:S(2)}, u32[]{:S(2)}) %collective-permute-start.8) | collective-permute-done | bytes 262176 | tf_op jit(solution)/shard_map/ppermute | solution.py:166
  59.5 2.1 %collective-permute-done.6.a_ref = f32[512,128]{1,0:T(8,128)S(1)} collective-permute-done((f32[512,128]{1,0:T(8,128)S(1)}, f32[512,128]{1,0:T(8,128)S(1)}, u32[]{:S(2)}, u32[]{:S(2)}) %collective-permute-start.6) | collective-permute-done | bytes 262176 | tf_op jit(solution)/shard_map/ppermute | solution.py:166
  63.3 2.8 %collective-permute-done.10.c_ref = f32[512,128]{1,0:T(8,128)S(1)} collective-permute-done((f32[512,128]{1,0:T(8,128)S(1)}, f32[512,128]{1,0:T(8,128)S(1)}, u32[]{:S(2)}, u32[]{:S(2)}) %collective-permute-start.10) | collective-permute-done | bytes 262176 | tf_op jit(solution)/shard_map/ppermute | solution.py:166
  66.1 2.3 %place_rows.1 = f32[2048,128]{1,0:T(8,128)} custom-call(s32[1,1024]{1,0:T(1,128)S(1)} %bitcast_add_fusion.place_ref, f32[1024,128]{1,0:T(8,128)S(1)} %get-tuple-element.86.mine_ref, f32[512,128]{1,0:T(8,128)S(1)} %collective-permute-done.6.a_ref, f32[512,128]{1,0:T(8,128)S(1)} %collective-permute-done.7.b_ref, f32[512,128]{1,0:T(8,128)S(1)} %collective-permute-done.10.c_ref, ...), custom_call_target="tpu_custom_call" | custom-call | flops 6291456 | bytes 6291456 | tf_op jit(solution)/shard_map/place_rows/pallas_call | solution.py:461
  68.4 6.1 %all-to-all-done.1 = f32[32,64,128]{2,1,0:T(8,128)S(1)} async-done(((f32[32,64,128]{2,1,0:T(8,128)}), f32[32,64,128]{2,1,0:T(8,128)S(1)}, u32[]{:S(2)}, u32[]{:S(2)}) %all-to-all-start.1) | async-done | bytes 1048608 | tf_op jit(solution)/shard_map/all_to_all | solution.py:448
  74.5 5.7 %all-to-all-start = ((f32[64,32,128]{2,1,0:T(8,128)}), f32[64,32,128]{2,1,0:T(8,128)S(1)}, u32[]{:S(2)}, u32[]{:S(2)}) async-start(f32[64,32,128]{2,1,0:T(8,128)} %bitcast.5), calls=%async_computation | async-start | bytes 2097152 | tf_op jit(solution)/shard_map/all_to_all | solution.py:464
  84.4 2.8 %collective-permute-start.14 = (f32[512,128]{1,0:T(8,128)S(1)}, f32[512,128]{1,0:T(8,128)S(1)}, u32[]{:S(2)}, u32[]{:S(2)}) collective-permute-start(f32[512,128]{1,0:T(8,128)S(1)} %get-tuple-element.105), channel_id=1, source_target_pairs={{0,2},{1,3},{2,0},{3,1},{4,6},{5,7},{6,4},{7,5},{8,10},{9,11},{10,... | collective-permute-start | bytes 786440 | tf_op jit(solution)/shard_map/ppermute | solution.py:302
  87.3 6.9 %collective-permute-done.13.a_ref = f32[512,128]{1,0:T(8,128)S(1)} collective-permute-done((f32[512,128]{1,0:T(8,128)S(1)}, f32[512,128]{1,0:T(8,128)S(1)}, u32[]{:S(2)}, u32[]{:S(2)}) %collective-permute-start.13) | collective-permute-done | bytes 262176 | tf_op jit(solution)/shard_map/ppermute | solution.py:302
  94.2 4.9 %collective-permute-done.14.b_ref = f32[512,128]{1,0:T(8,128)S(1)} collective-permute-done((f32[512,128]{1,0:T(8,128)S(1)}, f32[512,128]{1,0:T(8,128)S(1)}, u32[]{:S(2)}, u32[]{:S(2)}) %collective-permute-start.14) | collective-permute-done | bytes 262176 | tf_op jit(solution)/shard_map/ppermute | solution.py:302
  100.5 7.6 %all-to-all-done = f32[64,32,128]{2,1,0:T(8,128)S(1)} async-done(((f32[64,32,128]{2,1,0:T(8,128)}), f32[64,32,128]{2,1,0:T(8,128)S(1)}, u32[]{:S(2)}, u32[]{:S(2)}) %all-to-all-start) | async-done | bytes 1048608 | tf_op jit(solution)/shard_map/all_to_all | solution.py:464
  115.7 2.2 %collective-permute-start.20 = (f32[256,128]{1,0:T(8,128)S(1)}, f32[256,128]{1,0:T(8,128)S(1)}, u32[]{:S(2)}, u32[]{:S(2)}) collective-permute-start(f32[256,128]{1,0:T(8,128)S(1)} %get-tuple-element.117), channel_id=1, source_target_pairs={{0,3},{1,2},{2,1},{3,0},{4,7},{5,6},{6,5},{7,4},{8,11},{9,10},{10,... | collective-permute-start | bytes 393224 | tf_op jit(solution)/shard_map/ppermute | solution.py:166
  119.1 2.9 %collective-permute-done.20.c_ref = f32[256,128]{1,0:T(8,128)S(1)} collective-permute-done((f32[256,128]{1,0:T(8,128)S(1)}, f32[256,128]{1,0:T(8,128)S(1)}, u32[]{:S(2)}, u32[]{:S(2)}) %collective-permute-start.20) | collective-permute-done | bytes 131104 | tf_op jit(solution)/shard_map/ppermute | solution.py:166
  (53 shorter events, 32.0 us)
Async XLA Ops:
  2.6 16.3 %collective-permute-start.1 = (f32[1040,128]{1,0:T(8,128)S(1)}, f32[1040,128]{1,0:T(8,128)S(1)}, u32[]{:S(2)}, u32[]{:S(2)}) collective-permute-start(f32[1040,128]{1,0:T(8,128)S(1)} %get-tuple-element.73), channel_id=1, source_target_pairs={{0,3},{1,2},{2,1},{3,0},{4,7},{5,6},{6,5},{7,4},{8,11},{9,10},{10,... | collective-permute-start | bytes 1597448 | tf_op jit(solution)/shard_map/ppermute | solution.py:166
  5.7 15.0 %collective-permute-start = (f32[1040,128]{1,0:T(8,128)S(1)}, f32[1040,128]{1,0:T(8,128)S(1)}, u32[]{:S(2)}, u32[]{:S(2)}) collective-permute-start(f32[1040,128]{1,0:T(8,128)S(1)} %get-tuple-element.72.own_ref), channel_id=1, source_target_pairs={{0,1},{1,0},{2,3},{3,2},{4,5},{5,4},{6,7},{7,6},{8,9},{9,8},{10,11... | collective-permute-start | bytes 1597448 | tf_op jit(solution)/shard_map/ppermute | solution.py:166
  10.7 15.8 %collective-permute-start.4 = (f32[512,128]{1,0:T(8,128)}, f32[512,128]{1,0:T(8,128)}, u32[]{:S(2)}, u32[]{:S(2)}) collective-permute-start(f32[512,128]{1,0:T(8,128)} %get-tuple-element.76), channel_id=1, source_target_pairs={{0,1},{1,0},{2,3},{3,2},{4,5},{5,4},{6,7},{7,6},{8,9},{9,8},{10,11... | collective-permute-start | bytes 786440 | tf_op jit(solution)/shard_map/ppermute | solution.py:166
  12.6 13.8 %collective-permute-start.5 = (f32[512,128]{1,0:T(8,128)}, f32[512,128]{1,0:T(8,128)}, u32[]{:S(2)}, u32[]{:S(2)}) collective-permute-start(f32[512,128]{1,0:T(8,128)} %get-tuple-element.77), channel_id=1, source_target_pairs={{0,3},{1,2},{2,1},{3,0},{4,7},{5,6},{6,5},{7,4},{8,11},{9,10},{10,... | collective-permute-start | bytes 786440 | tf_op jit(solution)/shard_map/ppermute | solution.py:166
  20.8 11.1 %collective-permute-start.2 = (f32[776,128]{1,0:T(8,128)S(1)}, f32[776,128]{1,0:T(8,128)S(1)}, u32[]{:S(2)}, u32[]{:S(2)}) collective-permute-start(f32[776,128]{1,0:T(8,128)S(1)} %get-tuple-element.74), channel_id=1, source_target_pairs={{0,3},{1,2},{2,1},{3,0},{4,7},{5,6},{6,5},{7,4},{8,11},{9,10},{10,... | collective-permute-start | bytes 1191944 | tf_op jit(solution)/shard_map/ppermute | solution.py:166
  22.1 11.3 %collective-permute-start.3 = (f32[776,128]{1,0:T(8,128)S(1)}, f32[776,128]{1,0:T(8,128)S(1)}, u32[]{:S(2)}, u32[]{:S(2)}) collective-permute-start(f32[776,128]{1,0:T(8,128)S(1)} %get-tuple-element.75), channel_id=1, source_target_pairs={{0,1},{1,0},{2,3},{3,2},{4,5},{5,4},{6,7},{7,6},{8,9},{9,8},{10,11... | collective-permute-start | bytes 1191944 | tf_op jit(solution)/shard_map/ppermute | solution.py:166
  35.9 38.6 %all-to-all-start.1 = ((f32[32,64,128]{2,1,0:T(8,128)}), f32[32,64,128]{2,1,0:T(8,128)S(1)}, u32[]{:S(2)}, u32[]{:S(2)}) async-start(f32[32,64,128]{2,1,0:T(8,128)} %bitcast.8), calls=%async_computation.1 | async-start | bytes 2097152 | tf_op jit(solution)/shard_map/all_to_all | solution.py:448
  47.1 9.2 %collective-permute-start.8 = (f32[512,128]{1,0:T(8,128)S(1)}, f32[512,128]{1,0:T(8,128)S(1)}, u32[]{:S(2)}, u32[]{:S(2)}) collective-permute-start(f32[512,128]{1,0:T(8,128)S(1)} %get-tuple-element.91), channel_id=1, source_target_pairs={{0,1},{1,0},{2,3},{3,2},{4,5},{5,4},{6,7},{7,6},{8,9},{9,8},{10,11... | collective-permute-start | bytes 786440 | tf_op jit(solution)/shard_map/ppermute | solution.py:166
  47.5 10.5 %collective-permute-start.9 = (f32[512,128]{1,0:T(8,128)S(1)}, f32[512,128]{1,0:T(8,128)S(1)}, u32[]{:S(2)}, u32[]{:S(2)}) collective-permute-start(f32[512,128]{1,0:T(8,128)S(1)} %get-tuple-element.92), channel_id=1, source_target_pairs={{0,3},{1,2},{2,1},{3,0},{4,7},{5,6},{6,5},{7,4},{8,11},{9,10},{10,... | collective-permute-start | bytes 786440 | tf_op jit(solution)/shard_map/ppermute | solution.py:166
  48.8 12.8 %collective-permute-start.6 = (f32[512,128]{1,0:T(8,128)S(1)}, f32[512,128]{1,0:T(8,128)S(1)}, u32[]{:S(2)}, u32[]{:S(2)}) collective-permute-start(f32[512,128]{1,0:T(8,128)S(1)} %get-tuple-element.87), channel_id=1, source_target_pairs={{0,1},{1,0},{2,3},{3,2},{4,5},{5,4},{6,7},{7,6},{8,9},{9,8},{10,11... | collective-permute-start | bytes 786440 | tf_op jit(solution)/shard_map/ppermute | solution.py:166
  50.1 13.2 %collective-permute-start.7 = (f32[512,128]{1,0:T(8,128)S(1)}, f32[512,128]{1,0:T(8,128)S(1)}, u32[]{:S(2)}, u32[]{:S(2)}) collective-permute-start(f32[512,128]{1,0:T(8,128)S(1)} %get-tuple-element.88), channel_id=1, source_target_pairs={{0,3},{1,2},{2,1},{3,0},{4,7},{5,6},{6,5},{7,4},{8,11},{9,10},{10,... | collective-permute-start | bytes 786440 | tf_op jit(solution)/shard_map/ppermute | solution.py:166
  58.0 8.1 %collective-permute-start.10 = (f32[512,128]{1,0:T(8,128)S(1)}, f32[512,128]{1,0:T(8,128)S(1)}, u32[]{:S(2)}, u32[]{:S(2)}) collective-permute-start(f32[512,128]{1,0:T(8,128)S(1)} %get-tuple-element.93), channel_id=1, source_target_pairs={{0,3},{1,2},{2,1},{3,0},{4,7},{5,6},{6,5},{7,4},{8,11},{9,10},{10,... | collective-permute-start | bytes 786440 | tf_op jit(solution)/shard_map/ppermute | solution.py:166
  59.4 6.7 %collective-permute-start.11 = (f32[512,128]{1,0:T(8,128)S(1)}, f32[512,128]{1,0:T(8,128)S(1)}, u32[]{:S(2)}, u32[]{:S(2)}) collective-permute-start(f32[512,128]{1,0:T(8,128)S(1)} %get-tuple-element.94), channel_id=1, source_target_pairs={{0,1},{1,0},{2,3},{3,2},{4,5},{5,4},{6,7},{7,6},{8,9},{9,8},{10,11... | collective-permute-start | bytes 786440 | tf_op jit(solution)/shard_map/ppermute | solution.py:166
  74.5 33.6 %all-to-all-start = ((f32[64,32,128]{2,1,0:T(8,128)}), f32[64,32,128]{2,1,0:T(8,128)S(1)}, u32[]{:S(2)}, u32[]{:S(2)}) async-start(f32[64,32,128]{2,1,0:T(8,128)} %bitcast.5), calls=%async_computation | async-start | bytes 2097152 | tf_op jit(solution)/shard_map/all_to_all | solution.py:464
  80.3 2.0 %collective-permute-start.12 = (f32[1024,128]{1,0:T(8,128)S(1)}, f32[1024,128]{1,0:T(8,128)S(1)}, u32[]{:S(2)}, u32[]{:S(2)}) collective-permute-start(f32[1024,128]{1,0:T(8,128)S(1)} %other_core_sums.1), channel_id=1, source_target_pairs={{0,4},{4,0},{8,12},{12,8},{16,20},{20,16},{24,28},{28,24},{32,36},... | collective-permute-start | bytes 1572872 | tf_op jit(solution)/shard_map/ppermute | solution.py:346
  83.9 10.3 %collective-permute-start.13 = (f32[512,128]{1,0:T(8,128)S(1)}, f32[512,128]{1,0:T(8,128)S(1)}, u32[]{:S(2)}, u32[]{:S(2)}) collective-permute-start(f32[512,128]{1,0:T(8,128)S(1)} %get-tuple-element.104), channel_id=1, source_target_pairs={{0,1},{1,2},{2,3},{3,0},{4,5},{5,6},{6,7},{7,4},{8,9},{9,10},{10,1... | collective-permute-start | bytes 786440 | tf_op jit(solution)/shard_map/ppermute | solution.py:302
  84.4 14.8 %collective-permute-start.14 = (f32[512,128]{1,0:T(8,128)S(1)}, f32[512,128]{1,0:T(8,128)S(1)}, u32[]{:S(2)}, u32[]{:S(2)}) collective-permute-start(f32[512,128]{1,0:T(8,128)S(1)} %get-tuple-element.105), channel_id=1, source_target_pairs={{0,2},{1,3},{2,0},{3,1},{4,6},{5,7},{6,4},{7,5},{8,10},{9,11},{10,... | collective-permute-start | bytes 786440 | tf_op jit(solution)/shard_map/ppermute | solution.py:302
  87.2 12.5 %collective-permute-start.15 = (f32[512,128]{1,0:T(8,128)S(1)}, f32[512,128]{1,0:T(8,128)S(1)}, u32[]{:S(2)}, u32[]{:S(2)}) collective-permute-start(f32[512,128]{1,0:T(8,128)S(1)} %get-tuple-element.106), channel_id=1, source_target_pairs={{0,3},{1,0},{2,1},{3,2},{4,7},{5,4},{6,5},{7,6},{8,11},{9,8},{10,9... | collective-permute-start | bytes 786440 | tf_op jit(solution)/shard_map/ppermute | solution.py:302
  108.2 6.4 %collective-permute-start.18 = (f32[256,128]{1,0:T(8,128)S(1)}, f32[256,128]{1,0:T(8,128)S(1)}, u32[]{:S(2)}, u32[]{:S(2)}) collective-permute-start(f32[256,128]{1,0:T(8,128)S(1)} %get-tuple-element.115), channel_id=1, source_target_pairs={{0,1},{1,0},{2,3},{3,2},{4,5},{5,4},{6,7},{7,6},{8,9},{9,8},{10,11... | collective-permute-start | bytes 393224 | tf_op jit(solution)/shard_map/ppermute | solution.py:166
  108.7 6.9 %collective-permute-start.19 = (f32[256,128]{1,0:T(8,128)S(1)}, f32[256,128]{1,0:T(8,128)S(1)}, u32[]{:S(2)}, u32[]{:S(2)}) collective-permute-start(f32[256,128]{1,0:T(8,128)S(1)} %get-tuple-element.116), channel_id=1, source_target_pairs={{0,3},{1,2},{2,1},{3,0},{4,7},{5,6},{6,5},{7,4},{8,11},{9,10},{10,... | collective-permute-start | bytes 393224 | tf_op jit(solution)/shard_map/ppermute | solution.py:166
  110.2 8.9 %collective-permute-start.16 = (f32[256,128]{1,0:T(8,128)S(1)}, f32[256,128]{1,0:T(8,128)S(1)}, u32[]{:S(2)}, u32[]{:S(2)}) collective-permute-start(f32[256,128]{1,0:T(8,128)S(1)} %get-tuple-element.111), channel_id=1, source_target_pairs={{0,1},{1,0},{2,3},{3,2},{4,5},{5,4},{6,7},{7,6},{8,9},{9,8},{10,11... | collective-permute-start | bytes 393224 | tf_op jit(solution)/shard_map/ppermute | solution.py:166
  111.5 7.6 %collective-permute-start.17 = (f32[256,128]{1,0:T(8,128)S(1)}, f32[256,128]{1,0:T(8,128)S(1)}, u32[]{:S(2)}, u32[]{:S(2)}) collective-permute-start(f32[256,128]{1,0:T(8,128)S(1)} %get-tuple-element.112), channel_id=1, source_target_pairs={{0,3},{1,2},{2,1},{3,0},{4,7},{5,6},{6,5},{7,4},{8,11},{9,10},{10,... | collective-permute-start | bytes 393224 | tf_op jit(solution)/shard_map/ppermute | solution.py:166
  115.7 6.3 %collective-permute-start.20 = (f32[256,128]{1,0:T(8,128)S(1)}, f32[256,128]{1,0:T(8,128)S(1)}, u32[]{:S(2)}, u32[]{:S(2)}) collective-permute-start(f32[256,128]{1,0:T(8,128)S(1)} %get-tuple-element.117), channel_id=1, source_target_pairs={{0,3},{1,2},{2,1},{3,0},{4,7},{5,6},{6,5},{7,4},{8,11},{9,10},{10,... | collective-permute-start | bytes 393224 | tf_op jit(solution)/shard_map/ppermute | solution.py:166
  117.8 5.0 %collective-permute-start.21 = (f32[256,128]{1,0:T(8,128)S(1)}, f32[256,128]{1,0:T(8,128)S(1)}, u32[]{:S(2)}, u32[]{:S(2)}) collective-permute-start(f32[256,128]{1,0:T(8,128)S(1)} %get-tuple-element.118), channel_id=1, source_target_pairs={{0,1},{1,0},{2,3},{3,2},{4,5},{5,4},{6,7},{7,6},{8,9},{9,8},{10,11... | collective-permute-start | bytes 393224 | tf_op jit(solution)/shard_map/ppermute | solution.py:166
  (5 other events, 30.4 us)

commit v10 on v9

--- a/solution.py
+++ b/solution.py
@@ -97,10 +97,10 @@
 
 
 def front_kernel(
-    lost_ref, weight_hbm, member_ref, table_ref, grads_ref, ids_hbm, a_ref, b_ref,
+    lost_ref, weight_hbm, table_ref, grads_ref, ids_hbm, a_ref, b_ref,
     buf_ref, sem_ref, grad_sem, ids_ref, weight_ref, small_sem
 ):
-    member = member_ref[0]
+    member = lax.axis_index("code")
     part, lines = grads_ref.shape[0] // 2, ids_ref.shape[0] // 2
     half = buf_ref.shape[1]
     copies = [pltpu.make_async_copy(ids_hbm, ids_ref, small_sem.at[0])]
@@ -385,13 +385,13 @@
         front_kernel,
         "front_send",
         (flat(half + 2 * part), flat(half + 2 * part)),
-        [SMEM, HBM, SMEM, HBM, HBM, HBM],
+        [SMEM, HBM, HBM, HBM, HBM],
         (VMEM, VMEM),
         cost=3 << 20,
         scratch_shapes=buffers(2)
         + [pltpu.SemaphoreType.DMA((4,)), pltpu.VMEM((entries // 128, 128), jnp.int32)]
         + [pltpu.SMEM((members,), jnp.float32), pltpu.SemaphoreType.DMA((2,))],
-    )(*key, keep_out(adagrad_sums), keep_out(pending_grads), keep_out(pending_rows.reshape(-1, 128)))
+    )(lost_member, key[1], keep_out(adagrad_sums), keep_out(pending_grads), keep_out(pending_rows.reshape(-1, 128)))
     got_a, got_b = swap(send_a, 0, members), swap(send_b, 1, members)
 
     give_a, give_b, keep_c, keep_d, mine_sums = kernel_call(

time: 124 us -> 124 us (level)
  no operation moved by 1% of the time
where the time goes in v10:
time: 124 us
  waiting for transfers between devices  60.3 us (49%)
  starting transfers between devices  40.6 us (33%)
  Pallas kernels  19.3 us (16%)
  other arithmetic  1.87 us (2%)
  between operations  1.43 us (1%)
    ppermute x18, waiting for transfers between devices, swap(): return lax.ppermute(array, 'code', pairs)  32.5 us
    ppermute x18, starting transfers between devices, swap(): return lax.ppermute(array, 'code', pairs)  20 us
    ppermute x3, waiting for transfers between devices, turn(): lax.ppermute(array, 'code', [(i, (i + k) % members) for i in range(member...  12.4 us
    all_to_all x1, starting transfers between devices, per_device(): lax.all_to_all(out_sums, 'shard', 0, 0, tiled=True, axis_index_groups=sam...  11.2 us
    all_to_all x1, waiting for transfers between devices, per_device(): moved_rows = lax.all_to_all(out_rows, 'shard', 0, 0, tiled=True)  7.61 us
    all_to_all x1, waiting for transfers between devices, per_device(): lax.all_to_all(out_sums, 'shard', 0, 0, tiled=True, axis_index_groups=sam...  6.09 us
    all_to_all x1, starting transfers between devices, per_device(): moved_rows = lax.all_to_all(out_rows, 'shard', 0, 0, tiled=True)  5.71 us
    ppermute x3, starting transfers between devices, turn(): lax.ppermute(array, 'code', [(i, (i + k) % members) for i in range(member...  3.41 us
  transfers between devices with their start and end apart: 24, of which 20 were waited for; matrix products, arithmetic and copies ran while one was open for 2% of the time, Pallas kernels for 12%

profile of v10, /device:TPU:32, one launch (start us, length us, event | category | flops | bytes accessed | tf_op | source)
XLA Modules:
  0.0 123.6 jit_solution(14921575283299767063)
XLA Ops:
  2.6 3.1 %collective-permute-start.1 = (f32[1040,128]{1,0:T(8,128)S(1)}, f32[1040,128]{1,0:T(8,128)S(1)}, u32[]{:S(2)}, u32[]{:S(2)}) collective-permute-start(f32[1040,128]{1,0:T(8,128)S(1)} %get-tuple-element.73), channel_id=1, source_target_pairs={{0,3},{1,2},{2,1},{3,0},{4,7},{5,6},{6,5},{7,4},{8,11},{9,10},{10,... | collective-permute-start | bytes 1597448 | tf_op jit(solution)/shard_map/ppermute | solution.py:166
  5.9 1.9 %send_rows.1 = (f32[512,128]{1,0:T(8,128)S(1)}, f32[512,128]{1,0:T(8,128)S(1)}, f32[512,128]{1,0:T(8,128)S(1)}, f32[512,128]{1,0:T(8,128)S(1)}) custom-call(s32[1]{0:T(128)S(6)} %copy.11.lost_ref, f32[4]{0:T(128)} %weight_ref.7, s32[1]{0:T(128)} %bitcast.member_ref, f32[4096,128]{1,0:T(8,128)} %table_ref.6), custom_call_target="tpu_custom_call" | custom-call | flops 2097152 | bytes 2097152 | tf_op jit(solution)/shard_map/send_rows/pallas_call | solution.py:406
  7.8 2.9 %keep_sums.1 = (f32[512,128]{1,0:T(8,128)}, f32[512,128]{1,0:T(8,128)}, f32[512,128]{1,0:T(8,128)S(1)}, f32[512,128]{1,0:T(8,128)S(1)}, f32[1024,128]{1,0:T(8,128)S(1)}) custom-call(s32[1]{0:T(128)S(6)} %copy.11.lost_ref, f32[4]{0:T(128)} %weight_ref.7, s32[1]{0:T(128)} %bitcast.member_ref, f32[4096,128]{1,0:T(8,128)} %table_ref.5), custom_call_target="tpu_custom_call" | custom-call | flops 3145728 | bytes 3145728 | tf_op jit(solution)/shard_map/keep_sums/pallas_call | solution.py:397
  10.7 2.0 %collective-permute-start.4 = (f32[512,128]{1,0:T(8,128)}, f32[512,128]{1,0:T(8,128)}, u32[]{:S(2)}, u32[]{:S(2)}) collective-permute-start(f32[512,128]{1,0:T(8,128)} %get-tuple-element.76), channel_id=1, source_target_pairs={{0,1},{1,0},{2,3},{3,2},{4,5},{5,4},{6,7},{7,6},{8,9},{9,8},{10,11... | collective-permute-start | bytes 786440 | tf_op jit(solution)/shard_map/ppermute | solution.py:166
  13.4 5.5 %collective-permute-done.1.b_ref = f32[1040,128]{1,0:T(8,128)S(1)} collective-permute-done((f32[1040,128]{1,0:T(8,128)S(1)}, f32[1040,128]{1,0:T(8,128)S(1)}, u32[]{:S(2)}, u32[]{:S(2)}) %collective-permute-start.1) | collective-permute-done | bytes 532512 | tf_op jit(solution)/shard_map/ppermute | solution.py:166
  18.9 1.8 %collective-permute-done.a_ref = f32[1040,128]{1,0:T(8,128)S(1)} collective-permute-done((f32[1040,128]{1,0:T(8,128)S(1)}, f32[1040,128]{1,0:T(8,128)S(1)}, u32[]{:S(2)}, u32[]{:S(2)}) %collective-permute-start) | collective-permute-done | bytes 532512 | tf_op jit(solution)/shard_map/ppermute | solution.py:166
  23.4 3.1 %collective-permute-done.4.kept_a_ref = f32[512,128]{1,0:T(8,128)} collective-permute-done((f32[512,128]{1,0:T(8,128)}, f32[512,128]{1,0:T(8,128)}, u32[]{:S(2)}, u32[]{:S(2)}) %collective-permute-start.4) | collective-permute-done | bytes 262176 | tf_op jit(solution)/shard_map/ppermute | solution.py:166
  26.5 2.1 %pending_totals.1 = (f32[1024,128]{1,0:T(8,128)S(1)}, f32[1024,128]{1,0:T(8,128)S(1)}) custom-call(s32[1]{0:T(128)} %bitcast.member_ref, f32[1040,128]{1,0:T(8,128)S(1)} %get-tuple-element.72.own_ref, f32[1040,128]{1,0:T(8,128)S(1)} %collective-permute-done.a_ref, f32[1040,128]{1,0:T(8,128)S(1)} %collective-permute-done.1.b_ref, ...), custom_call_target="tpu_custom_call" | custom-call | flops 4194304 | bytes 4194304 | tf_op jit(solution)/shard_map/pending_totals/pallas_call | solution.py:424
  28.6 3.4 %collective-permute-done.2.c_ref = f32[776,128]{1,0:T(8,128)S(1)} collective-permute-done((f32[776,128]{1,0:T(8,128)S(1)}, f32[776,128]{1,0:T(8,128)S(1)}, u32[]{:S(2)}, u32[]{:S(2)}) %collective-permute-start.2) | collective-permute-done | bytes 397344 | tf_op jit(solution)/shard_map/ppermute | solution.py:166
  33.4 2.5 %place_sums.1 = (f32[2048,128]{1,0:T(8,128)}, f32[1024,128]{1,0:T(8,128)S(1)}, f32[1024,128]{1,0:T(8,128)S(1)}) custom-call(s32[1,1024]{1,0:T(1,128)S(1)} %bitcast_add_fusion.place_ref, f32[1024,128]{1,0:T(8,128)S(1)} %get-tuple-element.95.base_ref, f32[776,128]{1,0:T(8,128)S(1)} %collective-permute-done.2.c_ref, ...), custom_call_target="tpu_custom_call" | custom-call | flops 6291456 | bytes 6291456 | tf_op jit(solution)/shard_map/place_sums/pallas_call | solution.py:438
  35.9 11.2 %all-to-all-start.1 = ((f32[32,64,128]{2,1,0:T(8,128)}), f32[32,64,128]{2,1,0:T(8,128)S(1)}, u32[]{:S(2)}, u32[]{:S(2)}) async-start(f32[32,64,128]{2,1,0:T(8,128)} %bitcast.8), calls=%async_computation.1 | async-start | bytes 2097152 | tf_op jit(solution)/shard_map/all_to_all | solution.py:448
  51.9 1.9 %stay_rows.1 = (f32[512,128]{1,0:T(8,128)S(1)}, f32[512,128]{1,0:T(8,128)S(1)}, f32[1024,128]{1,0:T(8,128)S(1)}, f32[8,128]{1,0:T(8,128)S(1)}) custom-call(s32[1]{0:T(128)S(6)} %copy.11.lost_ref, f32[4]{0:T(128)} %weight_ref.7, s32[1]{0:T(128)} %bitcast.member_ref, f32[4096,128]{1,0:T(8,128)} %table_ref.6), custom_call_target="tpu_custom_call" | custom-call | flops 2097152 | bytes 2097152 | tf_op jit(solution)/shard_map/stay_rows/pallas_call | solution.py:450
  53.8 2.5 %collective-permute-done.8.a_ref = f32[512,128]{1,0:T(8,128)S(1)} collective-permute-done((f32[512,128]{1,0:T(8,128)S(1)}, f32[512,128]{1,0:T(8,128)S(1)}, u32[]{:S(2)}, u32[]{:S(2)}) %collective-permute-start.8) | collective-permute-done | bytes 262176 | tf_op jit(solution)/shard_map/ppermute | solution.py:166
  59.5 2.1 %collective-permute-done.6.a_ref = f32[512,128]{1,0:T(8,128)S(1)} collective-permute-done((f32[512,128]{1,0:T(8,128)S(1)}, f32[512,128]{1,0:T(8,128)S(1)}, u32[]{:S(2)}, u32[]{:S(2)}) %collective-permute-start.6) | collective-permute-done | bytes 262176 | tf_op jit(solution)/shard_map/ppermute | solution.py:166
  63.3 2.8 %collective-permute-done.10.c_ref = f32[512,128]{1,0:T(8,128)S(1)} collective-permute-done((f32[512,128]{1,0:T(8,128)S(1)}, f32[512,128]{1,0:T(8,128)S(1)}, u32[]{:S(2)}, u32[]{:S(2)}) %collective-permute-start.10) | collective-permute-done | bytes 262176 | tf_op jit(solution)/shard_map/ppermute | solution.py:166
  66.1 2.3 %place_rows.1 = f32[2048,128]{1,0:T(8,128)} custom-call(s32[1,1024]{1,0:T(1,128)S(1)} %bitcast_add_fusion.place_ref, f32[1024,128]{1,0:T(8,128)S(1)} %get-tuple-element.86.mine_ref, f32[512,128]{1,0:T(8,128)S(1)} %collective-permute-done.6.a_ref, f32[512,128]{1,0:T(8,128)S(1)} %collective-permute-done.7.b_ref, f32[512,128]{1,0:T(8,128)S(1)} %collective-permute-done.10.c_ref, ...), custom_call_target="tpu_custom_call" | custom-call | flops 6291456 | bytes 6291456 | tf_op jit(solution)/shard_map/place_rows/pallas_call | solution.py:461
  68.4 6.1 %all-to-all-done.1 = f32[32,64,128]{2,1,0:T(8,128)S(1)} async-done(((f32[32,64,128]{2,1,0:T(8,128)}), f32[32,64,128]{2,1,0:T(8,128)S(1)}, u32[]{:S(2)}, u32[]{:S(2)}) %all-to-all-start.1) | async-done | bytes 1048608 | tf_op jit(solution)/shard_map/all_to_all | solution.py:448
  74.5 5.7 %all-to-all-start = ((f32[64,32,128]{2,1,0:T(8,128)}), f32[64,32,128]{2,1,0:T(8,128)S(1)}, u32[]{:S(2)}, u32[]{:S(2)}) async-start(f32[64,32,128]{2,1,0:T(8,128)} %bitcast.5), calls=%async_computation | async-start | bytes 2097152 | tf_op jit(solution)/shard_map/all_to_all | solution.py:464
  84.4 2.8 %collective-permute-start.14 = (f32[512,128]{1,0:T(8,128)S(1)}, f32[512,128]{1,0:T(8,128)S(1)}, u32[]{:S(2)}, u32[]{:S(2)}) collective-permute-start(f32[512,128]{1,0:T(8,128)S(1)} %get-tuple-element.105), channel_id=1, source_target_pairs={{0,2},{1,3},{2,0},{3,1},{4,6},{5,7},{6,4},{7,5},{8,10},{9,11},{10,... | collective-permute-start | bytes 786440 | tf_op jit(solution)/shard_map/ppermute | solution.py:302
  87.3 6.9 %collective-permute-done.13.a_ref = f32[512,128]{1,0:T(8,128)S(1)} collective-permute-done((f32[512,128]{1,0:T(8,128)S(1)}, f32[512,128]{1,0:T(8,128)S(1)}, u32[]{:S(2)}, u32[]{:S(2)}) %collective-permute-start.13) | collective-permute-done | bytes 262176 | tf_op jit(solution)/shard_map/ppermute | solution.py:302
  94.2 4.9 %collective-permute-done.14.b_ref = f32[512,128]{1,0:T(8,128)S(1)} collective-permute-done((f32[512,128]{1,0:T(8,128)S(1)}, f32[512,128]{1,0:T(8,128)S(1)}, u32[]{:S(2)}, u32[]{:S(2)}) %collective-permute-start.14) | collective-permute-done | bytes 262176 | tf_op jit(solution)/shard_map/ppermute | solution.py:302
  100.5 7.6 %all-to-all-done = f32[64,32,128]{2,1,0:T(8,128)S(1)} async-done(((f32[64,32,128]{2,1,0:T(8,128)}), f32[64,32,128]{2,1,0:T(8,128)S(1)}, u32[]{:S(2)}, u32[]{:S(2)}) %all-to-all-start) | async-done | bytes 1048608 | tf_op jit(solution)/shard_map/all_to_all | solution.py:464
  115.7 2.2 %collective-permute-start.20 = (f32[256,128]{1,0:T(8,128)S(1)}, f32[256,128]{1,0:T(8,128)S(1)}, u32[]{:S(2)}, u32[]{:S(2)}) collective-permute-start(f32[256,128]{1,0:T(8,128)S(1)} %get-tuple-element.117), channel_id=1, source_target_pairs={{0,3},{1,2},{2,1},{3,0},{4,7},{5,6},{6,5},{7,4},{8,11},{9,10},{10,... | collective-permute-start | bytes 393224 | tf_op jit(solution)/shard_map/ppermute | solution.py:166
  119.1 2.9 %collective-permute-done.20.c_ref = f32[256,128]{1,0:T(8,128)S(1)} collective-permute-done((f32[256,128]{1,0:T(8,128)S(1)}, f32[256,128]{1,0:T(8,128)S(1)}, u32[]{:S(2)}, u32[]{:S(2)}) %collective-permute-start.20) | collective-permute-done | bytes 131104 | tf_op jit(solution)/shard_map/ppermute | solution.py:166
  (49 shorter events, 32.0 us)
Async XLA Ops:
  2.6 16.3 %collective-permute-start.1 = (f32[1040,128]{1,0:T(8,128)S(1)}, f32[1040,128]{1,0:T(8,128)S(1)}, u32[]{:S(2)}, u32[]{:S(2)}) collective-permute-start(f32[1040,128]{1,0:T(8,128)S(1)} %get-tuple-element.73), channel_id=1, source_target_pairs={{0,3},{1,2},{2,1},{3,0},{4,7},{5,6},{6,5},{7,4},{8,11},{9,10},{10,... | collective-permute-start | bytes 1597448 | tf_op jit(solution)/shard_map/ppermute | solution.py:166
  5.7 15.0 %collective-permute-start = (f32[1040,128]{1,0:T(8,128)S(1)}, f32[1040,128]{1,0:T(8,128)S(1)}, u32[]{:S(2)}, u32[]{:S(2)}) collective-permute-start(f32[1040,128]{1,0:T(8,128)S(1)} %get-tuple-element.72.own_ref), channel_id=1, source_target_pairs={{0,1},{1,0},{2,3},{3,2},{4,5},{5,4},{6,7},{7,6},{8,9},{9,8},{10,11... | collective-permute-start | bytes 1597448 | tf_op jit(solution)/shard_map/ppermute | solution.py:166
  10.7 15.8 %collective-permute-start.4 = (f32[512,128]{1,0:T(8,128)}, f32[512,128]{1,0:T(8,128)}, u32[]{:S(2)}, u32[]{:S(2)}) collective-permute-start(f32[512,128]{1,0:T(8,128)} %get-tuple-element.76), channel_id=1, source_target_pairs={{0,1},{1,0},{2,3},{3,2},{4,5},{5,4},{6,7},{7,6},{8,9},{9,8},{10,11... | collective-permute-start | bytes 786440 | tf_op jit(solution)/shard_map/ppermute | solution.py:166
  12.6 13.9 %collective-permute-start.5 = (f32[512,128]{1,0:T(8,128)}, f32[512,128]{1,0:T(8,128)}, u32[]{:S(2)}, u32[]{:S(2)}) collective-permute-start(f32[512,128]{1,0:T(8,128)} %get-tuple-element.77), channel_id=1, source_target_pairs={{0,3},{1,2},{2,1},{3,0},{4,7},{5,6},{6,5},{7,4},{8,11},{9,10},{10,... | collective-permute-start | bytes 786440 | tf_op jit(solution)/shard_map/ppermute | solution.py:166
  20.9 11.1 %collective-permute-start.2 = (f32[776,128]{1,0:T(8,128)S(1)}, f32[776,128]{1,0:T(8,128)S(1)}, u32[]{:S(2)}, u32[]{:S(2)}) collective-permute-start(f32[776,128]{1,0:T(8,128)S(1)} %get-tuple-element.74), channel_id=1, source_target_pairs={{0,3},{1,2},{2,1},{3,0},{4,7},{5,6},{6,5},{7,4},{8,11},{9,10},{10,... | collective-permute-start | bytes 1191944 | tf_op jit(solution)/shard_map/ppermute | solution.py:166
  22.1 11.3 %collective-permute-start.3 = (f32[776,128]{1,0:T(8,128)S(1)}, f32[776,128]{1,0:T(8,128)S(1)}, u32[]{:S(2)}, u32[]{:S(2)}) collective-permute-start(f32[776,128]{1,0:T(8,128)S(1)} %get-tuple-element.75), channel_id=1, source_target_pairs={{0,1},{1,0},{2,3},{3,2},{4,5},{5,4},{6,7},{7,6},{8,9},{9,8},{10,11... | collective-permute-start | bytes 1191944 | tf_op jit(solution)/shard_map/ppermute | solution.py:166
  35.9 38.6 %all-to-all-start.1 = ((f32[32,64,128]{2,1,0:T(8,128)}), f32[32,64,128]{2,1,0:T(8,128)S(1)}, u32[]{:S(2)}, u32[]{:S(2)}) async-start(f32[32,64,128]{2,1,0:T(8,128)} %bitcast.8), calls=%async_computation.1 | async-start | bytes 2097152 | tf_op jit(solution)/shard_map/all_to_all | solution.py:448
  47.1 9.2 %collective-permute-start.8 = (f32[512,128]{1,0:T(8,128)S(1)}, f32[512,128]{1,0:T(8,128)S(1)}, u32[]{:S(2)}, u32[]{:S(2)}) collective-permute-start(f32[512,128]{1,0:T(8,128)S(1)} %get-tuple-element.91), channel_id=1, source_target_pairs={{0,1},{1,0},{2,3},{3,2},{4,5},{5,4},{6,7},{7,6},{8,9},{9,8},{10,11... | collective-permute-start | bytes 786440 | tf_op jit(solution)/shard_map/ppermute | solution.py:166
  47.5 10.5 %collective-permute-start.9 = (f32[512,128]{1,0:T(8,128)S(1)}, f32[512,128]{1,0:T(8,128)S(1)}, u32[]{:S(2)}, u32[]{:S(2)}) collective-permute-start(f32[512,128]{1,0:T(8,128)S(1)} %get-tuple-element.92), channel_id=1, source_target_pairs={{0,3},{1,2},{2,1},{3,0},{4,7},{5,6},{6,5},{7,4},{8,11},{9,10},{10,... | collective-permute-start | bytes 786440 | tf_op jit(solution)/shard_map/ppermute | solution.py:166
  48.8 12.8 %collective-permute-start.6 = (f32[512,128]{1,0:T(8,128)S(1)}, f32[512,128]{1,0:T(8,128)S(1)}, u32[]{:S(2)}, u32[]{:S(2)}) collective-permute-start(f32[512,128]{1,0:T(8,128)S(1)} %get-tuple-element.87), channel_id=1, source_target_pairs={{0,1},{1,0},{2,3},{3,2},{4,5},{5,4},{6,7},{7,6},{8,9},{9,8},{10,11... | collective-permute-start | bytes 786440 | tf_op jit(solution)/shard_map/ppermute | solution.py:166
  50.1 13.2 %collective-permute-start.7 = (f32[512,128]{1,0:T(8,128)S(1)}, f32[512,128]{1,0:T(8,128)S(1)}, u32[]{:S(2)}, u32[]{:S(2)}) collective-permute-start(f32[512,128]{1,0:T(8,128)S(1)} %get-tuple-element.88), channel_id=1, source_target_pairs={{0,3},{1,2},{2,1},{3,0},{4,7},{5,6},{6,5},{7,4},{8,11},{9,10},{10,... | collective-permute-start | bytes 786440 | tf_op jit(solution)/shard_map/ppermute | solution.py:166
  58.0 8.1 %collective-permute-start.10 = (f32[512,128]{1,0:T(8,128)S(1)}, f32[512,128]{1,0:T(8,128)S(1)}, u32[]{:S(2)}, u32[]{:S(2)}) collective-permute-start(f32[512,128]{1,0:T(8,128)S(1)} %get-tuple-element.93), channel_id=1, source_target_pairs={{0,3},{1,2},{2,1},{3,0},{4,7},{5,6},{6,5},{7,4},{8,11},{9,10},{10,... | collective-permute-start | bytes 786440 | tf_op jit(solution)/shard_map/ppermute | solution.py:166
  59.4 6.7 %collective-permute-start.11 = (f32[512,128]{1,0:T(8,128)S(1)}, f32[512,128]{1,0:T(8,128)S(1)}, u32[]{:S(2)}, u32[]{:S(2)}) collective-permute-start(f32[512,128]{1,0:T(8,128)S(1)} %get-tuple-element.94), channel_id=1, source_target_pairs={{0,1},{1,0},{2,3},{3,2},{4,5},{5,4},{6,7},{7,6},{8,9},{9,8},{10,11... | collective-permute-start | bytes 786440 | tf_op jit(solution)/shard_map/ppermute | solution.py:166
  74.5 33.6 %all-to-all-start = ((f32[64,32,128]{2,1,0:T(8,128)}), f32[64,32,128]{2,1,0:T(8,128)S(1)}, u32[]{:S(2)}, u32[]{:S(2)}) async-start(f32[64,32,128]{2,1,0:T(8,128)} %bitcast.5), calls=%async_computation | async-start | bytes 2097152 | tf_op jit(solution)/shard_map/all_to_all | solution.py:464
  80.3 2.0 %collective-permute-start.12 = (f32[1024,128]{1,0:T(8,128)S(1)}, f32[1024,128]{1,0:T(8,128)S(1)}, u32[]{:S(2)}, u32[]{:S(2)}) collective-permute-start(f32[1024,128]{1,0:T(8,128)S(1)} %other_core_sums.1), channel_id=1, source_target_pairs={{0,4},{4,0},{8,12},{12,8},{16,20},{20,16},{24,28},{28,24},{32,36},... | collective-permute-start | bytes 1572872 | tf_op jit(solution)/shard_map/ppermute | solution.py:346
  83.9 10.3 %collective-permute-start.13 = (f32[512,128]{1,0:T(8,128)S(1)}, f32[512,128]{1,0:T(8,128)S(1)}, u32[]{:S(2)}, u32[]{:S(2)}) collective-permute-start(f32[512,128]{1,0:T(8,128)S(1)} %get-tuple-element.104), channel_id=1, source_target_pairs={{0,1},{1,2},{2,3},{3,0},{4,5},{5,6},{6,7},{7,4},{8,9},{9,10},{10,1... | collective-permute-start | bytes 786440 | tf_op jit(solution)/shard_map/ppermute | solution.py:302
  84.4 14.8 %collective-permute-start.14 = (f32[512,128]{1,0:T(8,128)S(1)}, f32[512,128]{1,0:T(8,128)S(1)}, u32[]{:S(2)}, u32[]{:S(2)}) collective-permute-start(f32[512,128]{1,0:T(8,128)S(1)} %get-tuple-element.105), channel_id=1, source_target_pairs={{0,2},{1,3},{2,0},{3,1},{4,6},{5,7},{6,4},{7,5},{8,10},{9,11},{10,... | collective-permute-start | bytes 786440 | tf_op jit(solution)/shard_map/ppermute | solution.py:302
  87.2 12.5 %collective-permute-start.15 = (f32[512,128]{1,0:T(8,128)S(1)}, f32[512,128]{1,0:T(8,128)S(1)}, u32[]{:S(2)}, u32[]{:S(2)}) collective-permute-start(f32[512,128]{1,0:T(8,128)S(1)} %get-tuple-element.106), channel_id=1, source_target_pairs={{0,3},{1,0},{2,1},{3,2},{4,7},{5,4},{6,5},{7,6},{8,11},{9,8},{10,9... | collective-permute-start | bytes 786440 | tf_op jit(solution)/shard_map/ppermute | solution.py:302
  108.2 6.4 %collective-permute-start.18 = (f32[256,128]{1,0:T(8,128)S(1)}, f32[256,128]{1,0:T(8,128)S(1)}, u32[]{:S(2)}, u32[]{:S(2)}) collective-permute-start(f32[256,128]{1,0:T(8,128)S(1)} %get-tuple-element.115), channel_id=1, source_target_pairs={{0,1},{1,0},{2,3},{3,2},{4,5},{5,4},{6,7},{7,6},{8,9},{9,8},{10,11... | collective-permute-start | bytes 393224 | tf_op jit(solution)/shard_map/ppermute | solution.py:166
  108.7 6.9 %collective-permute-start.19 = (f32[256,128]{1,0:T(8,128)S(1)}, f32[256,128]{1,0:T(8,128)S(1)}, u32[]{:S(2)}, u32[]{:S(2)}) collective-permute-start(f32[256,128]{1,0:T(8,128)S(1)} %get-tuple-element.116), channel_id=1, source_target_pairs={{0,3},{1,2},{2,1},{3,0},{4,7},{5,6},{6,5},{7,4},{8,11},{9,10},{10,... | collective-permute-start | bytes 393224 | tf_op jit(solution)/shard_map/ppermute | solution.py:166
  110.2 8.9 %collective-permute-start.16 = (f32[256,128]{1,0:T(8,128)S(1)}, f32[256,128]{1,0:T(8,128)S(1)}, u32[]{:S(2)}, u32[]{:S(2)}) collective-permute-start(f32[256,128]{1,0:T(8,128)S(1)} %get-tuple-element.111), channel_id=1, source_target_pairs={{0,1},{1,0},{2,3},{3,2},{4,5},{5,4},{6,7},{7,6},{8,9},{9,8},{10,11... | collective-permute-start | bytes 393224 | tf_op jit(solution)/shard_map/ppermute | solution.py:166
  111.5 7.6 %collective-permute-start.17 = (f32[256,128]{1,0:T(8,128)S(1)}, f32[256,128]{1,0:T(8,128)S(1)}, u32[]{:S(2)}, u32[]{:S(2)}) collective-permute-start(f32[256,128]{1,0:T(8,128)S(1)} %get-tuple-element.112), channel_id=1, source_target_pairs={{0,3},{1,2},{2,1},{3,0},{4,7},{5,6},{6,5},{7,4},{8,11},{9,10},{10,... | collective-permute-start | bytes 393224 | tf_op jit(solution)/shard_map/ppermute | solution.py:166
  115.7 6.3 %collective-permute-start.20 = (f32[256,128]{1,0:T(8,128)S(1)}, f32[256,128]{1,0:T(8,128)S(1)}, u32[]{:S(2)}, u32[]{:S(2)}) collective-permute-start(f32[256,128]{1,0:T(8,128)S(1)} %get-tuple-element.117), channel_id=1, source_target_pairs={{0,3},{1,2},{2,1},{3,0},{4,7},{5,6},{6,5},{7,4},{8,11},{9,10},{10,... | collective-permute-start | bytes 393224 | tf_op jit(solution)/shard_map/ppermute | solution.py:166
  117.9 5.0 %collective-permute-start.21 = (f32[256,128]{1,0:T(8,128)S(1)}, f32[256,128]{1,0:T(8,128)S(1)}, u32[]{:S(2)}, u32[]{:S(2)}) collective-permute-start(f32[256,128]{1,0:T(8,128)S(1)} %get-tuple-element.118), channel_id=1, source_target_pairs={{0,1},{1,0},{2,3},{3,2},{4,5},{5,4},{6,7},{7,6},{8,9},{9,8},{10,11... | collective-permute-start | bytes 393224 | tf_op jit(solution)/shard_map/ppermute | solution.py:166
  (3 other events, 16.6 us)

commit v11 on v10

--- a/solution.py
+++ b/solution.py
@@ -433,7 +433,7 @@
     scratch = [
         pltpu.VMEM((share, 256), jnp.bfloat16),
         pltpu.VMEM((slots, 128), jnp.float32),
-        pltpu.SemaphoreType.DMA((4,)),
+        pltpu.SemaphoreType.DMA((2,)),
     ]
     out_sums, new_sums, totals = kernel_call(
         sums_kernel,

time: 124 us -> 124 us (level)
  no operation moved by 1% of the time
where the time goes in v11:
time: 124 us
  waiting for transfers between devices  60.2 us (49%)
  starting transfers between devices  40.4 us (33%)
  Pallas kernels  19.6 us (16%)
  other arithmetic  1.87 us (2%)
  between operations  1.43 us (1%)
    ppermute x18, waiting for transfers between devices, swap(): return lax.ppermute(array, 'code', pairs)  32.5 us
    ppermute x18, starting transfers between devices, swap(): return lax.ppermute(array, 'code', pairs)  20 us
    ppermute x3, waiting for transfers between devices, turn(): lax.ppermute(array, 'code', [(i, (i + k) % members) for i in range(member...  12.4 us
    all_to_all x1, starting transfers between devices, per_device(): lax.all_to_all(out_sums, 'shard', 0, 0, tiled=True, axis_index_groups=sam...  11.2 us
    all_to_all x1, waiting for transfers between devices, per_device(): moved_rows = lax.all_to_all(out_rows, 'shard', 0, 0, tiled=True)  7.61 us
    all_to_all x1, waiting for transfers between devices, per_device(): lax.all_to_all(out_sums, 'shard', 0, 0, tiled=True, axis_index_groups=sam...  5.97 us
    all_to_all x1, starting transfers between devices, per_device(): moved_rows = lax.all_to_all(out_rows, 'shard', 0, 0, tiled=True)  5.53 us
    ppermute x3, starting transfers between devices, turn(): lax.ppermute(array, 'code', [(i, (i + k) % members) for i in range(member...  3.41 us
  transfers between devices with their start and end apart: 24, of which 20 were waited for; matrix products, arithmetic and copies ran while one was open for 2% of the time, Pallas kernels for 12%

profile of v11, /device:TPU:32, one launch (start us, length us, event | category | flops | bytes accessed | tf_op | source)
XLA Modules:
  0.0 123.5 jit_solution(422713487329409721)
XLA Ops:
  2.6 3.1 %collective-permute-start.1 = (f32[1040,128]{1,0:T(8,128)S(1)}, f32[1040,128]{1,0:T(8,128)S(1)}, u32[]{:S(2)}, u32[]{:S(2)}) collective-permute-start(f32[1040,128]{1,0:T(8,128)S(1)} %get-tuple-element.73), channel_id=1, source_target_pairs={{0,3},{1,2},{2,1},{3,0},{4,7},{5,6},{6,5},{7,4},{8,11},{9,10},{10,... | collective-permute-start | bytes 1597448 | tf_op jit(solution)/shard_map/ppermute | solution.py:166
  5.9 1.9 %send_rows.1 = (f32[512,128]{1,0:T(8,128)S(1)}, f32[512,128]{1,0:T(8,128)S(1)}, f32[512,128]{1,0:T(8,128)S(1)}, f32[512,128]{1,0:T(8,128)S(1)}) custom-call(s32[1]{0:T(128)S(6)} %copy.11.lost_ref, f32[4]{0:T(128)} %weight_ref.7, s32[1]{0:T(128)} %bitcast.member_ref, f32[4096,128]{1,0:T(8,128)} %table_ref.6), custom_call_target="tpu_custom_call" | custom-call | flops 2097152 | bytes 2097152 | tf_op jit(solution)/shard_map/send_rows/pallas_call | solution.py:406
  7.8 2.9 %keep_sums.1 = (f32[512,128]{1,0:T(8,128)}, f32[512,128]{1,0:T(8,128)}, f32[512,128]{1,0:T(8,128)S(1)}, f32[512,128]{1,0:T(8,128)S(1)}, f32[1024,128]{1,0:T(8,128)S(1)}) custom-call(s32[1]{0:T(128)S(6)} %copy.11.lost_ref, f32[4]{0:T(128)} %weight_ref.7, s32[1]{0:T(128)} %bitcast.member_ref, f32[4096,128]{1,0:T(8,128)} %table_ref.5), custom_call_target="tpu_custom_call" | custom-call | flops 3145728 | bytes 3145728 | tf_op jit(solution)/shard_map/keep_sums/pallas_call | solution.py:397
  10.7 2.0 %collective-permute-start.4 = (f32[512,128]{1,0:T(8,128)}, f32[512,128]{1,0:T(8,128)}, u32[]{:S(2)}, u32[]{:S(2)}) collective-permute-start(f32[512,128]{1,0:T(8,128)} %get-tuple-element.76), channel_id=1, source_target_pairs={{0,1},{1,0},{2,3},{3,2},{4,5},{5,4},{6,7},{7,6},{8,9},{9,8},{10,11... | collective-permute-start | bytes 786440 | tf_op jit(solution)/shard_map/ppermute | solution.py:166
  13.4 5.5 %collective-permute-done.1.b_ref = f32[1040,128]{1,0:T(8,128)S(1)} collective-permute-done((f32[1040,128]{1,0:T(8,128)S(1)}, f32[1040,128]{1,0:T(8,128)S(1)}, u32[]{:S(2)}, u32[]{:S(2)}) %collective-permute-start.1) | collective-permute-done | bytes 532512 | tf_op jit(solution)/shard_map/ppermute | solution.py:166
  18.9 1.8 %collective-permute-done.a_ref = f32[1040,128]{1,0:T(8,128)S(1)} collective-permute-done((f32[1040,128]{1,0:T(8,128)S(1)}, f32[1040,128]{1,0:T(8,128)S(1)}, u32[]{:S(2)}, u32[]{:S(2)}) %collective-permute-start) | collective-permute-done | bytes 532512 | tf_op jit(solution)/shard_map/ppermute | solution.py:166
  23.4 3.1 %collective-permute-done.4.kept_a_ref = f32[512,128]{1,0:T(8,128)} collective-permute-done((f32[512,128]{1,0:T(8,128)}, f32[512,128]{1,0:T(8,128)}, u32[]{:S(2)}, u32[]{:S(2)}) %collective-permute-start.4) | collective-permute-done | bytes 262176 | tf_op jit(solution)/shard_map/ppermute | solution.py:166
  26.5 2.1 %pending_totals.1 = (f32[1024,128]{1,0:T(8,128)S(1)}, f32[1024,128]{1,0:T(8,128)S(1)}) custom-call(s32[1]{0:T(128)} %bitcast.member_ref, f32[1040,128]{1,0:T(8,128)S(1)} %get-tuple-element.72.own_ref, f32[1040,128]{1,0:T(8,128)S(1)} %collective-permute-done.a_ref, f32[1040,128]{1,0:T(8,128)S(1)} %collective-permute-done.1.b_ref, ...), custom_call_target="tpu_custom_call" | custom-call | flops 4194304 | bytes 4194304 | tf_op jit(solution)/shard_map/pending_totals/pallas_call | solution.py:424
  28.6 3.4 %collective-permute-done.2.c_ref = f32[776,128]{1,0:T(8,128)S(1)} collective-permute-done((f32[776,128]{1,0:T(8,128)S(1)}, f32[776,128]{1,0:T(8,128)S(1)}, u32[]{:S(2)}, u32[]{:S(2)}) %collective-permute-start.2) | collective-permute-done | bytes 397344 | tf_op jit(solution)/shard_map/ppermute | solution.py:166
  33.4 2.6 %place_sums.1 = (f32[2048,128]{1,0:T(8,128)}, f32[1024,128]{1,0:T(8,128)S(1)}, f32[1024,128]{1,0:T(8,128)S(1)}) custom-call(s32[1,1024]{1,0:T(1,128)S(1)} %bitcast_add_fusion.place_ref, f32[1024,128]{1,0:T(8,128)S(1)} %get-tuple-element.95.base_ref, f32[776,128]{1,0:T(8,128)S(1)} %collective-permute-done.2.c_ref, ...), custom_call_target="tpu_custom_call" | custom-call | flops 6291456 | bytes 6291456 | tf_op jit(solution)/shard_map/place_sums/pallas_call | solution.py:438
  36.0 11.2 %all-to-all-start.1 = ((f32[32,64,128]{2,1,0:T(8,128)}), f32[32,64,128]{2,1,0:T(8,128)S(1)}, u32[]{:S(2)}, u32[]{:S(2)}) async-start(f32[32,64,128]{2,1,0:T(8,128)} %bitcast.8), calls=%async_computation.1 | async-start | bytes 2097152 | tf_op jit(solution)/shard_map/all_to_all | solution.py:448
  52.0 1.9 %stay_rows.1 = (f32[512,128]{1,0:T(8,128)S(1)}, f32[512,128]{1,0:T(8,128)S(1)}, f32[1024,128]{1,0:T(8,128)S(1)}, f32[8,128]{1,0:T(8,128)S(1)}) custom-call(s32[1]{0:T(128)S(6)} %copy.11.lost_ref, f32[4]{0:T(128)} %weight_ref.7, s32[1]{0:T(128)} %bitcast.member_ref, f32[4096,128]{1,0:T(8,128)} %table_ref.6), custom_call_target="tpu_custom_call" | custom-call | flops 2097152 | bytes 2097152 | tf_op jit(solution)/shard_map/stay_rows/pallas_call | solution.py:450
  53.9 2.5 %collective-permute-done.8.a_ref = f32[512,128]{1,0:T(8,128)S(1)} collective-permute-done((f32[512,128]{1,0:T(8,128)S(1)}, f32[512,128]{1,0:T(8,128)S(1)}, u32[]{:S(2)}, u32[]{:S(2)}) %collective-permute-start.8) | collective-permute-done | bytes 262176 | tf_op jit(solution)/shard_map/ppermute | solution.py:166
  59.6 2.1 %collective-permute-done.6.a_ref = f32[512,128]{1,0:T(8,128)S(1)} collective-permute-done((f32[512,128]{1,0:T(8,128)S(1)}, f32[512,128]{1,0:T(8,128)S(1)}, u32[]{:S(2)}, u32[]{:S(2)}) %collective-permute-start.6) | collective-permute-done | bytes 262176 | tf_op jit(solution)/shard_map/ppermute | solution.py:166
  63.4 2.8 %collective-permute-done.10.c_ref = f32[512,128]{1,0:T(8,128)S(1)} collective-permute-done((f32[512,128]{1,0:T(8,128)S(1)}, f32[512,128]{1,0:T(8,128)S(1)}, u32[]{:S(2)}, u32[]{:S(2)}) %collective-permute-start.10) | collective-permute-done | bytes 262176 | tf_op jit(solution)/shard_map/ppermute | solution.py:166
  66.2 2.4 %place_rows.1 = f32[2048,128]{1,0:T(8,128)} custom-call(s32[1,1024]{1,0:T(1,128)S(1)} %bitcast_add_fusion.place_ref, f32[1024,128]{1,0:T(8,128)S(1)} %get-tuple-element.86.mine_ref, f32[512,128]{1,0:T(8,128)S(1)} %collective-permute-done.6.a_ref, f32[512,128]{1,0:T(8,128)S(1)} %collective-permute-done.7.b_ref, f32[512,128]{1,0:T(8,128)S(1)} %collective-permute-done.10.c_ref, ...), custom_call_target="tpu_custom_call" | custom-call | flops 6291456 | bytes 6291456 | tf_op jit(solution)/shard_map/place_rows/pallas_call | solution.py:461
  68.7 6.0 %all-to-all-done.1 = f32[32,64,128]{2,1,0:T(8,128)S(1)} async-done(((f32[32,64,128]{2,1,0:T(8,128)}), f32[32,64,128]{2,1,0:T(8,128)S(1)}, u32[]{:S(2)}, u32[]{:S(2)}) %all-to-all-start.1) | async-done | bytes 1048608 | tf_op jit(solution)/shard_map/all_to_all | solution.py:448
  74.6 5.5 %all-to-all-start = ((f32[64,32,128]{2,1,0:T(8,128)}), f32[64,32,128]{2,1,0:T(8,128)S(1)}, u32[]{:S(2)}, u32[]{:S(2)}) async-start(f32[64,32,128]{2,1,0:T(8,128)} %bitcast.5), calls=%async_computation | async-start | bytes 2097152 | tf_op jit(solution)/shard_map/all_to_all | solution.py:464
  84.3 2.8 %collective-permute-start.14 = (f32[512,128]{1,0:T(8,128)S(1)}, f32[512,128]{1,0:T(8,128)S(1)}, u32[]{:S(2)}, u32[]{:S(2)}) collective-permute-start(f32[512,128]{1,0:T(8,128)S(1)} %get-tuple-element.105), channel_id=1, source_target_pairs={{0,2},{1,3},{2,0},{3,1},{4,6},{5,7},{6,4},{7,5},{8,10},{9,11},{10,... | collective-permute-start | bytes 786440 | tf_op jit(solution)/shard_map/ppermute | solution.py:302
  87.3 6.9 %collective-permute-done.13.a_ref = f32[512,128]{1,0:T(8,128)S(1)} collective-permute-done((f32[512,128]{1,0:T(8,128)S(1)}, f32[512,128]{1,0:T(8,128)S(1)}, u32[]{:S(2)}, u32[]{:S(2)}) %collective-permute-start.13) | collective-permute-done | bytes 262176 | tf_op jit(solution)/shard_map/ppermute | solution.py:302
  94.2 4.9 %collective-permute-done.14.b_ref = f32[512,128]{1,0:T(8,128)S(1)} collective-permute-done((f32[512,128]{1,0:T(8,128)S(1)}, f32[512,128]{1,0:T(8,128)S(1)}, u32[]{:S(2)}, u32[]{:S(2)}) %collective-permute-start.14) | collective-permute-done | bytes 262176 | tf_op jit(solution)/shard_map/ppermute | solution.py:302
  100.4 7.6 %all-to-all-done = f32[64,32,128]{2,1,0:T(8,128)S(1)} async-done(((f32[64,32,128]{2,1,0:T(8,128)}), f32[64,32,128]{2,1,0:T(8,128)S(1)}, u32[]{:S(2)}, u32[]{:S(2)}) %all-to-all-start) | async-done | bytes 1048608 | tf_op jit(solution)/shard_map/all_to_all | solution.py:464
  115.6 2.2 %collective-permute-start.20 = (f32[256,128]{1,0:T(8,128)S(1)}, f32[256,128]{1,0:T(8,128)S(1)}, u32[]{:S(2)}, u32[]{:S(2)}) collective-permute-start(f32[256,128]{1,0:T(8,128)S(1)} %get-tuple-element.117), channel_id=1, source_target_pairs={{0,3},{1,2},{2,1},{3,0},{4,7},{5,6},{6,5},{7,4},{8,11},{9,10},{10,... | collective-permute-start | bytes 393224 | tf_op jit(solution)/shard_map/ppermute | solution.py:166
  119.0 2.9 %collective-permute-done.20.c_ref = f32[256,128]{1,0:T(8,128)S(1)} collective-permute-done((f32[256,128]{1,0:T(8,128)S(1)}, f32[256,128]{1,0:T(8,128)S(1)}, u32[]{:S(2)}, u32[]{:S(2)}) %collective-permute-start.20) | collective-permute-done | bytes 131104 | tf_op jit(solution)/shard_map/ppermute | solution.py:166
  (49 shorter events, 32.0 us)
Async XLA Ops:
  2.6 16.3 %collective-permute-start.1 = (f32[1040,128]{1,0:T(8,128)S(1)}, f32[1040,128]{1,0:T(8,128)S(1)}, u32[]{:S(2)}, u32[]{:S(2)}) collective-permute-start(f32[1040,128]{1,0:T(8,128)S(1)} %get-tuple-element.73), channel_id=1, source_target_pairs={{0,3},{1,2},{2,1},{3,0},{4,7},{5,6},{6,5},{7,4},{8,11},{9,10},{10,... | collective-permute-start | bytes 1597448 | tf_op jit(solution)/shard_map/ppermute | solution.py:166
  5.7 15.0 %collective-permute-start = (f32[1040,128]{1,0:T(8,128)S(1)}, f32[1040,128]{1,0:T(8,128)S(1)}, u32[]{:S(2)}, u32[]{:S(2)}) collective-permute-start(f32[1040,128]{1,0:T(8,128)S(1)} %get-tuple-element.72.own_ref), channel_id=1, source_target_pairs={{0,1},{1,0},{2,3},{3,2},{4,5},{5,4},{6,7},{7,6},{8,9},{9,8},{10,11... | collective-permute-start | bytes 1597448 | tf_op jit(solution)/shard_map/ppermute | solution.py:166
  10.7 15.8 %collective-permute-start.4 = (f32[512,128]{1,0:T(8,128)}, f32[512,128]{1,0:T(8,128)}, u32[]{:S(2)}, u32[]{:S(2)}) collective-permute-start(f32[512,128]{1,0:T(8,128)} %get-tuple-element.76), channel_id=1, source_target_pairs={{0,1},{1,0},{2,3},{3,2},{4,5},{5,4},{6,7},{7,6},{8,9},{9,8},{10,11... | collective-permute-start | bytes 786440 | tf_op jit(solution)/shard_map/ppermute | solution.py:166
  12.6 13.9 %collective-permute-start.5 = (f32[512,128]{1,0:T(8,128)}, f32[512,128]{1,0:T(8,128)}, u32[]{:S(2)}, u32[]{:S(2)}) collective-permute-start(f32[512,128]{1,0:T(8,128)} %get-tuple-element.77), channel_id=1, source_target_pairs={{0,3},{1,2},{2,1},{3,0},{4,7},{5,6},{6,5},{7,4},{8,11},{9,10},{10,... | collective-permute-start | bytes 786440 | tf_op jit(solution)/shard_map/ppermute | solution.py:166
  20.9 11.1 %collective-permute-start.2 = (f32[776,128]{1,0:T(8,128)S(1)}, f32[776,128]{1,0:T(8,128)S(1)}, u32[]{:S(2)}, u32[]{:S(2)}) collective-permute-start(f32[776,128]{1,0:T(8,128)S(1)} %get-tuple-element.74), channel_id=1, source_target_pairs={{0,3},{1,2},{2,1},{3,0},{4,7},{5,6},{6,5},{7,4},{8,11},{9,10},{10,... | collective-permute-start | bytes 1191944 | tf_op jit(solution)/shard_map/ppermute | solution.py:166
  22.1 11.3 %collective-permute-start.3 = (f32[776,128]{1,0:T(8,128)S(1)}, f32[776,128]{1,0:T(8,128)S(1)}, u32[]{:S(2)}, u32[]{:S(2)}) collective-permute-start(f32[776,128]{1,0:T(8,128)S(1)} %get-tuple-element.75), channel_id=1, source_target_pairs={{0,1},{1,0},{2,3},{3,2},{4,5},{5,4},{6,7},{7,6},{8,9},{9,8},{10,11... | collective-permute-start | bytes 1191944 | tf_op jit(solution)/shard_map/ppermute | solution.py:166
  36.0 38.6 %all-to-all-start.1 = ((f32[32,64,128]{2,1,0:T(8,128)}), f32[32,64,128]{2,1,0:T(8,128)S(1)}, u32[]{:S(2)}, u32[]{:S(2)}) async-start(f32[32,64,128]{2,1,0:T(8,128)} %bitcast.8), calls=%async_computation.1 | async-start | bytes 2097152 | tf_op jit(solution)/shard_map/all_to_all | solution.py:448
  47.2 9.2 %collective-permute-start.8 = (f32[512,128]{1,0:T(8,128)S(1)}, f32[512,128]{1,0:T(8,128)S(1)}, u32[]{:S(2)}, u32[]{:S(2)}) collective-permute-start(f32[512,128]{1,0:T(8,128)S(1)} %get-tuple-element.91), channel_id=1, source_target_pairs={{0,1},{1,0},{2,3},{3,2},{4,5},{5,4},{6,7},{7,6},{8,9},{9,8},{10,11... | collective-permute-start | bytes 786440 | tf_op jit(solution)/shard_map/ppermute | solution.py:166
  47.6 10.5 %collective-permute-start.9 = (f32[512,128]{1,0:T(8,128)S(1)}, f32[512,128]{1,0:T(8,128)S(1)}, u32[]{:S(2)}, u32[]{:S(2)}) collective-permute-start(f32[512,128]{1,0:T(8,128)S(1)} %get-tuple-element.92), channel_id=1, source_target_pairs={{0,3},{1,2},{2,1},{3,0},{4,7},{5,6},{6,5},{7,4},{8,11},{9,10},{10,... | collective-permute-start | bytes 786440 | tf_op jit(solution)/shard_map/ppermute | solution.py:166
  48.9 12.8 %collective-permute-start.6 = (f32[512,128]{1,0:T(8,128)S(1)}, f32[512,128]{1,0:T(8,128)S(1)}, u32[]{:S(2)}, u32[]{:S(2)}) collective-permute-start(f32[512,128]{1,0:T(8,128)S(1)} %get-tuple-element.87), channel_id=1, source_target_pairs={{0,1},{1,0},{2,3},{3,2},{4,5},{5,4},{6,7},{7,6},{8,9},{9,8},{10,11... | collective-permute-start | bytes 786440 | tf_op jit(solution)/shard_map/ppermute | solution.py:166
  50.2 13.2 %collective-permute-start.7 = (f32[512,128]{1,0:T(8,128)S(1)}, f32[512,128]{1,0:T(8,128)S(1)}, u32[]{:S(2)}, u32[]{:S(2)}) collective-permute-start(f32[512,128]{1,0:T(8,128)S(1)} %get-tuple-element.88), channel_id=1, source_target_pairs={{0,3},{1,2},{2,1},{3,0},{4,7},{5,6},{6,5},{7,4},{8,11},{9,10},{10,... | collective-permute-start | bytes 786440 | tf_op jit(solution)/shard_map/ppermute | solution.py:166
  58.1 8.1 %collective-permute-start.10 = (f32[512,128]{1,0:T(8,128)S(1)}, f32[512,128]{1,0:T(8,128)S(1)}, u32[]{:S(2)}, u32[]{:S(2)}) collective-permute-start(f32[512,128]{1,0:T(8,128)S(1)} %get-tuple-element.93), channel_id=1, source_target_pairs={{0,3},{1,2},{2,1},{3,0},{4,7},{5,6},{6,5},{7,4},{8,11},{9,10},{10,... | collective-permute-start | bytes 786440 | tf_op jit(solution)/shard_map/ppermute | solution.py:166
  59.5 6.7 %collective-permute-start.11 = (f32[512,128]{1,0:T(8,128)S(1)}, f32[512,128]{1,0:T(8,128)S(1)}, u32[]{:S(2)}, u32[]{:S(2)}) collective-permute-start(f32[512,128]{1,0:T(8,128)S(1)} %get-tuple-element.94), channel_id=1, source_target_pairs={{0,1},{1,0},{2,3},{3,2},{4,5},{5,4},{6,7},{7,6},{8,9},{9,8},{10,11... | collective-permute-start | bytes 786440 | tf_op jit(solution)/shard_map/ppermute | solution.py:166
  74.6 33.4 %all-to-all-start = ((f32[64,32,128]{2,1,0:T(8,128)}), f32[64,32,128]{2,1,0:T(8,128)S(1)}, u32[]{:S(2)}, u32[]{:S(2)}) async-start(f32[64,32,128]{2,1,0:T(8,128)} %bitcast.5), calls=%async_computation | async-start | bytes 2097152 | tf_op jit(solution)/shard_map/all_to_all | solution.py:464
  80.2 2.0 %collective-permute-start.12 = (f32[1024,128]{1,0:T(8,128)S(1)}, f32[1024,128]{1,0:T(8,128)S(1)}, u32[]{:S(2)}, u32[]{:S(2)}) collective-permute-start(f32[1024,128]{1,0:T(8,128)S(1)} %other_core_sums.1), channel_id=1, source_target_pairs={{0,4},{4,0},{8,12},{12,8},{16,20},{20,16},{24,28},{28,24},{32,36},... | collective-permute-start | bytes 1572872 | tf_op jit(solution)/shard_map/ppermute | solution.py:346
  83.9 10.3 %collective-permute-start.13 = (f32[512,128]{1,0:T(8,128)S(1)}, f32[512,128]{1,0:T(8,128)S(1)}, u32[]{:S(2)}, u32[]{:S(2)}) collective-permute-start(f32[512,128]{1,0:T(8,128)S(1)} %get-tuple-element.104), channel_id=1, source_target_pairs={{0,1},{1,2},{2,3},{3,0},{4,5},{5,6},{6,7},{7,4},{8,9},{9,10},{10,1... | collective-permute-start | bytes 786440 | tf_op jit(solution)/shard_map/ppermute | solution.py:302
  84.3 14.8 %collective-permute-start.14 = (f32[512,128]{1,0:T(8,128)S(1)}, f32[512,128]{1,0:T(8,128)S(1)}, u32[]{:S(2)}, u32[]{:S(2)}) collective-permute-start(f32[512,128]{1,0:T(8,128)S(1)} %get-tuple-element.105), channel_id=1, source_target_pairs={{0,2},{1,3},{2,0},{3,1},{4,6},{5,7},{6,4},{7,5},{8,10},{9,11},{10,... | collective-permute-start | bytes 786440 | tf_op jit(solution)/shard_map/ppermute | solution.py:302
  87.1 12.5 %collective-permute-start.15 = (f32[512,128]{1,0:T(8,128)S(1)}, f32[512,128]{1,0:T(8,128)S(1)}, u32[]{:S(2)}, u32[]{:S(2)}) collective-permute-start(f32[512,128]{1,0:T(8,128)S(1)} %get-tuple-element.106), channel_id=1, source_target_pairs={{0,3},{1,0},{2,1},{3,2},{4,7},{5,4},{6,5},{7,6},{8,11},{9,8},{10,9... | collective-permute-start | bytes 786440 | tf_op jit(solution)/shard_map/ppermute | solution.py:302
  108.1 6.4 %collective-permute-start.18 = (f32[256,128]{1,0:T(8,128)S(1)}, f32[256,128]{1,0:T(8,128)S(1)}, u32[]{:S(2)}, u32[]{:S(2)}) collective-permute-start(f32[256,128]{1,0:T(8,128)S(1)} %get-tuple-element.115), channel_id=1, source_target_pairs={{0,1},{1,0},{2,3},{3,2},{4,5},{5,4},{6,7},{7,6},{8,9},{9,8},{10,11... | collective-permute-start | bytes 393224 | tf_op jit(solution)/shard_map/ppermute | solution.py:166
  108.6 6.9 %collective-permute-start.19 = (f32[256,128]{1,0:T(8,128)S(1)}, f32[256,128]{1,0:T(8,128)S(1)}, u32[]{:S(2)}, u32[]{:S(2)}) collective-permute-start(f32[256,128]{1,0:T(8,128)S(1)} %get-tuple-element.116), channel_id=1, source_target_pairs={{0,3},{1,2},{2,1},{3,0},{4,7},{5,6},{6,5},{7,4},{8,11},{9,10},{10,... | collective-permute-start | bytes 393224 | tf_op jit(solution)/shard_map/ppermute | solution.py:166
  110.1 8.9 %collective-permute-start.16 = (f32[256,128]{1,0:T(8,128)S(1)}, f32[256,128]{1,0:T(8,128)S(1)}, u32[]{:S(2)}, u32[]{:S(2)}) collective-permute-start(f32[256,128]{1,0:T(8,128)S(1)} %get-tuple-element.111), channel_id=1, source_target_pairs={{0,1},{1,0},{2,3},{3,2},{4,5},{5,4},{6,7},{7,6},{8,9},{9,8},{10,11... | collective-permute-start | bytes 393224 | tf_op jit(solution)/shard_map/ppermute | solution.py:166
  111.4 7.6 %collective-permute-start.17 = (f32[256,128]{1,0:T(8,128)S(1)}, f32[256,128]{1,0:T(8,128)S(1)}, u32[]{:S(2)}, u32[]{:S(2)}) collective-permute-start(f32[256,128]{1,0:T(8,128)S(1)} %get-tuple-element.112), channel_id=1, source_target_pairs={{0,3},{1,2},{2,1},{3,0},{4,7},{5,6},{6,5},{7,4},{8,11},{9,10},{10,... | collective-permute-start | bytes 393224 | tf_op jit(solution)/shard_map/ppermute | solution.py:166
  115.6 6.3 %collective-permute-start.20 = (f32[256,128]{1,0:T(8,128)S(1)}, f32[256,128]{1,0:T(8,128)S(1)}, u32[]{:S(2)}, u32[]{:S(2)}) collective-permute-start(f32[256,128]{1,0:T(8,128)S(1)} %get-tuple-element.117), channel_id=1, source_target_pairs={{0,3},{1,2},{2,1},{3,0},{4,7},{5,6},{6,5},{7,4},{8,11},{9,10},{10,... | collective-permute-start | bytes 393224 | tf_op jit(solution)/shard_map/ppermute | solution.py:166
  117.8 5.0 %collective-permute-start.21 = (f32[256,128]{1,0:T(8,128)S(1)}, f32[256,128]{1,0:T(8,128)S(1)}, u32[]{:S(2)}, u32[]{:S(2)}) collective-permute-start(f32[256,128]{1,0:T(8,128)S(1)} %get-tuple-element.118), channel_id=1, source_target_pairs={{0,1},{1,0},{2,3},{3,2},{4,5},{5,4},{6,7},{7,6},{8,9},{9,8},{10,11... | collective-permute-start | bytes 393224 | tf_op jit(solution)/shard_map/ppermute | solution.py:166
  (3 other events, 16.3 us)
